TPU v7x, 32 devices: a whole 2x2x4 slice. The times are simulated.
32 devices in a mesh: rep: 4 (over z), sec: 2 (over x), mdl: 4 (over y, core).
Axes of the slice: x: 2, y: 2, z: 4, core: 2. Of those that a mesh axis runs over, the one named last changes fastest.
Arguments:
- obs: bfloat16 [2, 2048, 1536], P('sec', 'rep'), may hold values from -6 to 6
- a_query: bfloat16 [1536, 1536], P(None, 'mdl'), may hold values from -0.15309311 to 0.15309311
- a_keyval: bfloat16 [2, 1536, 512], P(None, None, 'mdl'), may hold values from -0.15309311 to 0.15309311
- a_out: bfloat16 [1536, 1536], P('mdl'), may hold values from -0.15625 to 0.15625
- w_policy: bfloat16 [1536, 128], replicated, may hold values from -0.15625 to 0.15625
- c_in: bfloat16 [1536, 2048], P(None, 'mdl'), may hold values from -0.15309311 to 0.15309311
- c_query: bfloat16 [2048, 2048], P(None, 'mdl'), may hold values from -0.13258252 to 0.13258252
- c_keyval: bfloat16 [2, 2048, 512], P(None, None, 'mdl'), may hold values from -0.13258252 to 0.13258252
- c_out: bfloat16 [2048, 2048], P('mdl'), may hold values from -0.125 to 0.125
- w_value: bfloat16 [2048], replicated, may hold values from -0.110485435 to 0.110485435
- actions: int32 [2, 2048], P('sec', 'rep'), may hold values from 0 to 127
- advantages: float32 [2, 2048], P('sec', 'rep'), may hold values from -6 to 6
- old_logp: float32 [2, 2048], P('sec', 'rep'), may hold values from -7 to -4
- returns: float32 [2, 2048], P('sec', 'rep'), may hold values from -6 to 6
- robot_count: int32 [2], replicated, may hold values from 512 to 2048, as said below
Outputs:
- values: float32 [2, 2048], P('sec', ('rep', 'mdl'))
- grad_a_out: float32 [1536, 1536], P('mdl')
- grad_c_out: float32 [2048, 2048], P('mdl')
Inputs may be any that keep to these rules, and one draw needn't show every extreme that they name: `robot_count`: one of the two micro-batches holds all 2048 robots, the other at least 512; live robots are the first ones.
All inputs are finite; a program needn't handle non-finite values.
Results may differ from a plain program's by a relative error of at most 0.023.
Values may be sent and summed in bfloat16 or wider, within the bound.
No kernel may reach another device: no remote copies, remote signals or barrier semaphores. Data moves between devices by JAX's collectives and lax.ppermute only.
A program may use at most 128 MiB of HBM per device.

v0:
```python
import math

import jax
import jax.numpy as jnp
from jax import lax
from jax.sharding import PartitionSpec as P

HEAD = 128


epsilon = 1e-05
clip_range = 0.2
masked_score = -1e30


def rms_normed(values_in):
    return values_in * lax.rsqrt(jnp.mean(values_in * values_in, axis=-1, keepdims=True) + epsilon)


def norm_backward(source, normed, grad_in):
    factor = lax.rsqrt(jnp.mean(source * source, axis=-1, keepdims=True) + epsilon)
    return factor * (grad_in - normed * jnp.mean(grad_in * normed, axis=-1, keepdims=True))


def project(source, w_query, w_keyval):
    normed = rms_normed(source).astype(jnp.bfloat16)
    queries = (
        jnp.dot(normed, w_query, preferred_element_type=jnp.float32) * HEAD ** (-0.5)
    ).astype(jnp.bfloat16)
    keyval = jnp.einsum("rd,cdk->crk", normed, w_keyval, preferred_element_type=jnp.float32).astype(
        jnp.bfloat16
    )
    return (queries, keyval)


def policy_backward(hidden, action_ids, advantage, old_values, live_mask, live_total, w_policy):
    source = hidden.astype(jnp.float32)
    normed = rms_normed(source)
    logits = jnp.dot(normed.astype(jnp.bfloat16), w_policy, preferred_element_type=jnp.float32)
    log_probs = jax.nn.log_softmax(logits, axis=-1)
    onehot = (action_ids[:, None] == lax.broadcasted_iota(jnp.int32, logits.shape, 1)).astype(
        jnp.float32
    )
    chosen = jnp.sum(onehot * log_probs, axis=-1)
    prob_ratio = jnp.exp(chosen - old_values)
    plain_term = prob_ratio * advantage
    bounded = jnp.clip(prob_ratio, 1.0 - clip_range, 1.0 + clip_range) * advantage
    slope_term = jnp.where(
        live_mask & (plain_term <= bounded), -plain_term / live_total, jnp.float32(0.0)
    )
    dlogits = slope_term[:, None] * (onehot - jnp.exp(log_probs))
    dnormed = jnp.dot(dlogits, w_policy.astype(jnp.float32).T, precision=lax.Precision.HIGHEST)
    return norm_backward(source, normed, dnormed)


def value_backward(mixed_out, target, live_mask, live_total, w_value):
    normed = rms_normed(mixed_out)
    value_pred = jnp.dot(normed.astype(jnp.bfloat16), w_value, preferred_element_type=jnp.float32)
    slope_term = jnp.where(live_mask, value_pred - target, jnp.float32(0.0)) / live_total
    dnormed = slope_term[:, None] * w_value.astype(jnp.float32)[None, :]
    return (value_pred, norm_backward(mixed_out, normed, dnormed))


def split_heads(queries, kv_heads):
    row_count = queries.shape[0]
    groups = queries.shape[1] // HEAD // kv_heads
    return queries.reshape(row_count, kv_heads, groups, HEAD)


def start_state(heads_in):
    row_count, kv_heads, groups, _ = heads_in.shape
    row_top = jnp.full((kv_heads, groups, row_count), masked_score, jnp.float32)
    row_sum = jnp.zeros((kv_heads, groups, row_count), jnp.float32)
    acc_sum = jnp.zeros((kv_heads, groups, row_count, HEAD), jnp.float32)
    return (row_top, row_sum, acc_sum)


def make_fold(heads_in, robot_total, carried, piece):
    kv_heads = heads_in.shape[1]
    piece_rows = piece.shape[1]
    block_rows = math.gcd(piece_rows, 512)
    block_count = piece_rows // block_rows
    key_blocks = piece[0].reshape(block_count, block_rows, kv_heads, HEAD)
    value_blocks = piece[1].reshape(block_count, block_rows, kv_heads, HEAD)

    def absorb(inner, block_item):
        block_index, key_block, value_block = block_item
        first_key = block_index * block_rows
        row_top, row_sum, acc_sum = inner
        scores = jnp.einsum(
            "rkgd,jkd->kgrj", heads_in, key_block, preferred_element_type=jnp.float32
        )
        key_live = first_key + lax.iota(jnp.int32, block_rows) < robot_total
        scores = jnp.where(key_live, scores, masked_score)
        new_top = jnp.maximum(row_top, jnp.max(scores, axis=-1))
        rescale = jnp.exp(row_top - new_top)
        weights = jnp.exp(scores - new_top[..., None])
        row_sum = row_sum * rescale + jnp.sum(weights, axis=-1)
        value_float = value_block.astype(jnp.float32)
        acc_sum = acc_sum * rescale[..., None] + jnp.einsum(
            "kgrj,jkd->kgrd", weights, value_float, precision=lax.Precision.HIGHEST
        )
        return ((new_top, row_sum, acc_sum), None)

    result, _ = lax.scan(
        absorb, carried, (jnp.arange(block_count, dtype=jnp.int32), key_blocks, value_blocks)
    )
    return result


def finish_heads(carried):
    _, row_sum, acc_sum = carried
    combined = acc_sum / row_sum[..., None]
    kv_heads, groups, row_count, _ = combined.shape
    return (
        jnp.transpose(combined, (2, 0, 1, 3))
        .reshape(row_count, kv_heads * groups * HEAD)
        .astype(jnp.bfloat16)
    )


def on_device(
    obs,
    a_query,
    a_keyval,
    a_out,
    w_policy,
    c_in,
    c_query,
    c_keyval,
    c_out,
    w_value,
    actions,
    advantages,
    old_logp,
    returns,
    robot_count,
):
    row_count = obs.shape[1]
    batch_index = lax.axis_index("sec")
    robot_total = robot_count[batch_index]
    live_total = jnp.sum(robot_count).astype(jnp.float32)
    first_row = lax.axis_index("rep") * row_count
    live_mask = first_row + lax.iota(jnp.int32, row_count) < robot_total
    mdl_count = lax.axis_size("mdl")
    part_rows = row_count // mdl_count
    row_start = lax.axis_index("mdl") * part_rows
    obs_float = obs[0].astype(jnp.float32)
    queries, keyval = project(obs_float, a_query, a_keyval)
    heads_a = split_heads(queries, keyval.shape[2] // HEAD)
    state_a = make_fold(
        heads_a,
        robot_total,
        start_state(heads_a),
        lax.all_gather(keyval, "rep", axis=1, tiled=True),
    )
    attended = finish_heads(state_a)
    mixed_sum = lax.psum(jnp.dot(attended, a_out, preferred_element_type=jnp.float32), "mdl")
    hidden = (obs_float + mixed_sum).astype(jnp.bfloat16)
    dhidden = policy_backward(
        hidden, actions[0], advantages[0], old_logp[0], live_mask, live_total, w_policy
    ).astype(jnp.bfloat16)
    actor_grad = jnp.einsum("rh,rd->hd", attended, dhidden, preferred_element_type=jnp.float32)
    embed_part = jnp.dot(hidden, c_in, preferred_element_type=jnp.float32).astype(jnp.bfloat16)
    embedded = lax.all_gather(embed_part, "mdl", axis=1, tiled=True)
    embed_float = embedded.astype(jnp.float32)
    critic_queries, critic_keyval = project(embed_float, c_query, c_keyval)
    heads_c = split_heads(critic_queries, critic_keyval.shape[2] // HEAD)
    state_c = make_fold(
        heads_c,
        robot_total,
        start_state(heads_c),
        lax.all_gather(critic_keyval, "rep", axis=1, tiled=True),
    )
    critic_attended = finish_heads(state_c)
    critic_sum = lax.psum(
        jnp.dot(critic_attended, c_out, preferred_element_type=jnp.float32).astype(jnp.bfloat16),
        "mdl",
    ).astype(jnp.float32)
    value_pred, dmixed = value_backward(
        embed_float + critic_sum, returns[0], live_mask, live_total, w_value
    )
    value_part = lax.dynamic_slice_in_dim(value_pred, row_start, part_rows, 0)
    dmixed_all = dmixed.astype(jnp.bfloat16)
    critic_grad = jnp.einsum(
        "rh,rd->hd", critic_attended, dmixed_all, preferred_element_type=jnp.float32
    )
    actor_summed, critic_summed = (
        lax.psum(actor_grad.astype(jnp.bfloat16), ("rep", "sec")).astype(jnp.float32),
        lax.psum(critic_grad.astype(jnp.bfloat16), ("rep", "sec")).astype(jnp.float32),
    )
    return (value_part[None, :], actor_summed, critic_summed)


def solution(mesh):
    return jax.shard_map(
        on_device,
        mesh=mesh,
        in_specs=(
            P("sec", "rep", None),
            P(None, "mdl"),
            P(None, None, "mdl"),
            P("mdl", None),
            P(),
            P(None, "mdl"),
            P(None, "mdl"),
            P(None, None, "mdl"),
            P("mdl", None),
            P(),
            P("sec", "rep"),
            P("sec", "rep"),
            P("sec", "rep"),
            P("sec", "rep"),
            P(),
        ),
        out_specs=(P("sec", ("rep", "mdl")), P("mdl", None), P("mdl", None)),
        check_vma=False,
    )
```

profile of v0, /device:TPU:0, one launch (start us, length us, event | category | flops | bytes accessed | tf_op | source)
XLA Modules:
  0.0 506.0 jit_solution(5576411614513911845)
XLA Ops:
  12.2 3.4 fusion.85
  17.4 25.5 %all-gather.4.cloned.1.call-done = bf16[2,2048,128]{2,1,0:T(8,128)(2,1)} async-done(((bf16[2,512,128]{2,1,0:T(8,128)(2,1)}), bf16[2,2048,128]{2,1,0:T(8,128)(2,1)}) %all-gather.4.cloned.1.call-update) | async-done | bytes 1048592 | tf_op jit(solution)/shard_map/all_gather | solution.py:155
  45.2 47.0 %while.30 = (s32[]{:T(128)}, f32[1,3,512]{2,1,0:T(4,128)S(1)}, f32[1,3,512]{2,1,0:T(4,128)S(1)}, f32[1,3,512,128]{3,2,1,0:T(8,128)S(1)}, s32[4]{0:T(128)S(1)}, /...) while((s32[]{:T(128)}, f32[1,3,512]{2,1,0:T(4,128)S(1)}, ...), condition=%wide.region_4.5_spmd.clone, body=%wide.region_1.4_spmd.clone.sunk | while | flops 1415391232 | bytes 24348876 | solution.py:105
  53.0 3.9 fusion.148
  64.7 3.9 fusion.148
  76.5 3.9 fusion.148
  88.3 3.9 fusion.148
  94.6 3.9 fusion.118
  98.6 68.0 %all-reduce.5.cloned.1.call-done = f32[512,1536]{1,0:T(8,128)} async-done(((f32[512,1536]{1,0:T(8,128)}), f32[512,1536]{1,0:T(8,128)}) %all-reduce.5.cloned.1.call-update) | async-done | bytes 3145744 | tf_op jit(solution)/shard_map/psum | solution.py:158
  166.6 3.6 fusion.62
  173.2 22.8 %all-gather.6.cloned.1.call-done = bf16[512,2048]{1,0:T(8,128)(2,1)} async-done(((bf16[512,512]{1,0:T(8,128)(2,1)}), bf16[512,2048]{1,0:T(8,128)(2,1)}) %all-gather.6.cloned.1.call-update) | async-done | bytes 2097168 | tf_op jit(solution)/shard_map/all_gather | solution.py:165
  201.4 4.4 fusion.84
  207.9 21.4 %all-gather.8.cloned.1.call-done = bf16[2,2048,128]{2,1,0:T(8,128)(2,1)} async-done(((bf16[2,512,128]{2,1,0:T(8,128)(2,1)}), bf16[2,2048,128]{2,1,0:T(8,128)(2,1)}) %all-gather.8.cloned.1.call-update) | async-done | bytes 1048592 | tf_op jit(solution)/shard_map/all_gather | solution.py:173
  231.5 58.8 %while.31 = (s32[]{:T(128)}, f32[1,4,512]{2,1,0:T(4,128)S(1)}, f32[1,4,512]{2,1,0:T(4,128)}, f32[1,4,512,128]{3,2,1,0:T(8,128)S(1)}, s32[4]{0:T(128)S(1)}, /*ind...) while((s32[]{:T(128)}, f32[1,4,512]{2,1,0:T(4,128)S(1)}, ...), condition=%wide.region_10.11_spmd.clone, body=%wide.region_7.10_spmd.clone.sunk | while | flops 1887187968 | bytes 32446964 | solution.py:105
  233.9 3.8 bitcast_reduce_fusion.5
  241.2 4.9 fusion.153
  248.6 3.8 bitcast_reduce_fusion.5
  255.9 4.9 fusion.153
  263.3 3.8 bitcast_reduce_fusion.5
  270.6 4.9 fusion.153
  278.0 3.8 bitcast_reduce_fusion.5
  285.3 4.9 fusion.153
  299.6 47.0 %all-reduce.7.cloned.1.call-done = bf16[512,2048]{1,0:T(8,128)(2,1)} async-done(((bf16[512,2048]{1,0:T(8,128)(2,1)}), bf16[512,2048]{1,0:T(8,128)(2,1)}) %all-reduce.7.cloned.1.call-update) | async-done | bytes 2097168 | tf_op jit(solution)/shard_map/psum | solution.py:176
  360.4 133.1 %all-reduce.9.cloned.1.call-done = (bf16[384,1536]{1,0:T(8,128)(2,1)}, bf16[512,2048]{1,0:T(8,128)(2,1)}) async-done(((bf16[384,1536]{1,0:T(8,128)(2,1)}, bf16[512,2048]{1,0:T(8,128)(2,1)}), (bf16[384,1536]{1,0:T(8,128)(2,1)}, bf16[512,2048]{1,0:T(8,128)(2,1)})) %all-reduce.9.cloned.1.call-update) | async-done | bytes 3276816 | tf_op jit(solution)/shard_map/psum | solution.py:189
  (208 shorter events, 101.2 us)
Async XLA Ops:
  7.2 285.8 %copy-start = (bf16[512,2048]{1,0:T(8,128)(2,1)S(1)}, bf16[512,2048]{1,0:T(8,128)(2,1)}, u32[]{:S(2)}) copy-start(bf16[512,2048]{1,0:T(8,128)(2,1)} %param.27) | copy-start | bytes 6291460
  7.2 35.7 %all-gather.4.cloned.1.call-start = ((), (), s32[]{:S(2)}) async-start(), calls=%async_computation | async-start | bytes 1310720 | tf_op jit(solution)/shard_map/all_gather | solution.py:155
  12.1 4.7 copy-start.21
  12.1 154.5 %all-reduce.5.cloned.1.call-start = ((), (), s32[]{:S(2)}) async-start(), calls=%async_computation.1 | async-start | bytes 6291456 | tf_op jit(solution)/shard_map/psum | solution.py:158
  98.5 97.5 %all-gather.6.cloned.1.call-start = ((), (), s32[]{:S(2)}) async-start(), calls=%async_computation.2 | async-start | bytes 2621440 | tf_op jit(solution)/shard_map/all_gather | solution.py:165
  166.6 4.8 copy-start.19
  171.4 26.7 %copy-start.20 = (bf16[2,2048,128]{2,1,0:T(8,128)(2,1)S(1)}, bf16[2,2048,128]{2,1,0:T(8,128)(2,1)}, u32[]{:S(2)}) copy-start(bf16[2,2048,128]{2,1,0:T(8,128)(2,1)} %param.26) | copy-start | bytes 3145732
  173.2 56.1 %all-gather.8.cloned.1.call-start = ((), (), s32[]{:S(2)}) async-start(), calls=%async_computation.3 | async-start | bytes 1310720 | tf_op jit(solution)/shard_map/all_gather | solution.py:173
  201.2 145.5 %all-reduce.7.cloned.1.call-start = ((), (), s32[]{:S(2)}) async-start(), calls=%async_computation.4 | async-start | bytes 4194304 | tf_op jit(solution)/shard_map/psum | solution.py:176
  237.8 3.5 copy-start.12
  240.9 5.2 %copy-start.10 = (f32[1,4,512]{2,1,0:T(4,128)}, f32[1,4,512]{2,1,0:T(4,128)S(1)}, u32[]{:S(2)}) copy-start(f32[1,4,512]{2,1,0:T(4,128)S(1)} %bitcast_add_fusion.5) | copy-start | bytes 24580 | tf_op jit(solution)/shard_map/while
  241.2 5.0 copy-start.24
  255.6 5.2 %copy-start.10 = (f32[1,4,512]{2,1,0:T(4,128)}, f32[1,4,512]{2,1,0:T(4,128)S(1)}, u32[]{:S(2)}) copy-start(f32[1,4,512]{2,1,0:T(4,128)S(1)} %bitcast_add_fusion.5) | copy-start | bytes 24580 | tf_op jit(solution)/shard_map/while
  255.9 5.0 copy-start.24
  267.2 3.5 copy-start.12
  270.4 5.2 %copy-start.10 = (f32[1,4,512]{2,1,0:T(4,128)}, f32[1,4,512]{2,1,0:T(4,128)S(1)}, u32[]{:S(2)}) copy-start(f32[1,4,512]{2,1,0:T(4,128)S(1)} %bitcast_add_fusion.5) | copy-start | bytes 24580 | tf_op jit(solution)/shard_map/while
  270.6 5.0 copy-start.24
  285.1 5.2 %copy-start.10 = (f32[1,4,512]{2,1,0:T(4,128)}, f32[1,4,512]{2,1,0:T(4,128)S(1)}, u32[]{:S(2)}) copy-start(f32[1,4,512]{2,1,0:T(4,128)S(1)} %bitcast_add_fusion.5) | copy-start | bytes 24580 | tf_op jit(solution)/shard_map/while
  285.3 5.0 copy-start.24
  293.0 3.6 copy-start.13
  293.0 4.2 copy-start.15
  295.6 3.9 copy-start.14
  295.6 197.9 %all-reduce.9.cloned.1.call-start = ((), (), s32[]{:S(2)}) async-start(), calls=%async_computation.5 | async-start | bytes 6553600 | tf_op jit(solution)/shard_map/psum | solution.py:189
  346.7 3.5 copy-start.6
  (31 other events, 72.0 us)
Sparse Core Ops, SparseCore 0:
  12.2 30.6 all-gather.3
  98.6 67.9 all-reduce.4
  173.3 22.6 all-gather.5
  201.3 27.9 all-gather.7
  295.8 50.8 all-reduce.6
  360.0 133.5 all-reduce.8
where the time goes:
time: 507 us; the launch traced here: 506 us
  waiting for transfers between devices  318 us (63%)
  matrix products  95.7 us (19%)
  other arithmetic  49.5 us (10%)
  local copies, waits for them, and re-layouts  21.4 us (4%)
  between operations  15.1 us (3%)
  loops' own time  5.84 us (1%)
    psum x1, waiting for transfers between devices, on_device(): lax.psum(actor_grad.astype(jnp.bfloat16), ('rep', 'sec'))  133 us
    psum x1, waiting for transfers between devices, on_device(): lax.psum(jnp.dot(attended, a_out, preferred_element_type=jnp.float32), 'm...  68 us
    psum x1, waiting for transfers between devices, on_device(): lax.psum(jnp.dot(critic_attended, c_out, preferred_element_type=jnp.float...  47 us
    dot_general x8, matrix products, absorb(): jnp.einsum('kgrj,jkd->kgrd', weights, value_float, precision=lax.Precisio...  35.4 us
    dot_general x8, matrix products, absorb(): jnp.einsum('rkgd,jkd->kgrj', heads_in, key_block, preferred_element_type=...  28 us
    all_gather x1, waiting for transfers between devices, on_device(): lax.all_gather(keyval, 'rep', axis=1, tiled=True)  25.5 us
    reduce_sum x8, other arithmetic, absorb(): row_sum = row_sum * rescale + jnp.sum(weights, axis=-1)  23.1 us
    all_gather x1, waiting for transfers between devices, on_device(): embedded = lax.all_gather(embed_part, 'mdl', axis=1, tiled=True)  22.8 us
  transfers between devices with their start and end apart: 6, of which 6 were waited for; matrix products, arithmetic and copies ran while one was open for 3% of the time, Pallas kernels for 0%

commit v1 on v0

v1 whole, which is shorter than its diff:
```python
import functools
import math

import jax
import jax.numpy as jnp
from jax import lax
from jax.experimental import pallas as pl
from jax.experimental.pallas import tpu as pltpu
from jax.sharding import PartitionSpec as P

HEAD = 128
epsilon = 1e-05
clip_range = 0.2
masked_score = -1e30
LOG2E = 1.4426950408889634
F32 = jnp.float32
BF16 = jnp.bfloat16


def dot(a, b):
    return jnp.dot(a, b, preferred_element_type=F32)


def row_factor(source):
    return lax.rsqrt(jnp.mean(source * source, axis=-1, keepdims=True) + epsilon)


def attend_kernel(total_ref, q_ref, k_ref, v_ref, o_ref):
    keys = k_ref[0]
    vals = v_ref[0]
    count = keys.shape[0]
    scores = lax.dot_general(
        q_ref[...], keys, (((1,), (1,)), ((), ())), preferred_element_type=F32
    )
    live = lax.broadcasted_iota(jnp.int32, (1, count), 1) < total_ref[0]
    scores = jnp.where(live, scores, masked_score)
    top = jnp.max(scores, axis=-1, keepdims=True)
    weights = jnp.exp2(scores - top).astype(BF16)
    wide = jnp.concatenate([vals, jnp.ones_like(vals)], axis=1)
    both = dot(weights, wide)
    o_ref[...] = (both[:, :HEAD] / both[:, HEAD:]).astype(BF16)


def attend(queries, keyval, robot_total):
    rows, width = queries.shape
    count = keyval.shape[1]
    heads = width // HEAD
    groups = heads // (keyval.shape[2] // HEAD)
    block = math.gcd(rows, max(16, 256 * 2048 // max(count, 2048)))
    flops = 4 * rows * count * width
    return pl.pallas_call(
        attend_kernel,
        grid=(heads, rows // block),
        in_specs=[
            pl.BlockSpec(memory_space=pltpu.SMEM),
            pl.BlockSpec((block, HEAD), lambda h, i: (i, h)),
            pl.BlockSpec((1, count, HEAD), lambda h, i: (0, 0, h // groups)),
            pl.BlockSpec((1, count, HEAD), lambda h, i: (1, 0, h // groups)),
        ],
        out_specs=pl.BlockSpec((block, HEAD), lambda h, i: (i, h)),
        out_shape=jax.ShapeDtypeStruct((rows, width), BF16),
        compiler_params=pltpu.CompilerParams(vmem_limit_bytes=40 * 2**20),
        cost_estimate=pl.CostEstimate(
            flops=flops, bytes_accessed=4 * rows * width, transcendentals=rows * count * heads
        ),
        name="attend",
    )(robot_total.reshape(1), queries, keyval, keyval)


def gather_codes(size):
    codes = [0]
    bit = size // 2
    while bit >= 1:
        codes = codes + [c ^ bit for c in codes]
        bit //= 2
    return codes


def gather_blocks(block, axis):
    size = lax.axis_size(axis)
    blocks = [block]
    bit = size // 2
    while bit >= 1:
        perm = [(i, i ^ bit) for i in range(size)]
        blocks = blocks + [lax.ppermute(b, axis, perm) for b in blocks]
        bit //= 2
    return blocks


def on_device(
    obs,
    a_query,
    a_keyval,
    a_out,
    w_policy,
    c_in,
    c_query,
    c_keyval,
    c_out,
    w_value,
    actions,
    advantages,
    old_logp,
    returns,
    robot_count,
):
    row_count = obs.shape[1]
    batch_index = lax.axis_index("sec")
    robot_total = robot_count[batch_index]
    live_total = jnp.sum(robot_count).astype(F32)
    first_row = lax.axis_index("rep") * row_count
    live_mask = first_row + lax.iota(jnp.int32, row_count) < robot_total
    mdl_count = lax.axis_size("mdl")
    mdl_index = lax.axis_index("mdl")
    part_rows = row_count // mdl_count
    row_start = mdl_index * part_rows
    codes = gather_codes(mdl_count)
    score_scale = HEAD ** (-0.5) * LOG2E

    obs_in = obs[0]
    obs_float = obs_in.astype(F32)
    factor_a = row_factor(obs_float)
    keyval = jnp.stack([dot(obs_in, a_keyval[c]) * factor_a for c in range(2)]).astype(BF16)
    keyval_all = lax.all_gather(keyval, "rep", axis=1, tiled=True)

    a_out_blocks = gather_blocks(a_out, "mdl")
    c_in_blocks = gather_blocks(c_in, "mdl")
    c_out_blocks = gather_blocks(c_out, "mdl")

    queries = (dot(obs_in, a_query) * (factor_a * score_scale)).astype(BF16)
    attended = attend(queries, keyval_all, robot_total)
    attended_blocks = gather_blocks(attended, "mdl")
    hidden = obs_float
    for att, weight in zip(attended_blocks, a_out_blocks):
        hidden = hidden + dot(att, weight)
    hidden = hidden.astype(BF16)

    width_c = c_in.shape[1]
    c_in_all = jnp.zeros((c_in.shape[0], width_c * mdl_count), BF16)
    for code, weight in zip(codes, c_in_blocks):
        c_in_all = lax.dynamic_update_slice(c_in_all, weight, (0, (mdl_index ^ code) * width_c))
    embedded = dot(hidden, c_in_all).astype(BF16)
    embed_float = embedded.astype(F32)
    factor_c = row_factor(embed_float)
    critic_keyval = jnp.stack(
        [dot(embedded, c_keyval[c]) * factor_c for c in range(2)]
    ).astype(BF16)
    critic_keyval_all = lax.all_gather(critic_keyval, "rep", axis=1, tiled=True)
    critic_queries = (dot(embedded, c_query) * (factor_c * score_scale)).astype(BF16)

    source = hidden.astype(F32)
    factor_h = row_factor(source)
    logits = dot(hidden, w_policy) * factor_h
    log_probs = jax.nn.log_softmax(logits, axis=-1)
    onehot = (
        actions[0][:, None] == lax.broadcasted_iota(jnp.int32, logits.shape, 1)
    ).astype(F32)
    chosen = jnp.sum(onehot * log_probs, axis=-1)
    prob_ratio = jnp.exp(chosen - old_logp[0])
    plain_term = prob_ratio * advantages[0]
    bounded = jnp.clip(prob_ratio, 1.0 - clip_range, 1.0 + clip_range) * advantages[0]
    slope = jnp.where(live_mask & (plain_term <= bounded), -plain_term / live_total, F32(0.0))
    dlogits = slope[:, None] * (onehot - jnp.exp(log_probs))
    along = jnp.sum(dlogits * logits, axis=-1, keepdims=True) / source.shape[1]
    dnormed = dot(dlogits.astype(BF16), w_policy.T)
    dhidden = (factor_h * (dnormed - source * (factor_h * along))).astype(BF16)
    actor_grad = jnp.einsum("rh,rd->hd", attended, dhidden, preferred_element_type=F32)
    actor_summed = lax.psum(actor_grad.astype(BF16), ("rep", "sec"))

    critic_attended = attend(critic_queries, critic_keyval_all, robot_total)
    critic_blocks = gather_blocks(critic_attended, "mdl")
    mixed = embed_float
    for att, weight in zip(critic_blocks, c_out_blocks):
        mixed = mixed + dot(att, weight)

    w_value_float = w_value.astype(F32)
    factor_v = row_factor(mixed)
    value_pred = factor_v[:, 0] * jnp.sum(mixed * w_value_float[None, :], axis=-1)
    dvalues = jnp.where(live_mask, value_pred - returns[0], F32(0.0)) / live_total
    pull = factor_v[:, 0] * value_pred / mixed.shape[1]
    dmixed = (
        (factor_v * dvalues[:, None]) * (w_value_float[None, :] - mixed * pull[:, None])
    ).astype(BF16)
    critic_grad = jnp.einsum(
        "rh,rd->hd", critic_attended, dmixed, preferred_element_type=F32
    ).astype(BF16)
    critic_grad, actor_summed = lax.optimization_barrier((critic_grad, actor_summed))
    critic_summed = lax.psum(critic_grad, ("rep", "sec"))
    value_part = lax.dynamic_slice_in_dim(value_pred, row_start, part_rows, 0)
    return (value_part[None, :], actor_summed.astype(F32), critic_summed.astype(F32))


def solution(mesh):
    return jax.shard_map(
        on_device,
        mesh=mesh,
        in_specs=(
            P("sec", "rep", None),
            P(None, "mdl"),
            P(None, None, "mdl"),
            P("mdl", None),
            P(),
            P(None, "mdl"),
            P(None, "mdl"),
            P(None, None, "mdl"),
            P("mdl", None),
            P(),
            P("sec", "rep"),
            P("sec", "rep"),
            P("sec", "rep"),
            P("sec", "rep"),
            P(),
        ),
        out_specs=(P("sec", ("rep", "mdl")), P("mdl", None), P("mdl", None)),
        check_vma=False,
    )
```

time: 507 us -> 391 us (0.77)
  matrix products: 95.7 us -> 45.2 us
  waiting for transfers between devices: 318 us -> 269 us
  other arithmetic: 49.5 us -> 11.4 us
  Pallas kernels: 0 us -> 22.3 us
  starting transfers between devices: 0.65 us -> 11.3 us
  loops' own time: 5.84 us -> 0 us
    psum x3 -> x2, waiting for transfers between devices: 248 us -> 159 us  [the longest x1 102 us: on_device(): critic_summed = lax.psum(critic_grad, ('rep', 'sec'))]
    ppermute x0 -> x15, waiting for transfers between devices: none -> 84.6 us  [gather_blocks(): blocks = blocks + [lax.ppermute(b, axis, perm) for b in blocks]]
    dot_general x28 -> x18, matrix products: 95.7 us -> 45.2 us  [the longest x16 38.5 us: dot(): return jnp.dot(a, b, preferred_element_type=F32)]
    all_gather x3 -> x2, waiting for transfers between devices: 69.7 us -> 24.8 us  [the longest x1 24.8 us: on_device(): critic_keyval_all = lax.all_gather(critic_keyval, 'rep', axis=1, tiled=True)]
    reduce_sum x16 -> x5, other arithmetic: 35.7 us -> 2.82 us  [the longest x1 1.94 us: row_factor(): jnp.mean(source * source, axis=-1, keepdims=True) + epsilon]
    pallas_call x0 -> x2, Pallas kernels: none -> 22.3 us  [attend(): pl.pallas_call(attend_kernel, grid=(heads, rows // block), in_specs=[pl.B...]
    ppermute x0 -> x15, starting transfers between devices: none -> 11 us  [gather_blocks(): blocks = blocks + [lax.ppermute(b, axis, perm) for b in blocks]]
    dynamic_update_slice x0 -> x4, local copies, waits for them, and re-layouts: none -> 8.26 us  [on_device(): lax.dynamic_update_slice(c_in_all, weight, (0, (mdl_index ^ code) * width...]
  transfers between devices with their start and end apart: 6 -> 19, of which waited for: 6 -> 6; matrix products, arithmetic and copies ran while one was open for 3% -> 15% of each run, Pallas kernels for 0% -> 6%
where the time goes in v1:
time: 391 us
  waiting for transfers between devices  269 us (69%)
  matrix products  45.2 us (12%)
  Pallas kernels  22.3 us (6%)
  local copies, waits for them, and re-layouts  16.7 us (4%)
  between operations  14.8 us (4%)
  other arithmetic  11.4 us (3%)
  starting transfers between devices  11.3 us (3%)
    psum x1, waiting for transfers between devices, on_device(): critic_summed = lax.psum(critic_grad, ('rep', 'sec'))  102 us
    ppermute x15, waiting for transfers between devices, gather_blocks(): blocks = blocks + [lax.ppermute(b, axis, perm) for b in blocks]  84.6 us
    psum x1, waiting for transfers between devices, on_device(): actor_summed = lax.psum(actor_grad.astype(BF16), ('rep', 'sec'))  57.4 us
    dot_general x16, matrix products, dot(): return jnp.dot(a, b, preferred_element_type=F32)  38.5 us
    all_gather x1, waiting for transfers between devices, on_device(): critic_keyval_all = lax.all_gather(critic_keyval, 'rep', axis=1, tiled=True)  24.8 us
    pallas_call x2, Pallas kernels, attend(): pl.pallas_call(attend_kernel, grid=(heads, rows // block), in_specs=[pl.B...  22.3 us
    ppermute x15, starting transfers between devices, gather_blocks(): blocks = blocks + [lax.ppermute(b, axis, perm) for b in blocks]  11 us
    dynamic_update_slice x4, local copies, waits for them, and re-layouts, on_device(): lax.dynamic_update_slice(c_in_all, weight, (0, (mdl_index ^ code) * width...  8.26 us
  transfers between devices with their start and end apart: 19, of which 6 were waited for; matrix products, arithmetic and copies ran while one was open for 15% of the time, Pallas kernels for 6%

profile of v1, /device:TPU:0, one launch (start us, length us, event | category | flops | bytes accessed | tf_op | source)
XLA Modules:
  0.0 390.8 jit_solution(2385960002064293127)
XLA Ops:
  12.7 3.0 collective-permute-start.6
  20.1 2.7 fusion.29.q_ref
  22.9 3.4 broadcast_in_dim.13
  27.7 48.8 %collective-permute-done.1 = bf16[384,1536]{1,0:T(8,128)(2,1)} collective-permute-done((bf16[384,1536]{1,0:T(8,128)(2,1)}, bf16[384,1536]{1,0:T(8,128)(2,1)}, u32[]{:S(2)}, u32[]{:S(2)}) %collective-permute-start.1) | collective-permute-done | bytes 1179680 | tf_op jit(solution)/shard_map/ppermute | solution.py:85
  77.8 9.6 %attend.2 = bf16[512,384]{1,0:T(8,128)(2,1)S(1)} custom-call(s32[1]{0:T(128)} %dynamic_slice.6.total_ref, bf16[512,384]{1,0:T(8,128)(2,1)S(1)} %fusion.29.q_ref, bf16[2,2048,128]{2,1,0:T(8,128)(2,1)S(1)} %copy-done.2, bf16[2,2048,128]{2,1,0:T(8,128)(2,1)S(1)} %copy-done.2), custom_call_target="tpu_custom_call" | custom-call | flops 1610612736 | bytes 786432 | tf_op jit(solution)/shard_map/attend/pallas_call | solution.py:51
  88.0 2.8 constant_dynamic-update-slice_fusion.2
  92.8 2.7 constant_dynamic-update-slice_fusion.1
  95.6 2.3 convert_add_fusion.1
  98.4 30.6 %collective-permute-done = bf16[512,384]{1,0:T(8,128)(2,1)S(1)} collective-permute-done((bf16[512,384]{1,0:T(8,128)(2,1)S(1)}, bf16[512,384]{1,0:T(8,128)(2,1)S(1)}, u32[]{:S(2)}, u32[]{:S(2)}) %collective-permute-start) | collective-permute-done | bytes 393248 | tf_op jit(solution)/shard_map/ppermute | solution.py:85
  129.0 2.3 fusion.76
  134.1 2.3 fusion.6
  137.8 6.6 %fusion = (f32[512]{0:T(512)S(1)}, bf16[512,2048]{1,0:T(8,128)(2,1)S(1)}) fusion(bf16[512,1536]{1,0:T(8,128)(2,1)S(1)} %get-tuple-element.20, bf16[1536,2048]{1,0:T(8,128)(2,1)} %constant_dynamic-update-slice_fusion), kind=kOutput, calls=%fused_computation.2 | convolution fusion | flops 3225419264 | bytes 9963520 | tf_op jit(solution)/shard_map/dot_general | solution.py:21
  151.5 24.8 %all-gather.5.cloned.1.call-done.k_ref.v_ref = bf16[2,2048,128]{2,1,0:T(8,128)(2,1)} async-done(((bf16[2,512,128]{2,1,0:T(8,128)(2,1)}), bf16[2,2048,128]{2,1,0:T(8,128)(2,1)}) %all-gather.5.cloned.1.call-update) | async-done | bytes 1048592 | tf_op jit(solution)/shard_map/all_gather | solution.py:148
  177.6 12.7 %attend.3 = bf16[512,512]{1,0:T(8,128)(2,1)S(1)} custom-call(s32[1]{0:T(128)} %dynamic_slice.6.total_ref, bf16[512,512]{1,0:T(8,128)(2,1)S(1)} %fusion.28.q_ref, bf16[2,2048,128]{2,1,0:T(8,128)(2,1)S(1)} %copy-done.3, bf16[2,2048,128]{2,1,0:T(8,128)(2,1)S(1)} %copy-done.3), custom_call_target="tpu_custom_call" | custom-call | flops 2147483648 | bytes 1048576 | tf_op jit(solution)/shard_map/attend/pallas_call | solution.py:51
  191.8 3.9 convolution_convert_fusion.2
  195.8 2.8 fusion.77
  198.6 5.2 %collective-permute-done.9 = bf16[512,512]{1,0:T(8,128)(2,1)S(1)} collective-permute-done((bf16[512,512]{1,0:T(8,128)(2,1)S(1)}, bf16[512,512]{1,0:T(8,128)(2,1)S(1)}, u32[]{:S(2)}, u32[]{:S(2)}) %collective-permute-start.9) | collective-permute-done | bytes 524320 | tf_op jit(solution)/shard_map/ppermute | solution.py:85
  203.8 2.9 fusion.78
  206.7 3.0 fusion.79
  209.8 3.8 multiply_reduce_fusion.1
  214.2 2.8 convolution_convert_fusion
  217.0 57.4 %all-reduce.3.cloned.1.call-done = bf16[384,1536]{1,0:T(8,128)(2,1)} async-done(((bf16[384,1536]{1,0:T(8,128)(2,1)}), bf16[384,1536]{1,0:T(8,128)(2,1)}) %all-reduce.3.cloned.1.call-update) | async-done | bytes 1179664 | tf_op jit(solution)/shard_map/psum | solution.py:168
  278.0 102.1 %all-reduce.5.cloned.1.call-done = bf16[512,2048]{1,0:T(8,128)(2,1)} async-done(((bf16[512,2048]{1,0:T(8,128)(2,1)}), bf16[512,2048]{1,0:T(8,128)(2,1)}) %all-reduce.5.cloned.1.call-update) | async-done | bytes 2097168 | tf_op jit(solution)/shard_map/psum | solution.py:188
  380.1 4.1 %convert_element_type.69 = f32[512,2048]{1,0:T(8,128)} convert(bf16[512,2048]{1,0:T(8,128)(2,1)} %all-reduce.5.cloned.1.call-done) | non-fusion elementwise | flops 1048576 | bytes 6291456 | tf_op jit(solution)/shard_map/convert_element_type | solution.py:190
  (106 shorter events, 33.2 us)
Async XLA Ops:
  7.2 143.1 %copy-start = (bf16[2048,512]{1,0:T(8,128)(2,1)S(1)}, bf16[2048,512]{1,0:T(8,128)(2,1)}, u32[]{:S(2)}) copy-start(bf16[2048,512]{1,0:T(8,128)(2,1)} %param.21) | copy-start | bytes 6291460
  7.2 69.3 %all-gather.3.cloned.1.call-start = ((), (), s32[]{:S(2)}) async-start(), calls=%async_computation | async-start | bytes 1310720 | tf_op jit(solution)/shard_map/all_gather | solution.py:124
  11.3 8.8 %copy-start.15 = (bf16[2048]{0:T(1024)(128)(2,1)S(1)}, bf16[2048]{0:T(1024)(128)(2,1)}, u32[]{:S(2)}) copy-start(bf16[2048]{0:T(1024)(128)(2,1)} %param.24) | copy-start | bytes 12292
  12.6 163.7 %all-gather.5.cloned.1.call-start = ((), (), s32[]{:S(2)}) async-start(), calls=%async_computation.1 | async-start | bytes 1310720 | tf_op jit(solution)/shard_map/all_gather | solution.py:148
  12.7 74.7 %collective-permute-start.6 = (bf16[1536,512]{1,0:T(8,128)(2,1)}, bf16[1536,512]{1,0:T(8,128)(2,1)}, u32[]{:S(2)}, u32[]{:S(2)}) collective-permute-start(bf16[1536,512]{1,0:T(8,128)(2,1)} %param.20), channel_id=1, source_target_pairs={{0,2},{1,3},{2,0},{3,1},{4,6},{5,7},{6,4},{7,5},{8,10},{9,11},{10,... | collective-permute-start | bytes 4718600 | tf_op jit(solution)/shard_map/ppermute | solution.py:85
  15.7 60.8 %collective-permute-start.1 = (bf16[384,1536]{1,0:T(8,128)(2,1)}, bf16[384,1536]{1,0:T(8,128)(2,1)}, u32[]{:S(2)}, u32[]{:S(2)}) collective-permute-start(bf16[384,1536]{1,0:T(8,128)(2,1)} %param.18), channel_id=1, source_target_pairs={{0,2},{1,3},{2,0},{3,1},{4,6},{5,7},{6,4},{7,5},{8,10},{9,11},{10,... | collective-permute-start | bytes 3538952 | tf_op jit(solution)/shard_map/ppermute | solution.py:85
  15.8 74.9 %collective-permute-start.7 = (bf16[1536,512]{1,0:T(8,128)(2,1)}, bf16[1536,512]{1,0:T(8,128)(2,1)}, u32[]{:S(2)}, u32[]{:S(2)}) collective-permute-start(bf16[1536,512]{1,0:T(8,128)(2,1)} %param.20), channel_id=1, source_target_pairs={{0,1},{1,0},{2,3},{3,2},{4,5},{5,4},{6,7},{7,6},{8,9},{9,8},{10,11... | collective-permute-start | bytes 4718600 | tf_op jit(solution)/shard_map/ppermute | solution.py:85
  15.8 79.7 %collective-permute-start.3 = (bf16[384,1536]{1,0:T(8,128)(2,1)}, bf16[384,1536]{1,0:T(8,128)(2,1)}, u32[]{:S(2)}, u32[]{:S(2)}) collective-permute-start(bf16[384,1536]{1,0:T(8,128)(2,1)} %param.18), channel_id=1, source_target_pairs={{0,1},{1,0},{2,3},{3,2},{4,5},{5,4},{6,7},{7,6},{8,9},{9,8},{10,11... | collective-permute-start | bytes 3538952 | tf_op jit(solution)/shard_map/ppermute | solution.py:85
  16.3 117.2 %collective-permute-start.10 = (bf16[512,2048]{1,0:T(8,128)(2,1)}, bf16[512,2048]{1,0:T(8,128)(2,1)}, u32[]{:S(2)}, u32[]{:S(2)}) collective-permute-start(bf16[512,2048]{1,0:T(8,128)(2,1)} %param.23), channel_id=1, source_target_pairs={{0,2},{1,3},{2,0},{3,1},{4,6},{5,7},{6,4},{7,5},{8,10},{9,11},{10,... | collective-permute-start | bytes 6291464 | tf_op jit(solution)/shard_map/ppermute | solution.py:85
  76.5 57.5 %collective-permute-start.5 = (bf16[384,1536]{1,0:T(8,128)(2,1)}, bf16[384,1536]{1,0:T(8,128)(2,1)}, u32[]{:S(2)}, u32[]{:S(2)}) collective-permute-start(bf16[384,1536]{1,0:T(8,128)(2,1)} %collective-permute-done.1), channel_id=1, source_target_pairs={{0,1},{1,0},{2,3},{3,2},{4,5},{5,4},{6,7},{7,6},{8,9},{9,8},{10,11... | collective-permute-start | bytes 3538952 | tf_op jit(solution)/shard_map/ppermute | solution.py:85
  87.4 10.4 %collective-permute-start.2 = (bf16[512,384]{1,0:T(8,128)(2,1)S(1)}, bf16[512,384]{1,0:T(8,128)(2,1)S(1)}, u32[]{:S(2)}, u32[]{:S(2)}) collective-permute-start(bf16[512,384]{1,0:T(8,128)(2,1)S(1)} %attend.2), channel_id=1, source_target_pairs={{0,1},{1,0},{2,3},{3,2},{4,5},{5,4},{6,7},{7,6},{8,9},{9,8},{10,11... | collective-permute-start | bytes 1179656 | tf_op jit(solution)/shard_map/ppermute | solution.py:85
  90.7 38.2 %collective-permute-start = (bf16[512,384]{1,0:T(8,128)(2,1)S(1)}, bf16[512,384]{1,0:T(8,128)(2,1)S(1)}, u32[]{:S(2)}, u32[]{:S(2)}) collective-permute-start(bf16[512,384]{1,0:T(8,128)(2,1)S(1)} %attend.2), channel_id=1, source_target_pairs={{0,2},{1,3},{2,0},{3,1},{4,6},{5,7},{6,4},{7,5},{8,10},{9,11},{10,... | collective-permute-start | bytes 1179656 | tf_op jit(solution)/shard_map/ppermute | solution.py:85
  95.5 40.9 %collective-permute-start.8 = (bf16[1536,512]{1,0:T(8,128)(2,1)}, bf16[1536,512]{1,0:T(8,128)(2,1)S(1)}, u32[]{:S(2)}, u32[]{:S(2)}) collective-permute-start(bf16[1536,512]{1,0:T(8,128)(2,1)} %collective-permute-done.6), channel_id=1, source_target_pairs={{0,1},{1,0},{2,3},{3,2},{4,5},{5,4},{6,7},{7,6},{8,9},{9,8},{10,11... | collective-permute-start | bytes 4718600 | tf_op jit(solution)/shard_map/ppermute | solution.py:85
  97.8 108.9 %collective-permute-start.12 = (bf16[512,2048]{1,0:T(8,128)(2,1)}, bf16[512,2048]{1,0:T(8,128)(2,1)}, u32[]{:S(2)}, u32[]{:S(2)}) collective-permute-start(bf16[512,2048]{1,0:T(8,128)(2,1)} %param.23), channel_id=1, source_target_pairs={{0,1},{1,0},{2,3},{3,2},{4,5},{5,4},{6,7},{7,6},{8,9},{9,8},{10,11... | collective-permute-start | bytes 6291464 | tf_op jit(solution)/shard_map/ppermute | solution.py:85
  129.0 5.1 %collective-permute-start.4 = (bf16[512,384]{1,0:T(8,128)(2,1)S(1)}, bf16[512,384]{1,0:T(8,128)(2,1)S(1)}, u32[]{:S(2)}, u32[]{:S(2)}) collective-permute-start(bf16[512,384]{1,0:T(8,128)(2,1)S(1)} %collective-permute-done), channel_id=1, source_target_pairs={{0,1},{1,0},{2,3},{3,2},{4,5},{5,4},{6,7},{7,6},{8,9},{9,8},{10,11... | collective-permute-start | bytes 1179656 | tf_op jit(solution)/shard_map/ppermute | solution.py:85
  133.5 76.3 %collective-permute-start.14 = (bf16[512,2048]{1,0:T(8,128)(2,1)}, bf16[512,2048]{1,0:T(8,128)(2,1)}, u32[]{:S(2)}, u32[]{:S(2)}) collective-permute-start(bf16[512,2048]{1,0:T(8,128)(2,1)} %collective-permute-done.10), channel_id=1, source_target_pairs={{0,1},{1,0},{2,3},{3,2},{4,5},{5,4},{6,7},{7,6},{8,9},{9,8},{10,11... | collective-permute-start | bytes 6291464 | tf_op jit(solution)/shard_map/ppermute | solution.py:85
  136.4 8.1 %copy-start.6 = (bf16[512,1536]{1,0:T(8,128)(2,1)}, bf16[512,1536]{1,0:T(8,128)(2,1)S(1)}, u32[]{:S(2)}) copy-start(bf16[512,1536]{1,0:T(8,128)(2,1)S(1)} %get-tuple-element.20) | copy-start | bytes 4718596
  146.8 127.7 %all-reduce.3.cloned.1.call-start = ((), (), s32[]{:S(2)}) async-start(), calls=%async_computation.2 | async-start | bytes 2359296 | tf_op jit(solution)/shard_map/psum | solution.py:168
  177.5 14.2 %copy-start.13 = (bf16[1536,128]{1,0:T(8,128)(2,1)S(1)}, bf16[1536,128]{1,0:T(8,128)(2,1)}, u32[]{:S(2)}) copy-start(bf16[1536,128]{1,0:T(8,128)(2,1)} %param.19) | copy-start | bytes 1179652
  190.2 13.6 %collective-permute-start.9 = (bf16[512,512]{1,0:T(8,128)(2,1)S(1)}, bf16[512,512]{1,0:T(8,128)(2,1)S(1)}, u32[]{:S(2)}, u32[]{:S(2)}) collective-permute-start(bf16[512,512]{1,0:T(8,128)(2,1)S(1)} %attend.3), channel_id=1, source_target_pairs={{0,2},{1,3},{2,0},{3,1},{4,6},{5,7},{6,4},{7,5},{8,10},{9,11},{10,... | collective-permute-start | bytes 1572872 | tf_op jit(solution)/shard_map/ppermute | solution.py:85
  195.6 184.4 %all-reduce.5.cloned.1.call-start = ((), (), s32[]{:S(2)}) async-start(), calls=%async_computation.3 | async-start | bytes 4194304 | tf_op jit(solution)/shard_map/psum | solution.py:188
  195.7 11.0 %collective-permute-start.11 = (bf16[512,512]{1,0:T(8,128)(2,1)S(1)}, bf16[512,512]{1,0:T(8,128)(2,1)S(1)}, u32[]{:S(2)}, u32[]{:S(2)}) collective-permute-start(bf16[512,512]{1,0:T(8,128)(2,1)S(1)} %attend.3), channel_id=1, source_target_pairs={{0,1},{1,0},{2,3},{3,2},{4,5},{5,4},{6,7},{7,6},{8,9},{9,8},{10,11... | collective-permute-start | bytes 1572872 | tf_op jit(solution)/shard_map/ppermute | solution.py:85
  203.8 5.9 %collective-permute-start.13 = (bf16[512,512]{1,0:T(8,128)(2,1)S(1)}, bf16[512,512]{1,0:T(8,128)(2,1)S(1)}, u32[]{:S(2)}, u32[]{:S(2)}) collective-permute-start(bf16[512,512]{1,0:T(8,128)(2,1)S(1)} %collective-permute-done.9), channel_id=1, source_target_pairs={{0,1},{1,0},{2,3},{3,2},{4,5},{5,4},{6,7},{7,6},{8,9},{9,8},{10,11... | collective-permute-start | bytes 1572872 | tf_op jit(solution)/shard_map/ppermute | solution.py:85
  277.4 106.8 %copy-start.1 = (bf16[2048,512]{1,0:T(8,128)(2,1)S(1)}, bf16[2048,512]{1,0:T(8,128)(2,1)}, u32[]{:S(2)}) copy-start(bf16[2048,512]{1,0:T(8,128)(2,1)} %param.21) | copy-start | bytes 6291460
  (17 other events, 57.4 us)
Sparse Core Ops, SparseCore 0:
  12.8 30.6 all-gather.2
  146.9 29.3 all-gather.4
  195.8 78.6 all-reduce.2
  278.9 101.1 all-reduce.4

commit v2 on v1

v2 whole, which is shorter than its diff:
```python
import functools
import math

import jax
import jax.numpy as jnp
from jax import lax
from jax.experimental import pallas as pl
from jax.experimental.pallas import tpu as pltpu
from jax.sharding import PartitionSpec as P

HEAD = 128
epsilon = 1e-05
clip_range = 0.2
masked_score = -1e30
LOG2E = 1.4426950408889634
F32 = jnp.float32
BF16 = jnp.bfloat16
CHUNKS = 2
LIMIT = 48 * 2**20
VMEM = pl.BlockSpec(memory_space=pltpu.VMEM)


def dot(a, b):
    return jnp.dot(a, b, preferred_element_type=F32)


def tied(*items):
    return lax.optimization_barrier(items)


def row_factor(source):
    return lax.rsqrt(jnp.mean(source * source, axis=-1, keepdims=True) + epsilon)


def whole(shape):
    return pl.BlockSpec(shape, lambda *_: (0,) * len(shape))


def first_kernel(obs_ref, w_ref, kv_ref, factor_ref):
    rows = obs_ref[...]
    factor = row_factor(rows.astype(F32))
    both = dot(rows, jnp.concatenate([w_ref[0], w_ref[1]], axis=1)) * factor
    width = w_ref.shape[2]
    kv_ref[0] = both[:, :width].astype(BF16)
    kv_ref[1] = both[:, width:].astype(BF16)
    factor_ref[...] = jnp.broadcast_to(factor, factor_ref.shape)


def first_projection(obs, w_keyval):
    rows, depth = obs.shape
    width = w_keyval.shape[2]
    block = rows // 2
    return pl.pallas_call(
        first_kernel,
        grid=(rows // block,),
        in_specs=[pl.BlockSpec((block, depth), lambda i: (i, 0)), whole(w_keyval.shape)],
        out_specs=[
            pl.BlockSpec((2, block, width), lambda i: (0, i, 0)),
            pl.BlockSpec((block, HEAD), lambda i: (i, 0)),
        ],
        out_shape=[
            jax.ShapeDtypeStruct((2, rows, width), BF16),
            jax.ShapeDtypeStruct((rows, HEAD), F32),
        ],
        compiler_params=pltpu.CompilerParams(vmem_limit_bytes=LIMIT),
        cost_estimate=pl.CostEstimate(
            flops=4 * rows * depth * width, bytes_accessed=2 * rows * depth, transcendentals=0
        ),
        name="first_projection",
    )(obs, w_keyval)


def attend_kernel(total_ref, q_ref, k_ref, v_ref, o_ref):
    keys = k_ref[0]
    vals = v_ref[0]
    count = keys.shape[0]
    scores = lax.dot_general(
        q_ref[...], keys, (((1,), (1,)), ((), ())), preferred_element_type=F32
    )
    live = lax.broadcasted_iota(jnp.int32, (1, count), 1) < total_ref[0]
    scores = jnp.where(live, scores, masked_score)
    top = jnp.max(scores, axis=-1, keepdims=True)
    weights = jnp.exp2(scores - top).astype(BF16)
    wide = jnp.concatenate([vals, jnp.ones_like(vals)], axis=1)
    both = dot(weights, wide)
    o_ref[...] = (both[:, :HEAD] / both[:, HEAD:]).astype(BF16)


def attend(queries, keyval, robot_total):
    rows, width = queries.shape
    count = keyval.shape[1]
    heads = width // HEAD
    groups = heads // (keyval.shape[2] // HEAD)
    block = math.gcd(rows, max(16, 256 * 2048 // max(count, 2048)))
    flops = 4 * rows * count * width
    return pl.pallas_call(
        attend_kernel,
        grid=(heads, rows // block),
        in_specs=[
            pl.BlockSpec(memory_space=pltpu.SMEM),
            pl.BlockSpec((block, HEAD), lambda h, i: (i, h)),
            pl.BlockSpec((1, count, HEAD), lambda h, i: (0, 0, h // groups)),
            pl.BlockSpec((1, count, HEAD), lambda h, i: (1, 0, h // groups)),
        ],
        out_specs=pl.BlockSpec((block, HEAD), lambda h, i: (i, h)),
        out_shape=jax.ShapeDtypeStruct((rows, width), BF16),
        compiler_params=pltpu.CompilerParams(vmem_limit_bytes=LIMIT),
        cost_estimate=pl.CostEstimate(
            flops=flops, bytes_accessed=4 * rows * width, transcendentals=rows * count * heads
        ),
        name="attend",
    )(robot_total.reshape(1), queries, keyval, keyval)


def hidden_kernel(place_ref, obs_ref, t0, t1, t2, t3, w0, w1, w20, w21, w30, w31, o_ref):
    step = pl.program_id(0)

    def fill(w2, w3):
        total = obs_ref[...].astype(F32)
        for part, weight in ((t0, w0), (t1, w1), (t2, w2), (t3, w3)):
            total = total + dot(part[...], weight[...])
        o_ref[...] = total.astype(BF16)

    @pl.when(step == 0)
    def _():
        fill(w20, w30)

    @pl.when(step == 1)
    def _():
        fill(w21, w31)


def hidden_rows(place, obs, parts, full, halves):
    rows, depth = obs.shape
    inner, half = halves[0].shape
    moving = pl.BlockSpec((inner, half), lambda j, place: (0, place[0] ^ j))
    strip = pl.BlockSpec((rows, half), lambda j, place: (0, place[0] ^ j))
    return pl.pallas_call(
        hidden_kernel,
        grid_spec=pltpu.PrefetchScalarGridSpec(
            num_scalar_prefetch=1,
            grid=(2,),
            in_specs=[strip]
            + [whole(parts[0].shape)] * 4
            + [moving] * 2
            + [whole(halves[0].shape)] * 4,
            out_specs=strip,
        ),
        out_shape=jax.ShapeDtypeStruct((rows, depth), BF16),
        compiler_params=pltpu.CompilerParams(vmem_limit_bytes=LIMIT),
        cost_estimate=pl.CostEstimate(
            flops=8 * rows * depth * inner, bytes_accessed=8 * depth * inner, transcendentals=0
        ),
        name="hidden_rows",
    )(place, obs, *parts, *full, *halves)


def embed_kernel(
    place_ref, h_ref, w0, w1, w20, w21, w30, w31, wkv_ref, emb_ref, kv_ref, factor_ref
):
    step = pl.program_id(0)
    half = w0.shape[1]
    rows = h_ref.shape[0]

    def fill(w2, w3):
        for code, weight in enumerate((w0, w1, w2, w3)):
            column = ((place_ref[1] ^ code) * 2 + (place_ref[0] ^ step)) * half
            emb_ref[:, pl.ds(pl.multiple_of(column, half), half)] = dot(
                h_ref[...], weight[...]
            ).astype(BF16)

    @pl.when(step == 0)
    def _():
        fill(w20, w30)

    @pl.when(step == 1)
    def _():
        fill(w21, w31)
        width = wkv_ref.shape[2]
        both_w = jnp.concatenate([wkv_ref[0], wkv_ref[1]], axis=1)
        block = rows // 2
        for i in range(2):
            span = slice(i * block, (i + 1) * block)
            emb = emb_ref[span, :]
            factor = row_factor(emb.astype(F32))
            both = dot(emb, both_w) * factor
            kv_ref[0, span, :] = both[:, :width].astype(BF16)
            kv_ref[1, span, :] = both[:, width:].astype(BF16)
            factor_ref[span, :] = jnp.broadcast_to(factor, (block, HEAD))


def embed_rows(place, hidden, full, halves, w_keyval):
    rows, depth = hidden.shape
    half = halves[0].shape[1]
    wide = 8 * half
    width = w_keyval.shape[2]
    moving = pl.BlockSpec((depth, half), lambda j, place: (0, place[0] ^ j))
    return pl.pallas_call(
        embed_kernel,
        grid_spec=pltpu.PrefetchScalarGridSpec(
            num_scalar_prefetch=1,
            grid=(2,),
            in_specs=[whole(hidden.shape)]
            + [moving] * 2
            + [whole(halves[0].shape)] * 4
            + [whole(w_keyval.shape)],
            out_specs=[whole((rows, wide)), whole((2, rows, width)), whole((rows, HEAD))],
        ),
        out_shape=[
            jax.ShapeDtypeStruct((rows, wide), BF16),
            jax.ShapeDtypeStruct((2, rows, width), BF16),
            jax.ShapeDtypeStruct((rows, HEAD), F32),
        ],
        compiler_params=pltpu.CompilerParams(vmem_limit_bytes=LIMIT),
        cost_estimate=pl.CostEstimate(
            flops=2 * rows * depth * wide, bytes_accessed=2 * depth * wide, transcendentals=0
        ),
        name="embed_rows",
    )(place, hidden, *full, *halves, w_keyval)


def mixed_kernel(
    place_ref, emb_ref, t0, t1, t2, t3, w0, w1, w2, w3, wv_ref, ret_ref,
    value_ref, other_ref, own_ref, mixed_ref,
):
    step = pl.program_id(0)
    rows, wide = mixed_ref.shape
    strip = emb_ref.shape[1]
    total = emb_ref[...].astype(F32)
    for part, weight in ((t0, w0), (t1, w1), (t2, w2), (t3, w3)):
        total = total + dot(part[...], weight[...])
    mixed_ref[:, pl.ds(pl.multiple_of(step * strip, strip), strip)] = total

    @pl.when(step == pl.num_programs(0) - 1)
    def _():
        half = wide // 2
        block = rows // 4
        live_total = place_ref[4].astype(F32)

        @pl.loop(0, 4)
        def _(i):
            start = pl.multiple_of(i * block, block)
            span = pl.ds(start, block)
            weight = wv_ref[...].astype(F32)
            mixed = mixed_ref[span, :]
            factor = row_factor(mixed)
            value = factor * jnp.sum(mixed * weight, axis=-1, keepdims=True)
            row = place_ref[2] + start + lax.broadcasted_iota(jnp.int32, (block, 1), 0)
            gap = jnp.where(row < place_ref[3], value - ret_ref[span, :], F32(0.0)) / live_total
            lead = factor * gap
            pull = factor * value / wide
            value_ref[span, :] = jnp.broadcast_to(value, (block, HEAD))
            for out, side in ((own_ref, place_ref[0]), (other_ref, 1 - place_ref[0])):
                columns = pl.ds(pl.multiple_of(side * half, half), half)
                part = mixed_ref[span, columns]
                out[span, :] = (
                    lead * (wv_ref[:, columns].astype(F32) - part * pull)
                ).astype(BF16)


def mixed_rows(place, embedded, parts, weights, w_value, returns):
    rows, wide = embedded.shape
    inner = weights[0].shape[0]
    strip = wide // 4
    moving = pl.BlockSpec((inner, strip), lambda j, place: (0, j))
    return pl.pallas_call(
        mixed_kernel,
        grid_spec=pltpu.PrefetchScalarGridSpec(
            num_scalar_prefetch=1,
            grid=(4,),
            in_specs=[pl.BlockSpec((rows, strip), lambda j, place: (0, j))]
            + [whole(parts[0].shape)] * 4
            + [moving] * 4
            + [whole((1, wide)), whole((rows, 1))],
            out_specs=[
                whole((rows, HEAD)),
                whole((rows, wide // 2)),
                whole((rows, wide // 2)),
            ],
            scratch_shapes=[pltpu.VMEM((rows, wide), F32)],
        ),
        out_shape=[
            jax.ShapeDtypeStruct((rows, HEAD), F32),
            jax.ShapeDtypeStruct((rows, wide // 2), BF16),
            jax.ShapeDtypeStruct((rows, wide // 2), BF16),
        ],
        compiler_params=pltpu.CompilerParams(vmem_limit_bytes=LIMIT),
        cost_estimate=pl.CostEstimate(
            flops=8 * rows * wide * inner, bytes_accessed=8 * wide * inner, transcendentals=0
        ),
        name="mixed_rows",
    )(place, embedded, *parts, *weights, w_value.reshape(1, wide), returns.reshape(rows, 1))


def split_kernel(index_ref, own_ref, got_ref, *out_refs):
    count = len(out_refs)
    block = out_refs[0].shape[0]
    for k, out in enumerate(out_refs):
        owner = lax.rem(index_ref[0] + k, count)
        span = pl.ds(pl.multiple_of(owner * block, block), block)
        out[...] = (own_ref[span, :] + got_ref[span, :].astype(F32)).astype(BF16)


def split_sum(index, own, got, count):
    rows, wide = own.shape
    if (rows // count) % 16:
        got = got.astype(F32)
    shape = jax.ShapeDtypeStruct((rows // count, wide), BF16)
    return pl.pallas_call(
        split_kernel,
        in_specs=[pl.BlockSpec(memory_space=pltpu.SMEM), VMEM, VMEM],
        out_specs=[VMEM] * count,
        out_shape=[shape] * count,
        compiler_params=pltpu.CompilerParams(vmem_limit_bytes=LIMIT),
        cost_estimate=pl.CostEstimate(
            flops=rows * wide, bytes_accessed=8 * rows * wide, transcendentals=0
        ),
        name="split_sum",
    )(index, own, got)


def assemble_kernel(count, chunks, place_ref, *refs):
    out = refs[-1]
    block, strip = refs[0].shape
    for c in range(chunks):
        for side in range(2):
            for k in range(count):
                part = refs[(c * 2 + side) * count + k]
                owner = lax.rem(place_ref[1] + count - k, count)
                column = ((place_ref[0] ^ side) * chunks + c) * strip
                out[
                    pl.ds(pl.multiple_of(owner * block, block), block),
                    pl.ds(pl.multiple_of(column, strip), strip),
                ] = part[...].astype(F32)


def assemble(place, parts, count, chunks):
    block, strip = parts[0].shape
    rows, wide = block * count, strip * 2 * chunks
    return pl.pallas_call(
        functools.partial(assemble_kernel, count, chunks),
        in_specs=[pl.BlockSpec(memory_space=pltpu.SMEM)] + [VMEM] * len(parts),
        out_specs=VMEM,
        out_shape=jax.ShapeDtypeStruct((rows, wide), F32),
        compiler_params=pltpu.CompilerParams(vmem_limit_bytes=LIMIT),
        cost_estimate=pl.CostEstimate(
            flops=rows * wide, bytes_accessed=6 * rows * wide, transcendentals=0
        ),
        name="assemble",
    )(place, *parts)


def swap(block, axis, bit):
    size = lax.axis_size(axis)
    return lax.ppermute(block, axis, [(i, i ^ bit) for i in range(size)])


def shift(block, axis, step):
    size = lax.axis_size(axis)
    return lax.ppermute(block, axis, [(i, (i + step) % size) for i in range(size)])


def gather_parts(part):
    far = swap(part, "mdl", 2)
    return [part, swap(part, "mdl", 1), far, swap(far, "mdl", 1)], far


def product(left, right):
    return jnp.einsum("rh,rd->hd", left, right, preferred_element_type=F32)


def scatter_shifts(blocks):
    return [shift(block, "rep", k) for k, block in enumerate(blocks) if k > 0]


def shift_total(blocks, moved):
    total = blocks[0].astype(F32)
    for block in moved:
        total = total + block.astype(F32)
    return total.astype(BF16)


def gather_shifts(total):
    return [total] + [shift(total, "rep", k) for k in range(1, lax.axis_size("rep"))]


def half_of(weight, side):
    half = weight.shape[1] // 2
    return lax.dynamic_slice_in_dim(weight, side * half, half, 1)


def on_device(
    obs,
    a_query,
    a_keyval,
    a_out,
    w_policy,
    c_in,
    c_query,
    c_keyval,
    c_out,
    w_value,
    actions,
    advantages,
    old_logp,
    returns,
    robot_count,
):
    row_count = obs.shape[1]
    batch_index = lax.axis_index("sec")
    rep_index = lax.axis_index("rep")
    rep_count = lax.axis_size("rep")
    robot_total = robot_count[batch_index]
    live_sum = jnp.sum(robot_count)
    live_total = live_sum.astype(F32)
    first_row = rep_index * row_count
    live_mask = first_row + lax.iota(jnp.int32, row_count) < robot_total
    mdl_count = lax.axis_size("mdl")
    assert mdl_count == 4 and lax.axis_size("sec") == 2
    mdl_index = lax.axis_index("mdl")
    part_rows = row_count // mdl_count
    row_start = mdl_index * part_rows
    score_scale = HEAD ** (-0.5) * LOG2E
    rep_place = rep_index.reshape(1).astype(jnp.int32)
    place = jnp.stack([batch_index, mdl_index, first_row, robot_total, live_sum]).astype(jnp.int32)

    obs_in = obs[0]
    keyval, factor_a = first_projection(obs_in, a_keyval)
    keyval_all = lax.all_gather(keyval, "rep", axis=1, tiled=True)

    a_near = swap(a_out, "mdl", 1)
    c_near = swap(c_in, "mdl", 1)
    a_far0 = swap(half_of(a_out, batch_index), "mdl", 2)
    a_far0, c_src = tied(a_far0, half_of(c_in, batch_index))
    a_far1 = swap(a_far0, "sec", 1)
    c_far0 = swap(c_src, "mdl", 2)

    queries = (dot(obs_in, a_query) * (factor_a[:, :1] * score_scale)).astype(BF16)
    queries, a_far0 = tied(queries, a_far0)
    attended = attend(queries, keyval_all, robot_total)
    attended, a_far1, c_far0 = tied(attended, a_far1, c_far0)
    attended_parts, attended_far = gather_parts(attended)
    c_far1 = swap(c_far0, "sec", 1)
    a_halves = [a_far0, a_far1, swap(a_far0, "mdl", 1), swap(a_far1, "mdl", 1)]
    c_halves = [c_far0, c_far1, swap(c_far0, "mdl", 1), swap(c_far1, "mdl", 1)]
    hidden = hidden_rows(place, obs_in, attended_parts, [a_out, a_near], a_halves)

    attended_far, c_out_src = tied(attended_far, c_out)
    c_out_far = swap(c_out_src, "mdl", 2)

    embedded, critic_keyval, factor_c = embed_rows(
        place, hidden, [c_in, c_near], c_halves, c_keyval
    )
    critic_keyval_all = lax.all_gather(critic_keyval, "rep", axis=1, tiled=True)
    critic_queries = (dot(embedded, c_query) * (factor_c[:, :1] * score_scale)).astype(BF16)

    late_hidden, critic_keyval = tied(hidden, critic_keyval)
    source = late_hidden.astype(F32)
    factor_h = row_factor(source)
    logits = dot(late_hidden, w_policy) * factor_h
    log_probs = jax.nn.log_softmax(logits, axis=-1)
    onehot = (
        actions[0][:, None] == lax.broadcasted_iota(jnp.int32, logits.shape, 1)
    ).astype(F32)
    chosen = jnp.sum(onehot * log_probs, axis=-1)
    prob_ratio = jnp.exp(chosen - old_logp[0])
    plain_term = prob_ratio * advantages[0]
    bounded = jnp.clip(prob_ratio, 1.0 - clip_range, 1.0 + clip_range) * advantages[0]
    slope = jnp.where(live_mask & (plain_term <= bounded), -plain_term / live_total, F32(0.0))
    dlogits = slope[:, None] * (onehot - jnp.exp(log_probs))
    along = jnp.sum(dlogits * logits, axis=-1, keepdims=True) / source.shape[1]
    dnormed = dot(dlogits.astype(BF16), w_policy.T)
    dhidden = (factor_h * (dnormed - source * (factor_h * along))).astype(BF16)
    half_a = dhidden.shape[1] // 2
    got_a = swap(
        product(attended, lax.dynamic_slice_in_dim(dhidden, (1 - batch_index) * half_a, half_a, 1))
        .astype(BF16),
        "sec",
        1,
    )
    own_a = product(attended, lax.dynamic_slice_in_dim(dhidden, batch_index * half_a, half_a, 1))
    blocks_a = split_sum(rep_place, own_a, got_a, rep_count)
    critic_queries, *blocks_a = tied(critic_queries, *blocks_a)

    moved_a = scatter_shifts(blocks_a)
    critic_attended = attend(critic_queries, critic_keyval_all, robot_total)
    critic_attended, *moved_a = tied(critic_attended, *moved_a)
    critic_attended, c_out_far = tied(critic_attended, c_out_far)
    mine_a = gather_shifts(shift_total(blocks_a, moved_a))
    critic_parts, critic_far = gather_parts(critic_attended)
    critic_near, *mine_a = tied(critic_parts[3], *mine_a)
    critic_parts[3] = critic_near
    c_out_all = [c_out, swap(c_out, "mdl", 1), c_out_far, swap(c_out_far, "mdl", 1)]
    pieces_a = mine_a + [swap(block, "sec", 1) for block in mine_a]
    value_wide, d_other, d_own = mixed_rows(
        place, embedded, critic_parts, c_out_all, w_value, returns[0]
    )

    strip = d_own.shape[1] // CHUNKS
    spans = [slice(c * strip, (c + 1) * strip) for c in range(CHUNKS)]
    got = [
        swap(product(critic_attended, d_other[:, span]).astype(BF16), "sec", 1) for span in spans
    ]
    own = [product(critic_attended, d_own[:, span]) for span in spans]
    pieces = []
    for c in range(CHUNKS):
        blocks = split_sum(rep_place, own[c], got[c], rep_count)
        mine = gather_shifts(shift_total(blocks, scatter_shifts(blocks)))
        pieces += mine + [swap(block, "sec", 1) for block in mine]
    corner = jnp.stack([batch_index, rep_index]).astype(jnp.int32)
    actor_summed = assemble(corner, pieces_a, rep_count, 1)
    critic_summed = assemble(corner, pieces, rep_count, CHUNKS)

    value_part = lax.dynamic_slice_in_dim(value_wide, row_start, part_rows, 0)[:, 0]
    return (value_part[None, :], actor_summed, critic_summed)


def solution(mesh):
    return jax.shard_map(
        on_device,
        mesh=mesh,
        in_specs=(
            P("sec", "rep", None),
            P(None, "mdl"),
            P(None, None, "mdl"),
            P("mdl", None),
            P(),
            P(None, "mdl"),
            P(None, "mdl"),
            P(None, None, "mdl"),
            P("mdl", None),
            P(),
            P("sec", "rep"),
            P("sec", "rep"),
            P("sec", "rep"),
            P("sec", "rep"),
            P(),
        ),
        out_specs=(P("sec", ("rep", "mdl")), P("mdl", None), P("mdl", None)),
        check_vma=False,
    )
```

time: 391 us -> 282 us (0.72)
  waiting for transfers between devices: 269 us -> 113 us
  starting transfers between devices: 11.3 us -> 56.4 us
  matrix products: 45.2 us -> 9.96 us
  Pallas kernels: 22.3 us -> 57.3 us
  local copies, waits for them, and re-layouts: 16.7 us -> 24.1 us
  other arithmetic: 11.4 us -> 5.05 us
    psum x2 -> x0, waiting for transfers between devices: 159 us -> none  [the longest x1 102 us: on_device(): critic_summed = lax.psum(critic_grad, ('rep', 'sec'))]
    ppermute x15 -> x52, starting transfers between devices: 11 us -> 56.3 us  [the longest x34 29.8 us: swap(): return lax.ppermute(block, axis, [(i, i ^ bit) for i in range(size)])]
    pallas_call x0 -> x9, Pallas kernels: none -> 34.8 us  [the longest x1 10.1 us: mixed_rows(): pl.pallas_call(mixed_kernel, grid_spec=pltpu.PrefetchScalarGridSpec(num_s...]
    dot_general x16 -> x4, matrix products: 38.5 us -> 7.07 us  [dot(): return jnp.dot(a, b, preferred_element_type=F32)]
    all_gather x1, waiting for transfers between devices: 24.8 us -> 8.74 us  [on_device(): critic_keyval_all = lax.all_gather(critic_keyval, 'rep', axis=1, tiled=True)]
    ppermute x15 -> x52, waiting for transfers between devices: 84.6 us -> 99.1 us  [the longest x34 70 us: swap(): return lax.ppermute(block, axis, [(i, i ^ bit) for i in range(size)])]
    unnamed x44 -> x76, local copies, waits for them, and re-layouts: 3.81 us -> 17.5 us
    dynamic_update_slice x4 -> x0, local copies, waits for them, and re-layouts: 8.26 us -> none  [on_device(): lax.dynamic_update_slice(c_in_all, weight, (0, (mdl_index ^ code) * width...]
  transfers between devices with their start and end apart: 19 -> 54, of which waited for: 6 -> 19; matrix products, arithmetic and copies ran while one was open for 15% -> 8% of each run, Pallas kernels for 6% -> 19%
where the time goes in v2:
time: 282 us; the launch traced here: 281 us
  waiting for transfers between devices  113 us (40%)
  Pallas kernels  57.3 us (20%)
  starting transfers between devices  56.4 us (20%)
  local copies, waits for them, and re-layouts  24.1 us (9%)
  between operations  15.2 us (5%)
  matrix products  9.96 us (4%)
  other arithmetic  5.05 us (2%)
    ppermute x34, waiting for transfers between devices, swap(): return lax.ppermute(block, axis, [(i, i ^ bit) for i in range(size)])  70 us
    ppermute x34, starting transfers between devices, swap(): return lax.ppermute(block, axis, [(i, i ^ bit) for i in range(size)])  29.8 us
    ppermute x18, waiting for transfers between devices, shift(): lax.ppermute(block, axis, [(i, (i + step) % size) for i in range(size)])  29.1 us
    ppermute x18, starting transfers between devices, shift(): lax.ppermute(block, axis, [(i, (i + step) % size) for i in range(size)])  26.5 us
    pallas_call x2, Pallas kernels, attend(): pl.pallas_call(attend_kernel, grid=(heads, rows // block), in_specs=[pl.B...  22.5 us
    unnamed x76, local copies, waits for them, and re-layouts  17.5 us
    pallas_call x1, Pallas kernels, mixed_rows(): pl.pallas_call(mixed_kernel, grid_spec=pltpu.PrefetchScalarGridSpec(num_s...  10.1 us
    pallas_call x1, Pallas kernels, embed_rows(): pl.pallas_call(embed_kernel, grid_spec=pltpu.PrefetchScalarGridSpec(num_s...  9.58 us
  transfers between devices with their start and end apart: 54, of which 19 were waited for; matrix products, arithmetic and copies ran while one was open for 8% of the time, Pallas kernels for 19%

profile of v2, /device:TPU:0, one launch (start us, length us, event | category | flops | bytes accessed | tf_op | source)
XLA Modules:
  0.0 281.1 jit_solution(17532077801882191264)
XLA Ops:
  12.3 3.0 %collective-permute-start = (bf16[384,768]{1,0:T(8,128)(2,1)}, bf16[384,768]{1,0:T(8,128)(2,1)}, u32[]{:S(2)}, u32[]{:S(2)}) collective-permute-start(bf16[384,768]{1,0:T(8,128)(2,1)} %constant_dynamic-slice_fusion.1), channel_id=1, source_target_pairs={{0,2},{1,3},{2,0},{3,1},{4,6},{5,7},{6,4},{7,5},{8,10},{9,11},{10,... | collective-permute-start | bytes 1769480 | tf_op jit(solution)/shard_map/ppermute | solution.py:355
  17.4 11.6 %collective-permute-done.w20 = bf16[384,768]{1,0:T(8,128)(2,1)} collective-permute-done((bf16[384,768]{1,0:T(8,128)(2,1)}, bf16[384,768]{1,0:T(8,128)(2,1)}, u32[]{:S(2)}, u32[]{:S(2)}) %collective-permute-start) | collective-permute-done | bytes 589856 | tf_op jit(solution)/shard_map/ppermute | solution.py:355
  33.5 3.5 %fusion.5.q_ref = bf16[512,384]{1,0:T(8,128)(2,1)} fusion(bf16[1536,384]{1,0:T(8,128)(2,1)} %param.16, f32[512]{0:T(512)S(1)} %multiply_reduce_fusion.2, bf16[1,512,1536]{2,1,0:T(8,128)(2,1)} %param.15), kind=kOutput, calls=%fused_computation.12 | convolution fusion | flops 604372992 | bytes 3147776 | tf_op jit(solution)/shard_map/dot_general | solution.py:24
  37.0 5.2 %all-gather.3.cloned.1.call-done.k_ref.v_ref = bf16[2,2048,128]{2,1,0:T(8,128)(2,1)} async-done(((bf16[2,512,128]{2,1,0:T(8,128)(2,1)}), bf16[2,2048,128]{2,1,0:T(8,128)(2,1)}) %all-gather.3.cloned.1.call-update) | async-done | bytes 1048592 | tf_op jit(solution)/shard_map/all_gather | solution.py:429
  44.4 9.7 %attend.2.t0 = bf16[512,384]{1,0:T(8,128)(2,1)S(1)} custom-call(s32[1]{0:T(128)} %dynamic_slice.18.total_ref, bf16[512,384]{1,0:T(8,128)(2,1)S(1)} %copy-done.27, bf16[2,2048,128]{2,1,0:T(8,128)(2,1)S(1)} %copy-done.25, bf16[2,2048,128]{2,1,0:T(8,128)(2,1)S(1)} %copy-done.25), custom_call_target="tpu_custom_call" | custom-call | flops 1610612736 | bytes 786432 | tf_op jit(solution)/shard_map/attend/pallas_call | solution.py:96
  58.4 7.8 %collective-permute-done.4.t2 = bf16[512,384]{1,0:T(8,128)(2,1)} collective-permute-done((bf16[512,384]{1,0:T(8,128)(2,1)S(1)}, bf16[512,384]{1,0:T(8,128)(2,1)}, u32[]{:S(2)}, u32[]{:S(2)}) %collective-permute-start.4) | collective-permute-done | bytes 393248 | tf_op jit(solution)/shard_map/ppermute | solution.py:355
  66.2 7.4 %collective-permute-done.10.w21 = bf16[1536,256]{1,0:T(8,128)(2,1)} collective-permute-done((bf16[1536,256]{1,0:T(8,128)(2,1)}, bf16[1536,256]{1,0:T(8,128)(2,1)}, u32[]{:S(2)}, u32[]{:S(2)}) %collective-permute-start.10) | collective-permute-done | bytes 786464 | tf_op jit(solution)/shard_map/ppermute | solution.py:355
  81.2 7.4 %hidden_rows.1.h_ref = bf16[512,1536]{1,0:T(8,128)(2,1)} custom-call(s32[5]{0:T(128)S(1)} %stack.24.place_ref, bf16[512,1536]{1,0:T(8,128)(2,1)} %bitcast.26, bf16[512,384]{1,0:T(8,128)(2,1)S(1)} %copy-done.4, bf16[512,384]{1,0:T(8,128)(2,1)S(1)} %copy-done.8, bf16[512,384]{1,0:T(8,128)(2,1)} %collective-permute-done.4.t2, ...), custom_call_target="tpu_custom_call" | custom-call | flops 2415919104 | bytes 4718592 | tf_op jit(solution)/shard_map/hidden_rows/pallas_call | solution.py:138
  88.6 9.6 %embed_rows.1 = (bf16[512,2048]{1,0:T(8,128)(2,1)}, bf16[2,512,128]{2,1,0:T(8,128)(2,1)}, f32[512,128]{1,0:T(8,128)S(1)}) custom-call(s32[5]{0:T(128)S(1)} %stack.24.place_ref, bf16[512,1536]{1,0:T(8,128)(2,1)} %hidden_rows.1.h_ref, bf16[1536,512]{1,0:T(8,128)(2,1)} %w0.4, bf16[1536,512]{1,0:T(8,128)(2,1)} %collective-permute-done.9.w1, ...), custom_call_target="tpu_custom_call" | custom-call | flops 3221225472 | bytes 6291456 | tf_op jit(solution)/shard_map/embed_rows/pallas_call | solution.py:198
  107.6 11.2 %collective-permute-done.13.got_ref = bf16[384,768]{1,0:T(8,128)(2,1)S(1)} collective-permute-done((bf16[384,768]{1,0:T(8,128)(2,1)S(1)}, bf16[384,768]{1,0:T(8,128)(2,1)S(1)}, u32[]{:S(2)}, u32[]{:S(2)}) %collective-permute-start.13) | collective-permute-done | bytes 589856 | tf_op jit(solution)/shard_map/ppermute | solution.py:355
  124.0 8.7 %all-gather.5.cloned.1.call-done.k_ref.v_ref = bf16[2,2048,128]{2,1,0:T(8,128)(2,1)} async-done(((bf16[2,512,128]{2,1,0:T(8,128)(2,1)}), bf16[2,2048,128]{2,1,0:T(8,128)(2,1)}) %all-gather.5.cloned.1.call-update) | async-done | bytes 1048592 | tf_op jit(solution)/shard_map/all_gather | solution.py:454
  135.0 12.8 %attend.3.t0 = bf16[512,512]{1,0:T(8,128)(2,1)S(1)} custom-call(s32[1]{0:T(128)} %dynamic_slice.18.total_ref, bf16[512,512]{1,0:T(8,128)(2,1)S(1)} %copy-done.28, bf16[2,2048,128]{2,1,0:T(8,128)(2,1)S(1)} %copy-done.26, bf16[2,2048,128]{2,1,0:T(8,128)(2,1)S(1)} %copy-done.26), custom_call_target="tpu_custom_call" | custom-call | flops 2147483648 | bytes 1048576 | tf_op jit(solution)/shard_map/attend/pallas_call | solution.py:96
  150.4 12.5 %collective-permute-done.19.t2 = bf16[512,512]{1,0:T(8,128)(2,1)} collective-permute-done((bf16[512,512]{1,0:T(8,128)(2,1)S(1)}, bf16[512,512]{1,0:T(8,128)(2,1)}, u32[]{:S(2)}, u32[]{:S(2)}) %collective-permute-start.19) | collective-permute-done | bytes 524320 | tf_op jit(solution)/shard_map/ppermute | solution.py:355
  164.0 8.0 %collective-permute-done.21.refs_1_ = bf16[96,768]{1,0:T(8,128)(2,1)S(1)} collective-permute-done((bf16[96,768]{1,0:T(8,128)(2,1)S(1)}, bf16[96,768]{1,0:T(8,128)(2,1)S(1)}, u32[]{:S(2)}, u32[]{:S(2)}) %collective-permute-start.21) | collective-permute-done | bytes 147488 | tf_op jit(solution)/shard_map/ppermute | solution.py:360
  172.0 7.7 %collective-permute-done.22.refs_2_ = bf16[96,768]{1,0:T(8,128)(2,1)S(1)} collective-permute-done((bf16[96,768]{1,0:T(8,128)(2,1)S(1)}, bf16[96,768]{1,0:T(8,128)(2,1)S(1)}, u32[]{:S(2)}, u32[]{:S(2)}) %collective-permute-start.22) | collective-permute-done | bytes 147488 | tf_op jit(solution)/shard_map/ppermute | solution.py:360
  181.3 4.2 %collective-permute-done.23.refs_3_ = bf16[96,768]{1,0:T(8,128)(2,1)S(1)} collective-permute-done((bf16[96,768]{1,0:T(8,128)(2,1)S(1)}, bf16[96,768]{1,0:T(8,128)(2,1)S(1)}, u32[]{:S(2)}, u32[]{:S(2)}) %collective-permute-start.23) | collective-permute-done | bytes 147488 | tf_op jit(solution)/shard_map/ppermute | solution.py:360
  187.0 10.1 %mixed_rows.1 = (f32[512,128]{1,0:T(8,128)S(1)}, bf16[512,1024]{1,0:T(8,128)(2,1)S(1)}, bf16[512,1024]{1,0:T(8,128)(2,1)S(1)}) custom-call(s32[5]{0:T(128)S(1)} %stack.24.place_ref, bf16[512,2048]{1,0:T(8,128)(2,1)} %get-tuple-element.57.emb_ref, bf16[512,512]{1,0:T(8,128)(2,1)S(1)} %attend.3.t0, bf16[512,512]{1,0:T(8,128)(2,1)} %collective-permute-done.18.t1, ...), custom_call_target="tpu_custom_call" | custom-call | flops 4294967296 | bytes 8388608 | tf_op jit(solution)/shard_map/mixed_rows/pallas_call | solution.py:266
  200.7 11.8 %collective-permute-done.41.got_ref = bf16[512,512]{1,0:T(8,128)(2,1)S(1)} collective-permute-done((bf16[512,512]{1,0:T(8,128)(2,1)S(1)}, bf16[512,512]{1,0:T(8,128)(2,1)S(1)}, u32[]{:S(2)}, u32[]{:S(2)}) %collective-permute-start.41) | collective-permute-done | bytes 524320 | tf_op jit(solution)/shard_map/ppermute | solution.py:355
  212.7 3.1 %collective-permute-start.43 = (bf16[128,512]{1,0:T(8,128)(2,1)S(1)}, bf16[128,512]{1,0:T(8,128)(2,1)S(1)}, u32[]{:S(2)}, u32[]{:S(2)}) collective-permute-start(bf16[128,512]{1,0:T(8,128)(2,1)S(1)} %get-tuple-element.91), channel_id=1, source_target_pairs={{0,16},{8,24},{16,0},{24,8},{1,17},{9,25},{17,1},{25,9},{2,18},{10... | collective-permute-start | bytes 393224 | tf_op jit(solution)/shard_map/ppermute | solution.py:360
  217.0 4.6 %collective-permute-done.30.got_ref = bf16[512,512]{1,0:T(8,128)(2,1)S(1)} collective-permute-done((bf16[512,512]{1,0:T(8,128)(2,1)S(1)}, bf16[512,512]{1,0:T(8,128)(2,1)S(1)}, u32[]{:S(2)}, u32[]{:S(2)}) %collective-permute-start.30) | collective-permute-done | bytes 524320 | tf_op jit(solution)/shard_map/ppermute | solution.py:355
  233.1 4.0 %collective-permute-done.32 = bf16[128,512]{1,0:T(8,128)(2,1)S(1)} collective-permute-done((bf16[128,512]{1,0:T(8,128)(2,1)S(1)}, bf16[128,512]{1,0:T(8,128)(2,1)S(1)}, u32[]{:S(2)}, u32[]{:S(2)}) %collective-permute-start.32) | collective-permute-done | bytes 131104 | tf_op jit(solution)/shard_map/ppermute | solution.py:360
  237.1 5.7 %collective-permute-start.47 = (bf16[128,512]{1,0:T(8,128)(2,1)S(1)}, bf16[128,512]{1,0:T(8,128)(2,1)}, u32[]{:S(2)}, u32[]{:S(2)}) collective-permute-start(bf16[128,512]{1,0:T(8,128)(2,1)S(1)} %add_convert_fusion.1.refs_8_), channel_id=1, source_target_pairs={{0,24},{8,0},{16,8},{24,16},{1,25},{9,1},{17,9},{25,17},{2,26},{10... | collective-permute-start | bytes 393224 | tf_op jit(solution)/shard_map/ppermute | solution.py:360
  244.0 2.9 %collective-permute-start.34 = (bf16[128,512]{1,0:T(8,128)(2,1)S(1)}, bf16[128,512]{1,0:T(8,128)(2,1)}, u32[]{:S(2)}, u32[]{:S(2)}) collective-permute-start(bf16[128,512]{1,0:T(8,128)(2,1)S(1)} %add_convert_fusion.2.refs_0_), channel_id=1, source_target_pairs={{0,8},{8,16},{16,24},{24,0},{1,9},{9,17},{17,25},{25,1},{2,10},{10... | collective-permute-start | bytes 393224 | tf_op jit(solution)/shard_map/ppermute | solution.py:360
  270.5 3.7 %assemble.3 = f32[512,2048]{1,0:T(8,128)} custom-call(s32[2]{0:T(128)S(1)} %pad_add_fusion.place_ref, bf16[128,512]{1,0:T(8,128)(2,1)S(1)} %add_convert_fusion.2.refs_0_, bf16[128,512]{1,0:T(8,128)(2,1)} %collective-permute-done.34.refs_1_, bf16[128,512]{1,0:T(8,128)(2,1)} %collective-permute-done.35.refs_2_, ...), custom_call_target="tpu_custom_call" | custom-call | flops 1048576 | bytes 6291456 | tf_op jit(solution)/shard_map/assemble/pallas_call | solution.py:340
  (205 shorter events, 89.9 us)
Async XLA Ops:
  7.2 35.0 %all-gather.3.cloned.1.call-start = ((), (), s32[]{:S(2)}) async-start(), calls=%async_computation | async-start | bytes 1310720 | tf_op jit(solution)/shard_map/all_gather | solution.py:429
  11.4 121.4 %all-gather.5.cloned.1.call-start = ((), (), s32[]{:S(2)}) async-start(), calls=%async_computation.1 | async-start | bytes 1310720 | tf_op jit(solution)/shard_map/all_gather | solution.py:454
  12.3 16.6 %collective-permute-start = (bf16[384,768]{1,0:T(8,128)(2,1)}, bf16[384,768]{1,0:T(8,128)(2,1)}, u32[]{:S(2)}, u32[]{:S(2)}) collective-permute-start(bf16[384,768]{1,0:T(8,128)(2,1)} %constant_dynamic-slice_fusion.1), channel_id=1, source_target_pairs={{0,2},{1,3},{2,0},{3,1},{4,6},{5,7},{6,4},{7,5},{8,10},{9,11},{10,... | collective-permute-start | bytes 1769480 | tf_op jit(solution)/shard_map/ppermute | solution.py:355
  28.9 25.2 %collective-permute-start.2 = (bf16[1536,256]{1,0:T(8,128)(2,1)}, bf16[1536,256]{1,0:T(8,128)(2,1)}, u32[]{:S(2)}, u32[]{:S(2)}) collective-permute-start(bf16[1536,256]{1,0:T(8,128)(2,1)} %constant_dynamic-slice_fusion), channel_id=1, source_target_pairs={{0,2},{1,3},{2,0},{3,1},{4,6},{5,7},{6,4},{7,5},{8,10},{9,11},{10,... | collective-permute-start | bytes 2359304 | tf_op jit(solution)/shard_map/ppermute | solution.py:355
  30.7 23.4 %collective-permute-start.1 = (bf16[384,768]{1,0:T(8,128)(2,1)}, bf16[384,768]{1,0:T(8,128)(2,1)}, u32[]{:S(2)}, u32[]{:S(2)}) collective-permute-start(bf16[384,768]{1,0:T(8,128)(2,1)} %collective-permute-done.w20), channel_id=1, source_target_pairs={{0,4},{4,0},{1,5},{5,1},{2,6},{6,2},{3,7},{7,3},{8,12},{12,8},{9,1... | collective-permute-start | bytes 1769480 | tf_op jit(solution)/shard_map/ppermute | solution.py:355
  32.2 25.7 %collective-permute-start.6 = (bf16[384,1536]{1,0:T(8,128)(2,1)S(1)}, bf16[384,1536]{1,0:T(8,128)(2,1)}, u32[]{:S(2)}, u32[]{:S(2)}) collective-permute-start(bf16[384,1536]{1,0:T(8,128)(2,1)S(1)} %copy-done.2), channel_id=1, source_target_pairs={{0,1},{1,0},{2,3},{3,2},{4,5},{5,4},{6,7},{7,6},{8,9},{9,8},{10,11... | collective-permute-start | bytes 3538952 | tf_op jit(solution)/shard_map/ppermute | solution.py:355
  32.2 56.4 %collective-permute-start.9 = (bf16[1536,512]{1,0:T(8,128)(2,1)}, bf16[1536,512]{1,0:T(8,128)(2,1)}, u32[]{:S(2)}, u32[]{:S(2)}) collective-permute-start(bf16[1536,512]{1,0:T(8,128)(2,1)} %w0.4), channel_id=1, source_target_pairs={{0,1},{1,0},{2,3},{3,2},{4,5},{5,4},{6,7},{7,6},{8,9},{9,8},{10,11... | collective-permute-start | bytes 4718600 | tf_op jit(solution)/shard_map/ppermute | solution.py:355
  37.0 20.1 %collective-permute-start.7 = (bf16[384,768]{1,0:T(8,128)(2,1)}, bf16[384,768]{1,0:T(8,128)(2,1)}, u32[]{:S(2)}, u32[]{:S(2)}) collective-permute-start(bf16[384,768]{1,0:T(8,128)(2,1)} %collective-permute-done.w20), channel_id=1, source_target_pairs={{0,1},{1,0},{2,3},{3,2},{4,5},{5,4},{6,7},{7,6},{8,9},{9,8},{10,11... | collective-permute-start | bytes 1769480 | tf_op jit(solution)/shard_map/ppermute | solution.py:355
  54.1 19.5 %collective-permute-start.10 = (bf16[1536,256]{1,0:T(8,128)(2,1)}, bf16[1536,256]{1,0:T(8,128)(2,1)}, u32[]{:S(2)}, u32[]{:S(2)}) collective-permute-start(bf16[1536,256]{1,0:T(8,128)(2,1)} %collective-permute-done.2.w20), channel_id=1, source_target_pairs={{0,4},{4,0},{1,5},{5,1},{2,6},{6,2},{3,7},{7,3},{8,12},{12,8},{9,1... | collective-permute-start | bytes 2359304 | tf_op jit(solution)/shard_map/ppermute | solution.py:355
  57.1 16.5 %collective-permute-start.3 = (bf16[512,384]{1,0:T(8,128)(2,1)S(1)}, bf16[512,384]{1,0:T(8,128)(2,1)S(1)}, u32[]{:S(2)}, u32[]{:S(2)}) collective-permute-start(bf16[512,384]{1,0:T(8,128)(2,1)S(1)} %attend.2.t0), channel_id=1, source_target_pairs={{0,1},{1,0},{2,3},{3,2},{4,5},{5,4},{6,7},{7,6},{8,9},{9,8},{10,11... | collective-permute-start | bytes 1179656 | tf_op jit(solution)/shard_map/ppermute | solution.py:355
  57.9 19.7 %collective-permute-start.8 = (bf16[384,768]{1,0:T(8,128)(2,1)}, bf16[384,768]{1,0:T(8,128)(2,1)}, u32[]{:S(2)}, u32[]{:S(2)}) collective-permute-start(bf16[384,768]{1,0:T(8,128)(2,1)} %collective-permute-done.1.w21), channel_id=1, source_target_pairs={{0,1},{1,0},{2,3},{3,2},{4,5},{5,4},{6,7},{7,6},{8,9},{9,8},{10,11... | collective-permute-start | bytes 1769480 | tf_op jit(solution)/shard_map/ppermute | solution.py:355
  66.2 22.4 %collective-permute-start.11 = (bf16[1536,256]{1,0:T(8,128)(2,1)}, bf16[1536,256]{1,0:T(8,128)(2,1)}, u32[]{:S(2)}, u32[]{:S(2)}) collective-permute-start(bf16[1536,256]{1,0:T(8,128)(2,1)} %collective-permute-done.2.w20), channel_id=1, source_target_pairs={{0,1},{1,0},{2,3},{3,2},{4,5},{5,4},{6,7},{7,6},{8,9},{9,8},{10,11... | collective-permute-start | bytes 2359304 | tf_op jit(solution)/shard_map/ppermute | solution.py:355
  77.6 109.4 %collective-permute-start.24 = (bf16[512,2048]{1,0:T(8,128)(2,1)}, bf16[512,2048]{1,0:T(8,128)(2,1)}, u32[]{:S(2)}, u32[]{:S(2)}) collective-permute-start(bf16[512,2048]{1,0:T(8,128)(2,1)} %w0.5), channel_id=1, source_target_pairs={{0,1},{1,0},{2,3},{3,2},{4,5},{5,4},{6,7},{7,6},{8,9},{9,8},{10,11... | collective-permute-start | bytes 6291464 | tf_op jit(solution)/shard_map/ppermute | solution.py:355
  77.6 70.3 %collective-permute-start.17 = (bf16[512,2048]{1,0:T(8,128)(2,1)}, bf16[512,2048]{1,0:T(8,128)(2,1)}, u32[]{:S(2)}, u32[]{:S(2)}) collective-permute-start(bf16[512,2048]{1,0:T(8,128)(2,1)} %w0.5), channel_id=1, source_target_pairs={{0,2},{1,3},{2,0},{3,1},{4,6},{5,7},{6,4},{7,5},{8,10},{9,11},{10,... | collective-permute-start | bytes 6291464 | tf_op jit(solution)/shard_map/ppermute | solution.py:355
  119.0 28.9 %collective-permute-start.14 = (bf16[96,768]{1,0:T(8,128)(2,1)S(1)}, bf16[96,768]{1,0:T(8,128)(2,1)S(1)}, u32[]{:S(2)}, u32[]{:S(2)}) collective-permute-start(bf16[96,768]{1,0:T(8,128)(2,1)S(1)} %get-tuple-element.66), channel_id=1, source_target_pairs={{0,8},{8,16},{16,24},{24,0},{1,9},{9,17},{17,25},{25,1},{2,10},{10... | collective-permute-start | bytes 442376 | tf_op jit(solution)/shard_map/ppermute | solution.py:360
  120.4 27.5 %collective-permute-start.15 = (bf16[96,768]{1,0:T(8,128)(2,1)S(1)}, bf16[96,768]{1,0:T(8,128)(2,1)}, u32[]{:S(2)}, u32[]{:S(2)}) collective-permute-start(bf16[96,768]{1,0:T(8,128)(2,1)S(1)} %get-tuple-element.67), channel_id=1, source_target_pairs={{0,16},{8,24},{16,0},{24,8},{1,17},{9,25},{17,1},{25,9},{2,18},{10... | collective-permute-start | bytes 442376 | tf_op jit(solution)/shard_map/ppermute | solution.py:360
  121.8 26.1 %collective-permute-start.16 = (bf16[96,768]{1,0:T(8,128)(2,1)S(1)}, bf16[96,768]{1,0:T(8,128)(2,1)}, u32[]{:S(2)}, u32[]{:S(2)}) collective-permute-start(bf16[96,768]{1,0:T(8,128)(2,1)S(1)} %get-tuple-element.68), channel_id=1, source_target_pairs={{0,24},{8,0},{16,8},{24,16},{1,25},{9,1},{17,9},{25,17},{2,26},{10... | collective-permute-start | bytes 442376 | tf_op jit(solution)/shard_map/ppermute | solution.py:360
  147.9 39.1 %collective-permute-start.25 = (bf16[512,2048]{1,0:T(8,128)(2,1)}, bf16[512,2048]{1,0:T(8,128)(2,1)}, u32[]{:S(2)}, u32[]{:S(2)}) collective-permute-start(bf16[512,2048]{1,0:T(8,128)(2,1)} %collective-permute-done.17.w2), channel_id=1, source_target_pairs={{0,1},{1,0},{2,3},{3,2},{4,5},{5,4},{6,7},{7,6},{8,9},{9,8},{10,11... | collective-permute-start | bytes 6291464 | tf_op jit(solution)/shard_map/ppermute | solution.py:355
  150.2 36.8 %collective-permute-start.18 = (bf16[512,512]{1,0:T(8,128)(2,1)S(1)}, bf16[512,512]{1,0:T(8,128)(2,1)}, u32[]{:S(2)}, u32[]{:S(2)}) collective-permute-start(bf16[512,512]{1,0:T(8,128)(2,1)S(1)} %attend.3.t0), channel_id=1, source_target_pairs={{0,1},{1,0},{2,3},{3,2},{4,5},{5,4},{6,7},{7,6},{8,9},{9,8},{10,11... | collective-permute-start | bytes 1572872 | tf_op jit(solution)/shard_map/ppermute | solution.py:355
  162.8 22.6 %collective-permute-start.20 = (bf16[512,512]{1,0:T(8,128)(2,1)}, bf16[512,512]{1,0:T(8,128)(2,1)}, u32[]{:S(2)}, u32[]{:S(2)}) collective-permute-start(bf16[512,512]{1,0:T(8,128)(2,1)} %collective-permute-done.19.t2), channel_id=1, source_target_pairs={{0,1},{1,0},{2,3},{3,2},{4,5},{5,4},{6,7},{7,6},{8,9},{9,8},{10,11... | collective-permute-start | bytes 1572872 | tf_op jit(solution)/shard_map/ppermute | solution.py:355
  185.5 36.8 %collective-permute-start.26 = (bf16[96,768]{1,0:T(8,128)(2,1)S(1)}, bf16[96,768]{1,0:T(8,128)(2,1)S(1)}, u32[]{:S(2)}, u32[]{:S(2)}) collective-permute-start(bf16[96,768]{1,0:T(8,128)(2,1)S(1)} %add_convert_fusion.refs_0_), channel_id=1, source_target_pairs={{0,4},{4,0},{1,5},{5,1},{2,6},{6,2},{3,7},{7,3},{8,12},{12,8},{9,1... | collective-permute-start | bytes 442376 | tf_op jit(solution)/shard_map/ppermute | solution.py:355
  198.6 23.0 %collective-permute-start.30 = (bf16[512,512]{1,0:T(8,128)(2,1)S(1)}, bf16[512,512]{1,0:T(8,128)(2,1)S(1)}, u32[]{:S(2)}, u32[]{:S(2)}) collective-permute-start(bf16[512,512]{1,0:T(8,128)(2,1)S(1)} %convolution_convert_fusion.2), channel_id=1, source_target_pairs={{0,4},{4,0},{1,5},{5,1},{2,6},{6,2},{3,7},{7,3},{8,12},{12,8},{9,1... | collective-permute-start | bytes 1572872 | tf_op jit(solution)/shard_map/ppermute | solution.py:355
  226.4 16.3 %collective-permute-start.33 = (bf16[128,512]{1,0:T(8,128)(2,1)S(1)}, bf16[128,512]{1,0:T(8,128)(2,1)S(1)}, u32[]{:S(2)}, u32[]{:S(2)}) collective-permute-start(bf16[128,512]{1,0:T(8,128)(2,1)S(1)} %get-tuple-element.88), channel_id=1, source_target_pairs={{0,24},{8,0},{16,8},{24,16},{1,25},{9,1},{17,9},{25,17},{2,26},{10... | collective-permute-start | bytes 393224 | tf_op jit(solution)/shard_map/ppermute | solution.py:360
  230.2 16.6 %collective-permute-start.45 = (bf16[128,512]{1,0:T(8,128)(2,1)S(1)}, bf16[128,512]{1,0:T(8,128)(2,1)S(1)}, u32[]{:S(2)}, u32[]{:S(2)}) collective-permute-start(bf16[128,512]{1,0:T(8,128)(2,1)S(1)} %add_convert_fusion.1.refs_8_), channel_id=1, source_target_pairs={{0,8},{8,16},{16,24},{24,0},{1,9},{9,17},{17,25},{25,1},{2,10},{10... | collective-permute-start | bytes 393224 | tf_op jit(solution)/shard_map/ppermute | solution.py:360
  (68 other events, 653.3 us)
Sparse Core Ops, SparseCore 0:
  11.5 30.6 all-gather.2
  98.3 34.4 all-gather.4

commit v3 on v2

v3 whole, which is shorter than its diff:
```python
import functools
import math

import jax
import jax.numpy as jnp
from jax import lax
from jax.experimental import pallas as pl
from jax.experimental.pallas import tpu as pltpu
from jax.sharding import PartitionSpec as P

HEAD = 128
epsilon = 1e-05
clip_range = 0.2
masked_score = -1e30
LOG2E = 1.4426950408889634
F32 = jnp.float32
BF16 = jnp.bfloat16
CHUNKS = 2
LIMIT = 40 * 2**20
SMALL = 20 * 2**20
VMEM = pl.BlockSpec(memory_space=pltpu.VMEM)


def dot(a, b):
    return jnp.dot(a, b, preferred_element_type=F32)


def tied(*items):
    return lax.optimization_barrier(items)


def row_factor(source):
    return lax.rsqrt(jnp.mean(source * source, axis=-1, keepdims=True) + epsilon)


def whole(shape):
    return pl.BlockSpec(shape, lambda *_: (0,) * len(shape))


def first_kernel(obs_ref, w_ref, kv_ref, factor_ref):
    rows = obs_ref[...]
    factor = row_factor(rows.astype(F32))
    both = dot(rows, jnp.concatenate([w_ref[0], w_ref[1]], axis=1)) * factor
    width = w_ref.shape[2]
    kv_ref[0] = both[:, :width].astype(BF16)
    kv_ref[1] = both[:, width:].astype(BF16)
    factor_ref[...] = jnp.broadcast_to(factor, factor_ref.shape)


def first_projection(obs, w_keyval):
    rows, depth = obs.shape
    width = w_keyval.shape[2]
    block = rows // 2
    return pl.pallas_call(
        first_kernel,
        grid=(rows // block,),
        in_specs=[pl.BlockSpec((block, depth), lambda i: (i, 0)), whole(w_keyval.shape)],
        out_specs=[
            pl.BlockSpec((2, block, width), lambda i: (0, i, 0)),
            pl.BlockSpec((block, HEAD), lambda i: (i, 0)),
        ],
        out_shape=[
            jax.ShapeDtypeStruct((2, rows, width), BF16),
            jax.ShapeDtypeStruct((rows, HEAD), F32),
        ],
        compiler_params=pltpu.CompilerParams(vmem_limit_bytes=LIMIT),
        cost_estimate=pl.CostEstimate(
            flops=4 * rows * depth * width, bytes_accessed=2 * rows * depth, transcendentals=0
        ),
        name="first_projection",
    )(obs, w_keyval)


def attend_blocks(groups, units, left_ref, q_ref, kv_refs):
    def fetch(head, span):
        kv_head = head // groups
        columns = slice(kv_head * HEAD, (kv_head + 1) * HEAD)
        query = q_ref[span, head * HEAD : (head + 1) * HEAD]
        lane = lax.broadcasted_iota(jnp.int32, query.shape, 1)
        query = jnp.concatenate([query, (lane == 0).astype(BF16)], axis=1)
        scores = []
        for p, ref in enumerate(kv_refs):
            keys = ref[0, :, columns]
            key = lax.broadcasted_iota(jnp.int32, keys.shape, 0)
            lane = lax.broadcasted_iota(jnp.int32, keys.shape, 1)
            dead = (key >= left_ref[p]) & (lane == 0)
            bias = jnp.where(dead, F32(masked_score), F32(0.0)).astype(BF16)
            keys = jnp.concatenate([keys, bias], axis=1)
            scores.append(
                lax.dot_general(
                    query, keys, (((1,), (1,)), ((), ())), preferred_element_type=F32
                )
            )
        return scores

    def values(head, p):
        kv_head = head // groups
        vals = kv_refs[p][1, :, kv_head * HEAD : (kv_head + 1) * HEAD]
        return jnp.concatenate([vals, jnp.ones_like(vals)], axis=1)

    ahead = fetch(*units[0])
    for i, (head, span) in enumerate(units):
        scores = ahead
        if i + 1 < len(units):
            ahead = fetch(*units[i + 1])
        yield head, span, scores, functools.partial(values, head)


def weigh(scores, top, values):
    total = None
    for p, part in enumerate(scores):
        both = dot(jnp.exp2(part - top).astype(BF16), values(p))
        total = both if total is None else total + both
    return total


def highest(scores):
    return functools.reduce(
        jnp.maximum, [jnp.max(part, axis=-1, keepdims=True) for part in scores]
    )


def open_kernel(groups, units, left_ref, q_ref, *refs):
    *kv_refs, wide_ref, top_ref = refs
    for head, span, scores, values in attend_blocks(groups, units, left_ref, q_ref, kv_refs):
        top = highest(scores)
        wide_ref[span, head * 2 * HEAD : (head + 1) * 2 * HEAD] = weigh(scores, top, values)
        top_ref[span, head * HEAD : (head + 1) * HEAD] = jnp.broadcast_to(
            top, (top.shape[0], HEAD)
        )


def close_kernel(groups, units, left_ref, q_ref, wide_ref, top_ref, *refs):
    *kv_refs, o_ref = refs
    for head, span, scores, values in attend_blocks(groups, units, left_ref, q_ref, kv_refs):
        before = top_ref[span, head * HEAD : head * HEAD + 1]
        top = jnp.maximum(before, highest(scores))
        wide = wide_ref[span, head * 2 * HEAD : (head + 1) * 2 * HEAD]
        wide = wide * jnp.exp2(before - top) + weigh(scores, top, values)
        o_ref[span, head * HEAD : (head + 1) * HEAD] = (
            wide[:, :HEAD] / wide[:, HEAD:]
        ).astype(BF16)


def attend_call(queries, pieces, left, state):
    rows, width = queries.shape
    heads = width // HEAD
    groups = heads // (pieces[0].shape[2] // HEAD)
    block = min(rows, 256)
    units = [
        (head, slice(i, i + block)) for head in range(heads) for i in range(0, rows, block)
    ]
    count = len(pieces) * pieces[0].shape[1]
    if state:
        body, name = close_kernel, "attend_close"
        out = jax.ShapeDtypeStruct((rows, width), BF16)
    else:
        body, name = open_kernel, "attend_open"
        out = [
            jax.ShapeDtypeStruct((rows, 2 * width), F32),
            jax.ShapeDtypeStruct((rows, width), F32),
        ]
    return pl.pallas_call(
        functools.partial(body, groups, units),
        in_specs=[pl.BlockSpec(memory_space=pltpu.SMEM)] + [VMEM] * (1 + len(state) + len(pieces)),
        out_specs=VMEM if state else [VMEM] * 2,
        out_shape=out,
        compiler_params=pltpu.CompilerParams(vmem_limit_bytes=LIMIT),
        cost_estimate=pl.CostEstimate(
            flops=24 * rows * count * width,
            bytes_accessed=4 * rows * width,
            transcendentals=rows * count * heads,
        ),
        name=name,
    )(left, queries, *state, *pieces)


def joined(refs, columns=slice(None)):
    return jnp.concatenate([ref[:, columns] for ref in refs], axis=0)


def hidden_kernel(place_ref, obs_ref, t0, t1, t2, t3, w0, w1, w20, w21, w30, w31, o_ref):
    half = w20.shape[1]
    tile = half // 3
    for side, (w2, w3) in enumerate(((w20, w30), (w21, w31))):
        start = (place_ref[0] ^ side) * half
        for i in range(3):
            near = pl.ds(pl.multiple_of(start + i * tile, HEAD), tile)
            far = slice(i * tile, (i + 1) * tile)
            weight = jnp.concatenate([w0[:, near], w1[:, near], w2[:, far], w3[:, far]], axis=0)
            parts = jnp.concatenate([t0[...], t1[...], t2[...], t3[...]], axis=1)
            o_ref[:, near] = (obs_ref[:, near].astype(F32) + dot(parts, weight)).astype(BF16)


def hidden_rows(place, obs, parts, full, halves):
    rows, depth = obs.shape
    inner = halves[0].shape[0]
    return pl.pallas_call(
        hidden_kernel,
        in_specs=[pl.BlockSpec(memory_space=pltpu.SMEM)] + [VMEM] * 11,
        out_specs=VMEM,
        out_shape=jax.ShapeDtypeStruct((rows, depth), BF16),
        compiler_params=pltpu.CompilerParams(vmem_limit_bytes=SMALL),
        cost_estimate=pl.CostEstimate(
            flops=8 * rows * depth * inner, bytes_accessed=8 * depth * inner, transcendentals=0
        ),
        name="hidden_rows",
    )(place, obs, *parts, *full, *halves)


def embed_kernel(place_ref, h_ref, w0, w1, *refs):
    far, (wkv_ref, emb_ref, kv_ref, factor_ref) = refs[:-4], refs[-4:]
    chunks = len(far) // 4
    half = far[0].shape[1]
    rows = h_ref.shape[0]
    for side in range(2):
        start = (place_ref[0] ^ side) * half
        near = pl.ds(pl.multiple_of(start, half), half)
        for code in range(4):
            if code < 2:
                weight = (w0, w1)[code][:, near]
            else:
                first = ((code - 2) * 2 + side) * chunks
                weight = joined(far[first : first + chunks])
            column = (place_ref[1] ^ code) * 2 * half + start
            emb_ref[:, pl.ds(pl.multiple_of(column, half), half)] = dot(
                h_ref[...], weight
            ).astype(BF16)
    width = wkv_ref.shape[2]
    both_w = jnp.concatenate([wkv_ref[0], wkv_ref[1]], axis=1)
    block = rows // 2
    for i in range(2):
        span = slice(i * block, (i + 1) * block)
        emb = emb_ref[span, :]
        factor = row_factor(emb.astype(F32))
        both = dot(emb, both_w) * factor
        kv_ref[0, span, :] = both[:, :width].astype(BF16)
        kv_ref[1, span, :] = both[:, width:].astype(BF16)
        factor_ref[span, :] = jnp.broadcast_to(factor, (block, HEAD))


def embed_rows(place, hidden, full, far, w_keyval):
    rows, depth = hidden.shape
    wide = full[0].shape[1] * 4
    width = w_keyval.shape[2]
    return pl.pallas_call(
        embed_kernel,
        in_specs=[pl.BlockSpec(memory_space=pltpu.SMEM)] + [VMEM] * (4 + len(far)),
        out_specs=[VMEM] * 3,
        out_shape=[
            jax.ShapeDtypeStruct((rows, wide), BF16),
            jax.ShapeDtypeStruct((2, rows, width), BF16),
            jax.ShapeDtypeStruct((rows, HEAD), F32),
        ],
        compiler_params=pltpu.CompilerParams(vmem_limit_bytes=SMALL),
        cost_estimate=pl.CostEstimate(
            flops=2 * rows * depth * wide, bytes_accessed=2 * depth * wide, transcendentals=0
        ),
        name="embed_rows",
    )(place, hidden, *full, *far, w_keyval)


def mixed_kernel(
    place_ref, emb_ref, t0, t1, t2, t3, w0, w1, w2, w3, wv_ref, ret_ref,
    value_ref, other_ref, own_ref, mixed_ref,
):
    rows, wide = mixed_ref.shape
    tile = 256

    @pl.loop(0, wide // tile)
    def _(j):
        columns = pl.ds(pl.multiple_of(j * tile, tile), tile)
        parts = jnp.concatenate([t0[...], t1[...], t2[...], t3[...]], axis=1)
        mixed_ref[:, columns] = emb_ref[:, columns].astype(F32) + dot(
            parts, joined((w0, w1, w2, w3), columns)
        )

    half = wide // 2
    block = rows // 8
    live_total = place_ref[4].astype(F32)

    @pl.loop(0, 8)
    def _(i):
        start = pl.multiple_of(i * block, block)
        span = pl.ds(start, block)
        weight = wv_ref[...].astype(F32)
        mixed = mixed_ref[span, :]
        factor = row_factor(mixed)
        value = factor * jnp.sum(mixed * weight, axis=-1, keepdims=True)
        row = place_ref[2] + start + lax.broadcasted_iota(jnp.int32, (block, 1), 0)
        gap = jnp.where(row < place_ref[3], value - ret_ref[span, :], F32(0.0)) / live_total
        lead = factor * gap
        pull = factor * value / wide
        value_ref[span, :] = jnp.broadcast_to(value, (block, HEAD))
        for out, side in ((own_ref, place_ref[0]), (other_ref, 1 - place_ref[0])):
            columns = pl.ds(pl.multiple_of(side * half, half), half)
            part = mixed_ref[span, columns]
            out[span, :] = (lead * (wv_ref[:, columns].astype(F32) - part * pull)).astype(BF16)


def mixed_rows(place, embedded, parts, weights, w_value, returns):
    rows, wide = embedded.shape
    inner = weights[0].shape[0]
    return pl.pallas_call(
        mixed_kernel,
        in_specs=[pl.BlockSpec(memory_space=pltpu.SMEM)] + [VMEM] * 11,
        out_specs=[VMEM] * 3,
        out_shape=[
            jax.ShapeDtypeStruct((rows, HEAD), F32),
            jax.ShapeDtypeStruct((rows, wide // 2), BF16),
            jax.ShapeDtypeStruct((rows, wide // 2), BF16),
        ],
        scratch_shapes=[pltpu.VMEM((rows, wide), F32)],
        compiler_params=pltpu.CompilerParams(vmem_limit_bytes=SMALL),
        cost_estimate=pl.CostEstimate(
            flops=8 * rows * wide * inner, bytes_accessed=8 * wide * inner, transcendentals=0
        ),
        name="mixed_rows",
    )(place, embedded, *parts, *weights, w_value.reshape(1, wide), returns.reshape(rows, 1))


def gather_codes(size):
    codes, bit = [0], size // 2
    while bit >= 1:
        codes = codes + [code ^ bit for code in codes]
        bit //= 2
    return codes


def split_kernel(codes, index_ref, own_ref, got_ref, keep_ref, send_ref):
    block = own_ref.shape[0] // len(codes)
    side = len(codes) // 2
    for k, code in enumerate(codes):
        span = pl.ds(pl.multiple_of((index_ref[0] ^ code) * block, block), block)
        out = (keep_ref, send_ref)[k // side]
        at = k % side * block
        out[at : at + block, :] = own_ref[span, :] + got_ref[span, :].astype(F32)


def split_sum(index, own, got, count):
    rows, wide = own.shape
    if (rows // count) % 16:
        got = got.astype(F32)
    shape = jax.ShapeDtypeStruct((rows // 2, wide), F32)
    return pl.pallas_call(
        functools.partial(split_kernel, gather_codes(count)),
        in_specs=[pl.BlockSpec(memory_space=pltpu.SMEM), VMEM, VMEM],
        out_specs=[VMEM] * 2,
        out_shape=[shape] * 2,
        compiler_params=pltpu.CompilerParams(vmem_limit_bytes=SMALL),
        cost_estimate=pl.CostEstimate(
            flops=rows * wide, bytes_accessed=8 * rows * wide, transcendentals=0
        ),
        name="split_sum",
    )(index, own, got)


def assemble_kernel(codes, chunks, place_ref, *refs):
    parts = refs[: len(codes) * 2 * chunks]
    out, wide_ref, sems = refs[len(parts) :]
    block, strip = parts[0].shape
    copies = []
    for c in range(chunks):
        for side in range(2):
            for k, code in enumerate(codes):
                at = (c * 2 + side) * len(codes) + k
                row = pl.multiple_of((place_ref[1] ^ code) * block, block)
                column = pl.multiple_of(((place_ref[0] ^ side) * chunks + c) * strip, strip)
                wide_ref[at] = parts[at][...].astype(F32)
                copy = pltpu.make_async_copy(
                    wide_ref.at[at],
                    out.at[pl.ds(row, block), pl.ds(column, strip)],
                    sems.at[at],
                )
                copy.start()
                copies.append(copy)
    for copy in copies:
        copy.wait()


def assemble(place, parts, count, chunks):
    block, strip = parts[0].shape
    rows, wide = block * count, strip * 2 * chunks
    return pl.pallas_call(
        functools.partial(assemble_kernel, gather_codes(count), chunks),
        in_specs=[pl.BlockSpec(memory_space=pltpu.SMEM)] + [VMEM] * len(parts),
        out_specs=pl.BlockSpec(memory_space=pl.ANY),
        out_shape=jax.ShapeDtypeStruct((rows, wide), F32),
        scratch_shapes=[
            pltpu.VMEM((len(parts), block, strip), F32),
            pltpu.SemaphoreType.DMA((len(parts),)),
        ],
        compiler_params=pltpu.CompilerParams(vmem_limit_bytes=SMALL),
        cost_estimate=pl.CostEstimate(
            flops=rows * wide, bytes_accessed=6 * rows * wide, transcendentals=0
        ),
        name="assemble",
    )(place, *parts)


def swap(block, axis, bit):
    size = lax.axis_size(axis)
    return lax.ppermute(block, axis, [(i, i ^ bit) for i in range(size)])


def gather_blocks(block, axis):
    blocks, bit = [block], lax.axis_size(axis) // 2
    while bit >= 1:
        blocks = blocks + [swap(item, axis, bit) for item in blocks]
        bit //= 2
    return blocks


def gather_parts(part):
    far = swap(part, "mdl", 2)
    return [part, swap(part, "mdl", 1), far, swap(far, "mdl", 1)], far


def product(left, right):
    return jnp.einsum("rh,rd->hd", left, right, preferred_element_type=F32)


def halve(keep, got):
    total = keep + got.astype(F32)
    side = total.shape[0] // 2
    return total[:side], total[side:].astype(BF16)


def scatter_rest(keep, got):
    bit = 2
    while bit < lax.axis_size("rep"):
        keep, send = halve(keep, got)
        got = swap(send, "rep", bit)
        bit *= 2
    return (keep + got.astype(F32)).astype(BF16)


def half_of(weight, side):
    half = weight.shape[1] // 2
    return lax.dynamic_slice_in_dim(weight, side * half, half, 1)


def on_device(
    obs,
    a_query,
    a_keyval,
    a_out,
    w_policy,
    c_in,
    c_query,
    c_keyval,
    c_out,
    w_value,
    actions,
    advantages,
    old_logp,
    returns,
    robot_count,
):
    row_count = obs.shape[1]
    batch_index = lax.axis_index("sec")
    rep_index = lax.axis_index("rep")
    rep_count = lax.axis_size("rep")
    robot_total = robot_count[batch_index]
    live_sum = jnp.sum(robot_count)
    live_total = live_sum.astype(F32)
    first_row = rep_index * row_count
    live_mask = first_row + lax.iota(jnp.int32, row_count) < robot_total
    mdl_count = lax.axis_size("mdl")
    assert mdl_count == 4 and lax.axis_size("sec") == 2
    mdl_index = lax.axis_index("mdl")
    part_rows = row_count // mdl_count
    row_start = mdl_index * part_rows
    score_scale = HEAD ** (-0.5) * LOG2E
    rep_place = rep_index.reshape(1).astype(jnp.int32)
    place = jnp.stack([batch_index, mdl_index, first_row, robot_total, live_sum]).astype(jnp.int32)

    codes = gather_codes(rep_count)
    left = jnp.stack(
        [jnp.clip(robot_total - (rep_index ^ code) * row_count, 0, row_count) for code in codes]
    ).astype(jnp.int32)

    obs_in = obs[0]
    keyval, factor_a = first_projection(obs_in, a_keyval)
    pieces_k = gather_blocks(keyval, "rep")

    a_near = swap(a_out, "mdl", 1)
    c_near = swap(c_in, "mdl", 1)
    a_far0 = swap(half_of(a_out, batch_index), "mdl", 2)
    c_half = half_of(c_in, batch_index)
    c_cut = c_half.shape[0] // 2
    c_a0 = swap(c_half[:c_cut], "mdl", 2)
    c_b0 = swap(c_half[c_cut:], "mdl", 2)

    queries = (dot(obs_in, a_query) * (factor_a[:, :1] * score_scale)).astype(BF16)
    queries, a_far0 = tied(queries, a_far0)
    a_far1 = swap(a_far0, "sec", 1)
    state = attend_call(queries, pieces_k[:-1], left[:-1], [])
    *state, c_a0 = tied(*state, c_a0)
    c_a1 = swap(c_a0, "sec", 1)
    attended = attend_call(queries, pieces_k[-1:], left[-1:], state)
    attended_near = swap(attended, "mdl", 1)
    attended_far = swap(attended, "mdl", 2)
    attended_near, c_b0 = tied(attended_near, c_b0)
    c_b1 = swap(c_b0, "sec", 1)
    attended_parts = [attended, attended_near, attended_far, swap(attended_far, "mdl", 1)]
    a_halves = [a_far0, a_far1, swap(a_far0, "mdl", 1), swap(a_far1, "mdl", 1)]
    hidden = hidden_rows(place, obs_in, attended_parts, [a_out, a_near], a_halves)
    hidden, c_b1 = tied(hidden, c_b1)
    c_far = [c_a0, c_b0, c_a1, c_b1]
    c_far = c_far + [swap(item, "mdl", 1) for item in c_far]

    attended_far, c_out_src = tied(attended_far, c_out)
    c_out_far = swap(c_out_src, "mdl", 2)

    embedded, critic_keyval, factor_c = embed_rows(place, hidden, [c_in, c_near], c_far, c_keyval)
    pieces_c = gather_blocks(critic_keyval, "rep")
    critic_queries = (dot(embedded, c_query) * (factor_c[:, :1] * score_scale)).astype(BF16)

    late_hidden, critic_keyval = tied(hidden, critic_keyval)
    source = late_hidden.astype(F32)
    factor_h = row_factor(source)
    logits = dot(late_hidden, w_policy) * factor_h
    log_probs = jax.nn.log_softmax(logits, axis=-1)
    onehot = (
        actions[0][:, None] == lax.broadcasted_iota(jnp.int32, logits.shape, 1)
    ).astype(F32)
    chosen = jnp.sum(onehot * log_probs, axis=-1)
    prob_ratio = jnp.exp(chosen - old_logp[0])
    plain_term = prob_ratio * advantages[0]
    bounded = jnp.clip(prob_ratio, 1.0 - clip_range, 1.0 + clip_range) * advantages[0]
    slope = jnp.where(live_mask & (plain_term <= bounded), -plain_term / live_total, F32(0.0))
    dlogits = slope[:, None] * (onehot - jnp.exp(log_probs))
    along = jnp.sum(dlogits * logits, axis=-1, keepdims=True) / source.shape[1]
    dnormed = dot(dlogits.astype(BF16), w_policy.T)
    dhidden = (factor_h * (dnormed - source * (factor_h * along))).astype(BF16)
    half_a = dhidden.shape[1] // 2
    got_a = swap(
        product(attended, lax.dynamic_slice_in_dim(dhidden, (1 - batch_index) * half_a, half_a, 1))
        .astype(BF16),
        "sec",
        1,
    )
    own_a = product(attended, lax.dynamic_slice_in_dim(dhidden, batch_index * half_a, half_a, 1))

    state_c = attend_call(critic_queries, pieces_c[:-1], left[:-1], [])
    *state_c, got_a = tied(*state_c, got_a)
    keep_a, send_a = split_sum(rep_place, own_a, got_a, rep_count)
    moved_a = swap(send_a.astype(BF16), "rep", 1)
    critic_attended = attend_call(critic_queries, pieces_c[-1:], left[-1:], state_c)
    critic_attended, moved_a, c_out_far = tied(critic_attended, moved_a, c_out_far)
    critic_parts, critic_far = gather_parts(critic_attended)
    mine_a = gather_blocks(scatter_rest(keep_a, moved_a), "rep")
    critic_parts[3], *mine_a = tied(critic_parts[3], *mine_a)
    c_out_all = [c_out, swap(c_out, "mdl", 1), c_out_far, swap(c_out_far, "mdl", 1)]
    pieces_a = mine_a + [swap(block, "sec", 1) for block in mine_a]
    value_wide, d_other, d_own = mixed_rows(
        place, embedded, critic_parts, c_out_all, w_value, returns[0]
    )

    strip = d_own.shape[1] // CHUNKS
    spans = [slice(c * strip, (c + 1) * strip) for c in range(CHUNKS)]
    got = [
        swap(product(critic_attended, d_other[:, span]).astype(BF16), "sec", 1) for span in spans
    ]
    own = [product(critic_attended, d_own[:, span]) for span in spans]
    pieces = []
    for c in range(CHUNKS):
        keep, send = split_sum(rep_place, own[c], got[c], rep_count)
        moved = swap(send.astype(BF16), "rep", 1)
        mine = gather_blocks(scatter_rest(keep, moved), "rep")
        pieces += mine + [swap(block, "sec", 1) for block in mine]
    corner = jnp.stack([batch_index, rep_index]).astype(jnp.int32)
    actor_summed = assemble(corner, pieces_a, rep_count, 1)
    critic_summed = assemble(corner, pieces, rep_count, CHUNKS)

    value_part = lax.dynamic_slice_in_dim(value_wide, row_start, part_rows, 0)[:, 0]
    return (value_part[None, :], actor_summed, critic_summed)


def solution(mesh):
    return jax.shard_map(
        on_device,
        mesh=mesh,
        in_specs=(
            P("sec", "rep", None),
            P(None, "mdl"),
            P(None, None, "mdl"),
            P("mdl", None),
            P(),
            P(None, "mdl"),
            P(None, "mdl"),
            P(None, None, "mdl"),
            P("mdl", None),
            P(),
            P("sec", "rep"),
            P("sec", "rep"),
            P("sec", "rep"),
            P("sec", "rep"),
            P(),
        ),
        out_specs=(P("sec", ("rep", "mdl")), P("mdl", None), P("mdl", None)),
        check_vma=False,
    )
```

time: 282 us -> 272 us (0.965)
  local copies, waits for them, and re-layouts: 24.1 us -> 42.2 us
  Pallas kernels: 57.3 us -> 43.1 us
  waiting for transfers between devices: 113 us -> 124 us
  starting transfers between devices: 56.4 us -> 45.8 us
  between operations: 15.2 us -> 4.67 us
    ppermute x34 -> x59, waiting for transfers between devices: 70 us -> 124 us  [swap(): return lax.ppermute(block, axis, [(i, i ^ bit) for i in range(size)])]
    ppermute x18 -> x0, waiting for transfers between devices: 29.1 us -> none  [shift(): lax.ppermute(block, axis, [(i, (i + step) % size) for i in range(size)])]
    ppermute x18 -> x0, starting transfers between devices: 26.5 us -> none  [shift(): lax.ppermute(block, axis, [(i, (i + step) % size) for i in range(size)])]
    unnamed x76 -> x118, local copies, waits for them, and re-layouts: 17.5 us -> 35.7 us
    ppermute x34 -> x59, starting transfers between devices: 29.8 us -> 45.8 us  [swap(): return lax.ppermute(block, axis, [(i, i ^ bit) for i in range(size)])]
    pallas_call x10 -> x12, Pallas kernels: 55.8 us -> 41.7 us  [the longest x4 12.8 us: attend_call(): pl.pallas_call(functools.partial(body, groups, units), in_specs=[pl.Block...]
    all_gather x2 -> x0, waiting for transfers between devices: 13.9 us -> none  [the longest x1 8.74 us: on_device(): critic_keyval_all = lax.all_gather(critic_keyval, 'rep', axis=1, tiled=True)]
  transfers between devices with their start and end apart: 54 -> 59, of which waited for: 19 -> 26; matrix products, arithmetic and copies ran while one was open for 8% -> 6% of each run, Pallas kernels for 19% -> 10%
where the time goes in v3:
time: 272 us; the launch traced here: 271 us
  waiting for transfers between devices  124 us (46%)
  starting transfers between devices  45.8 us (17%)
  Pallas kernels  43.1 us (16%)
  local copies, waits for them, and re-layouts  42.2 us (16%)
  matrix products  8.29 us (3%)
  between operations  4.67 us (2%)
  other arithmetic  2.78 us (1%)
    ppermute x59, waiting for transfers between devices, swap(): return lax.ppermute(block, axis, [(i, i ^ bit) for i in range(size)])  124 us
    ppermute x59, starting transfers between devices, swap(): return lax.ppermute(block, axis, [(i, i ^ bit) for i in range(size)])  45.8 us
    unnamed x118, local copies, waits for them, and re-layouts  35.7 us
    pallas_call x4, Pallas kernels, attend_call(): pl.pallas_call(functools.partial(body, groups, units), in_specs=[pl.Block...  12.8 us
    pallas_call x1, Pallas kernels, mixed_rows(): pl.pallas_call(mixed_kernel, in_specs=[pl.BlockSpec(memory_space=pltpu.SM...  11.3 us
    pallas_call x1, Pallas kernels, embed_rows(): pl.pallas_call(embed_kernel, in_specs=[pl.BlockSpec(memory_space=pltpu.SM...  7.36 us
    dot_general x4, matrix products, dot(): return jnp.dot(a, b, preferred_element_type=F32)  5.46 us
  transfers between devices with their start and end apart: 59, of which 26 were waited for; matrix products, arithmetic and copies ran while one was open for 6% of the time, Pallas kernels for 10%

profile of v3, /device:TPU:0, one launch (start us, length us, event | category | flops | bytes accessed | tf_op | source)
XLA Modules:
  0.0 271.4 jit_solution(3890336843770956916)
XLA Ops:
  4.8 4.0 %collective-permute-start.1 = (bf16[2,512,128]{2,1,0:T(8,128)(2,1)}, bf16[2,512,128]{2,1,0:T(8,128)(2,1)}, u32[]{:S(2)}, u32[]{:S(2)}) collective-permute-start(bf16[2,512,128]{2,1,0:T(8,128)(2,1)} %get-tuple-element.45.refs_0_), channel_id=1, source_target_pairs={{0,16},{8,24},{16,0},{24,8},{1,17},{9,25},{17,1},{25,9},{2,18},{10... | collective-permute-start | bytes 786440 | tf_op jit(solution)/shard_map/ppermute | solution.py:403
  23.5 4.3 %collective-permute-done.w20 = bf16[384,768]{1,0:T(8,128)(2,1)} collective-permute-done((bf16[384,768]{1,0:T(8,128)(2,1)}, bf16[384,768]{1,0:T(8,128)(2,1)}, u32[]{:S(2)}, u32[]{:S(2)}) %collective-permute-start) | collective-permute-done | bytes 589856 | tf_op jit(solution)/shard_map/ppermute | solution.py:403
  27.8 4.1 %attend_open.2 = (f32[512,768]{1,0:T(8,128)S(1)}, f32[512,384]{1,0:T(8,128)S(1)}) custom-call(s32[3]{0:T(128)S(1)} %pad_add_fusion.left_ref, bf16[512,384]{1,0:T(8,128)(2,1)S(1)} %fusion.4.q_ref, bf16[2,512,128]{2,1,0:T(8,128)(2,1)} %get-tuple-element.45.refs_0_, bf16[2,512,128]{2,1,0:T(8,128)(2,1)} %collective-permute-done.1.refs_1_, ...), custom_call_target="tpu_custom_call" | custom-call | flops 7247757312 | bytes 786432 | tf_op jit(solution)/shard_map/attend_open/pallas_call | solution.py:163
  31.9 4.4 %collective-permute-done.3.refs_0_ = bf16[768,256]{1,0:T(8,128)(2,1)} collective-permute-done((bf16[768,256]{1,0:T(8,128)(2,1)}, bf16[768,256]{1,0:T(8,128)(2,1)}, u32[]{:S(2)}, u32[]{:S(2)}) %collective-permute-start.3) | collective-permute-done | bytes 393248 | tf_op jit(solution)/shard_map/ppermute | solution.py:403
  46.3 5.1 %collective-permute-done.7.t2 = bf16[512,384]{1,0:T(8,128)(2,1)} collective-permute-done((bf16[512,384]{1,0:T(8,128)(2,1)S(1)}, bf16[512,384]{1,0:T(8,128)(2,1)}, u32[]{:S(2)}, u32[]{:S(2)}) %collective-permute-start.7) | collective-permute-done | bytes 393248 | tf_op jit(solution)/shard_map/ppermute | solution.py:403
  51.4 3.9 %collective-permute-done.10.w21 = bf16[384,768]{1,0:T(8,128)(2,1)} collective-permute-done((bf16[384,768]{1,0:T(8,128)(2,1)}, bf16[384,768]{1,0:T(8,128)(2,1)}, u32[]{:S(2)}, u32[]{:S(2)}) %collective-permute-start.10) | collective-permute-done | bytes 589856 | tf_op jit(solution)/shard_map/ppermute | solution.py:403
  55.3 7.4 %collective-permute-done.15.refs_2_ = bf16[768,256]{1,0:T(8,128)(2,1)S(1)} collective-permute-done((bf16[768,256]{1,0:T(8,128)(2,1)}, bf16[768,256]{1,0:T(8,128)(2,1)S(1)}, u32[]{:S(2)}, u32[]{:S(2)}) %collective-permute-start.15) | collective-permute-done | bytes 393248 | tf_op jit(solution)/shard_map/ppermute | solution.py:403
  72.9 4.7 %hidden_rows.1.h_ref = bf16[512,1536]{1,0:T(8,128)(2,1)S(1)} custom-call(s32[5]{0:T(128)S(1)} %stack.39.place_ref, bf16[512,1536]{1,0:T(8,128)(2,1)S(1)} %bitcast.31, bf16[512,384]{1,0:T(8,128)(2,1)S(1)} %copy-done.8, bf16[512,384]{1,0:T(8,128)(2,1)S(1)} %copy-done.14, bf16[512,384]{1,0:T(8,128)(2,1)} %collective-permute-done.7.t2, ...), custom_call_target="tpu_custom_call" | custom-call | flops 2415919104 | bytes 4718592 | tf_op jit(solution)/shard_map/hidden_rows/pallas_call | solution.py:198
  85.2 7.4 %embed_rows.1 = (bf16[512,2048]{1,0:T(8,128)(2,1)S(1)}, bf16[2,512,128]{2,1,0:T(8,128)(2,1)S(1)}, f32[512,128]{1,0:T(8,128)S(1)}) custom-call(s32[5]{0:T(128)S(1)} %stack.39.place_ref, bf16[512,1536]{1,0:T(8,128)(2,1)S(1)} %copy-done.3, bf16[1536,512]{1,0:T(8,128)(2,1)} %w0.4, bf16[1536,512]{1,0:T(8,128)(2,1)} %collective-permute-done.14.w1, ...), custom_call_target="tpu_custom_call" | custom-call | flops 3221225472 | bytes 6291456 | tf_op jit(solution)/shard_map/embed_rows/pallas_call | solution.py:246
  99.5 7.9 %collective-permute-done.20.refs_1_ = bf16[2,512,128]{2,1,0:T(8,128)(2,1)S(1)} collective-permute-done((bf16[2,512,128]{2,1,0:T(8,128)(2,1)S(1)}, bf16[2,512,128]{2,1,0:T(8,128)(2,1)S(1)}, u32[]{:S(2)}, u32[]{:S(2)}) %collective-permute-start.20) | collective-permute-done | bytes 262176 | tf_op jit(solution)/shard_map/ppermute | solution.py:403
  107.4 4.4 %attend_open.3 = (f32[512,1024]{1,0:T(8,128)S(1)}, f32[512,512]{1,0:T(8,128)S(1)}) custom-call(s32[3]{0:T(128)S(1)} %pad_add_fusion.left_ref, bf16[512,512]{1,0:T(8,128)(2,1)S(1)} %fusion.3.q_ref, bf16[2,512,128]{2,1,0:T(8,128)(2,1)S(1)} %get-tuple-element.58.refs_0_, bf16[2,512,128]{2,1,0:T(8,128)(2,1)S(1)} %collective-permute-done.20.refs_1_, ...), custom_call_target="tpu_custom_call" | custom-call | flops 9663676416 | bytes 1048576 | tf_op jit(solution)/shard_map/attend_open/pallas_call | solution.py:163
  119.0 3.0 %collective-permute-done.24 = bf16[192,768]{1,0:T(8,128)(2,1)S(1)} collective-permute-done((bf16[192,768]{1,0:T(8,128)(2,1)S(1)}, bf16[192,768]{1,0:T(8,128)(2,1)S(1)}, u32[]{:S(2)}, u32[]{:S(2)}) %collective-permute-start.24) | collective-permute-done | bytes 294944 | tf_op jit(solution)/shard_map/ppermute | solution.py:403
  122.0 6.3 %collective-permute-done.25.w2 = bf16[512,2048]{1,0:T(8,128)(2,1)} collective-permute-done((bf16[512,2048]{1,0:T(8,128)(2,1)}, bf16[512,2048]{1,0:T(8,128)(2,1)}, u32[]{:S(2)}, u32[]{:S(2)}) %collective-permute-start.25) | collective-permute-done | bytes 2097184 | tf_op jit(solution)/shard_map/ppermute | solution.py:403
  130.3 12.3 %collective-permute-done.27.t2 = bf16[512,512]{1,0:T(8,128)(2,1)S(1)} collective-permute-done((bf16[512,512]{1,0:T(8,128)(2,1)S(1)}, bf16[512,512]{1,0:T(8,128)(2,1)S(1)}, u32[]{:S(2)}, u32[]{:S(2)}) %collective-permute-start.27) | collective-permute-done | bytes 524320 | tf_op jit(solution)/shard_map/ppermute | solution.py:403
  143.1 9.9 %collective-permute-done.30.refs_1_ = bf16[96,768]{1,0:T(8,128)(2,1)S(1)} collective-permute-done((bf16[96,768]{1,0:T(8,128)(2,1)S(1)}, bf16[96,768]{1,0:T(8,128)(2,1)S(1)}, u32[]{:S(2)}, u32[]{:S(2)}) %collective-permute-start.30) | collective-permute-done | bytes 147488 | tf_op jit(solution)/shard_map/ppermute | solution.py:403
  153.0 5.8 %collective-permute-done.31.refs_2_ = bf16[96,768]{1,0:T(8,128)(2,1)S(1)} collective-permute-done((bf16[96,768]{1,0:T(8,128)(2,1)S(1)}, bf16[96,768]{1,0:T(8,128)(2,1)S(1)}, u32[]{:S(2)}, u32[]{:S(2)}) %collective-permute-start.31) | collective-permute-done | bytes 147488 | tf_op jit(solution)/shard_map/ppermute | solution.py:403
  159.2 4.7 %collective-permute-done.32.refs_3_ = bf16[96,768]{1,0:T(8,128)(2,1)S(1)} collective-permute-done((bf16[96,768]{1,0:T(8,128)(2,1)S(1)}, bf16[96,768]{1,0:T(8,128)(2,1)S(1)}, u32[]{:S(2)}, u32[]{:S(2)}) %collective-permute-start.32) | collective-permute-done | bytes 147488 | tf_op jit(solution)/shard_map/ppermute | solution.py:403
  170.0 11.3 %mixed_rows.1 = (f32[512,128]{1,0:T(8,128)S(1)}, bf16[512,1024]{1,0:T(8,128)(2,1)S(1)}, bf16[512,1024]{1,0:T(8,128)(2,1)S(1)}) custom-call(s32[5]{0:T(128)S(1)} %stack.39.place_ref, bf16[512,2048]{1,0:T(8,128)(2,1)S(1)} %copy-done.51, bf16[512,512]{1,0:T(8,128)(2,1)S(1)} %attend_close.3.t0, bf16[512,512]{1,0:T(8,128)(2,1)S(1)} %copy-done.47, ...), custom_call_target="tpu_custom_call" | custom-call | flops 4294967296 | bytes 8388608 | tf_op jit(solution)/shard_map/mixed_rows/pallas_call | solution.py:304
  184.9 11.8 %collective-permute-done.49.got_ref = bf16[512,512]{1,0:T(8,128)(2,1)S(1)} collective-permute-done((bf16[512,512]{1,0:T(8,128)(2,1)S(1)}, bf16[512,512]{1,0:T(8,128)(2,1)S(1)}, u32[]{:S(2)}, u32[]{:S(2)}) %collective-permute-start.49) | collective-permute-done | bytes 524320 | tf_op jit(solution)/shard_map/ppermute | solution.py:403
  197.8 7.1 %collective-permute-done.39.got_ref = bf16[512,512]{1,0:T(8,128)(2,1)S(1)} collective-permute-done((bf16[512,512]{1,0:T(8,128)(2,1)S(1)}, bf16[512,512]{1,0:T(8,128)(2,1)S(1)}, u32[]{:S(2)}, u32[]{:S(2)}) %collective-permute-start.39) | collective-permute-done | bytes 524320 | tf_op jit(solution)/shard_map/ppermute | solution.py:403
  212.7 9.7 %collective-permute-done.51 = bf16[128,512]{1,0:T(8,128)(2,1)S(1)} collective-permute-done((bf16[128,512]{1,0:T(8,128)(2,1)S(1)}, bf16[128,512]{1,0:T(8,128)(2,1)S(1)}, u32[]{:S(2)}, u32[]{:S(2)}) %collective-permute-start.51) | collective-permute-done | bytes 131104 | tf_op jit(solution)/shard_map/ppermute | solution.py:403
  222.4 8.8 %collective-permute-done.41 = bf16[128,512]{1,0:T(8,128)(2,1)S(1)} collective-permute-done((bf16[128,512]{1,0:T(8,128)(2,1)S(1)}, bf16[128,512]{1,0:T(8,128)(2,1)S(1)}, u32[]{:S(2)}, u32[]{:S(2)}) %collective-permute-start.41) | collective-permute-done | bytes 131104 | tf_op jit(solution)/shard_map/ppermute | solution.py:403
  231.3 3.7 %collective-permute-start.53 = (bf16[128,512]{1,0:T(8,128)(2,1)S(1)}, bf16[128,512]{1,0:T(8,128)(2,1)S(1)}, u32[]{:S(2)}, u32[]{:S(2)}) collective-permute-start(bf16[128,512]{1,0:T(8,128)(2,1)S(1)} %fusion.15.refs_8_), channel_id=1, source_target_pairs={{0,8},{8,0},{16,24},{24,16},{1,9},{9,1},{17,25},{25,17},{2,10},{10... | collective-permute-start | bytes 393224 | tf_op jit(solution)/shard_map/ppermute | solution.py:403
  268.0 3.2 %assemble.3 = f32[512,2048]{1,0:T(8,128)} custom-call(s32[2]{0:T(128)S(1)} %pad_add_fusion.1.place_ref, bf16[128,512]{1,0:T(8,128)(2,1)S(1)} %fusion.16.refs_0_, bf16[128,512]{1,0:T(8,128)(2,1)S(1)} %copy-done.22, bf16[128,512]{1,0:T(8,128)(2,1)S(1)} %copy-done.24, bf16[128,512]{1,0:T(8,128)(2,1)S(1)} %copy-done.32, bf16[128,512]{1,0:T(8,128)(2,1)S(1)} %copy-done.26, ...), custom_call_target="tpu_custom_call" | custom-call | flops 1048576 | bytes 6291456 | tf_op jit(solution)/shard_map/assemble/pallas_call | solution.py:384
  (267 shorter events, 111.5 us)
Async XLA Ops:
  4.8 18.2 %collective-permute-start.1 = (bf16[2,512,128]{2,1,0:T(8,128)(2,1)}, bf16[2,512,128]{2,1,0:T(8,128)(2,1)}, u32[]{:S(2)}, u32[]{:S(2)}) collective-permute-start(bf16[2,512,128]{2,1,0:T(8,128)(2,1)} %get-tuple-element.45.refs_0_), channel_id=1, source_target_pairs={{0,16},{8,24},{16,0},{24,8},{1,17},{9,25},{17,1},{25,9},{2,18},{10... | collective-permute-start | bytes 786440 | tf_op jit(solution)/shard_map/ppermute | solution.py:403
  8.8 19.0 %collective-permute-start.2 = (bf16[2,512,128]{2,1,0:T(8,128)(2,1)}, bf16[2,512,128]{2,1,0:T(8,128)(2,1)}, u32[]{:S(2)}, u32[]{:S(2)}) collective-permute-start(bf16[2,512,128]{2,1,0:T(8,128)(2,1)} %get-tuple-element.45.refs_0_), channel_id=1, source_target_pairs={{0,8},{8,0},{16,24},{24,16},{1,9},{9,1},{17,25},{25,17},{2,10},{10... | collective-permute-start | bytes 786440 | tf_op jit(solution)/shard_map/ppermute | solution.py:403
  11.3 16.6 %collective-permute-start = (bf16[384,768]{1,0:T(8,128)(2,1)}, bf16[384,768]{1,0:T(8,128)(2,1)}, u32[]{:S(2)}, u32[]{:S(2)}) collective-permute-start(bf16[384,768]{1,0:T(8,128)(2,1)} %constant_dynamic-slice_fusion.1), channel_id=1, source_target_pairs={{0,2},{1,3},{2,0},{3,1},{4,6},{5,7},{6,4},{7,5},{8,10},{9,11},{10,... | collective-permute-start | bytes 1769480 | tf_op jit(solution)/shard_map/ppermute | solution.py:403
  14.8 21.4 %collective-permute-start.3 = (bf16[768,256]{1,0:T(8,128)(2,1)}, bf16[768,256]{1,0:T(8,128)(2,1)}, u32[]{:S(2)}, u32[]{:S(2)}) collective-permute-start(bf16[768,256]{1,0:T(8,128)(2,1)} %get-tuple-element.84), channel_id=1, source_target_pairs={{0,2},{1,3},{2,0},{3,1},{4,6},{5,7},{6,4},{7,5},{8,10},{9,11},{10,... | collective-permute-start | bytes 1179656 | tf_op jit(solution)/shard_map/ppermute | solution.py:403
  15.3 27.7 %collective-permute-start.6 = (bf16[768,256]{1,0:T(8,128)(2,1)}, bf16[768,256]{1,0:T(8,128)(2,1)}, u32[]{:S(2)}, u32[]{:S(2)}) collective-permute-start(bf16[768,256]{1,0:T(8,128)(2,1)} %get-tuple-element.83), channel_id=1, source_target_pairs={{0,2},{1,3},{2,0},{3,1},{4,6},{5,7},{6,4},{7,5},{8,10},{9,11},{10,... | collective-permute-start | bytes 1179656 | tf_op jit(solution)/shard_map/ppermute | solution.py:403
  38.3 29.5 %collective-permute-start.9 = (bf16[384,1536]{1,0:T(8,128)(2,1)S(1)}, bf16[384,1536]{1,0:T(8,128)(2,1)}, u32[]{:S(2)}, u32[]{:S(2)}) collective-permute-start(bf16[384,1536]{1,0:T(8,128)(2,1)S(1)} %copy-done.6), channel_id=1, source_target_pairs={{0,1},{1,0},{2,3},{3,2},{4,5},{5,4},{6,7},{7,6},{8,9},{9,8},{10,11... | collective-permute-start | bytes 3538952 | tf_op jit(solution)/shard_map/ppermute | solution.py:403
  38.8 16.5 %collective-permute-start.10 = (bf16[384,768]{1,0:T(8,128)(2,1)}, bf16[384,768]{1,0:T(8,128)(2,1)}, u32[]{:S(2)}, u32[]{:S(2)}) collective-permute-start(bf16[384,768]{1,0:T(8,128)(2,1)} %collective-permute-done.w20), channel_id=1, source_target_pairs={{0,4},{4,0},{1,5},{5,1},{2,6},{6,2},{3,7},{7,3},{8,12},{12,8},{9,1... | collective-permute-start | bytes 1769480 | tf_op jit(solution)/shard_map/ppermute | solution.py:403
  43.0 38.5 %collective-permute-start.14 = (bf16[1536,512]{1,0:T(8,128)(2,1)}, bf16[1536,512]{1,0:T(8,128)(2,1)}, u32[]{:S(2)}, u32[]{:S(2)}) collective-permute-start(bf16[1536,512]{1,0:T(8,128)(2,1)} %w0.4), channel_id=1, source_target_pairs={{0,1},{1,0},{2,3},{3,2},{4,5},{5,4},{6,7},{7,6},{8,9},{9,8},{10,11... | collective-permute-start | bytes 4718600 | tf_op jit(solution)/shard_map/ppermute | solution.py:403
  43.8 18.9 %collective-permute-start.15 = (bf16[768,256]{1,0:T(8,128)(2,1)}, bf16[768,256]{1,0:T(8,128)(2,1)S(1)}, u32[]{:S(2)}, u32[]{:S(2)}) collective-permute-start(bf16[768,256]{1,0:T(8,128)(2,1)} %collective-permute-done.3.refs_0_), channel_id=1, source_target_pairs={{0,4},{4,0},{1,5},{5,1},{2,6},{6,2},{3,7},{7,3},{8,12},{12,8},{9,1... | collective-permute-start | bytes 1179656 | tf_op jit(solution)/shard_map/ppermute | solution.py:403
  64.3 14.5 %collective-permute-start.13 = (bf16[768,256]{1,0:T(8,128)(2,1)}, bf16[768,256]{1,0:T(8,128)(2,1)}, u32[]{:S(2)}, u32[]{:S(2)}) collective-permute-start(bf16[768,256]{1,0:T(8,128)(2,1)} %collective-permute-done.6.refs_1_), channel_id=1, source_target_pairs={{0,4},{4,0},{1,5},{5,1},{2,6},{6,2},{3,7},{7,3},{8,12},{12,8},{9,1... | collective-permute-start | bytes 1179656 | tf_op jit(solution)/shard_map/ppermute | solution.py:403
  79.9 84.1 %collective-permute-start.33 = (bf16[512,2048]{1,0:T(8,128)(2,1)}, bf16[512,2048]{1,0:T(8,128)(2,1)}, u32[]{:S(2)}, u32[]{:S(2)}) collective-permute-start(bf16[512,2048]{1,0:T(8,128)(2,1)} %w0.5), channel_id=1, source_target_pairs={{0,1},{1,0},{2,3},{3,2},{4,5},{5,4},{6,7},{7,6},{8,9},{9,8},{10,11... | collective-permute-start | bytes 6291464 | tf_op jit(solution)/shard_map/ppermute | solution.py:403
  80.0 48.3 %collective-permute-start.25 = (bf16[512,2048]{1,0:T(8,128)(2,1)}, bf16[512,2048]{1,0:T(8,128)(2,1)}, u32[]{:S(2)}, u32[]{:S(2)}) collective-permute-start(bf16[512,2048]{1,0:T(8,128)(2,1)} %w0.5), channel_id=1, source_target_pairs={{0,2},{1,3},{2,0},{3,1},{4,6},{5,7},{6,4},{7,5},{8,10},{9,11},{10,... | collective-permute-start | bytes 6291464 | tf_op jit(solution)/shard_map/ppermute | solution.py:403
  92.6 14.8 %collective-permute-start.20 = (bf16[2,512,128]{2,1,0:T(8,128)(2,1)S(1)}, bf16[2,512,128]{2,1,0:T(8,128)(2,1)S(1)}, u32[]{:S(2)}, u32[]{:S(2)}) collective-permute-start(bf16[2,512,128]{2,1,0:T(8,128)(2,1)S(1)} %get-tuple-element.58.refs_0_), channel_id=1, source_target_pairs={{0,16},{8,24},{16,0},{24,8},{1,17},{9,25},{17,1},{25,9},{2,18},{10... | collective-permute-start | bytes 786440 | tf_op jit(solution)/shard_map/ppermute | solution.py:403
  93.0 14.4 %collective-permute-start.21 = (bf16[2,512,128]{2,1,0:T(8,128)(2,1)S(1)}, bf16[2,512,128]{2,1,0:T(8,128)(2,1)S(1)}, u32[]{:S(2)}, u32[]{:S(2)}) collective-permute-start(bf16[2,512,128]{2,1,0:T(8,128)(2,1)S(1)} %get-tuple-element.58.refs_0_), channel_id=1, source_target_pairs={{0,8},{8,0},{16,24},{24,16},{1,9},{9,1},{17,25},{25,17},{2,10},{10... | collective-permute-start | bytes 786440 | tf_op jit(solution)/shard_map/ppermute | solution.py:403
  97.0 15.4 %collective-permute-start.22 = (bf16[384,768]{1,0:T(8,128)(2,1)S(1)}, bf16[384,768]{1,0:T(8,128)(2,1)S(1)}, u32[]{:S(2)}, u32[]{:S(2)}) collective-permute-start(bf16[384,768]{1,0:T(8,128)(2,1)S(1)} %convolution_convert_fusion), channel_id=1, source_target_pairs={{0,4},{4,0},{1,5},{5,1},{2,6},{6,2},{3,7},{7,3},{8,12},{12,8},{9,1... | collective-permute-start | bytes 1769480 | tf_op jit(solution)/shard_map/ppermute | solution.py:403
  128.3 36.4 %collective-permute-start.34 = (bf16[512,2048]{1,0:T(8,128)(2,1)}, bf16[512,2048]{1,0:T(8,128)(2,1)}, u32[]{:S(2)}, u32[]{:S(2)}) collective-permute-start(bf16[512,2048]{1,0:T(8,128)(2,1)} %collective-permute-done.25.w2), channel_id=1, source_target_pairs={{0,1},{1,0},{2,3},{3,2},{4,5},{5,4},{6,7},{7,6},{8,9},{9,8},{10,11... | collective-permute-start | bytes 6291464 | tf_op jit(solution)/shard_map/ppermute | solution.py:403
  130.3 33.6 %collective-permute-start.26 = (bf16[512,512]{1,0:T(8,128)(2,1)S(1)}, bf16[512,512]{1,0:T(8,128)(2,1)S(1)}, u32[]{:S(2)}, u32[]{:S(2)}) collective-permute-start(bf16[512,512]{1,0:T(8,128)(2,1)S(1)} %attend_close.3.t0), channel_id=1, source_target_pairs={{0,1},{1,0},{2,3},{3,2},{4,5},{5,4},{6,7},{7,6},{8,9},{9,8},{10,11... | collective-permute-start | bytes 1572872 | tf_op jit(solution)/shard_map/ppermute | solution.py:403
  142.6 21.3 %collective-permute-start.28 = (bf16[512,512]{1,0:T(8,128)(2,1)S(1)}, bf16[512,512]{1,0:T(8,128)(2,1)}, u32[]{:S(2)}, u32[]{:S(2)}) collective-permute-start(bf16[512,512]{1,0:T(8,128)(2,1)S(1)} %collective-permute-done.27.t2), channel_id=1, source_target_pairs={{0,1},{1,0},{2,3},{3,2},{4,5},{5,4},{6,7},{7,6},{8,9},{9,8},{10,11... | collective-permute-start | bytes 1572872 | tf_op jit(solution)/shard_map/ppermute | solution.py:403
  181.8 14.9 %collective-permute-start.49 = (bf16[512,512]{1,0:T(8,128)(2,1)S(1)}, bf16[512,512]{1,0:T(8,128)(2,1)S(1)}, u32[]{:S(2)}, u32[]{:S(2)}) collective-permute-start(bf16[512,512]{1,0:T(8,128)(2,1)S(1)} %convolution_convert_fusion.1), channel_id=1, source_target_pairs={{0,4},{4,0},{1,5},{5,1},{2,6},{6,2},{3,7},{7,3},{8,12},{12,8},{9,1... | collective-permute-start | bytes 1572872 | tf_op jit(solution)/shard_map/ppermute | solution.py:403
  182.8 22.1 %collective-permute-start.39 = (bf16[512,512]{1,0:T(8,128)(2,1)S(1)}, bf16[512,512]{1,0:T(8,128)(2,1)S(1)}, u32[]{:S(2)}, u32[]{:S(2)}) collective-permute-start(bf16[512,512]{1,0:T(8,128)(2,1)S(1)} %convolution_convert_fusion.2), channel_id=1, source_target_pairs={{0,4},{4,0},{1,5},{5,1},{2,6},{6,2},{3,7},{7,3},{8,12},{12,8},{9,1... | collective-permute-start | bytes 1572872 | tf_op jit(solution)/shard_map/ppermute | solution.py:403
  206.1 25.2 %collective-permute-start.35 = (bf16[96,768]{1,0:T(8,128)(2,1)S(1)}, bf16[96,768]{1,0:T(8,128)(2,1)S(1)}, u32[]{:S(2)}, u32[]{:S(2)}) collective-permute-start(bf16[96,768]{1,0:T(8,128)(2,1)S(1)} %fusion.14.refs_0_), channel_id=1, source_target_pairs={{0,4},{4,0},{1,5},{5,1},{2,6},{6,2},{3,7},{7,3},{8,12},{12,8},{9,1... | collective-permute-start | bytes 442376 | tf_op jit(solution)/shard_map/ppermute | solution.py:403
  206.7 28.3 %collective-permute-start.36 = (bf16[96,768]{1,0:T(8,128)(2,1)S(1)}, bf16[96,768]{1,0:T(8,128)(2,1)S(1)}, u32[]{:S(2)}, u32[]{:S(2)}) collective-permute-start(bf16[96,768]{1,0:T(8,128)(2,1)S(1)} %collective-permute-done.30.refs_1_), channel_id=1, source_target_pairs={{0,4},{4,0},{1,5},{5,1},{2,6},{6,2},{3,7},{7,3},{8,12},{12,8},{9,1... | collective-permute-start | bytes 442376 | tf_op jit(solution)/shard_map/ppermute | solution.py:403
  208.2 27.4 %collective-permute-start.37 = (bf16[96,768]{1,0:T(8,128)(2,1)S(1)}, bf16[96,768]{1,0:T(8,128)(2,1)S(1)}, u32[]{:S(2)}, u32[]{:S(2)}) collective-permute-start(bf16[96,768]{1,0:T(8,128)(2,1)S(1)} %collective-permute-done.31.refs_2_), channel_id=1, source_target_pairs={{0,4},{4,0},{1,5},{5,1},{2,6},{6,2},{3,7},{7,3},{8,12},{12,8},{9,1... | collective-permute-start | bytes 442376 | tf_op jit(solution)/shard_map/ppermute | solution.py:403
  208.7 26.9 %collective-permute-start.38 = (bf16[96,768]{1,0:T(8,128)(2,1)S(1)}, bf16[96,768]{1,0:T(8,128)(2,1)S(1)}, u32[]{:S(2)}, u32[]{:S(2)}) collective-permute-start(bf16[96,768]{1,0:T(8,128)(2,1)S(1)} %collective-permute-done.32.refs_3_), channel_id=1, source_target_pairs={{0,4},{4,0},{1,5},{5,1},{2,6},{6,2},{3,7},{7,3},{8,12},{12,8},{9,1... | collective-permute-start | bytes 442376 | tf_op jit(solution)/shard_map/ppermute | solution.py:403
  (94 other events, 653.6 us)

commit v4 on v3

v4 whole, which is shorter than its diff:
```python
import functools
import math

import jax
import jax.numpy as jnp
from jax import lax
from jax.experimental import pallas as pl
from jax.experimental.pallas import tpu as pltpu
from jax.sharding import PartitionSpec as P

HEAD = 128
epsilon = 1e-05
clip_range = 0.2
masked_score = -1e30
LOG2E = 1.4426950408889634
F32 = jnp.float32
BF16 = jnp.bfloat16
CHUNKS = 2
TABLE = 6
LIMIT = 40 * 2**20
VMEM = pl.BlockSpec(memory_space=pltpu.VMEM)
SMEM = pl.BlockSpec(memory_space=pltpu.SMEM)
HBM = pl.BlockSpec(memory_space=pltpu.HBM)


def dot(a, b):
    return jnp.dot(a, b, preferred_element_type=F32)


def tied(*items):
    return lax.optimization_barrier(items)


def row_factor(source):
    return lax.rsqrt(jnp.mean(source * source, axis=-1, keepdims=True) + epsilon)


def start_copies(pairs, sems):
    copies = [
        pltpu.make_async_copy(source, target, sems.at[i])
        for i, (source, target) in enumerate(pairs)
    ]
    for copy in copies:
        copy.start()
    return copies


def first_kernel(obs_hbm, w_hbm, kv_ref, factor_ref, obs_ref, w_ref, sems):
    rows, depth = obs_ref.shape
    width = w_hbm.shape[2]
    block = rows // 2
    spans = [slice(i * block, (i + 1) * block) for i in range(2)]
    copies = start_copies(
        [(w_hbm.at[c], w_ref.at[:, c * width : (c + 1) * width]) for c in range(2)]
        + [(obs_hbm.at[span], obs_ref.at[span]) for span in spans],
        sems,
    )
    for i, span in enumerate(spans):
        copies[2 + i].wait()
        part = obs_ref[span, :]
        factor = row_factor(part.astype(F32))
        if i == 0:
            copies[0].wait()
            copies[1].wait()
        both = dot(part, w_ref[...]) * factor
        kv_ref[0, span, :] = both[:, :width].astype(BF16)
        kv_ref[1, span, :] = both[:, width:].astype(BF16)
        factor_ref[span, :] = jnp.broadcast_to(factor, (block, HEAD))


def first_projection(obs, w_keyval):
    rows, depth = obs.shape
    width = w_keyval.shape[2]
    return pl.pallas_call(
        first_kernel,
        in_specs=[HBM] * 2,
        out_specs=[VMEM] * 2,
        out_shape=[
            jax.ShapeDtypeStruct((2, rows, width), BF16),
            jax.ShapeDtypeStruct((rows, HEAD), F32),
        ],
        scratch_shapes=[
            pltpu.VMEM((rows, depth), BF16),
            pltpu.VMEM((depth, 2 * width), BF16),
            pltpu.SemaphoreType.DMA((4,)),
        ],
        compiler_params=pltpu.CompilerParams(vmem_limit_bytes=LIMIT),
        cost_estimate=pl.CostEstimate(
            flops=4 * rows * depth * width, bytes_accessed=2 * rows * depth, transcendentals=0
        ),
        name="first_projection",
    )(obs, w_keyval)


def attend_blocks(groups, units, first, left_ref, q_ref, kv_refs):
    def fetch(head, span):
        kv_head = head // groups
        columns = slice(kv_head * HEAD, (kv_head + 1) * HEAD)
        query = q_ref[span, head * HEAD : (head + 1) * HEAD]
        lane = lax.broadcasted_iota(jnp.int32, query.shape, 1)
        query = jnp.concatenate([query, (lane == 0).astype(BF16)], axis=1)
        scores = []
        for p, ref in enumerate(kv_refs):
            keys = ref[0, :, columns]
            key = lax.broadcasted_iota(jnp.int32, keys.shape, 0)
            lane = lax.broadcasted_iota(jnp.int32, keys.shape, 1)
            dead = (key >= left_ref[first + p]) & (lane == 0)
            bias = jnp.where(dead, F32(masked_score), F32(0.0)).astype(BF16)
            keys = jnp.concatenate([keys, bias], axis=1)
            scores.append(
                lax.dot_general(
                    query, keys, (((1,), (1,)), ((), ())), preferred_element_type=F32
                )
            )
        return scores

    def values(head, p):
        kv_head = head // groups
        vals = kv_refs[p][1, :, kv_head * HEAD : (kv_head + 1) * HEAD]
        return jnp.concatenate([vals, jnp.ones_like(vals)], axis=1)

    ahead = fetch(*units[0])
    for i, (head, span) in enumerate(units):
        scores = ahead
        if i + 1 < len(units):
            ahead = fetch(*units[i + 1])
        yield head, span, scores, functools.partial(values, head)


def weigh(scores, top, values):
    total = None
    for p, part in enumerate(scores):
        both = dot(jnp.exp2(part - top).astype(BF16), values(p))
        total = both if total is None else total + both
    return total


def highest(scores):
    return functools.reduce(
        jnp.maximum, [jnp.max(part, axis=-1, keepdims=True) for part in scores]
    )


def open_kernel(groups, units, first, left_ref, q_ref, *refs):
    *kv_refs, wide_ref, top_ref = refs
    for head, span, scores, values in attend_blocks(
        groups, units, first, left_ref, q_ref, kv_refs
    ):
        top = highest(scores)
        wide_ref[span, head * 2 * HEAD : (head + 1) * 2 * HEAD] = weigh(scores, top, values)
        top_ref[span, head * HEAD : (head + 1) * HEAD] = jnp.broadcast_to(
            top, (top.shape[0], HEAD)
        )


def close_kernel(groups, units, first, left_ref, q_ref, wide_ref, top_ref, *refs):
    *kv_refs, o_ref = refs
    for head, span, scores, values in attend_blocks(
        groups, units, first, left_ref, q_ref, kv_refs
    ):
        before = top_ref[span, head * HEAD : head * HEAD + 1]
        top = jnp.maximum(before, highest(scores))
        wide = wide_ref[span, head * 2 * HEAD : (head + 1) * 2 * HEAD]
        wide = wide * jnp.exp2(before - top) + weigh(scores, top, values)
        o_ref[span, head * HEAD : (head + 1) * HEAD] = (
            wide[:, :HEAD] / wide[:, HEAD:]
        ).astype(BF16)


def attend_call(queries, pieces, first, place, state):
    rows, width = queries.shape
    heads = width // HEAD
    groups = heads // (pieces[0].shape[2] // HEAD)
    block = min(rows, 256)
    units = [
        (head, slice(i, i + block)) for head in range(heads) for i in range(0, rows, block)
    ]
    count = len(pieces) * pieces[0].shape[1]
    weight = 1 if state else 24
    if state:
        body, name = close_kernel, "attend_close"
        out = jax.ShapeDtypeStruct((rows, width), BF16)
    else:
        body, name = open_kernel, "attend_open"
        out = [
            jax.ShapeDtypeStruct((rows, 2 * width), F32),
            jax.ShapeDtypeStruct((rows, width), F32),
        ]
    return pl.pallas_call(
        functools.partial(body, groups, units, TABLE + first),
        in_specs=[SMEM] + [VMEM] * (1 + len(state) + len(pieces)),
        out_specs=VMEM if state else [VMEM] * 2,
        out_shape=out,
        compiler_params=pltpu.CompilerParams(vmem_limit_bytes=LIMIT),
        cost_estimate=pl.CostEstimate(
            flops=weight * rows * count * width,
            bytes_accessed=4 * rows * width,
            transcendentals=rows * count,
        ),
        name=name,
    )(place, queries, *state, *pieces)


def hidden_kernel(
    place_ref, obs_hbm, t0, t1, t2, t3, w0, w1, w20, w21, w30, w31, o_ref, obs_ref, w_ref, sems
):
    inner, half = w20.shape
    starts = [pl.multiple_of((place_ref[0] ^ side) * half, HEAD) for side in range(2)]
    pairs = []
    for side, (w2, w3) in enumerate(((w20, w30), (w21, w31))):
        columns = pl.ds(starts[side], half)
        for k, source in enumerate((w0.at[:, columns], w1.at[:, columns], w2, w3)):
            pairs.append((source, w_ref.at[side, k * inner : (k + 1) * inner]))
        pairs.append((obs_hbm.at[:, columns], obs_ref.at[side]))
    copies = start_copies(pairs, sems)
    tile = half // 3
    for side in range(2):
        for copy in copies[side * 5 : (side + 1) * 5]:
            copy.wait()
        for i in range(3):
            strip = slice(i * tile, (i + 1) * tile)
            parts = jnp.concatenate([t0[...], t1[...], t2[...], t3[...]], axis=1)
            total = obs_ref[side, :, strip].astype(F32) + dot(parts, w_ref[side, :, strip])
            column = pl.multiple_of(starts[side] + i * tile, HEAD)
            o_ref[:, pl.ds(column, tile)] = total.astype(BF16)


def hidden_rows(place, obs, parts, full, halves):
    rows, depth = obs.shape
    inner, half = halves[0].shape
    return pl.pallas_call(
        hidden_kernel,
        in_specs=[SMEM, HBM] + [VMEM] * 4 + [HBM] * 6,
        out_specs=VMEM,
        out_shape=jax.ShapeDtypeStruct((rows, depth), BF16),
        scratch_shapes=[
            pltpu.VMEM((2, rows, half), BF16),
            pltpu.VMEM((2, 4 * inner, half), BF16),
            pltpu.SemaphoreType.DMA((10,)),
        ],
        compiler_params=pltpu.CompilerParams(vmem_limit_bytes=LIMIT),
        cost_estimate=pl.CostEstimate(
            flops=8 * rows * depth * inner, bytes_accessed=8 * depth * inner, transcendentals=0
        ),
        name="hidden_rows",
    )(place, obs, *parts, *full, *halves)


def embed_kernel(place_ref, h_ref, w0, w1, *refs):
    far, (wkv_hbm, emb_ref, kv_ref, factor_ref, w_ref, wkv_ref, sems) = refs[:-7], refs[-7:]
    chunks = len(far) // 4
    cut, half = far[0].shape
    rows = h_ref.shape[0]
    width = wkv_hbm.shape[2]
    starts = [pl.multiple_of((place_ref[0] ^ side) * half, half) for side in range(2)]
    pairs, tiles = [], []
    for code in range(4):
        for side in range(2):
            before = len(pairs)
            target = w_ref.at[code * 2 + side]
            if code < 2:
                pairs.append(((w0, w1)[code].at[:, pl.ds(starts[side], half)], target))
            else:
                for c in range(chunks):
                    source = far[((code - 2) * 2 + side) * chunks + c]
                    pairs.append((source, target.at[c * cut : (c + 1) * cut]))
            tiles.append((code, side, before, len(pairs)))
    pairs += [(wkv_hbm.at[c], wkv_ref.at[:, c * width : (c + 1) * width]) for c in range(2)]
    copies = start_copies(pairs, sems)
    for code, side, first, last in tiles:
        for copy in copies[first:last]:
            copy.wait()
        column = (place_ref[1] ^ code) * 2 * half + starts[side]
        emb_ref[:, pl.ds(pl.multiple_of(column, half), half)] = dot(
            h_ref[...], w_ref[code * 2 + side]
        ).astype(BF16)
    for copy in copies[-2:]:
        copy.wait()
    block = rows // 2
    for i in range(2):
        span = slice(i * block, (i + 1) * block)
        emb = emb_ref[span, :]
        factor = row_factor(emb.astype(F32))
        both = dot(emb, wkv_ref[...]) * factor
        kv_ref[0, span, :] = both[:, :width].astype(BF16)
        kv_ref[1, span, :] = both[:, width:].astype(BF16)
        factor_ref[span, :] = jnp.broadcast_to(factor, (block, HEAD))


def embed_rows(place, hidden, full, far, w_keyval):
    rows, depth = hidden.shape
    half = far[0].shape[1]
    wide = half * 8
    width = w_keyval.shape[2]
    return pl.pallas_call(
        embed_kernel,
        in_specs=[SMEM, VMEM] + [HBM] * (3 + len(far)),
        out_specs=[VMEM] * 3,
        out_shape=[
            jax.ShapeDtypeStruct((rows, wide), BF16),
            jax.ShapeDtypeStruct((2, rows, width), BF16),
            jax.ShapeDtypeStruct((rows, HEAD), F32),
        ],
        scratch_shapes=[
            pltpu.VMEM((8, depth, half), BF16),
            pltpu.VMEM((wide, 2 * width), BF16),
            pltpu.SemaphoreType.DMA((6 + len(far),)),
        ],
        compiler_params=pltpu.CompilerParams(vmem_limit_bytes=LIMIT),
        cost_estimate=pl.CostEstimate(
            flops=2 * rows * depth * wide, bytes_accessed=2 * depth * wide, transcendentals=0
        ),
        name="embed_rows",
    )(place, hidden, *full, *far, w_keyval)


def mixed_kernel(place_ref, emb_ref, t0, t1, t2, t3, wv_ref, ret_ref, *refs):
    weights, (value_ref, other_ref, own_ref, mixed_ref, w_ref, sems) = refs[:-6], refs[-6:]
    rows, wide = mixed_ref.shape
    strips, _, strip = w_ref.shape
    copies = []
    for j in range(strips):
        columns = slice(j * strip, (j + 1) * strip)
        pairs = []
        for i, weight in enumerate(weights):
            height = weight.shape[0]
            if i < 2:
                top = i * height
            else:
                code, side, cut = 2 + (i - 2) // 4, (i - 2) // 2 % 2, (i - 2) % 2
                top = (code * 2 + (place_ref[0] ^ side)) * 2 * height + cut * height
                top = pl.multiple_of(top, height)
            pairs.append((weight.at[:, columns], w_ref.at[j, pl.ds(top, height)]))
        copies.append(start_copies(pairs, sems.at[j]))
    for j in range(strips):
        for copy in copies[j]:
            copy.wait()
        columns = slice(j * strip, (j + 1) * strip)
        parts = jnp.concatenate([t0[...], t1[...], t2[...], t3[...]], axis=1)
        mixed_ref[:, columns] = emb_ref[:, columns].astype(F32) + dot(parts, w_ref[j])

    half = wide // 2
    block = 32
    live_total = place_ref[4].astype(F32)

    @pl.loop(0, rows // block)
    def _(i):
        start = pl.multiple_of(i * block, block)
        span = pl.ds(start, block)
        mixed = mixed_ref[span, :]
        factor = row_factor(mixed)
        value = factor * jnp.sum(mixed * wv_ref[...].astype(F32), axis=-1, keepdims=True)
        row = place_ref[2] + start + lax.broadcasted_iota(jnp.int32, (block, 1), 0)
        gap = jnp.where(row < place_ref[3], value - ret_ref[span, :], F32(0.0)) / live_total
        lead = factor * gap
        pull = lead * factor * value / wide
        value_ref[span, :] = jnp.broadcast_to(value, (block, HEAD))
        for out, side in ((own_ref, place_ref[0]), (other_ref, 1 - place_ref[0])):
            columns = pl.ds(pl.multiple_of(side * half, half), half)
            part = mixed_ref[span, columns]
            out[span, :] = (lead * wv_ref[:, columns].astype(F32) - part * pull).astype(BF16)


def mixed_rows(place, embedded, parts, weights, w_value, returns):
    rows, wide = embedded.shape
    depth = sum(weight.shape[0] for weight in weights)
    return pl.pallas_call(
        mixed_kernel,
        in_specs=[SMEM] + [VMEM] * 7 + [HBM] * len(weights),
        out_specs=[VMEM] * 3,
        out_shape=[
            jax.ShapeDtypeStruct((rows, HEAD), F32),
            jax.ShapeDtypeStruct((rows, wide // 2), BF16),
            jax.ShapeDtypeStruct((rows, wide // 2), BF16),
        ],
        scratch_shapes=[
            pltpu.VMEM((rows, wide), F32),
            pltpu.VMEM((8, depth, wide // 8), BF16),
            pltpu.SemaphoreType.DMA((8, len(weights))),
        ],
        compiler_params=pltpu.CompilerParams(vmem_limit_bytes=LIMIT),
        cost_estimate=pl.CostEstimate(
            flops=2 * rows * wide * depth, bytes_accessed=2 * wide * depth, transcendentals=0
        ),
        name="mixed_rows",
    )(
        place, embedded, *parts, w_value.reshape(1, wide), returns.reshape(rows, 1), *weights
    )


def gather_codes(size):
    codes, bit = [0], size // 2
    while bit >= 1:
        codes = codes + [code ^ bit for code in codes]
        bit //= 2
    return codes


def split_kernel(codes, index_ref, own_ref, got_ref, keep_ref, send_ref):
    block = own_ref.shape[0] // len(codes)
    side = len(codes) // 2
    for k, code in enumerate(codes):
        span = pl.ds(pl.multiple_of((index_ref[0] ^ code) * block, block), block)
        out = (keep_ref, send_ref)[k // side]
        at = k % side * block
        total = own_ref[span, :] + got_ref[span, :].astype(F32)
        out[at : at + block, :] = total.astype(out.dtype)


def split_sum(index, own, got, count):
    rows, wide = own.shape
    if (rows // count) % 16:
        got = got.astype(F32)
    return pl.pallas_call(
        functools.partial(split_kernel, gather_codes(count)),
        in_specs=[SMEM, VMEM, VMEM],
        out_specs=[VMEM] * 2,
        out_shape=[
            jax.ShapeDtypeStruct((rows // 2, wide), F32),
            jax.ShapeDtypeStruct((rows // 2, wide), got.dtype),
        ],
        compiler_params=pltpu.CompilerParams(vmem_limit_bytes=LIMIT),
        cost_estimate=pl.CostEstimate(
            flops=rows * wide, bytes_accessed=8 * rows * wide, transcendentals=0
        ),
        name="split_sum",
    )(index, own, got)


def assemble_kernel(codes, chunks, place_ref, *refs):
    parts = refs[: len(codes) * 2 * chunks]
    out, got_ref, wide_ref, got_sems, sems = refs[len(parts) :]
    block, strip = parts[0].shape
    got = start_copies([(part, got_ref.at[i]) for i, part in enumerate(parts)], got_sems)
    copies = []
    for c in range(chunks):
        for side in range(2):
            for k, code in enumerate(codes):
                at = (c * 2 + side) * len(codes) + k
                row = pl.multiple_of((place_ref[5] ^ code) * block, block)
                column = pl.multiple_of(((place_ref[0] ^ side) * chunks + c) * strip, strip)
                got[at].wait()
                wide_ref[at] = got_ref[at].astype(F32)
                copy = pltpu.make_async_copy(
                    wide_ref.at[at],
                    out.at[pl.ds(row, block), pl.ds(column, strip)],
                    sems.at[at],
                )
                copy.start()
                copies.append(copy)
    for copy in copies:
        copy.wait()


def assemble(place, parts, count, chunks):
    block, strip = parts[0].shape
    rows, wide = block * count, strip * 2 * chunks
    return pl.pallas_call(
        functools.partial(assemble_kernel, gather_codes(count), chunks),
        in_specs=[SMEM] + [HBM] * len(parts),
        out_specs=pl.BlockSpec(memory_space=pl.ANY),
        out_shape=jax.ShapeDtypeStruct((rows, wide), F32),
        scratch_shapes=[
            pltpu.VMEM((len(parts), block, strip), BF16),
            pltpu.VMEM((len(parts), block, strip), F32),
            pltpu.SemaphoreType.DMA((len(parts),)),
            pltpu.SemaphoreType.DMA((len(parts),)),
        ],
        compiler_params=pltpu.CompilerParams(vmem_limit_bytes=LIMIT),
        cost_estimate=pl.CostEstimate(
            flops=rows * wide, bytes_accessed=6 * rows * wide, transcendentals=0
        ),
        name="assemble",
    )(place, *parts)


def swap(block, axis, bit):
    size = lax.axis_size(axis)
    return lax.ppermute(block, axis, [(i, i ^ bit) for i in range(size)])


def gather_blocks(block, axis):
    blocks, bit = [block], lax.axis_size(axis) // 2
    while bit >= 1:
        blocks = blocks + [swap(item, axis, bit) for item in blocks]
        bit //= 2
    return blocks


def gather_parts(part):
    far = swap(part, "mdl", 2)
    return [part, swap(part, "mdl", 1), far, swap(far, "mdl", 1)], far


def product(left, right):
    return jnp.einsum("rh,rd->hd", left, right, preferred_element_type=F32)


def halve(keep, got):
    total = keep + got.astype(F32)
    side = total.shape[0] // 2
    return total[:side], total[side:].astype(BF16)


def half_of(weight, side):
    half = weight.shape[1] // 2
    return lax.dynamic_slice_in_dim(weight, side * half, half, 1)


def on_device(
    obs,
    a_query,
    a_keyval,
    a_out,
    w_policy,
    c_in,
    c_query,
    c_keyval,
    c_out,
    w_value,
    actions,
    advantages,
    old_logp,
    returns,
    robot_count,
):
    row_count = obs.shape[1]
    batch_index = lax.axis_index("sec")
    rep_index = lax.axis_index("rep")
    rep_count = lax.axis_size("rep")
    robot_total = robot_count[batch_index]
    live_sum = jnp.sum(robot_count)
    live_total = live_sum.astype(F32)
    first_row = rep_index * row_count
    live_mask = first_row + lax.iota(jnp.int32, row_count) < robot_total
    mdl_count = lax.axis_size("mdl")
    assert mdl_count == 4 and lax.axis_size("sec") == 2
    mdl_index = lax.axis_index("mdl")
    part_rows = row_count // mdl_count
    row_start = mdl_index * part_rows
    score_scale = HEAD ** (-0.5) * LOG2E
    rep_place = rep_index.reshape(1).astype(jnp.int32)

    place = jnp.stack(
        [batch_index, mdl_index, first_row, robot_total, live_sum, rep_index]
        + [
            jnp.clip(robot_total - (rep_index ^ code) * row_count, 0, row_count)
            for code in gather_codes(rep_count)
        ]
    ).astype(jnp.int32)

    obs_in = obs[0]
    keyval, factor_a = first_projection(obs_in, a_keyval)
    pieces_k = gather_blocks(keyval, "rep")

    a_near = swap(a_out, "mdl", 1)
    c_near = swap(c_in, "mdl", 1)
    a_far0 = swap(half_of(a_out, batch_index), "mdl", 2)
    c_half = half_of(c_in, batch_index)
    c_cut = c_half.shape[0] // 2
    c_a0 = swap(c_half[:c_cut], "mdl", 2)
    c_b0 = swap(c_half[c_cut:], "mdl", 2)

    queries = (dot(obs_in, a_query) * (factor_a[:, :1] * score_scale)).astype(BF16)
    queries, a_far0 = tied(queries, a_far0)
    a_far1 = swap(a_far0, "sec", 1)
    state = attend_call(queries, pieces_k[:-1], 0, place, [])
    *state, c_a0 = tied(*state, c_a0)
    c_a1 = swap(c_a0, "sec", 1)
    *state, c_b0, a_far1 = tied(*state, c_b0, a_far1)
    c_b1 = swap(c_b0, "sec", 1)
    attended = attend_call(queries, pieces_k[-1:], rep_count - 1, place, state)
    attended_far = swap(attended, "mdl", 2)
    attended, attended_far, c_a1 = tied(attended, attended_far, c_a1)
    attended_near = swap(attended, "mdl", 1)
    attended_parts = [attended, attended_near, attended_far, swap(attended_far, "mdl", 1)]
    a_halves = [a_far0, a_far1, swap(a_far0, "mdl", 1), swap(a_far1, "mdl", 1)]
    hidden = hidden_rows(place, obs_in, attended_parts, [a_out, a_near], a_halves)
    c_far = [c_a0, c_b0, c_a1, c_b1]
    c_far = c_far + [swap(item, "mdl", 1) for item in c_far]

    out_half = c_out.shape[0] // 2
    out_cut = out_half // 2
    out_src = lax.dynamic_slice_in_dim(c_out, batch_index * out_half, out_half, 0)
    attended_far, out_src = tied(attended_far, out_src)
    out_a0 = swap(out_src[:out_cut], "mdl", 2)
    out_b0 = swap(out_src[out_cut:], "mdl", 2)

    embedded, critic_keyval, factor_c = embed_rows(place, hidden, [c_in, c_near], c_far, c_keyval)
    pieces_c = gather_blocks(critic_keyval, "rep")
    critic_queries = (dot(embedded, c_query) * (factor_c[:, :1] * score_scale)).astype(BF16)

    late_hidden, critic_keyval = tied(hidden, critic_keyval)
    source = late_hidden.astype(F32)
    factor_h = row_factor(source)
    logits = dot(late_hidden, w_policy) * factor_h
    log_probs = jax.nn.log_softmax(logits, axis=-1)
    onehot = (
        actions[0][:, None] == lax.broadcasted_iota(jnp.int32, logits.shape, 1)
    ).astype(F32)
    chosen = jnp.sum(onehot * log_probs, axis=-1)
    prob_ratio = jnp.exp(chosen - old_logp[0])
    plain_term = prob_ratio * advantages[0]
    bounded = jnp.clip(prob_ratio, 1.0 - clip_range, 1.0 + clip_range) * advantages[0]
    slope = jnp.where(live_mask & (plain_term <= bounded), -plain_term / live_total, F32(0.0))
    dlogits = slope[:, None] * (onehot - jnp.exp(log_probs))
    along = jnp.sum(dlogits * logits, axis=-1, keepdims=True) / source.shape[1]
    dnormed = dot(dlogits.astype(BF16), w_policy.T)
    dhidden = (factor_h * (dnormed - source * (factor_h * along))).astype(BF16)
    half_a = dhidden.shape[1] // 2
    got_a = swap(
        product(attended, lax.dynamic_slice_in_dim(dhidden, (1 - batch_index) * half_a, half_a, 1))
        .astype(BF16),
        "sec",
        1,
    )
    own_a = product(attended, lax.dynamic_slice_in_dim(dhidden, batch_index * half_a, half_a, 1))

    critic_queries, out_a0 = tied(critic_queries, out_a0)
    out_a1 = swap(out_a0, "sec", 1)
    state_c = attend_call(critic_queries, pieces_c[:-1], 0, place, [])
    *state_c, got_a, pieces_c[-1], out_b0 = tied(*state_c, got_a, pieces_c[-1], out_b0)
    out_b1 = swap(out_b0, "sec", 1)
    keep_a, send_a = split_sum(rep_place, own_a, got_a, rep_count)
    moved_a = swap(send_a.astype(BF16), "rep", 1)
    critic_attended = attend_call(critic_queries, pieces_c[-1:], rep_count - 1, place, state_c)
    critic_attended, moved_a = tied(critic_attended, moved_a)
    critic_far = swap(critic_attended, "mdl", 2)
    critic_near = swap(critic_attended, "mdl", 1)
    bit = 2
    while bit < rep_count:
        keep_a, send_a = halve(keep_a, moved_a)
        moved_a = swap(send_a, "rep", bit)
        bit *= 2
    critic_near, out_a1, moved_a = tied(critic_near, out_a1, moved_a)
    mine_a = gather_blocks((keep_a + moved_a.astype(F32)).astype(BF16), "rep")
    critic_parts = [critic_attended, critic_near, critic_far, swap(critic_far, "mdl", 1)]
    out_far = [out_a0, out_b0, out_a1, out_b1]
    c_out_all = [c_out, swap(c_out, "mdl", 1)] + out_far
    c_out_all += [swap(item, "mdl", 1) for item in out_far]
    value_wide, d_other, d_own = mixed_rows(
        place, embedded, critic_parts, c_out_all, w_value, returns[0]
    )
    theirs_a = [swap(block, "sec", 1) for block in mine_a]
    d_other, *theirs_a[:-1] = tied(d_other, *theirs_a[:-1])
    pieces_a = mine_a + theirs_a

    strip = d_own.shape[1] // CHUNKS
    spans = [slice(c * strip, (c + 1) * strip) for c in range(CHUNKS)]
    got = [
        swap(product(critic_attended, d_other[:, span]).astype(BF16), "sec", 1) for span in spans
    ]
    own = [product(critic_attended, d_own[:, span]) for span in spans]
    value_part = lax.dynamic_slice_in_dim(value_wide, row_start, part_rows, 0)[:, 0]
    got[0], value_part = tied(got[0], value_part)
    actor_summed = assemble(place, pieces_a, rep_count, 1)
    got[1], actor_summed = tied(got[1], actor_summed)
    pieces, marks = [], []
    for c in range(CHUNKS):
        arrived = got[c]
        if c > 0:
            arrived, _ = tied(arrived, marks[0])
        keep, send = split_sum(rep_place, own[c], arrived, rep_count)
        bit, trail = 1, []
        while bit < rep_count:
            arrived = swap(send.astype(BF16), "rep", bit)
            bit *= 2
            if c > 0:
                arrived, _ = tied(arrived, marks[min(len(trail) + 1, len(marks) - 1)])
            if bit < rep_count:
                keep, send = halve(keep, arrived)
                trail.append(keep)
        total = (keep + arrived.astype(F32)).astype(BF16)
        trail.append(total)
        mine = gather_blocks(total, "rep")
        trail.append(mine[1])
        marks = trail
        pieces += mine + [swap(block, "sec", 1) for block in mine]
    critic_summed = assemble(place, pieces, rep_count, CHUNKS)

    return (value_part[None, :], actor_summed, critic_summed)


def solution(mesh):
    return jax.shard_map(
        on_device,
        mesh=mesh,
        in_specs=(
            P("sec", "rep", None),
            P(None, "mdl"),
            P(None, None, "mdl"),
            P("mdl", None),
            P(),
            P(None, "mdl"),
            P(None, "mdl"),
            P(None, None, "mdl"),
            P("mdl", None),
            P(),
            P("sec", "rep"),
            P("sec", "rep"),
            P("sec", "rep"),
            P("sec", "rep"),
            P(),
        ),
        out_specs=(P("sec", ("rep", "mdl")), P("mdl", None), P("mdl", None)),
        check_vma=False,
    )
```

time: 272 us -> 269 us (0.989); the launches traced: 271 us -> 265 us
  waiting for transfers between devices: 124 us -> 104 us
  local copies, waits for them, and re-layouts: 42.2 us -> 24.2 us
  starting transfers between devices: 45.8 us -> 61.9 us
  Pallas kernels: 43.1 us -> 59.1 us
    unnamed x118 -> x82, local copies, waits for them, and re-layouts: 35.7 us -> 15 us
    ppermute x59 -> x65, waiting for transfers between devices: 124 us -> 104 us  [swap(): return lax.ppermute(block, axis, [(i, i ^ bit) for i in range(size)])]
    ppermute x59 -> x65, starting transfers between devices: 45.8 us -> 61.9 us  [swap(): return lax.ppermute(block, axis, [(i, i ^ bit) for i in range(size)])]
    pallas_call x8, Pallas kernels: 37.6 us -> 49.7 us  [the longest x1 16.7 us: mixed_rows(): pl.pallas_call(mixed_kernel, in_specs=[SMEM] + [VMEM] * 7 + [HBM] * len(w...]
    pallas_call x2, Pallas kernels: 5.23 us -> 9.18 us  [assemble(): pl.pallas_call(functools.partial(assemble_kernel, gather_codes(count), ch...]
  transfers between devices with their start and end apart: 59 -> 65, of which waited for: 26 -> 29; matrix products, arithmetic and copies ran while one was open for 6% -> 7% of each run, Pallas kernels for 10% -> 20%
where the time goes in v4:
time: 269 us; the launch traced here: 265 us
  waiting for transfers between devices  104 us (39%)
  starting transfers between devices  61.9 us (23%)
  Pallas kernels  59.1 us (22%)
  local copies, waits for them, and re-layouts  24.2 us (9%)
  matrix products  9.18 us (3%)
  between operations  4.69 us (2%)
    ppermute x65, waiting for transfers between devices, swap(): return lax.ppermute(block, axis, [(i, i ^ bit) for i in range(size)])  104 us
    ppermute x65, starting transfers between devices, swap(): return lax.ppermute(block, axis, [(i, i ^ bit) for i in range(size)])  61.9 us
    pallas_call x1, Pallas kernels, mixed_rows(): pl.pallas_call(mixed_kernel, in_specs=[SMEM] + [VMEM] * 7 + [HBM] * len(w...  16.7 us
    unnamed x82, local copies, waits for them, and re-layouts  15 us
    pallas_call x4, Pallas kernels, attend_call(): pl.pallas_call(functools.partial(body, groups, units, TABLE + first), in_...  13.8 us
    pallas_call x1, Pallas kernels, embed_rows(): pl.pallas_call(embed_kernel, in_specs=[SMEM, VMEM] + [HBM] * (3 + len(far...  10.6 us
    pallas_call x2, Pallas kernels, assemble(): pl.pallas_call(functools.partial(assemble_kernel, gather_codes(count), ch...  9.18 us
    pallas_call x1, Pallas kernels, hidden_rows(): pl.pallas_call(hidden_kernel, in_specs=[SMEM, HBM] + [VMEM] * 4 + [HBM] *...  6.2 us
  transfers between devices with their start and end apart: 65, of which 29 were waited for; matrix products, arithmetic and copies ran while one was open for 7% of the time, Pallas kernels for 20%

profile of v4, /device:TPU:0, one launch (start us, length us, event | category | flops | bytes accessed | tf_op | source)
XLA Modules:
  0.0 265.5 jit_solution(41829100837791554)
XLA Ops:
  2.7 3.0 %collective-permute-start = (bf16[384,768]{1,0:T(8,128)(2,1)}, bf16[384,768]{1,0:T(8,128)(2,1)S(1)}, u32[]{:S(2)}, u32[]{:S(2)}) collective-permute-start(bf16[384,768]{1,0:T(8,128)(2,1)} %constant_dynamic-slice_fusion.2), channel_id=1, source_target_pairs={{0,2},{1,3},{2,0},{3,1},{4,6},{5,7},{6,4},{7,5},{8,10},{9,11},{10,... | collective-permute-start | bytes 1769480 | tf_op jit(solution)/shard_map/ppermute | solution.py:479
  28.5 4.0 %attend_open.2 = (f32[512,768]{1,0:T(8,128)S(1)}, f32[512,384]{1,0:T(8,128)S(1)}) custom-call(s32[10]{0:T(128)S(1)} %stack.39.left_ref.place_ref, bf16[512,384]{1,0:T(8,128)(2,1)S(1)} %fusion.5.q_ref, bf16[2,512,128]{2,1,0:T(8,128)(2,1)} %get-tuple-element.60.refs_0_, bf16[2,512,128]{2,1,0:T(8,128)(2,1)S(1)} %collective-permute-done.1.refs_1_, ...), custom_call_target="tpu_custom_call" | custom-call | flops 7247757312 | bytes 786432 | tf_op jit(solution)/shard_map/attend_open/pallas_call | solution.py:189
  33.1 3.5 %collective-permute-done.4.refs_1_ = bf16[768,256]{1,0:T(8,128)(2,1)} collective-permute-done((bf16[768,256]{1,0:T(8,128)(2,1)S(1)}, bf16[768,256]{1,0:T(8,128)(2,1)}, u32[]{:S(2)}, u32[]{:S(2)}) %collective-permute-start.4) | collective-permute-done | bytes 393248 | tf_op jit(solution)/shard_map/ppermute | solution.py:479
  36.7 6.7 %collective-permute-done.5.w21 = bf16[384,768]{1,0:T(8,128)(2,1)} collective-permute-done((bf16[384,768]{1,0:T(8,128)(2,1)S(1)}, bf16[384,768]{1,0:T(8,128)(2,1)}, u32[]{:S(2)}, u32[]{:S(2)}) %collective-permute-start.5) | collective-permute-done | bytes 589856 | tf_op jit(solution)/shard_map/ppermute | solution.py:479
  46.5 3.9 %collective-permute-done.8.refs_2_ = bf16[768,256]{1,0:T(8,128)(2,1)S(1)} collective-permute-done((bf16[768,256]{1,0:T(8,128)(2,1)}, bf16[768,256]{1,0:T(8,128)(2,1)S(1)}, u32[]{:S(2)}, u32[]{:S(2)}) %collective-permute-start.8) | collective-permute-done | bytes 393248 | tf_op jit(solution)/shard_map/ppermute | solution.py:479
  50.4 7.1 %collective-permute-done.7.t2 = bf16[512,384]{1,0:T(8,128)(2,1)S(1)} collective-permute-done((bf16[512,384]{1,0:T(8,128)(2,1)S(1)}, bf16[512,384]{1,0:T(8,128)(2,1)S(1)}, u32[]{:S(2)}, u32[]{:S(2)}) %collective-permute-start.7) | collective-permute-done | bytes 393248 | tf_op jit(solution)/shard_map/ppermute | solution.py:479
  62.4 6.2 %collective-permute-done.15.refs_3_ = bf16[768,256]{1,0:T(8,128)(2,1)} collective-permute-done((bf16[768,256]{1,0:T(8,128)(2,1)}, bf16[768,256]{1,0:T(8,128)(2,1)}, u32[]{:S(2)}, u32[]{:S(2)}) %collective-permute-start.15) | collective-permute-done | bytes 393248 | tf_op jit(solution)/shard_map/ppermute | solution.py:479
  69.8 6.2 %hidden_rows.1.h_ref = bf16[512,1536]{1,0:T(8,128)(2,1)S(1)} custom-call(s32[10]{0:T(128)S(1)} %stack.39.left_ref.place_ref, bf16[512,1536]{1,0:T(8,128)(2,1)S(1)} %bitcast.31, bf16[512,384]{1,0:T(8,128)(2,1)S(1)} %attend_close.2.t0, bf16[512,384]{1,0:T(8,128)(2,1)} %collective-permute-done.9.t1, bf16[512,384]{1,0:T(8,128)(2,1)S(1)} %collective-permute-done.7.t2, ...), custom_call_target="tpu_custom_call" | custom-call | flops 2415919104 | bytes 4718592 | tf_op jit(solution)/shard_map/hidden_rows/pallas_call | solution.py:231
  78.2 10.6 %embed_rows.1 = (bf16[512,2048]{1,0:T(8,128)(2,1)S(1)}, bf16[2,512,128]{2,1,0:T(8,128)(2,1)S(1)}, f32[512,128]{1,0:T(8,128)S(1)}) custom-call(s32[10]{0:T(128)S(1)} %stack.39.left_ref.place_ref, bf16[512,1536]{1,0:T(8,128)(2,1)S(1)} %hidden_rows.1.h_ref, bf16[1536,512]{1,0:T(8,128)(2,1)} %w0.3, bf16[1536,512]{1,0:T(8,128)(2,1)} %collective-permute-done.14.w1, ...), custom_call_target="tpu_custom_call" | custom-call | flops 3221225472 | bytes 6291456 | tf_op jit(solution)/shard_map/embed_rows/pallas_call | solution.py:295
  98.0 5.5 %collective-permute-done.21.refs_1_ = bf16[2,512,128]{2,1,0:T(8,128)(2,1)S(1)} collective-permute-done((bf16[2,512,128]{2,1,0:T(8,128)(2,1)S(1)}, bf16[2,512,128]{2,1,0:T(8,128)(2,1)S(1)}, u32[]{:S(2)}, u32[]{:S(2)}) %collective-permute-start.21) | collective-permute-done | bytes 262176 | tf_op jit(solution)/shard_map/ppermute | solution.py:479
  103.5 4.4 %attend_open.3 = (f32[512,1024]{1,0:T(8,128)S(1)}, f32[512,512]{1,0:T(8,128)S(1)}) custom-call(s32[10]{0:T(128)S(1)} %stack.39.left_ref.place_ref, bf16[512,512]{1,0:T(8,128)(2,1)S(1)} %fusion.4.q_ref, bf16[2,512,128]{2,1,0:T(8,128)(2,1)S(1)} %get-tuple-element.78.refs_0_, bf16[2,512,128]{2,1,0:T(8,128)(2,1)S(1)} %collective-permute-done.21.refs_1_, ...), custom_call_target="tpu_custom_call" | custom-call | flops 9663676416 | bytes 1048576 | tf_op jit(solution)/shard_map/attend_open/pallas_call | solution.py:189
  111.4 11.4 %collective-permute-start.26 = (bf16[192,768]{1,0:T(8,128)(2,1)S(1)}, bf16[192,768]{1,0:T(8,128)(2,1)S(1)}, u32[]{:S(2)}, u32[]{:S(2)}) collective-permute-start(bf16[192,768]{1,0:T(8,128)(2,1)S(1)} %get-tuple-element.86), channel_id=1, source_target_pairs={{0,8},{8,0},{16,24},{24,16},{1,9},{9,1},{17,25},{25,17},{2,10},{10... | collective-permute-start | bytes 884744 | tf_op jit(solution)/shard_map/ppermute | solution.py:479
  124.8 3.0 %attend_close.3.t0 = bf16[512,512]{1,0:T(8,128)(2,1)S(1)} custom-call(s32[10]{0:T(128)S(1)} %stack.39.left_ref.place_ref, bf16[512,512]{1,0:T(8,128)(2,1)S(1)} %fusion.4.q_ref, f32[512,1024]{1,0:T(8,128)S(1)} %get-tuple-element.82.wide_ref, f32[512,512]{1,0:T(8,128)S(1)} %get-tuple-element.83.top_ref, bf16[2,512,128]{2,1,0:T(8,128)(2,1)S(1)} %collective-permute-done.24.refs_0_), custom_call_target="tpu_custom_call" | custom-call | flops 134217728 | bytes 1048576 | tf_op jit(solution)/shard_map/attend_close/pallas_call | solution.py:189
  130.2 7.5 %collective-permute-done.28.refs_4_ = bf16[128,2048]{1,0:T(8,128)(2,1)} collective-permute-done((bf16[128,2048]{1,0:T(8,128)(2,1)S(1)}, bf16[128,2048]{1,0:T(8,128)(2,1)}, u32[]{:S(2)}, u32[]{:S(2)}) %collective-permute-start.28) | collective-permute-done | bytes 524320 | tf_op jit(solution)/shard_map/ppermute | solution.py:479
  138.5 6.6 %collective-permute-done.29 = bf16[96,768]{1,0:T(8,128)(2,1)S(1)} collective-permute-done((bf16[96,768]{1,0:T(8,128)(2,1)S(1)}, bf16[96,768]{1,0:T(8,128)(2,1)S(1)}, u32[]{:S(2)}, u32[]{:S(2)}) %collective-permute-start.29) | collective-permute-done | bytes 147488 | tf_op jit(solution)/shard_map/ppermute | solution.py:479
  152.2 6.7 %collective-permute-done.39.refs_1_ = bf16[96,768]{1,0:T(8,128)(2,1)S(1)} collective-permute-done((bf16[96,768]{1,0:T(8,128)(2,1)S(1)}, bf16[96,768]{1,0:T(8,128)(2,1)S(1)}, u32[]{:S(2)}, u32[]{:S(2)}) %collective-permute-start.39) | collective-permute-done | bytes 147488 | tf_op jit(solution)/shard_map/ppermute | solution.py:479
  170.9 16.7 %mixed_rows.1 = (f32[512,128]{1,0:T(8,128)S(1)}, bf16[512,1024]{1,0:T(8,128)(2,1)S(1)}, bf16[512,1024]{1,0:T(8,128)(2,1)S(1)}) custom-call(s32[10]{0:T(128)S(1)} %stack.39.left_ref.place_ref, bf16[512,2048]{1,0:T(8,128)(2,1)S(1)} %copy-done.31, bf16[512,512]{1,0:T(8,128)(2,1)S(1)} %attend_close.3.t0, bf16[512,512]{1,0:T(8,128)(2,1)S(1)} %copy-done.19, ...), custom_call_target="tpu_custom_call" | custom-call | flops 4294967296 | bytes 8388608 | tf_op jit(solution)/shard_map/mixed_rows/pallas_call | solution.py:367
  190.5 5.1 %collective-permute-done.45.refs_3_ = bf16[96,768]{1,0:T(8,128)(2,1)S(1)} collective-permute-done((bf16[96,768]{1,0:T(8,128)(2,1)S(1)}, bf16[96,768]{1,0:T(8,128)(2,1)S(1)}, u32[]{:S(2)}, u32[]{:S(2)}) %collective-permute-start.45) | collective-permute-done | bytes 147488 | tf_op jit(solution)/shard_map/ppermute | solution.py:479
  199.1 5.7 %collective-permute-done.43.got_ref = bf16[512,512]{1,0:T(8,128)(2,1)S(1)} collective-permute-done((bf16[512,512]{1,0:T(8,128)(2,1)}, bf16[512,512]{1,0:T(8,128)(2,1)S(1)}, u32[]{:S(2)}, u32[]{:S(2)}) %collective-permute-start.43) | collective-permute-done | bytes 524320 | tf_op jit(solution)/shard_map/ppermute | solution.py:479
  206.0 5.8 %collective-permute-done.47 = bf16[256,512]{1,0:T(8,128)(2,1)S(1)} collective-permute-done((bf16[256,512]{1,0:T(8,128)(2,1)S(1)}, bf16[256,512]{1,0:T(8,128)(2,1)S(1)}, u32[]{:S(2)}, u32[]{:S(2)}) %collective-permute-start.47) | collective-permute-done | bytes 262176 | tf_op jit(solution)/shard_map/ppermute | solution.py:479
  212.8 3.6 %assemble.2 = f32[384,1536]{1,0:T(8,128)} custom-call(s32[10]{0:T(128)S(1)} %stack.39.left_ref.place_ref, bf16[96,768]{1,0:T(8,128)(2,1)S(1)} %fusion.15.refs_0_, bf16[96,768]{1,0:T(8,128)(2,1)S(1)} %collective-permute-done.39.refs_1_, bf16[96,768]{1,0:T(8,128)(2,1)S(1)} %collective-permute-done.41.refs_2_, ...), custom_call_target="tpu_custom_call" | custom-call | flops 589824 | bytes 3538944 | tf_op jit(solution)/shard_map/assemble/pallas_call | solution.py:458
  219.3 5.1 %collective-permute-done.56 = bf16[256,512]{1,0:T(8,128)(2,1)S(1)} collective-permute-done((bf16[256,512]{1,0:T(8,128)(2,1)S(1)}, bf16[256,512]{1,0:T(8,128)(2,1)S(1)}, u32[]{:S(2)}, u32[]{:S(2)}) %collective-permute-start.56) | collective-permute-done | bytes 262176 | tf_op jit(solution)/shard_map/ppermute | solution.py:479
  229.0 5.8 %collective-permute-done.57 = bf16[128,512]{1,0:T(8,128)(2,1)S(1)} collective-permute-done((bf16[128,512]{1,0:T(8,128)(2,1)S(1)}, bf16[128,512]{1,0:T(8,128)(2,1)S(1)}, u32[]{:S(2)}, u32[]{:S(2)}) %collective-permute-start.57) | collective-permute-done | bytes 131104 | tf_op jit(solution)/shard_map/ppermute | solution.py:479
  259.7 5.6 %assemble.3 = f32[512,2048]{1,0:T(8,128)} custom-call(s32[10]{0:T(128)S(1)} %stack.39.left_ref.place_ref, bf16[128,512]{1,0:T(8,128)(2,1)S(1)} %add_convert_fusion.refs_0_, bf16[128,512]{1,0:T(8,128)(2,1)S(1)} %collective-permute-done.49.refs_1_, bf16[128,512]{1,0:T(8,128)(2,1)S(1)} %collective-permute-done.50.refs_2_, ...), custom_call_target="tpu_custom_call" | custom-call | flops 1048576 | bytes 6291456 | tf_op jit(solution)/shard_map/assemble/pallas_call | solution.py:458
  (240 shorter events, 111.1 us)
Async XLA Ops:
  2.7 23.9 %collective-permute-start = (bf16[384,768]{1,0:T(8,128)(2,1)}, bf16[384,768]{1,0:T(8,128)(2,1)S(1)}, u32[]{:S(2)}, u32[]{:S(2)}) collective-permute-start(bf16[384,768]{1,0:T(8,128)(2,1)} %constant_dynamic-slice_fusion.2), channel_id=1, source_target_pairs={{0,2},{1,3},{2,0},{3,1},{4,6},{5,7},{6,4},{7,5},{8,10},{9,11},{10,... | collective-permute-start | bytes 1769480 | tf_op jit(solution)/shard_map/ppermute | solution.py:479
  14.3 45.5 %collective-permute-start.11 = (bf16[384,1536]{1,0:T(8,128)(2,1)}, bf16[384,1536]{1,0:T(8,128)(2,1)}, u32[]{:S(2)}, u32[]{:S(2)}) collective-permute-start(bf16[384,1536]{1,0:T(8,128)(2,1)} %w0.2), channel_id=1, source_target_pairs={{0,1},{1,0},{2,3},{3,2},{4,5},{5,4},{6,7},{7,6},{8,9},{9,8},{10,11... | collective-permute-start | bytes 3538952 | tf_op jit(solution)/shard_map/ppermute | solution.py:479
  16.4 16.1 %collective-permute-start.3 = (bf16[768,256]{1,0:T(8,128)(2,1)}, bf16[768,256]{1,0:T(8,128)(2,1)}, u32[]{:S(2)}, u32[]{:S(2)}) collective-permute-start(bf16[768,256]{1,0:T(8,128)(2,1)} %get-tuple-element.114), channel_id=1, source_target_pairs={{0,2},{1,3},{2,0},{3,1},{4,6},{5,7},{6,4},{7,5},{8,10},{9,11},{10,... | collective-permute-start | bytes 1179656 | tf_op jit(solution)/shard_map/ppermute | solution.py:479
  26.6 16.8 %collective-permute-start.6 = (bf16[2,512,128]{2,1,0:T(8,128)(2,1)S(1)}, bf16[2,512,128]{2,1,0:T(8,128)(2,1)S(1)}, u32[]{:S(2)}, u32[]{:S(2)}) collective-permute-start(bf16[2,512,128]{2,1,0:T(8,128)(2,1)S(1)} %collective-permute-done.1.refs_1_), channel_id=1, source_target_pairs={{0,8},{8,0},{16,24},{24,16},{1,9},{9,1},{17,25},{25,17},{2,10},{10... | collective-permute-start | bytes 786440 | tf_op jit(solution)/shard_map/ppermute | solution.py:479
  27.1 16.3 %collective-permute-start.5 = (bf16[384,768]{1,0:T(8,128)(2,1)S(1)}, bf16[384,768]{1,0:T(8,128)(2,1)}, u32[]{:S(2)}, u32[]{:S(2)}) collective-permute-start(bf16[384,768]{1,0:T(8,128)(2,1)S(1)} %collective-permute-done.w20), channel_id=1, source_target_pairs={{0,4},{4,0},{1,5},{5,1},{2,6},{6,2},{3,7},{7,3},{8,12},{12,8},{9,1... | collective-permute-start | bytes 1769480 | tf_op jit(solution)/shard_map/ppermute | solution.py:479
  32.5 17.8 %collective-permute-start.8 = (bf16[768,256]{1,0:T(8,128)(2,1)}, bf16[768,256]{1,0:T(8,128)(2,1)S(1)}, u32[]{:S(2)}, u32[]{:S(2)}) collective-permute-start(bf16[768,256]{1,0:T(8,128)(2,1)} %collective-permute-done.3.refs_0_), channel_id=1, source_target_pairs={{0,4},{4,0},{1,5},{5,1},{2,6},{6,2},{3,7},{7,3},{8,12},{12,8},{9,1... | collective-permute-start | bytes 1179656 | tf_op jit(solution)/shard_map/ppermute | solution.py:479
  36.7 22.3 %collective-permute-start.12 = (bf16[384,768]{1,0:T(8,128)(2,1)S(1)}, bf16[384,768]{1,0:T(8,128)(2,1)S(1)}, u32[]{:S(2)}, u32[]{:S(2)}) collective-permute-start(bf16[384,768]{1,0:T(8,128)(2,1)S(1)} %collective-permute-done.w20), channel_id=1, source_target_pairs={{0,1},{1,0},{2,3},{3,2},{4,5},{5,4},{6,7},{7,6},{8,9},{9,8},{10,11... | collective-permute-start | bytes 1769480 | tf_op jit(solution)/shard_map/ppermute | solution.py:479
  43.4 33.3 %collective-permute-start.14 = (bf16[1536,512]{1,0:T(8,128)(2,1)}, bf16[1536,512]{1,0:T(8,128)(2,1)}, u32[]{:S(2)}, u32[]{:S(2)}) collective-permute-start(bf16[1536,512]{1,0:T(8,128)(2,1)} %w0.3), channel_id=1, source_target_pairs={{0,1},{1,0},{2,3},{3,2},{4,5},{5,4},{6,7},{7,6},{8,9},{9,8},{10,11... | collective-permute-start | bytes 4718600 | tf_op jit(solution)/shard_map/ppermute | solution.py:479
  50.4 18.2 %collective-permute-start.13 = (bf16[384,768]{1,0:T(8,128)(2,1)}, bf16[384,768]{1,0:T(8,128)(2,1)}, u32[]{:S(2)}, u32[]{:S(2)}) collective-permute-start(bf16[384,768]{1,0:T(8,128)(2,1)} %collective-permute-done.5.w21), channel_id=1, source_target_pairs={{0,1},{1,0},{2,3},{3,2},{4,5},{5,4},{6,7},{7,6},{8,9},{9,8},{10,11... | collective-permute-start | bytes 1769480 | tf_op jit(solution)/shard_map/ppermute | solution.py:479
  76.0 70.6 %collective-permute-start.32 = (bf16[512,2048]{1,0:T(8,128)(2,1)S(1)}, bf16[512,2048]{1,0:T(8,128)(2,1)S(1)}, u32[]{:S(2)}, u32[]{:S(2)}) collective-permute-start(bf16[512,2048]{1,0:T(8,128)(2,1)S(1)} %copy-done.10), channel_id=1, source_target_pairs={{0,1},{1,0},{2,3},{3,2},{4,5},{5,4},{6,7},{7,6},{8,9},{9,8},{10,11... | collective-permute-start | bytes 6291464 | tf_op jit(solution)/shard_map/ppermute | solution.py:479
  76.1 20.3 %collective-permute-start.20 = (bf16[128,2048]{1,0:T(8,128)(2,1)S(1)}, bf16[128,2048]{1,0:T(8,128)(2,1)S(1)}, u32[]{:S(2)}, u32[]{:S(2)}) collective-permute-start(bf16[128,2048]{1,0:T(8,128)(2,1)S(1)} %get-tuple-element.116), channel_id=1, source_target_pairs={{0,2},{1,3},{2,0},{3,1},{4,6},{5,7},{6,4},{7,5},{8,10},{9,11},{10,... | collective-permute-start | bytes 1572872 | tf_op jit(solution)/shard_map/ppermute | solution.py:479
  76.7 31.2 %collective-permute-start.25 = (bf16[128,2048]{1,0:T(8,128)(2,1)S(1)}, bf16[128,2048]{1,0:T(8,128)(2,1)S(1)}, u32[]{:S(2)}, u32[]{:S(2)}) collective-permute-start(bf16[128,2048]{1,0:T(8,128)(2,1)S(1)} %get-tuple-element.115), channel_id=1, source_target_pairs={{0,2},{1,3},{2,0},{3,1},{4,6},{5,7},{6,4},{7,5},{8,10},{9,11},{10,... | collective-permute-start | bytes 1572872 | tf_op jit(solution)/shard_map/ppermute | solution.py:479
  111.4 17.2 %collective-permute-start.26 = (bf16[192,768]{1,0:T(8,128)(2,1)S(1)}, bf16[192,768]{1,0:T(8,128)(2,1)S(1)}, u32[]{:S(2)}, u32[]{:S(2)}) collective-permute-start(bf16[192,768]{1,0:T(8,128)(2,1)S(1)} %get-tuple-element.86), channel_id=1, source_target_pairs={{0,8},{8,0},{16,24},{24,16},{1,9},{9,1},{17,25},{25,17},{2,10},{10... | collective-permute-start | bytes 884744 | tf_op jit(solution)/shard_map/ppermute | solution.py:479
  122.8 15.0 %collective-permute-start.28 = (bf16[128,2048]{1,0:T(8,128)(2,1)S(1)}, bf16[128,2048]{1,0:T(8,128)(2,1)}, u32[]{:S(2)}, u32[]{:S(2)}) collective-permute-start(bf16[128,2048]{1,0:T(8,128)(2,1)S(1)} %collective-permute-done.20.refs_2_), channel_id=1, source_target_pairs={{0,4},{4,0},{1,5},{5,1},{2,6},{6,2},{3,7},{7,3},{8,12},{12,8},{9,1... | collective-permute-start | bytes 1572872 | tf_op jit(solution)/shard_map/ppermute | solution.py:479
  124.3 21.8 %collective-permute-start.33 = (bf16[128,2048]{1,0:T(8,128)(2,1)S(1)}, bf16[128,2048]{1,0:T(8,128)(2,1)}, u32[]{:S(2)}, u32[]{:S(2)}) collective-permute-start(bf16[128,2048]{1,0:T(8,128)(2,1)S(1)} %collective-permute-done.25.refs_3_), channel_id=1, source_target_pairs={{0,4},{4,0},{1,5},{5,1},{2,6},{6,2},{3,7},{7,3},{8,12},{12,8},{9,1... | collective-permute-start | bytes 1572872 | tf_op jit(solution)/shard_map/ppermute | solution.py:479
  128.6 17.5 %collective-permute-start.27 = (bf16[512,512]{1,0:T(8,128)(2,1)S(1)}, bf16[512,512]{1,0:T(8,128)(2,1)S(1)}, u32[]{:S(2)}, u32[]{:S(2)}) collective-permute-start(bf16[512,512]{1,0:T(8,128)(2,1)S(1)} %attend_close.3.t0), channel_id=1, source_target_pairs={{0,1},{1,0},{2,3},{3,2},{4,5},{5,4},{6,7},{7,6},{8,9},{9,8},{10,11... | collective-permute-start | bytes 1572872 | tf_op jit(solution)/shard_map/ppermute | solution.py:479
  128.6 18.1 %collective-permute-start.30 = (bf16[512,512]{1,0:T(8,128)(2,1)S(1)}, bf16[512,512]{1,0:T(8,128)(2,1)S(1)}, u32[]{:S(2)}, u32[]{:S(2)}) collective-permute-start(bf16[512,512]{1,0:T(8,128)(2,1)S(1)} %attend_close.3.t0), channel_id=1, source_target_pairs={{0,2},{1,3},{2,0},{3,1},{4,6},{5,7},{6,4},{7,5},{8,10},{9,11},{10,... | collective-permute-start | bytes 1572872 | tf_op jit(solution)/shard_map/ppermute | solution.py:479
  146.1 14.9 %collective-permute-start.37 = (bf16[128,2048]{1,0:T(8,128)(2,1)}, bf16[128,2048]{1,0:T(8,128)(2,1)}, u32[]{:S(2)}, u32[]{:S(2)}) collective-permute-start(bf16[128,2048]{1,0:T(8,128)(2,1)} %collective-permute-done.33.refs_5_), channel_id=1, source_target_pairs={{0,1},{1,0},{2,3},{3,2},{4,5},{5,4},{6,7},{7,6},{8,9},{9,8},{10,11... | collective-permute-start | bytes 1572872 | tf_op jit(solution)/shard_map/ppermute | solution.py:479
  146.6 15.9 %collective-permute-start.36 = (bf16[128,2048]{1,0:T(8,128)(2,1)}, bf16[128,2048]{1,0:T(8,128)(2,1)}, u32[]{:S(2)}, u32[]{:S(2)}) collective-permute-start(bf16[128,2048]{1,0:T(8,128)(2,1)} %collective-permute-done.28.refs_4_), channel_id=1, source_target_pairs={{0,1},{1,0},{2,3},{3,2},{4,5},{5,4},{6,7},{7,6},{8,9},{9,8},{10,11... | collective-permute-start | bytes 1572872 | tf_op jit(solution)/shard_map/ppermute | solution.py:479
  146.7 15.8 %collective-permute-start.31 = (bf16[512,512]{1,0:T(8,128)(2,1)S(1)}, bf16[512,512]{1,0:T(8,128)(2,1)}, u32[]{:S(2)}, u32[]{:S(2)}) collective-permute-start(bf16[512,512]{1,0:T(8,128)(2,1)S(1)} %collective-permute-done.30.t2), channel_id=1, source_target_pairs={{0,1},{1,0},{2,3},{3,2},{4,5},{5,4},{6,7},{7,6},{8,9},{9,8},{10,11... | collective-permute-start | bytes 1572872 | tf_op jit(solution)/shard_map/ppermute | solution.py:479
  159.0 29.7 %collective-permute-start.38 = (bf16[96,768]{1,0:T(8,128)(2,1)S(1)}, bf16[96,768]{1,0:T(8,128)(2,1)S(1)}, u32[]{:S(2)}, u32[]{:S(2)}) collective-permute-start(bf16[96,768]{1,0:T(8,128)(2,1)S(1)} %fusion.15.refs_0_), channel_id=1, source_target_pairs={{0,4},{4,0},{1,5},{5,1},{2,6},{6,2},{3,7},{7,3},{8,12},{12,8},{9,1... | collective-permute-start | bytes 442376 | tf_op jit(solution)/shard_map/ppermute | solution.py:479
  160.5 28.2 %collective-permute-start.40 = (bf16[96,768]{1,0:T(8,128)(2,1)S(1)}, bf16[96,768]{1,0:T(8,128)(2,1)S(1)}, u32[]{:S(2)}, u32[]{:S(2)}) collective-permute-start(bf16[96,768]{1,0:T(8,128)(2,1)S(1)} %collective-permute-done.39.refs_1_), channel_id=1, source_target_pairs={{0,4},{4,0},{1,5},{5,1},{2,6},{6,2},{3,7},{7,3},{8,12},{12,8},{9,1... | collective-permute-start | bytes 442376 | tf_op jit(solution)/shard_map/ppermute | solution.py:479
  161.0 27.6 %collective-permute-start.42 = (bf16[96,768]{1,0:T(8,128)(2,1)S(1)}, bf16[96,768]{1,0:T(8,128)(2,1)S(1)}, u32[]{:S(2)}, u32[]{:S(2)}) collective-permute-start(bf16[96,768]{1,0:T(8,128)(2,1)S(1)} %collective-permute-done.41.refs_2_), channel_id=1, source_target_pairs={{0,4},{4,0},{1,5},{5,1},{2,6},{6,2},{3,7},{7,3},{8,12},{12,8},{9,1... | collective-permute-start | bytes 442376 | tf_op jit(solution)/shard_map/ppermute | solution.py:479
  195.6 17.2 %collective-permute-start.46 = (bf16[96,768]{1,0:T(8,128)(2,1)S(1)}, bf16[96,768]{1,0:T(8,128)(2,1)S(1)}, u32[]{:S(2)}, u32[]{:S(2)}) collective-permute-start(bf16[96,768]{1,0:T(8,128)(2,1)S(1)} %collective-permute-done.45.refs_3_), channel_id=1, source_target_pairs={{0,4},{4,0},{1,5},{5,1},{2,6},{6,2},{3,7},{7,3},{8,12},{12,8},{9,1... | collective-permute-start | bytes 442376 | tf_op jit(solution)/shard_map/ppermute | solution.py:479
  (82 other events, 709.0 us)

commit v5 on v4

--- a/solution.py
+++ b/solution.py
@@ -20,7 +20,7 @@
 LIMIT = 40 * 2**20
 VMEM = pl.BlockSpec(memory_space=pltpu.VMEM)
 SMEM = pl.BlockSpec(memory_space=pltpu.SMEM)
-HBM = pl.BlockSpec(memory_space=pltpu.HBM)
+ANY = pl.BlockSpec(memory_space=pl.ANY)
 
 
 def dot(a, b):
@@ -73,7 +73,7 @@
     width = w_keyval.shape[2]
     return pl.pallas_call(
         first_kernel,
-        in_specs=[HBM] * 2,
+        in_specs=[ANY] * 2,
         out_specs=[VMEM] * 2,
         out_shape=[
             jax.ShapeDtypeStruct((2, rows, width), BF16),
@@ -202,190 +202,211 @@
 
 
 def hidden_kernel(
-    place_ref, obs_hbm, t0, t1, t2, t3, w0, w1, w20, w21, w30, w31, o_ref, obs_ref, w_ref, sems
+    obs_any, t0, t1, t2, t3, w0, w1, w2, w3, c_any, o_ref, emb_ref, obs_ref, w_ref, c_ref, sum_ref, sems
 ):
-    inner, half = w20.shape
-    starts = [pl.multiple_of((place_ref[0] ^ side) * half, HEAD) for side in range(2)]
-    pairs = []
-    for side, (w2, w3) in enumerate(((w20, w30), (w21, w31))):
-        columns = pl.ds(starts[side], half)
-        for k, source in enumerate((w0.at[:, columns], w1.at[:, columns], w2, w3)):
-            pairs.append((source, w_ref.at[side, k * inner : (k + 1) * inner]))
-        pairs.append((obs_hbm.at[:, columns], obs_ref.at[side]))
-    copies = start_copies(pairs, sems)
-    tile = half // 3
-    for side in range(2):
-        for copy in copies[side * 5 : (side + 1) * 5]:
-            copy.wait()
-        for i in range(3):
-            strip = slice(i * tile, (i + 1) * tile)
-            parts = jnp.concatenate([t0[...], t1[...], t2[...], t3[...]], axis=1)
-            total = obs_ref[side, :, strip].astype(F32) + dot(parts, w_ref[side, :, strip])
-            column = pl.multiple_of(starts[side] + i * tile, HEAD)
-            o_ref[:, pl.ds(column, tile)] = total.astype(BF16)
-
-
-def hidden_rows(place, obs, parts, full, halves):
+    inner, depth = w0.shape
+    tile = depth // 3
+    pairs = [(obs_any, obs_ref)]
+    pairs += [
+        (w, w_ref.at[k * inner : (k + 1) * inner]) for k, w in enumerate((w0, w1, w2, w3))
+    ]
+    copies = start_copies(pairs + [(c_any, c_ref)], sems)
+    for copy in copies[:3]:
+        copy.wait()
+    tiles = [slice(i * tile, (i + 1) * tile) for i in range(3)]
+    for strip in tiles:
+        parts = jnp.concatenate([t0[...], t1[...]], axis=1)
+        sum_ref[:, strip] = obs_ref[:, strip].astype(F32) + dot(parts, w_ref[: 2 * inner, strip])
+    for copy in copies[3:5]:
+        copy.wait()
+    for strip in tiles:
+        parts = jnp.concatenate([t2[...], t3[...]], axis=1)
+        total = sum_ref[:, strip] + dot(parts, w_ref[2 * inner :, strip])
+        o_ref[:, strip] = total.astype(BF16)
+    copies[5].wait()
+    emb_ref[...] = dot(o_ref[...], c_ref[...]).astype(BF16)
+
+
+def hidden_rows(obs, parts, weights, c_in):
     rows, depth = obs.shape
-    inner, half = halves[0].shape
+    inner = weights[0].shape[0]
+    width = c_in.shape[1]
     return pl.pallas_call(
         hidden_kernel,
-        in_specs=[SMEM, HBM] + [VMEM] * 4 + [HBM] * 6,
-        out_specs=VMEM,
-        out_shape=jax.ShapeDtypeStruct((rows, depth), BF16),
+        in_specs=[ANY] + [VMEM] * 4 + [ANY] * 5,
+        out_specs=[VMEM] * 2,
+        out_shape=[
+            jax.ShapeDtypeStruct((rows, depth), BF16),
+            jax.ShapeDtypeStruct((rows, width), BF16),
+        ],
         scratch_shapes=[
-            pltpu.VMEM((2, rows, half), BF16),
-            pltpu.VMEM((2, 4 * inner, half), BF16),
-            pltpu.SemaphoreType.DMA((10,)),
+            pltpu.VMEM((rows, depth), BF16),
+            pltpu.VMEM((4 * inner, depth), BF16),
+            pltpu.VMEM((depth, width), BF16),
+            pltpu.VMEM((rows, depth), F32),
+            pltpu.SemaphoreType.DMA((6,)),
         ],
         compiler_params=pltpu.CompilerParams(vmem_limit_bytes=LIMIT),
         cost_estimate=pl.CostEstimate(
             flops=8 * rows * depth * inner, bytes_accessed=8 * depth * inner, transcendentals=0
         ),
         name="hidden_rows",
-    )(place, obs, *parts, *full, *halves)
-
-
-def embed_kernel(place_ref, h_ref, w0, w1, *refs):
-    far, (wkv_hbm, emb_ref, kv_ref, factor_ref, w_ref, wkv_ref, sems) = refs[:-7], refs[-7:]
-    chunks = len(far) // 4
-    cut, half = far[0].shape
-    rows = h_ref.shape[0]
-    width = wkv_hbm.shape[2]
-    starts = [pl.multiple_of((place_ref[0] ^ side) * half, half) for side in range(2)]
-    pairs, tiles = [], []
-    for code in range(4):
-        for side in range(2):
-            before = len(pairs)
-            target = w_ref.at[code * 2 + side]
-            if code < 2:
-                pairs.append(((w0, w1)[code].at[:, pl.ds(starts[side], half)], target))
-            else:
-                for c in range(chunks):
-                    source = far[((code - 2) * 2 + side) * chunks + c]
-                    pairs.append((source, target.at[c * cut : (c + 1) * cut]))
-            tiles.append((code, side, before, len(pairs)))
-    pairs += [(wkv_hbm.at[c], wkv_ref.at[:, c * width : (c + 1) * width]) for c in range(2)]
-    copies = start_copies(pairs, sems)
-    for code, side, first, last in tiles:
-        for copy in copies[first:last]:
-            copy.wait()
-        column = (place_ref[1] ^ code) * 2 * half + starts[side]
-        emb_ref[:, pl.ds(pl.multiple_of(column, half), half)] = dot(
-            h_ref[...], w_ref[code * 2 + side]
-        ).astype(BF16)
-    for copy in copies[-2:]:
+    )(obs, *parts, *weights, c_in)
+
+
+def join_kernel(place_ref, e0, e1, e2, e3, wkv_any, kv_ref, factor_ref, emb_ref, wkv_ref, sems):
+    rows, wide = emb_ref.shape
+    width = wkv_any.shape[2]
+    strip = e0.shape[1]
+    copies = start_copies(
+        [(wkv_any.at[c], wkv_ref.at[:, c * width : (c + 1) * width]) for c in range(2)], sems
+    )
+    starts = [pl.multiple_of((place_ref[1] ^ code) * strip, strip) for code in range(4)]
+    parts = (e0, e1, e2, e3)
+    for copy in copies:
         copy.wait()
     block = rows // 2
     for i in range(2):
         span = slice(i * block, (i + 1) * block)
-        emb = emb_ref[span, :]
-        factor = row_factor(emb.astype(F32))
-        both = dot(emb, wkv_ref[...]) * factor
+        square, both = 0.0, 0.0
+        for part, start in zip(parts, starts):
+            emb = part[span, :]
+            wide_emb = emb.astype(F32)
+            square = square + jnp.sum(wide_emb * wide_emb, axis=-1, keepdims=True)
+            both = both + dot(emb, wkv_ref[pl.ds(start, strip), :])
+            emb_ref[span, pl.ds(start, strip)] = emb
+        factor = lax.rsqrt(square / wide + epsilon)
+        both = both * factor
         kv_ref[0, span, :] = both[:, :width].astype(BF16)
         kv_ref[1, span, :] = both[:, width:].astype(BF16)
         factor_ref[span, :] = jnp.broadcast_to(factor, (block, HEAD))
 
 
-def embed_rows(place, hidden, full, far, w_keyval):
-    rows, depth = hidden.shape
-    half = far[0].shape[1]
-    wide = half * 8
+def join_rows(place, parts, w_keyval):
+    rows, strip = parts[0].shape
+    wide = 4 * strip
     width = w_keyval.shape[2]
     return pl.pallas_call(
-        embed_kernel,
-        in_specs=[SMEM, VMEM] + [HBM] * (3 + len(far)),
+        join_kernel,
+        in_specs=[SMEM] + [VMEM] * 4 + [ANY],
         out_specs=[VMEM] * 3,
         out_shape=[
-            jax.ShapeDtypeStruct((rows, wide), BF16),
             jax.ShapeDtypeStruct((2, rows, width), BF16),
             jax.ShapeDtypeStruct((rows, HEAD), F32),
-        ],
-        scratch_shapes=[
-            pltpu.VMEM((8, depth, half), BF16),
-            pltpu.VMEM((wide, 2 * width), BF16),
-            pltpu.SemaphoreType.DMA((6 + len(far),)),
-        ],
+            jax.ShapeDtypeStruct((rows, wide), BF16),
+        ],
+        scratch_shapes=[pltpu.VMEM((wide, 2 * width), BF16), pltpu.SemaphoreType.DMA((2,))],
         compiler_params=pltpu.CompilerParams(vmem_limit_bytes=LIMIT),
         cost_estimate=pl.CostEstimate(
-            flops=2 * rows * depth * wide, bytes_accessed=2 * depth * wide, transcendentals=0
-        ),
-        name="embed_rows",
-    )(place, hidden, *full, *far, w_keyval)
-
-
-def mixed_kernel(place_ref, emb_ref, t0, t1, t2, t3, wv_ref, ret_ref, *refs):
-    weights, (value_ref, other_ref, own_ref, mixed_ref, w_ref, sems) = refs[:-6], refs[-6:]
-    rows, wide = mixed_ref.shape
-    strips, _, strip = w_ref.shape
-    copies = []
-    for j in range(strips):
-        columns = slice(j * strip, (j + 1) * strip)
-        pairs = []
-        for i, weight in enumerate(weights):
-            height = weight.shape[0]
-            if i < 2:
-                top = i * height
-            else:
-                code, side, cut = 2 + (i - 2) // 4, (i - 2) // 2 % 2, (i - 2) % 2
-                top = (code * 2 + (place_ref[0] ^ side)) * 2 * height + cut * height
-                top = pl.multiple_of(top, height)
-            pairs.append((weight.at[:, columns], w_ref.at[j, pl.ds(top, height)]))
-        copies.append(start_copies(pairs, sems.at[j]))
-    for j in range(strips):
-        for copy in copies[j]:
-            copy.wait()
-        columns = slice(j * strip, (j + 1) * strip)
-        parts = jnp.concatenate([t0[...], t1[...], t2[...], t3[...]], axis=1)
-        mixed_ref[:, columns] = emb_ref[:, columns].astype(F32) + dot(parts, w_ref[j])
-
+            flops=4 * rows * wide * width, bytes_accessed=4 * rows * wide, transcendentals=0
+        ),
+        name="join_rows",
+    )(place, *parts, w_keyval)
+
+
+def part_kernel(
+    place_ref, att_ref, c_any, send_ref, keep_ref, their_ref, my_ref, c_ref, sems
+):
+    rows, inner = att_ref.shape
+    wide = c_ref.shape[1]
+    block = rows // 4
+    half = inner // 2
+    core = place_ref[1] % 2
+    copies = start_copies(
+        [
+            (c_any.at[i * half : (i + 1) * half], c_ref.at[i * half : (i + 1) * half])
+            for i in range(2)
+        ],
+        sems,
+    )
+    for out, side in ((their_ref, 1 - core), (my_ref, core)):
+        for i in range(2):
+            span = pl.ds(pl.multiple_of((side + 2 * i) * block, block), block)
+            out[i * block : (i + 1) * block, :] = att_ref[span, :]
+    for copy in copies:
+        copy.wait()
+    tile = 512
+    for out, source in ((send_ref, their_ref), (keep_ref, my_ref)):
+        for j in range(wide // tile):
+            columns = slice(j * tile, (j + 1) * tile)
+            out[:, columns] = dot(source[...], c_ref[:, columns]).astype(out.dtype)
+
+
+def part_rows(place, attended, c_out):
+    rows, inner = attended.shape
+    wide = c_out.shape[1]
+    return pl.pallas_call(
+        part_kernel,
+        in_specs=[SMEM, VMEM, ANY],
+        out_specs=[VMEM] * 4,
+        out_shape=[
+            jax.ShapeDtypeStruct((rows // 2, wide), BF16),
+            jax.ShapeDtypeStruct((rows // 2, wide), F32),
+            jax.ShapeDtypeStruct((rows // 2, inner), BF16),
+            jax.ShapeDtypeStruct((rows // 2, inner), BF16),
+        ],
+        scratch_shapes=[pltpu.VMEM((inner, wide), BF16), pltpu.SemaphoreType.DMA((2,))],
+        compiler_params=pltpu.CompilerParams(vmem_limit_bytes=LIMIT),
+        cost_estimate=pl.CostEstimate(
+            flops=2 * rows * wide * inner, bytes_accessed=8 * wide * inner, transcendentals=0
+        ),
+        name="part_rows",
+    )(place, attended, c_out)
+
+
+def mixed_kernel(
+    place_ref, emb_ref, mine_ref, got_ref, wv_ref, ret_ref, value_ref, other_ref, own_ref, mixed_ref
+):
+    rows, wide = mine_ref.shape
     half = wide // 2
+    piece = rows // 2
     block = 32
+    core = place_ref[1] % 2
     live_total = place_ref[4].astype(F32)
 
     @pl.loop(0, rows // block)
     def _(i):
         start = pl.multiple_of(i * block, block)
         span = pl.ds(start, block)
-        mixed = mixed_ref[span, :]
+        place = (core + start // piece * 2) * piece + start % piece
+        there = pl.ds(pl.multiple_of(place, block), block)
+        mixed = (
+            emb_ref[there, :].astype(F32)
+            + mine_ref[span, :].astype(F32)
+            + got_ref[span, :].astype(F32)
+        )
+        mixed_ref[...] = mixed
         factor = row_factor(mixed)
         value = factor * jnp.sum(mixed * wv_ref[...].astype(F32), axis=-1, keepdims=True)
-        row = place_ref[2] + start + lax.broadcasted_iota(jnp.int32, (block, 1), 0)
-        gap = jnp.where(row < place_ref[3], value - ret_ref[span, :], F32(0.0)) / live_total
+        row = place_ref[2] + place + lax.broadcasted_iota(jnp.int32, (block, 1), 0)
+        gap = jnp.where(row < place_ref[3], value - ret_ref[there, :], F32(0.0)) / live_total
         lead = factor * gap
         pull = lead * factor * value / wide
         value_ref[span, :] = jnp.broadcast_to(value, (block, HEAD))
         for out, side in ((own_ref, place_ref[0]), (other_ref, 1 - place_ref[0])):
             columns = pl.ds(pl.multiple_of(side * half, half), half)
-            part = mixed_ref[span, columns]
+            part = mixed_ref[:, columns]
             out[span, :] = (lead * wv_ref[:, columns].astype(F32) - part * pull).astype(BF16)
 
 
-def mixed_rows(place, embedded, parts, weights, w_value, returns):
-    rows, wide = embedded.shape
-    depth = sum(weight.shape[0] for weight in weights)
+def mixed_rows(place, embedded, mine, got, w_value, returns):
+    rows, wide = mine.shape
     return pl.pallas_call(
         mixed_kernel,
-        in_specs=[SMEM] + [VMEM] * 7 + [HBM] * len(weights),
+        in_specs=[SMEM] + [VMEM] * 5,
         out_specs=[VMEM] * 3,
         out_shape=[
             jax.ShapeDtypeStruct((rows, HEAD), F32),
             jax.ShapeDtypeStruct((rows, wide // 2), BF16),
             jax.ShapeDtypeStruct((rows, wide // 2), BF16),
         ],
-        scratch_shapes=[
-            pltpu.VMEM((rows, wide), F32),
-            pltpu.VMEM((8, depth, wide // 8), BF16),
-            pltpu.SemaphoreType.DMA((8, len(weights))),
-        ],
+        scratch_shapes=[pltpu.VMEM((32, wide), F32)],
         compiler_params=pltpu.CompilerParams(vmem_limit_bytes=LIMIT),
         cost_estimate=pl.CostEstimate(
-            flops=2 * rows * wide * depth, bytes_accessed=2 * wide * depth, transcendentals=0
+            flops=10 * rows * wide, bytes_accessed=12 * rows * wide, transcendentals=0
         ),
         name="mixed_rows",
-    )(
-        place, embedded, *parts, w_value.reshape(1, wide), returns.reshape(rows, 1), *weights
-    )
+    )(place, embedded, mine, got, w_value.reshape(1, wide), returns.reshape(-1, 1))
 
 
 def gather_codes(size):
@@ -427,39 +448,39 @@
     )(index, own, got)
 
 
-def assemble_kernel(codes, chunks, place_ref, *refs):
-    parts = refs[: len(codes) * 2 * chunks]
-    out, got_ref, wide_ref, got_sems, sems = refs[len(parts) :]
+def assemble_kernel(codes, chunk, chunks, place_ref, *refs):
+    parts = refs[: len(codes) * 2]
+    out, got_ref, wide_ref, got_sems, sems = refs[-5:]
     block, strip = parts[0].shape
     got = start_copies([(part, got_ref.at[i]) for i, part in enumerate(parts)], got_sems)
     copies = []
-    for c in range(chunks):
-        for side in range(2):
-            for k, code in enumerate(codes):
-                at = (c * 2 + side) * len(codes) + k
-                row = pl.multiple_of((place_ref[5] ^ code) * block, block)
-                column = pl.multiple_of(((place_ref[0] ^ side) * chunks + c) * strip, strip)
-                got[at].wait()
-                wide_ref[at] = got_ref[at].astype(F32)
-                copy = pltpu.make_async_copy(
-                    wide_ref.at[at],
-                    out.at[pl.ds(row, block), pl.ds(column, strip)],
-                    sems.at[at],
-                )
-                copy.start()
-                copies.append(copy)
+    for side in range(2):
+        for k, code in enumerate(codes):
+            at = side * len(codes) + k
+            row = pl.multiple_of((place_ref[5] ^ code) * block, block)
+            column = pl.multiple_of(((place_ref[0] ^ side) * chunks + chunk) * strip, strip)
+            got[at].wait()
+            wide_ref[at] = got_ref[at].astype(F32)
+            copy = pltpu.make_async_copy(
+                wide_ref.at[at],
+                out.at[pl.ds(row, block), pl.ds(column, strip)],
+                sems.at[at],
+            )
+            copy.start()
+            copies.append(copy)
     for copy in copies:
         copy.wait()
 
 
-def assemble(place, parts, count, chunks):
+def assemble(place, parts, count, chunk, chunks, before):
     block, strip = parts[0].shape
     rows, wide = block * count, strip * 2 * chunks
     return pl.pallas_call(
-        functools.partial(assemble_kernel, gather_codes(count), chunks),
-        in_specs=[SMEM] + [HBM] * len(parts),
-        out_specs=pl.BlockSpec(memory_space=pl.ANY),
+        functools.partial(assemble_kernel, gather_codes(count), chunk, chunks),
+        in_specs=[SMEM] + [ANY] * (len(parts) + len(before)),
+        out_specs=ANY,
         out_shape=jax.ShapeDtypeStruct((rows, wide), F32),
+        input_output_aliases={1 + len(parts): 0} if before else {},
         scratch_shapes=[
             pltpu.VMEM((len(parts), block, strip), BF16),
             pltpu.VMEM((len(parts), block, strip), F32),
@@ -471,7 +492,7 @@
             flops=rows * wide, bytes_accessed=6 * rows * wide, transcendentals=0
         ),
         name="assemble",
-    )(place, *parts)
+    )(place, *parts, *before)
 
 
 def swap(block, axis, bit):
@@ -500,11 +521,6 @@
     total = keep + got.astype(F32)
     side = total.shape[0] // 2
     return total[:side], total[side:].astype(BF16)
-
-
-def half_of(weight, side):
-    half = weight.shape[1] // 2
-    return lax.dynamic_slice_in_dim(weight, side * half, half, 1)
 
 
 def on_device(
@@ -536,8 +552,7 @@
     mdl_count = lax.axis_size("mdl")
     assert mdl_count == 4 and lax.axis_size("sec") == 2
     mdl_index = lax.axis_index("mdl")
-    part_rows = row_count // mdl_count
-    row_start = mdl_index * part_rows
+    value_rows = row_count // mdl_count
     score_scale = HEAD ** (-0.5) * LOG2E
     rep_place = rep_index.reshape(1).astype(jnp.int32)
 
@@ -553,40 +568,23 @@
     keyval, factor_a = first_projection(obs_in, a_keyval)
     pieces_k = gather_blocks(keyval, "rep")
 
-    a_near = swap(a_out, "mdl", 1)
-    c_near = swap(c_in, "mdl", 1)
-    a_far0 = swap(half_of(a_out, batch_index), "mdl", 2)
-    c_half = half_of(c_in, batch_index)
-    c_cut = c_half.shape[0] // 2
-    c_a0 = swap(c_half[:c_cut], "mdl", 2)
-    c_b0 = swap(c_half[c_cut:], "mdl", 2)
-
+    a_far = swap(a_out, "mdl", 2)
     queries = (dot(obs_in, a_query) * (factor_a[:, :1] * score_scale)).astype(BF16)
-    queries, a_far0 = tied(queries, a_far0)
-    a_far1 = swap(a_far0, "sec", 1)
     state = attend_call(queries, pieces_k[:-1], 0, place, [])
-    *state, c_a0 = tied(*state, c_a0)
-    c_a1 = swap(c_a0, "sec", 1)
-    *state, c_b0, a_far1 = tied(*state, c_b0, a_far1)
-    c_b1 = swap(c_b0, "sec", 1)
     attended = attend_call(queries, pieces_k[-1:], rep_count - 1, place, state)
+    attended, a_far = tied(attended, a_far)
     attended_far = swap(attended, "mdl", 2)
-    attended, attended_far, c_a1 = tied(attended, attended_far, c_a1)
-    attended_near = swap(attended, "mdl", 1)
-    attended_parts = [attended, attended_near, attended_far, swap(attended_far, "mdl", 1)]
-    a_halves = [a_far0, a_far1, swap(a_far0, "mdl", 1), swap(a_far1, "mdl", 1)]
-    hidden = hidden_rows(place, obs_in, attended_parts, [a_out, a_near], a_halves)
-    c_far = [c_a0, c_b0, c_a1, c_b1]
-    c_far = c_far + [swap(item, "mdl", 1) for item in c_far]
-
-    out_half = c_out.shape[0] // 2
-    out_cut = out_half // 2
-    out_src = lax.dynamic_slice_in_dim(c_out, batch_index * out_half, out_half, 0)
-    attended_far, out_src = tied(attended_far, out_src)
-    out_a0 = swap(out_src[:out_cut], "mdl", 2)
-    out_b0 = swap(out_src[out_cut:], "mdl", 2)
-
-    embedded, critic_keyval, factor_c = embed_rows(place, hidden, [c_in, c_near], c_far, c_keyval)
+    a_all = [a_out, swap(a_out, "mdl", 1), a_far, swap(a_far, "mdl", 1)]
+    attended_parts = [
+        attended,
+        swap(attended, "mdl", 1),
+        attended_far,
+        swap(attended_far, "mdl", 1),
+    ]
+    hidden, embed_part = hidden_rows(obs_in, attended_parts, a_all, c_in)
+
+    embed_parts, _ = gather_parts(embed_part)
+    critic_keyval, factor_c, embedded = join_rows(place, embed_parts, c_keyval)
     pieces_c = gather_blocks(critic_keyval, "rep")
     critic_queries = (dot(embedded, c_query) * (factor_c[:, :1] * score_scale)).astype(BF16)
 
@@ -616,50 +614,45 @@
     )
     own_a = product(attended, lax.dynamic_slice_in_dim(dhidden, batch_index * half_a, half_a, 1))
 
-    critic_queries, out_a0 = tied(critic_queries, out_a0)
-    out_a1 = swap(out_a0, "sec", 1)
     state_c = attend_call(critic_queries, pieces_c[:-1], 0, place, [])
-    *state_c, got_a, pieces_c[-1], out_b0 = tied(*state_c, got_a, pieces_c[-1], out_b0)
-    out_b1 = swap(out_b0, "sec", 1)
+    *state_c, got_a, pieces_c[-1] = tied(*state_c, got_a, pieces_c[-1])
     keep_a, send_a = split_sum(rep_place, own_a, got_a, rep_count)
     moved_a = swap(send_a.astype(BF16), "rep", 1)
     critic_attended = attend_call(critic_queries, pieces_c[-1:], rep_count - 1, place, state_c)
-    critic_attended, moved_a = tied(critic_attended, moved_a)
-    critic_far = swap(critic_attended, "mdl", 2)
-    critic_near = swap(critic_attended, "mdl", 1)
+
+    send_m, keep_m, their_att, my_att = part_rows(place, critic_attended, c_out)
+    got_m = swap(send_m, "mdl", 1)
+    got_m, moved_a = tied(got_m, moved_a)
+    mine_m = (keep_m + got_m.astype(F32)).astype(BF16)
     bit = 2
     while bit < rep_count:
         keep_a, send_a = halve(keep_a, moved_a)
         moved_a = swap(send_a, "rep", bit)
         bit *= 2
-    critic_near, out_a1, moved_a = tied(critic_near, out_a1, moved_a)
+    theirs_m = swap(mine_m, "mdl", 2)
     mine_a = gather_blocks((keep_a + moved_a.astype(F32)).astype(BF16), "rep")
-    critic_parts = [critic_attended, critic_near, critic_far, swap(critic_far, "mdl", 1)]
-    out_far = [out_a0, out_b0, out_a1, out_b1]
-    c_out_all = [c_out, swap(c_out, "mdl", 1)] + out_far
-    c_out_all += [swap(item, "mdl", 1) for item in out_far]
+    theirs_a = [swap(block, "sec", 1) for block in mine_a]
+    theirs_m, *theirs_a[:-1] = tied(theirs_m, *theirs_a[:-1])
     value_wide, d_other, d_own = mixed_rows(
-        place, embedded, critic_parts, c_out_all, w_value, returns[0]
+        place, embedded, mine_m, theirs_m, w_value, returns[0]
     )
-    theirs_a = [swap(block, "sec", 1) for block in mine_a]
-    d_other, *theirs_a[:-1] = tied(d_other, *theirs_a[:-1])
-    pieces_a = mine_a + theirs_a
+    e_other = swap(d_other, "mdl", 1)
+    e_own = swap(d_own, "mdl", 1)
 
     strip = d_own.shape[1] // CHUNKS
     spans = [slice(c * strip, (c + 1) * strip) for c in range(CHUNKS)]
-    got = [
-        swap(product(critic_attended, d_other[:, span]).astype(BF16), "sec", 1) for span in spans
-    ]
-    own = [product(critic_attended, d_own[:, span]) for span in spans]
-    value_part = lax.dynamic_slice_in_dim(value_wide, row_start, part_rows, 0)[:, 0]
+
+    def both(mine, other, span):
+        return product(my_att, mine[:, span]) + product(their_att, other[:, span])
+
+    got = [swap(both(d_other, e_other, span).astype(BF16), "sec", 1) for span in spans]
+    own = [both(d_own, e_own, span) for span in spans]
+    value_part = lax.dynamic_slice_in_dim(value_wide, mdl_index // 2 * value_rows, value_rows, 0)[:, 0]
     got[0], value_part = tied(got[0], value_part)
-    actor_summed = assemble(place, pieces_a, rep_count, 1)
-    got[1], actor_summed = tied(got[1], actor_summed)
-    pieces, marks = [], []
+    actor_summed = assemble(place, mine_a + theirs_a, rep_count, 0, 1, [])
+    marks, result = [], []
     for c in range(CHUNKS):
         arrived = got[c]
-        if c > 0:
-            arrived, _ = tied(arrived, marks[0])
         keep, send = split_sum(rep_place, own[c], arrived, rep_count)
         bit, trail = 1, []
         while bit < rep_count:
@@ -667,6 +660,8 @@
             bit *= 2
             if c > 0:
                 arrived, _ = tied(arrived, marks[min(len(trail) + 1, len(marks) - 1)])
+            elif not trail:
+                arrived, actor_summed, *got[1:] = tied(arrived, actor_summed, *got[1:])
             if bit < rep_count:
                 keep, send = halve(keep, arrived)
                 trail.append(keep)
@@ -675,10 +670,10 @@
         mine = gather_blocks(total, "rep")
         trail.append(mine[1])
         marks = trail
-        pieces += mine + [swap(block, "sec", 1) for block in mine]
-    critic_summed = assemble(place, pieces, rep_count, CHUNKS)
-
-    return (value_part[None, :], actor_summed, critic_summed)
+        theirs = [swap(block, "sec", 1) for block in mine]
+        result = [assemble(place, mine + theirs, rep_count, c, CHUNKS, result)]
+
+    return (value_part[None, :], actor_summed, result[0])
 
 
 def solution(mesh):

time: 269 us -> 235 us (0.87)
  Pallas kernels: 59.1 us -> 40.6 us
  starting transfers between devices: 61.9 us -> 47.6 us
  local copies, waits for them, and re-layouts: 24.2 us -> 13.5 us
  waiting for transfers between devices: 104 us -> 113 us
    pallas_call x4 -> x5, Pallas kernels: 35.8 us -> 16.7 us  [the longest x1 6.38 us: hidden_rows(): pl.pallas_call(hidden_kernel, in_specs=[ANY] + [VMEM] * 4 + [ANY] * 5, ou...]
    ppermute x65 -> x49, starting transfers between devices: 61.9 us -> 47.6 us  [swap(): return lax.ppermute(block, axis, [(i, i ^ bit) for i in range(size)])]
    ppermute x65 -> x49, waiting for transfers between devices: 104 us -> 113 us  [swap(): return lax.ppermute(block, axis, [(i, i ^ bit) for i in range(size)])]
    unnamed x82 -> x54, local copies, waits for them, and re-layouts: 15 us -> 8.06 us
    dynamic_slice x2 -> x0, local copies, waits for them, and re-layouts: 3.49 us -> none  [the longest x1 2.08 us: half_of(): return lax.dynamic_slice_in_dim(weight, side * half, half, 1)]
    slice x3 -> x1, local copies, waits for them, and re-layouts: 3.64 us -> 0.63 us  [on_device(): lax.dynamic_slice_in_dim(value_wide, mdl_index // 2 * value_rows, value_r...]
    pallas_call x2 -> x3, Pallas kernels: 9.18 us -> 9.84 us  [assemble(): pl.pallas_call(functools.partial(assemble_kernel, gather_codes(count), ch...]
  transfers between devices with their start and end apart: 65 -> 49, of which waited for: 29 -> 24; matrix products, arithmetic and copies ran while one was open for 7% -> 8% of each run, Pallas kernels for 20% -> 10%
where the time goes in v5:
time: 235 us; the launch traced here: 234 us
  waiting for transfers between devices  113 us (48%)
  starting transfers between devices  47.6 us (20%)
  Pallas kernels  40.6 us (17%)
  local copies, waits for them, and re-layouts  13.5 us (6%)
  matrix products  10.4 us (4%)
  between operations  4.5 us (2%)
  other arithmetic  4.03 us (2%)
    ppermute x49, waiting for transfers between devices, swap(): return lax.ppermute(block, axis, [(i, i ^ bit) for i in range(size)])  113 us
    ppermute x49, starting transfers between devices, swap(): return lax.ppermute(block, axis, [(i, i ^ bit) for i in range(size)])  47.6 us
    pallas_call x4, Pallas kernels, attend_call(): pl.pallas_call(functools.partial(body, groups, units, TABLE + first), in_...  13.7 us
    pallas_call x3, Pallas kernels, assemble(): pl.pallas_call(functools.partial(assemble_kernel, gather_codes(count), ch...  9.84 us
    unnamed x54, local copies, waits for them, and re-layouts  8.06 us
    pallas_call x1, Pallas kernels, hidden_rows(): pl.pallas_call(hidden_kernel, in_specs=[ANY] + [VMEM] * 4 + [ANY] * 5, ou...  6.38 us
    dot_general x4, matrix products, dot(): return jnp.dot(a, b, preferred_element_type=F32)  5.47 us
    dot_general x10, matrix products, product(): return jnp.einsum('rh,rd->hd', left, right, preferred_element_type=F32)  4.89 us
  transfers between devices with their start and end apart: 49, of which 24 were waited for; matrix products, arithmetic and copies ran while one was open for 8% of the time, Pallas kernels for 10%

profile of v5, /device:TPU:0, one launch (start us, length us, event | category | flops | bytes accessed | tf_op | source)
XLA Modules:
  0.0 233.9 jit_solution(7595510514791074054)
XLA Ops:
  20.1 3.5 %collective-permute-done.refs_1_ = bf16[2,512,128]{2,1,0:T(8,128)(2,1)S(1)} collective-permute-done((bf16[2,512,128]{2,1,0:T(8,128)(2,1)S(1)}, bf16[2,512,128]{2,1,0:T(8,128)(2,1)S(1)}, u32[]{:S(2)}, u32[]{:S(2)}) %collective-permute-start) | collective-permute-done | bytes 262176 | tf_op jit(solution)/shard_map/ppermute | solution.py:500
  24.0 3.5 %attend_open.2 = (f32[512,768]{1,0:T(8,128)S(1)}, f32[512,384]{1,0:T(8,128)S(1)}) custom-call(s32[10]{0:T(128)S(1)} %stack.39.left_ref.place_ref, bf16[512,384]{1,0:T(8,128)(2,1)S(1)} %fusion.6.q_ref, bf16[2,512,128]{2,1,0:T(8,128)(2,1)S(1)} %get-tuple-element.48.refs_0_, bf16[2,512,128]{2,1,0:T(8,128)(2,1)S(1)} %collective-permute-done.refs_1_, ...), custom_call_target="tpu_custom_call" | custom-call | flops 7247757312 | bytes 786432 | tf_op jit(solution)/shard_map/attend_open/pallas_call | solution.py:189
  33.4 10.7 %collective-permute-done.5.t2 = bf16[512,384]{1,0:T(8,128)(2,1)S(1)} collective-permute-done((bf16[512,384]{1,0:T(8,128)(2,1)S(1)}, bf16[512,384]{1,0:T(8,128)(2,1)S(1)}, u32[]{:S(2)}, u32[]{:S(2)}) %collective-permute-start.5) | collective-permute-done | bytes 393248 | tf_op jit(solution)/shard_map/ppermute | solution.py:500
  45.8 6.4 %hidden_rows.1 = (bf16[512,1536]{1,0:T(8,128)(2,1)S(1)}, bf16[512,512]{1,0:T(8,128)(2,1)}) custom-call(bf16[512,1536]{1,0:T(8,128)(2,1)S(1)} %bitcast.35, bf16[512,384]{1,0:T(8,128)(2,1)S(1)} %attend_close.2.t0, bf16[512,384]{1,0:T(8,128)(2,1)S(1)} %collective-permute-done.4.t1, bf16[512,384]{1,0:T(8,128)(2,1)S(1)} %collective-permute-done.5.t2, ...), custom_call_target="tpu_custom_call" | custom-call | flops 2415919104 | bytes 4718592 | tf_op jit(solution)/shard_map/hidden_rows/pallas_call | solution.py:234
  53.9 13.7 %collective-permute-done.10.e2 = bf16[512,512]{1,0:T(8,128)(2,1)} collective-permute-done((bf16[512,512]{1,0:T(8,128)(2,1)}, bf16[512,512]{1,0:T(8,128)(2,1)}, u32[]{:S(2)}, u32[]{:S(2)}) %collective-permute-start.10) | collective-permute-done | bytes 524320 | tf_op jit(solution)/shard_map/ppermute | solution.py:500
  82.1 6.0 %collective-permute-done.12.refs_1_ = bf16[2,512,128]{2,1,0:T(8,128)(2,1)S(1)} collective-permute-done((bf16[2,512,128]{2,1,0:T(8,128)(2,1)S(1)}, bf16[2,512,128]{2,1,0:T(8,128)(2,1)S(1)}, u32[]{:S(2)}, u32[]{:S(2)}) %collective-permute-start.12) | collective-permute-done | bytes 262176 | tf_op jit(solution)/shard_map/ppermute | solution.py:500
  88.2 4.5 %attend_open.3 = (f32[512,1024]{1,0:T(8,128)S(1)}, f32[512,512]{1,0:T(8,128)S(1)}) custom-call(s32[10]{0:T(128)S(1)} %stack.39.left_ref.place_ref, bf16[512,512]{1,0:T(8,128)(2,1)S(1)} %fusion.5.q_ref, bf16[2,512,128]{2,1,0:T(8,128)(2,1)S(1)} %get-tuple-element.56.refs_0_, bf16[2,512,128]{2,1,0:T(8,128)(2,1)S(1)} %collective-permute-done.12.refs_1_, ...), custom_call_target="tpu_custom_call" | custom-call | flops 9663676416 | bytes 1048576 | tf_op jit(solution)/shard_map/attend_open/pallas_call | solution.py:189
  94.5 3.2 %attend_close.3.att_ref = bf16[512,512]{1,0:T(8,128)(2,1)S(1)} custom-call(s32[10]{0:T(128)S(1)} %stack.39.left_ref.place_ref, bf16[512,512]{1,0:T(8,128)(2,1)S(1)} %fusion.5.q_ref, f32[512,1024]{1,0:T(8,128)S(1)} %get-tuple-element.61.wide_ref, f32[512,512]{1,0:T(8,128)S(1)} %get-tuple-element.62.top_ref, ...), custom_call_target="tpu_custom_call" | custom-call | flops 134217728 | bytes 1048576 | tf_op jit(solution)/shard_map/attend_close/pallas_call | solution.py:189
  105.6 8.0 %collective-permute-done.17 = bf16[192,768]{1,0:T(8,128)(2,1)S(1)} collective-permute-done((bf16[192,768]{1,0:T(8,128)(2,1)S(1)}, bf16[192,768]{1,0:T(8,128)(2,1)S(1)}, u32[]{:S(2)}, u32[]{:S(2)}) %collective-permute-start.17) | collective-permute-done | bytes 294944 | tf_op jit(solution)/shard_map/ppermute | solution.py:500
  117.4 7.6 %collective-permute-done.19 = bf16[96,768]{1,0:T(8,128)(2,1)S(1)} collective-permute-done((bf16[96,768]{1,0:T(8,128)(2,1)S(1)}, bf16[96,768]{1,0:T(8,128)(2,1)S(1)}, u32[]{:S(2)}, u32[]{:S(2)}) %collective-permute-start.19) | collective-permute-done | bytes 147488 | tf_op jit(solution)/shard_map/ppermute | solution.py:500
  125.2 3.4 %collective-permute-start.23 = (bf16[96,768]{1,0:T(8,128)(2,1)S(1)}, bf16[96,768]{1,0:T(8,128)(2,1)}, u32[]{:S(2)}, u32[]{:S(2)}) collective-permute-start(bf16[96,768]{1,0:T(8,128)(2,1)S(1)} %fusion.10.refs_0_), channel_id=1, source_target_pairs={{0,8},{8,0},{16,24},{24,16},{1,9},{9,1},{17,25},{25,17},{2,10},{10... | collective-permute-start | bytes 442376 | tf_op jit(solution)/shard_map/ppermute | solution.py:500
  128.5 5.9 %collective-permute-done.21.refs_1_ = bf16[96,768]{1,0:T(8,128)(2,1)} collective-permute-done((bf16[96,768]{1,0:T(8,128)(2,1)S(1)}, bf16[96,768]{1,0:T(8,128)(2,1)}, u32[]{:S(2)}, u32[]{:S(2)}) %collective-permute-start.21) | collective-permute-done | bytes 147488 | tf_op jit(solution)/shard_map/ppermute | solution.py:500
  141.4 3.1 %collective-permute-done.24.refs_6_ = bf16[96,768]{1,0:T(8,128)(2,1)} collective-permute-done((bf16[96,768]{1,0:T(8,128)(2,1)}, bf16[96,768]{1,0:T(8,128)(2,1)}, u32[]{:S(2)}, u32[]{:S(2)}) %collective-permute-start.24) | collective-permute-done | bytes 147488 | tf_op jit(solution)/shard_map/ppermute | solution.py:500
  149.4 3.6 %mixed_rows.1 = (f32[256,128]{1,0:T(8,128)S(1)}, bf16[256,1024]{1,0:T(8,128)(2,1)S(1)}, bf16[256,1024]{1,0:T(8,128)(2,1)S(1)}) custom-call(s32[10]{0:T(128)S(1)} %copy-done.18, bf16[512,2048]{1,0:T(8,128)(2,1)S(1)} %copy-done.9, bf16[256,2048]{1,0:T(8,128)(2,1)S(1)} %add_convert_fusion.mine_ref, bf16[256,2048]{1,0:T(8,128)(2,1)} %collective-permute-done.18.got_ref, ...), custom_call_target="tpu_custom_call" | custom-call | flops 5242880 | bytes 6291456 | tf_op jit(solution)/shard_map/mixed_rows/pallas_call | solution.py:394
  154.6 3.1 %assemble.3 = f32[384,1536]{1,0:T(8,128)} custom-call(s32[10]{0:T(128)S(1)} %copy-done.18, bf16[96,768]{1,0:T(8,128)(2,1)S(1)} %fusion.10.refs_0_, bf16[96,768]{1,0:T(8,128)(2,1)} %collective-permute-done.21.refs_1_, bf16[96,768]{1,0:T(8,128)(2,1)} %collective-permute-done.23.refs_2_, bf16[96,768]{1,0:T(8,128)(2,1)} %collective-permute-done.29.refs_3_, ...), custom_call_target="tpu_custom_call" | custom-call | flops 589824 | bytes 3538944 | tf_op jit(solution)/shard_map/assemble/pallas_call | solution.py:478
  161.5 12.0 %collective-permute-done.26.got_ref = bf16[512,512]{1,0:T(8,128)(2,1)S(1)} collective-permute-done((bf16[512,512]{1,0:T(8,128)(2,1)S(1)}, bf16[512,512]{1,0:T(8,128)(2,1)S(1)}, u32[]{:S(2)}, u32[]{:S(2)}) %collective-permute-start.26) | collective-permute-done | bytes 524320 | tf_op jit(solution)/shard_map/ppermute | solution.py:500
  175.8 8.1 %collective-permute-done.31.got_ref = bf16[512,512]{1,0:T(8,128)(2,1)S(1)} collective-permute-done((bf16[512,512]{1,0:T(8,128)(2,1)S(1)}, bf16[512,512]{1,0:T(8,128)(2,1)S(1)}, u32[]{:S(2)}, u32[]{:S(2)}) %collective-permute-start.31) | collective-permute-done | bytes 524320 | tf_op jit(solution)/shard_map/ppermute | solution.py:500
  186.9 5.4 %collective-permute-done.33 = bf16[128,512]{1,0:T(8,128)(2,1)S(1)} collective-permute-done((bf16[128,512]{1,0:T(8,128)(2,1)S(1)}, bf16[128,512]{1,0:T(8,128)(2,1)S(1)}, u32[]{:S(2)}, u32[]{:S(2)}) %collective-permute-start.33) | collective-permute-done | bytes 131104 | tf_op jit(solution)/shard_map/ppermute | solution.py:500
  193.8 3.3 %collective-permute-done.32 = bf16[256,512]{1,0:T(8,128)(2,1)S(1)} collective-permute-done((bf16[256,512]{1,0:T(8,128)(2,1)S(1)}, bf16[256,512]{1,0:T(8,128)(2,1)S(1)}, u32[]{:S(2)}, u32[]{:S(2)}) %collective-permute-start.32) | collective-permute-done | bytes 262176 | tf_op jit(solution)/shard_map/ppermute | solution.py:500
  202.0 3.7 %collective-permute-done.34 = bf16[128,512]{1,0:T(8,128)(2,1)S(1)} collective-permute-done((bf16[128,512]{1,0:T(8,128)(2,1)S(1)}, bf16[128,512]{1,0:T(8,128)(2,1)S(1)}, u32[]{:S(2)}, u32[]{:S(2)}) %collective-permute-start.34) | collective-permute-done | bytes 131104 | tf_op jit(solution)/shard_map/ppermute | solution.py:500
  210.3 3.5 %collective-permute-done.36.refs_1_ = bf16[128,512]{1,0:T(8,128)(2,1)S(1)} collective-permute-done((bf16[128,512]{1,0:T(8,128)(2,1)S(1)}, bf16[128,512]{1,0:T(8,128)(2,1)S(1)}, u32[]{:S(2)}, u32[]{:S(2)}) %collective-permute-start.36) | collective-permute-done | bytes 131104 | tf_op jit(solution)/shard_map/ppermute | solution.py:500
  221.1 3.4 %assemble.4.refs_8_ = f32[512,2048]{1,0:T(8,128)} custom-call(s32[10]{0:T(128)S(1)} %copy-done.19, bf16[128,512]{1,0:T(8,128)(2,1)S(1)} %fusion.12.refs_0_, bf16[128,512]{1,0:T(8,128)(2,1)S(1)} %collective-permute-done.35.refs_1_, bf16[128,512]{1,0:T(8,128)(2,1)S(1)} %collective-permute-done.43.refs_2_, ...), custom_call_target="tpu_custom_call" | custom-call | flops 1048576 | bytes 6291456 | tf_op jit(solution)/shard_map/assemble/pallas_call | solution.py:478
  224.5 4.5 %collective-permute-done.41.refs_6_ = bf16[128,512]{1,0:T(8,128)(2,1)S(1)} collective-permute-done((bf16[128,512]{1,0:T(8,128)(2,1)S(1)}, bf16[128,512]{1,0:T(8,128)(2,1)S(1)}, u32[]{:S(2)}, u32[]{:S(2)}) %collective-permute-start.41) | collective-permute-done | bytes 131104 | tf_op jit(solution)/shard_map/ppermute | solution.py:500
  230.4 3.4 %assemble.5 = f32[512,2048]{1,0:T(8,128)} custom-call(s32[10]{0:T(128)S(1)} %copy-done.19, bf16[128,512]{1,0:T(8,128)(2,1)S(1)} %fusion.11.refs_0_, bf16[128,512]{1,0:T(8,128)(2,1)S(1)} %collective-permute-done.36.refs_1_, bf16[128,512]{1,0:T(8,128)(2,1)S(1)} %collective-permute-done.37.refs_2_, ...), custom_call_target="tpu_custom_call", output_to_operand_aliasing={{}: (9, {})} | custom-call | flops 1048576 | bytes 6291456 | tf_op jit(solution)/shard_map/assemble/pallas_call | solution.py:478
  (183 shorter events, 96.0 us)
Async XLA Ops:
  0.7 31.8 %collective-permute-start.3 = (bf16[384,1536]{1,0:T(8,128)(2,1)}, bf16[384,1536]{1,0:T(8,128)(2,1)}, u32[]{:S(2)}, u32[]{:S(2)}) collective-permute-start(bf16[384,1536]{1,0:T(8,128)(2,1)} %w0.1), channel_id=1, source_target_pairs={{0,2},{1,3},{2,0},{3,1},{4,6},{5,7},{6,4},{7,5},{8,10},{9,11},{10,... | collective-permute-start | bytes 3538952 | tf_op jit(solution)/shard_map/ppermute | solution.py:500
  7.9 16.1 %collective-permute-start.1 = (bf16[2,512,128]{2,1,0:T(8,128)(2,1)S(1)}, bf16[2,512,128]{2,1,0:T(8,128)(2,1)S(1)}, u32[]{:S(2)}, u32[]{:S(2)}) collective-permute-start(bf16[2,512,128]{2,1,0:T(8,128)(2,1)S(1)} %get-tuple-element.48.refs_0_), channel_id=1, source_target_pairs={{0,8},{8,0},{16,24},{24,16},{1,9},{9,1},{17,25},{25,17},{2,10},{10... | collective-permute-start | bytes 786440 | tf_op jit(solution)/shard_map/ppermute | solution.py:500
  9.5 14.1 %collective-permute-start = (bf16[2,512,128]{2,1,0:T(8,128)(2,1)S(1)}, bf16[2,512,128]{2,1,0:T(8,128)(2,1)S(1)}, u32[]{:S(2)}, u32[]{:S(2)}) collective-permute-start(bf16[2,512,128]{2,1,0:T(8,128)(2,1)S(1)} %get-tuple-element.48.refs_0_), channel_id=1, source_target_pairs={{0,16},{8,24},{16,0},{24,8},{1,17},{9,25},{17,1},{25,9},{2,18},{10... | collective-permute-start | bytes 786440 | tf_op jit(solution)/shard_map/ppermute | solution.py:500
  12.1 32.0 %collective-permute-start.7 = (bf16[384,1536]{1,0:T(8,128)(2,1)}, bf16[384,1536]{1,0:T(8,128)(2,1)}, u32[]{:S(2)}, u32[]{:S(2)}) collective-permute-start(bf16[384,1536]{1,0:T(8,128)(2,1)} %w0.1), channel_id=1, source_target_pairs={{0,1},{1,0},{2,3},{3,2},{4,5},{5,4},{6,7},{7,6},{8,9},{9,8},{10,11... | collective-permute-start | bytes 3538952 | tf_op jit(solution)/shard_map/ppermute | solution.py:500
  32.4 13.3 %collective-permute-start.8 = (bf16[384,1536]{1,0:T(8,128)(2,1)}, bf16[384,1536]{1,0:T(8,128)(2,1)S(1)}, u32[]{:S(2)}, u32[]{:S(2)}) collective-permute-start(bf16[384,1536]{1,0:T(8,128)(2,1)} %collective-permute-done.3.w2), channel_id=1, source_target_pairs={{0,1},{1,0},{2,3},{3,2},{4,5},{5,4},{6,7},{7,6},{8,9},{9,8},{10,11... | collective-permute-start | bytes 3538952 | tf_op jit(solution)/shard_map/ppermute | solution.py:500
  32.5 11.5 %collective-permute-start.5 = (bf16[512,384]{1,0:T(8,128)(2,1)S(1)}, bf16[512,384]{1,0:T(8,128)(2,1)S(1)}, u32[]{:S(2)}, u32[]{:S(2)}) collective-permute-start(bf16[512,384]{1,0:T(8,128)(2,1)S(1)} %attend_close.2.t0), channel_id=1, source_target_pairs={{0,2},{1,3},{2,0},{3,1},{4,6},{5,7},{6,4},{7,5},{8,10},{9,11},{10,... | collective-permute-start | bytes 1179656 | tf_op jit(solution)/shard_map/ppermute | solution.py:500
  33.2 10.9 %collective-permute-start.4 = (bf16[512,384]{1,0:T(8,128)(2,1)S(1)}, bf16[512,384]{1,0:T(8,128)(2,1)S(1)}, u32[]{:S(2)}, u32[]{:S(2)}) collective-permute-start(bf16[512,384]{1,0:T(8,128)(2,1)S(1)} %attend_close.2.t0), channel_id=1, source_target_pairs={{0,1},{1,0},{2,3},{3,2},{4,5},{5,4},{6,7},{7,6},{8,9},{9,8},{10,11... | collective-permute-start | bytes 1179656 | tf_op jit(solution)/shard_map/ppermute | solution.py:500
  53.3 14.3 %collective-permute-start.10 = (bf16[512,512]{1,0:T(8,128)(2,1)}, bf16[512,512]{1,0:T(8,128)(2,1)}, u32[]{:S(2)}, u32[]{:S(2)}) collective-permute-start(bf16[512,512]{1,0:T(8,128)(2,1)} %get-tuple-element.53.e0), channel_id=1, source_target_pairs={{0,2},{1,3},{2,0},{3,1},{4,6},{5,7},{6,4},{7,5},{8,10},{9,11},{10,... | collective-permute-start | bytes 1572872 | tf_op jit(solution)/shard_map/ppermute | solution.py:500
  53.9 14.3 %collective-permute-start.9 = (bf16[512,512]{1,0:T(8,128)(2,1)}, bf16[512,512]{1,0:T(8,128)(2,1)}, u32[]{:S(2)}, u32[]{:S(2)}) collective-permute-start(bf16[512,512]{1,0:T(8,128)(2,1)} %get-tuple-element.53.e0), channel_id=1, source_target_pairs={{0,1},{1,0},{2,3},{3,2},{4,5},{5,4},{6,7},{7,6},{8,9},{9,8},{10,11... | collective-permute-start | bytes 1572872 | tf_op jit(solution)/shard_map/ppermute | solution.py:500
  72.6 15.6 %collective-permute-start.13 = (bf16[2,512,128]{2,1,0:T(8,128)(2,1)S(1)}, bf16[2,512,128]{2,1,0:T(8,128)(2,1)S(1)}, u32[]{:S(2)}, u32[]{:S(2)}) collective-permute-start(bf16[2,512,128]{2,1,0:T(8,128)(2,1)S(1)} %get-tuple-element.56.refs_0_), channel_id=1, source_target_pairs={{0,8},{8,0},{16,24},{24,16},{1,9},{9,1},{17,25},{25,17},{2,10},{10... | collective-permute-start | bytes 786440 | tf_op jit(solution)/shard_map/ppermute | solution.py:500
  73.5 14.6 %collective-permute-start.12 = (bf16[2,512,128]{2,1,0:T(8,128)(2,1)S(1)}, bf16[2,512,128]{2,1,0:T(8,128)(2,1)S(1)}, u32[]{:S(2)}, u32[]{:S(2)}) collective-permute-start(bf16[2,512,128]{2,1,0:T(8,128)(2,1)S(1)} %get-tuple-element.56.refs_0_), channel_id=1, source_target_pairs={{0,16},{8,24},{16,0},{24,8},{1,17},{9,25},{17,1},{25,9},{2,18},{10... | collective-permute-start | bytes 786440 | tf_op jit(solution)/shard_map/ppermute | solution.py:500
  79.3 15.2 %collective-permute-start.14 = (bf16[384,768]{1,0:T(8,128)(2,1)S(1)}, bf16[384,768]{1,0:T(8,128)(2,1)S(1)}, u32[]{:S(2)}, u32[]{:S(2)}) collective-permute-start(bf16[384,768]{1,0:T(8,128)(2,1)S(1)} %convolution_convert_fusion), channel_id=1, source_target_pairs={{0,4},{4,0},{1,5},{5,1},{2,6},{6,2},{3,7},{7,3},{8,12},{12,8},{9,1... | collective-permute-start | bytes 1769480 | tf_op jit(solution)/shard_map/ppermute | solution.py:500
  102.2 11.4 %collective-permute-start.16 = (bf16[256,2048]{1,0:T(8,128)(2,1)}, bf16[256,2048]{1,0:T(8,128)(2,1)}, u32[]{:S(2)}, u32[]{:S(2)}) collective-permute-start(bf16[256,2048]{1,0:T(8,128)(2,1)} %get-tuple-element.66), channel_id=1, source_target_pairs={{0,1},{1,0},{2,3},{3,2},{4,5},{5,4},{6,7},{7,6},{8,9},{9,8},{10,11... | collective-permute-start | bytes 3145736 | tf_op jit(solution)/shard_map/ppermute | solution.py:500
  115.2 32.0 %collective-permute-start.18 = (bf16[256,2048]{1,0:T(8,128)(2,1)S(1)}, bf16[256,2048]{1,0:T(8,128)(2,1)}, u32[]{:S(2)}, u32[]{:S(2)}) collective-permute-start(bf16[256,2048]{1,0:T(8,128)(2,1)S(1)} %add_convert_fusion.mine_ref), channel_id=1, source_target_pairs={{0,2},{1,3},{2,0},{3,1},{4,6},{5,7},{6,4},{7,5},{8,10},{9,11},{10,... | collective-permute-start | bytes 3145736 | tf_op jit(solution)/shard_map/ppermute | solution.py:500
  125.2 10.8 %collective-permute-start.23 = (bf16[96,768]{1,0:T(8,128)(2,1)S(1)}, bf16[96,768]{1,0:T(8,128)(2,1)}, u32[]{:S(2)}, u32[]{:S(2)}) collective-permute-start(bf16[96,768]{1,0:T(8,128)(2,1)S(1)} %fusion.10.refs_0_), channel_id=1, source_target_pairs={{0,8},{8,0},{16,24},{24,16},{1,9},{9,1},{17,25},{25,17},{2,10},{10... | collective-permute-start | bytes 442376 | tf_op jit(solution)/shard_map/ppermute | solution.py:500
  136.5 10.7 %collective-permute-start.22 = (bf16[96,768]{1,0:T(8,128)(2,1)}, bf16[96,768]{1,0:T(8,128)(2,1)}, u32[]{:S(2)}, u32[]{:S(2)}) collective-permute-start(bf16[96,768]{1,0:T(8,128)(2,1)} %collective-permute-done.21.refs_1_), channel_id=1, source_target_pairs={{0,4},{4,0},{1,5},{5,1},{2,6},{6,2},{3,7},{7,3},{8,12},{12,8},{9,1... | collective-permute-start | bytes 442376 | tf_op jit(solution)/shard_map/ppermute | solution.py:500
  140.8 13.8 %collective-permute-start.30 = (bf16[96,768]{1,0:T(8,128)(2,1)}, bf16[96,768]{1,0:T(8,128)(2,1)S(1)}, u32[]{:S(2)}, u32[]{:S(2)}) collective-permute-start(bf16[96,768]{1,0:T(8,128)(2,1)} %collective-permute-done.29.refs_3_), channel_id=1, source_target_pairs={{0,4},{4,0},{1,5},{5,1},{2,6},{6,2},{3,7},{7,3},{8,12},{12,8},{9,1... | collective-permute-start | bytes 442376 | tf_op jit(solution)/shard_map/ppermute | solution.py:500
  158.7 14.8 %collective-permute-start.26 = (bf16[512,512]{1,0:T(8,128)(2,1)S(1)}, bf16[512,512]{1,0:T(8,128)(2,1)S(1)}, u32[]{:S(2)}, u32[]{:S(2)}) collective-permute-start(bf16[512,512]{1,0:T(8,128)(2,1)S(1)} %fusion.3), channel_id=1, source_target_pairs={{0,4},{4,0},{1,5},{5,1},{2,6},{6,2},{3,7},{7,3},{8,12},{12,8},{9,1... | collective-permute-start | bytes 1572872 | tf_op jit(solution)/shard_map/ppermute | solution.py:500
  160.6 23.3 %collective-permute-start.31 = (bf16[512,512]{1,0:T(8,128)(2,1)S(1)}, bf16[512,512]{1,0:T(8,128)(2,1)S(1)}, u32[]{:S(2)}, u32[]{:S(2)}) collective-permute-start(bf16[512,512]{1,0:T(8,128)(2,1)S(1)} %fusion.4), channel_id=1, source_target_pairs={{0,4},{4,0},{1,5},{5,1},{2,6},{6,2},{3,7},{7,3},{8,12},{12,8},{9,1... | collective-permute-start | bytes 1572872 | tf_op jit(solution)/shard_map/ppermute | solution.py:500
  186.8 10.3 %collective-permute-start.32 = (bf16[256,512]{1,0:T(8,128)(2,1)S(1)}, bf16[256,512]{1,0:T(8,128)(2,1)S(1)}, u32[]{:S(2)}, u32[]{:S(2)}) collective-permute-start(bf16[256,512]{1,0:T(8,128)(2,1)S(1)} %get-tuple-element.86), channel_id=1, source_target_pairs={{0,8},{8,0},{16,24},{24,16},{1,9},{9,1},{17,25},{25,17},{2,10},{10... | collective-permute-start | bytes 786440 | tf_op jit(solution)/shard_map/ppermute | solution.py:500
  198.6 11.7 %collective-permute-start.45 = (bf16[128,512]{1,0:T(8,128)(2,1)S(1)}, bf16[128,512]{1,0:T(8,128)(2,1)S(1)}, u32[]{:S(2)}, u32[]{:S(2)}) collective-permute-start(bf16[128,512]{1,0:T(8,128)(2,1)S(1)} %fusion.12.refs_0_), channel_id=1, source_target_pairs={{0,4},{4,0},{1,5},{5,1},{2,6},{6,2},{3,7},{7,3},{8,12},{12,8},{9,1... | collective-permute-start | bytes 393224 | tf_op jit(solution)/shard_map/ppermute | solution.py:500
  216.5 12.5 %collective-permute-start.40 = (bf16[128,512]{1,0:T(8,128)(2,1)S(1)}, bf16[128,512]{1,0:T(8,128)(2,1)S(1)}, u32[]{:S(2)}, u32[]{:S(2)}) collective-permute-start(bf16[128,512]{1,0:T(8,128)(2,1)S(1)} %collective-permute-done.36.refs_1_), channel_id=1, source_target_pairs={{0,4},{4,0},{1,5},{5,1},{2,6},{6,2},{3,7},{7,3},{8,12},{12,8},{9,1... | collective-permute-start | bytes 393224 | tf_op jit(solution)/shard_map/ppermute | solution.py:500
  218.0 11.0 %collective-permute-start.41 = (bf16[128,512]{1,0:T(8,128)(2,1)S(1)}, bf16[128,512]{1,0:T(8,128)(2,1)S(1)}, u32[]{:S(2)}, u32[]{:S(2)}) collective-permute-start(bf16[128,512]{1,0:T(8,128)(2,1)S(1)} %collective-permute-done.37.refs_2_), channel_id=1, source_target_pairs={{0,4},{4,0},{1,5},{5,1},{2,6},{6,2},{3,7},{7,3},{8,12},{12,8},{9,1... | collective-permute-start | bytes 393224 | tf_op jit(solution)/shard_map/ppermute | solution.py:500
  219.6 10.7 %collective-permute-start.42 = (bf16[128,512]{1,0:T(8,128)(2,1)S(1)}, bf16[128,512]{1,0:T(8,128)(2,1)S(1)}, u32[]{:S(2)}, u32[]{:S(2)}) collective-permute-start(bf16[128,512]{1,0:T(8,128)(2,1)S(1)} %collective-permute-done.38.refs_3_), channel_id=1, source_target_pairs={{0,4},{4,0},{1,5},{5,1},{2,6},{6,2},{3,7},{7,3},{8,12},{12,8},{9,1... | collective-permute-start | bytes 393224 | tf_op jit(solution)/shard_map/ppermute | solution.py:500
  (52 other events, 556.4 us)

commit v6 on v5

--- a/solution.py
+++ b/solution.py
@@ -17,10 +17,12 @@
 BF16 = jnp.bfloat16
 CHUNKS = 2
 TABLE = 6
+ROWS = (0, 2, 1, 3)
 LIMIT = 40 * 2**20
 VMEM = pl.BlockSpec(memory_space=pltpu.VMEM)
 SMEM = pl.BlockSpec(memory_space=pltpu.SMEM)
 ANY = pl.BlockSpec(memory_space=pl.ANY)
+HBM = pl.BlockSpec(memory_space=pltpu.HBM)
 
 
 def dot(a, b):
@@ -73,7 +75,7 @@
     width = w_keyval.shape[2]
     return pl.pallas_call(
         first_kernel,
-        in_specs=[ANY] * 2,
+        in_specs=[HBM] * 2,
         out_specs=[VMEM] * 2,
         out_shape=[
             jax.ShapeDtypeStruct((2, rows, width), BF16),
@@ -90,6 +92,33 @@
         ),
         name="first_projection",
     )(obs, w_keyval)
+
+
+def query_kernel(scale, obs_hbm, w_hbm, factor_ref, q_ref, obs_ref, w_ref, sems):
+    for copy in start_copies([(w_hbm, w_ref), (obs_hbm, obs_ref)], sems):
+        copy.wait()
+    q_ref[...] = (dot(obs_ref[...], w_ref[...]) * (factor_ref[:, :1] * scale)).astype(BF16)
+
+
+def query_projection(obs, w_query, factor, scale):
+    rows, depth = obs.shape
+    width = w_query.shape[1]
+    return pl.pallas_call(
+        functools.partial(query_kernel, scale),
+        in_specs=[HBM, HBM, VMEM],
+        out_specs=VMEM,
+        out_shape=jax.ShapeDtypeStruct((rows, width), BF16),
+        scratch_shapes=[
+            pltpu.VMEM((rows, depth), BF16),
+            pltpu.VMEM((depth, width), BF16),
+            pltpu.SemaphoreType.DMA((2,)),
+        ],
+        compiler_params=pltpu.CompilerParams(vmem_limit_bytes=LIMIT),
+        cost_estimate=pl.CostEstimate(
+            flops=2 * rows * depth * width, bytes_accessed=2 * rows * depth, transcendentals=0
+        ),
+        name="query_projection",
+    )(obs, w_query, factor)
 
 
 def attend_blocks(groups, units, first, left_ref, q_ref, kv_refs):
@@ -201,57 +230,78 @@
     )(place, queries, *state, *pieces)
 
 
-def hidden_kernel(
-    obs_any, t0, t1, t2, t3, w0, w1, w2, w3, c_any, o_ref, emb_ref, obs_ref, w_ref, c_ref, sum_ref, sems
-):
+def near_kernel(obs_hbm, t0, t1, w0, w1, sum_ref, obs_ref, w_ref, sems):
     inner, depth = w0.shape
     tile = depth // 3
-    pairs = [(obs_any, obs_ref)]
-    pairs += [
-        (w, w_ref.at[k * inner : (k + 1) * inner]) for k, w in enumerate((w0, w1, w2, w3))
-    ]
-    copies = start_copies(pairs + [(c_any, c_ref)], sems)
-    for copy in copies[:3]:
+    pairs = [(obs_hbm, obs_ref), (w0, w_ref.at[:inner]), (w1, w_ref.at[inner:])]
+    for copy in start_copies(pairs, sems):
         copy.wait()
-    tiles = [slice(i * tile, (i + 1) * tile) for i in range(3)]
-    for strip in tiles:
+    for i in range(3):
+        strip = slice(i * tile, (i + 1) * tile)
         parts = jnp.concatenate([t0[...], t1[...]], axis=1)
-        sum_ref[:, strip] = obs_ref[:, strip].astype(F32) + dot(parts, w_ref[: 2 * inner, strip])
-    for copy in copies[3:5]:
-        copy.wait()
-    for strip in tiles:
-        parts = jnp.concatenate([t2[...], t3[...]], axis=1)
-        total = sum_ref[:, strip] + dot(parts, w_ref[2 * inner :, strip])
-        o_ref[:, strip] = total.astype(BF16)
-    copies[5].wait()
-    emb_ref[...] = dot(o_ref[...], c_ref[...]).astype(BF16)
-
-
-def hidden_rows(obs, parts, weights, c_in):
+        sum_ref[:, strip] = obs_ref[:, strip].astype(F32) + dot(parts, w_ref[:, strip])
+
+
+def near_rows(obs, parts, weights):
     rows, depth = obs.shape
     inner = weights[0].shape[0]
+    return pl.pallas_call(
+        near_kernel,
+        in_specs=[HBM] + [VMEM] * 2 + [HBM, ANY],
+        out_specs=VMEM,
+        out_shape=jax.ShapeDtypeStruct((rows, depth), F32),
+        scratch_shapes=[
+            pltpu.VMEM((rows, depth), BF16),
+            pltpu.VMEM((2 * inner, depth), BF16),
+            pltpu.SemaphoreType.DMA((3,)),
+        ],
+        compiler_params=pltpu.CompilerParams(vmem_limit_bytes=LIMIT),
+        cost_estimate=pl.CostEstimate(
+            flops=4 * rows * depth * inner, bytes_accessed=4 * depth * inner, transcendentals=0
+        ),
+        name="near_rows",
+    )(obs, *parts, *weights)
+
+
+def hidden_kernel(sum_ref, t2, t3, w2, w3, c_hbm, o_ref, emb_ref, w_ref, c_ref, sems):
+    inner, depth = w2.shape
+    tile = depth // 3
+    copies = start_copies(
+        [(w2, w_ref.at[:inner]), (w3, w_ref.at[inner:]), (c_hbm, c_ref)], sems
+    )
+    copies[0].wait()
+    copies[1].wait()
+    for i in range(3):
+        strip = slice(i * tile, (i + 1) * tile)
+        parts = jnp.concatenate([t2[...], t3[...]], axis=1)
+        o_ref[:, strip] = (sum_ref[:, strip] + dot(parts, w_ref[:, strip])).astype(BF16)
+    copies[2].wait()
+    emb_ref[...] = dot(o_ref[...], c_ref[...]).astype(BF16)
+
+
+def hidden_rows(near_sum, parts, weights, c_in):
+    rows, depth = near_sum.shape
+    inner = weights[0].shape[0]
     width = c_in.shape[1]
     return pl.pallas_call(
         hidden_kernel,
-        in_specs=[ANY] + [VMEM] * 4 + [ANY] * 5,
+        in_specs=[VMEM] * 3 + [ANY] * 2 + [HBM],
         out_specs=[VMEM] * 2,
         out_shape=[
             jax.ShapeDtypeStruct((rows, depth), BF16),
             jax.ShapeDtypeStruct((rows, width), BF16),
         ],
         scratch_shapes=[
-            pltpu.VMEM((rows, depth), BF16),
-            pltpu.VMEM((4 * inner, depth), BF16),
+            pltpu.VMEM((2 * inner, depth), BF16),
             pltpu.VMEM((depth, width), BF16),
-            pltpu.VMEM((rows, depth), F32),
-            pltpu.SemaphoreType.DMA((6,)),
+            pltpu.SemaphoreType.DMA((3,)),
         ],
         compiler_params=pltpu.CompilerParams(vmem_limit_bytes=LIMIT),
         cost_estimate=pl.CostEstimate(
             flops=8 * rows * depth * inner, bytes_accessed=8 * depth * inner, transcendentals=0
         ),
         name="hidden_rows",
-    )(obs, *parts, *weights, c_in)
+    )(near_sum, *parts, *weights, c_in)
 
 
 def join_kernel(place_ref, e0, e1, e2, e3, wkv_any, kv_ref, factor_ref, emb_ref, wkv_ref, sems):
@@ -288,7 +338,7 @@
     width = w_keyval.shape[2]
     return pl.pallas_call(
         join_kernel,
-        in_specs=[SMEM] + [VMEM] * 4 + [ANY],
+        in_specs=[SMEM] + [VMEM] * 4 + [HBM],
         out_specs=[VMEM] * 3,
         out_shape=[
             jax.ShapeDtypeStruct((2, rows, width), BF16),
@@ -304,32 +354,23 @@
     )(place, *parts, w_keyval)
 
 
-def part_kernel(
-    place_ref, att_ref, c_any, send_ref, keep_ref, their_ref, my_ref, c_ref, sems
-):
+def part_kernel(place_ref, att_ref, c_hbm, send_ref, keep_ref, order_ref, c_ref, sems):
     rows, inner = att_ref.shape
     wide = c_ref.shape[1]
     block = rows // 4
     half = inner // 2
-    core = place_ref[1] % 2
-    copies = start_copies(
-        [
-            (c_any.at[i * half : (i + 1) * half], c_ref.at[i * half : (i + 1) * half])
-            for i in range(2)
-        ],
-        sems,
-    )
-    for out, side in ((their_ref, 1 - core), (my_ref, core)):
-        for i in range(2):
-            span = pl.ds(pl.multiple_of((side + 2 * i) * block, block), block)
-            out[i * block : (i + 1) * block, :] = att_ref[span, :]
+    spans = [slice(i * half, (i + 1) * half) for i in range(2)]
+    copies = start_copies([(c_hbm.at[span], c_ref.at[span]) for span in spans], sems)
+    for at, code in enumerate(ROWS):
+        start = pl.multiple_of((place_ref[1] ^ code) * block, block)
+        order_ref[at * block : (at + 1) * block, :] = att_ref[pl.ds(start, block), :]
     for copy in copies:
         copy.wait()
     tile = 512
-    for out, source in ((send_ref, their_ref), (keep_ref, my_ref)):
+    for out, source in ((send_ref, order_ref[2 * block :, :]), (keep_ref, order_ref[: 2 * block, :])):
         for j in range(wide // tile):
             columns = slice(j * tile, (j + 1) * tile)
-            out[:, columns] = dot(source[...], c_ref[:, columns]).astype(out.dtype)
+            out[:, columns] = dot(source, c_ref[:, columns]).astype(out.dtype)
 
 
 def part_rows(place, attended, c_out):
@@ -337,13 +378,12 @@
     wide = c_out.shape[1]
     return pl.pallas_call(
         part_kernel,
-        in_specs=[SMEM, VMEM, ANY],
-        out_specs=[VMEM] * 4,
+        in_specs=[SMEM, VMEM, HBM],
+        out_specs=[VMEM] * 3,
         out_shape=[
             jax.ShapeDtypeStruct((rows // 2, wide), BF16),
             jax.ShapeDtypeStruct((rows // 2, wide), F32),
-            jax.ShapeDtypeStruct((rows // 2, inner), BF16),
-            jax.ShapeDtypeStruct((rows // 2, inner), BF16),
+            jax.ShapeDtypeStruct((rows, inner), BF16),
         ],
         scratch_shapes=[pltpu.VMEM((inner, wide), BF16), pltpu.SemaphoreType.DMA((2,))],
         compiler_params=pltpu.CompilerParams(vmem_limit_bytes=LIMIT),
@@ -355,31 +395,30 @@
 
 
 def mixed_kernel(
-    place_ref, emb_ref, mine_ref, got_ref, wv_ref, ret_ref, value_ref, other_ref, own_ref, mixed_ref
+    place_ref, emb_any, keep_ref, near_ref, got_ref, wv_ref, ret_ref,
+    value_ref, other_ref, own_ref, emb_ref, mixed_ref, sem,
 ):
-    rows, wide = mine_ref.shape
+    rows, wide = got_ref.shape
     half = wide // 2
-    piece = rows // 2
     block = 32
-    core = place_ref[1] % 2
+    base = pl.multiple_of(place_ref[1] * rows, rows)
+    copy = pltpu.make_async_copy(emb_any.at[pl.ds(base, rows)], emb_ref, sem)
+    copy.start()
     live_total = place_ref[4].astype(F32)
+    copy.wait()
 
     @pl.loop(0, rows // block)
     def _(i):
         start = pl.multiple_of(i * block, block)
         span = pl.ds(start, block)
-        place = (core + start // piece * 2) * piece + start % piece
-        there = pl.ds(pl.multiple_of(place, block), block)
-        mixed = (
-            emb_ref[there, :].astype(F32)
-            + mine_ref[span, :].astype(F32)
-            + got_ref[span, :].astype(F32)
+        mixed = emb_ref[span, :].astype(F32) + (
+            keep_ref[span, :] + near_ref[span, :].astype(F32) + got_ref[span, :].astype(F32)
         )
         mixed_ref[...] = mixed
         factor = row_factor(mixed)
         value = factor * jnp.sum(mixed * wv_ref[...].astype(F32), axis=-1, keepdims=True)
-        row = place_ref[2] + place + lax.broadcasted_iota(jnp.int32, (block, 1), 0)
-        gap = jnp.where(row < place_ref[3], value - ret_ref[there, :], F32(0.0)) / live_total
+        row = place_ref[2] + base + start + lax.broadcasted_iota(jnp.int32, (block, 1), 0)
+        gap = jnp.where(row < place_ref[3], value - ret_ref[span, :], F32(0.0)) / live_total
         lead = factor * gap
         pull = lead * factor * value / wide
         value_ref[span, :] = jnp.broadcast_to(value, (block, HEAD))
@@ -389,24 +428,28 @@
             out[span, :] = (lead * wv_ref[:, columns].astype(F32) - part * pull).astype(BF16)
 
 
-def mixed_rows(place, embedded, mine, got, w_value, returns):
-    rows, wide = mine.shape
+def mixed_rows(place, embedded, keep, near, got, w_value, returns):
+    rows, wide = got.shape
     return pl.pallas_call(
         mixed_kernel,
-        in_specs=[SMEM] + [VMEM] * 5,
+        in_specs=[SMEM, ANY] + [VMEM] * 5,
         out_specs=[VMEM] * 3,
         out_shape=[
             jax.ShapeDtypeStruct((rows, HEAD), F32),
             jax.ShapeDtypeStruct((rows, wide // 2), BF16),
             jax.ShapeDtypeStruct((rows, wide // 2), BF16),
         ],
-        scratch_shapes=[pltpu.VMEM((32, wide), F32)],
+        scratch_shapes=[
+            pltpu.VMEM((rows, wide), BF16),
+            pltpu.VMEM((32, wide), F32),
+            pltpu.SemaphoreType.DMA,
+        ],
         compiler_params=pltpu.CompilerParams(vmem_limit_bytes=LIMIT),
         cost_estimate=pl.CostEstimate(
             flops=10 * rows * wide, bytes_accessed=12 * rows * wide, transcendentals=0
         ),
         name="mixed_rows",
-    )(place, embedded, mine, got, w_value.reshape(1, wide), returns.reshape(-1, 1))
+    )(place, embedded, keep, near, got, w_value, returns)
 
 
 def gather_codes(size):
@@ -432,13 +475,14 @@
     rows, wide = own.shape
     if (rows // count) % 16:
         got = got.astype(F32)
+    send_type = BF16 if (rows // count) % 16 == 0 else F32
     return pl.pallas_call(
         functools.partial(split_kernel, gather_codes(count)),
         in_specs=[SMEM, VMEM, VMEM],
         out_specs=[VMEM] * 2,
         out_shape=[
             jax.ShapeDtypeStruct((rows // 2, wide), F32),
-            jax.ShapeDtypeStruct((rows // 2, wide), got.dtype),
+            jax.ShapeDtypeStruct((rows // 2, wide), send_type),
         ],
         compiler_params=pltpu.CompilerParams(vmem_limit_bytes=LIMIT),
         cost_estimate=pl.CostEstimate(
@@ -500,10 +544,11 @@
     return lax.ppermute(block, axis, [(i, i ^ bit) for i in range(size)])
 
 
-def gather_blocks(block, axis):
+def gather_blocks(block, axis, late=None):
     blocks, bit = [block], lax.axis_size(axis) // 2
     while bit >= 1:
-        blocks = blocks + [swap(item, axis, bit) for item in blocks]
+        sources = blocks if bit > 1 or late is None else [late] + blocks[1:]
+        blocks = blocks + [swap(item, axis, bit) for item in sources]
         bit //= 2
     return blocks
 
@@ -566,27 +611,28 @@
 
     obs_in = obs[0]
     keyval, factor_a = first_projection(obs_in, a_keyval)
-    pieces_k = gather_blocks(keyval, "rep")
-
     a_far = swap(a_out, "mdl", 2)
-    queries = (dot(obs_in, a_query) * (factor_a[:, :1] * score_scale)).astype(BF16)
+    queries = query_projection(obs_in, a_query, factor_a, score_scale)
+    late_keyval, queries = tied(keyval, queries)
+    pieces_k = gather_blocks(keyval, "rep", late_keyval)
     state = attend_call(queries, pieces_k[:-1], 0, place, [])
     attended = attend_call(queries, pieces_k[-1:], rep_count - 1, place, state)
     attended, a_far = tied(attended, a_far)
     attended_far = swap(attended, "mdl", 2)
-    a_all = [a_out, swap(a_out, "mdl", 1), a_far, swap(a_far, "mdl", 1)]
-    attended_parts = [
-        attended,
-        swap(attended, "mdl", 1),
-        attended_far,
-        swap(attended_far, "mdl", 1),
-    ]
-    hidden, embed_part = hidden_rows(obs_in, attended_parts, a_all, c_in)
+    attended_near = swap(attended, "mdl", 1)
+    near_sum = near_rows(obs_in, [attended, attended_near], [a_out, swap(a_out, "mdl", 1)])
+    hidden, embed_part = hidden_rows(
+        near_sum,
+        [attended_far, swap(attended_far, "mdl", 1)],
+        [a_far, swap(a_far, "mdl", 1)],
+        c_in,
+    )
 
     embed_parts, _ = gather_parts(embed_part)
     critic_keyval, factor_c, embedded = join_rows(place, embed_parts, c_keyval)
-    pieces_c = gather_blocks(critic_keyval, "rep")
     critic_queries = (dot(embedded, c_query) * (factor_c[:, :1] * score_scale)).astype(BF16)
+    late_keyval, critic_queries = tied(critic_keyval, critic_queries)
+    pieces_c = gather_blocks(critic_keyval, "rep", late_keyval)
 
     late_hidden, critic_keyval = tied(hidden, critic_keyval)
     source = late_hidden.astype(F32)
@@ -614,54 +660,71 @@
     )
     own_a = product(attended, lax.dynamic_slice_in_dim(dhidden, batch_index * half_a, half_a, 1))
 
+    wide = w_value.shape[0]
+    target = lax.dynamic_slice_in_dim(returns[0], mdl_index * value_rows, value_rows, 0)
+    critic_queries, own_a, w_row, target = tied(
+        critic_queries, own_a, w_value.reshape(1, wide), target.reshape(value_rows, 1)
+    )
     state_c = attend_call(critic_queries, pieces_c[:-1], 0, place, [])
     *state_c, got_a, pieces_c[-1] = tied(*state_c, got_a, pieces_c[-1])
     keep_a, send_a = split_sum(rep_place, own_a, got_a, rep_count)
+    *state_c, send_a = tied(*state_c, send_a)
     moved_a = swap(send_a.astype(BF16), "rep", 1)
     critic_attended = attend_call(critic_queries, pieces_c[-1:], rep_count - 1, place, state_c)
 
-    send_m, keep_m, their_att, my_att = part_rows(place, critic_attended, c_out)
-    got_m = swap(send_m, "mdl", 1)
-    got_m, moved_a = tied(got_m, moved_a)
-    mine_m = (keep_m + got_m.astype(F32)).astype(BF16)
+    send_m, keep_m, att_rows = part_rows(place, critic_attended, c_out)
+    near_m = swap(send_m, "mdl", 1)
+    send_y = (keep_m[value_rows:] + near_m[value_rows:].astype(F32)).astype(BF16)
+    got_y = swap(send_y, "mdl", 2)
+    att_there = swap(critic_attended, "sec", 1)
+    got_y, moved_a = tied(got_y, moved_a)
+    value_wide, d_other, d_own = mixed_rows(
+        place, embedded, keep_m, near_m, got_y, w_row, target
+    )
+
+    d_there = swap(d_other, "sec", 1)
+    d_far = swap(d_own, "mdl", 2)
+    d_near = swap(d_own, "mdl", 1)
     bit = 2
     while bit < rep_count:
         keep_a, send_a = halve(keep_a, moved_a)
         moved_a = swap(send_a, "rep", bit)
         bit *= 2
-    theirs_m = swap(mine_m, "mdl", 2)
+    there_far = swap(d_there, "mdl", 2)
+    there_near = swap(d_there, "mdl", 1)
+    own_rows = jnp.concatenate([d_own, d_far, d_near, swap(d_far, "mdl", 1)], axis=0)
+    there_far, moved_a = tied(there_far, moved_a)
+    there_rows = jnp.concatenate(
+        [d_there, there_far, there_near, swap(there_far, "mdl", 1)], axis=0
+    )
+    att_there = jnp.concatenate(
+        [
+            lax.dynamic_slice_in_dim(att_there, (mdl_index ^ code) * value_rows, value_rows, 0)
+            for code in ROWS
+        ],
+        axis=0,
+    )
+    value_part, there_rows = tied(value_wide[:, 0], there_rows)
     mine_a = gather_blocks((keep_a + moved_a.astype(F32)).astype(BF16), "rep")
     theirs_a = [swap(block, "sec", 1) for block in mine_a]
-    theirs_m, *theirs_a[:-1] = tied(theirs_m, *theirs_a[:-1])
-    value_wide, d_other, d_own = mixed_rows(
-        place, embedded, mine_m, theirs_m, w_value, returns[0]
-    )
-    e_other = swap(d_other, "mdl", 1)
-    e_own = swap(d_own, "mdl", 1)
+    actor_summed = assemble(place, mine_a + theirs_a, rep_count, 0, 1, [])
 
     strip = d_own.shape[1] // CHUNKS
-    spans = [slice(c * strip, (c + 1) * strip) for c in range(CHUNKS)]
-
-    def both(mine, other, span):
-        return product(my_att, mine[:, span]) + product(their_att, other[:, span])
-
-    got = [swap(both(d_other, e_other, span).astype(BF16), "sec", 1) for span in spans]
-    own = [both(d_own, e_own, span) for span in spans]
-    value_part = lax.dynamic_slice_in_dim(value_wide, mdl_index // 2 * value_rows, value_rows, 0)[:, 0]
-    got[0], value_part = tied(got[0], value_part)
-    actor_summed = assemble(place, mine_a + theirs_a, rep_count, 0, 1, [])
     marks, result = [], []
     for c in range(CHUNKS):
-        arrived = got[c]
-        keep, send = split_sum(rep_place, own[c], arrived, rep_count)
+        span = slice(c * strip, (c + 1) * strip)
+        keep, send = split_sum(
+            rep_place,
+            product(att_rows, own_rows[:, span]),
+            product(att_there, there_rows[:, span]),
+            rep_count,
+        )
         bit, trail = 1, []
         while bit < rep_count:
             arrived = swap(send.astype(BF16), "rep", bit)
             bit *= 2
             if c > 0:
                 arrived, _ = tied(arrived, marks[min(len(trail) + 1, len(marks) - 1)])
-            elif not trail:
-                arrived, actor_summed, *got[1:] = tied(arrived, actor_summed, *got[1:])
             if bit < rep_count:
                 keep, send = halve(keep, arrived)
                 trail.append(keep)

time: 235 us -> 220 us (0.936)
  waiting for transfers between devices: 113 us -> 94.4 us
  starting transfers between devices: 47.6 us -> 54.4 us
  matrix products: 10.4 us -> 5.6 us
  Pallas kernels: 40.6 us -> 43.9 us
    ppermute x49 -> x53, waiting for transfers between devices: 113 us -> 94.4 us  [swap(): return lax.ppermute(block, axis, [(i, i ^ bit) for i in range(size)])]
    ppermute x49 -> x53, starting transfers between devices: 47.6 us -> 54.4 us  [swap(): return lax.ppermute(block, axis, [(i, i ^ bit) for i in range(size)])]
    dot_general x4 -> x3, matrix products: 5.47 us -> 2.76 us  [dot(): return jnp.dot(a, b, preferred_element_type=F32)]
    dot_general x10 -> x6, matrix products: 4.89 us -> 2.84 us  [product(): return jnp.einsum('rh,rd->hd', left, right, preferred_element_type=F32)]
    pallas_call x5 -> x7, Pallas kernels: 16.7 us -> 18.2 us  [the longest x1 4.54 us: hidden_rows(): pl.pallas_call(hidden_kernel, in_specs=[VMEM] * 3 + [ANY] * 2 + [HBM], ou...]
    unnamed x54 -> x49, local copies, waits for them, and re-layouts: 8.06 us -> 7.03 us
  transfers between devices with their start and end apart: 49 -> 53, of which waited for: 24 -> 26; matrix products, arithmetic and copies ran while one was open for 8% -> 7% of each run, Pallas kernels for 10% -> 11%
where the time goes in v6:
time: 220 us
  waiting for transfers between devices  94.4 us (43%)
  starting transfers between devices  54.4 us (25%)
  Pallas kernels  43.9 us (20%)
  local copies, waits for them, and re-layouts  11.9 us (5%)
  matrix products  5.6 us (3%)
  between operations  4.86 us (2%)
  other arithmetic  4.45 us (2%)
    ppermute x53, waiting for transfers between devices, swap(): return lax.ppermute(block, axis, [(i, i ^ bit) for i in range(size)])  94.4 us
    ppermute x53, starting transfers between devices, swap(): return lax.ppermute(block, axis, [(i, i ^ bit) for i in range(size)])  54.4 us
    pallas_call x4, Pallas kernels, attend_call(): pl.pallas_call(functools.partial(body, groups, units, TABLE + first), in_...  15.1 us
    pallas_call x3, Pallas kernels, assemble(): pl.pallas_call(functools.partial(assemble_kernel, gather_codes(count), ch...  10.3 us
    unnamed x49, local copies, waits for them, and re-layouts  7.03 us
    pallas_call x1, Pallas kernels, hidden_rows(): pl.pallas_call(hidden_kernel, in_specs=[VMEM] * 3 + [ANY] * 2 + [HBM], ou...  4.54 us
  transfers between devices with their start and end apart: 53, of which 26 were waited for; matrix products, arithmetic and copies ran while one was open for 7% of the time, Pallas kernels for 11%

profile of v6, /device:TPU:0, one launch (start us, length us, event | category | flops | bytes accessed | tf_op | source)
XLA Modules:
  0.0 219.6 jit_solution(8796169204197571059)
XLA Ops:
  0.6 3.0 %collective-permute-start.3 = (bf16[384,1536]{1,0:T(8,128)(2,1)}, bf16[384,1536]{1,0:T(8,128)(2,1)}, u32[]{:S(2)}, u32[]{:S(2)}) collective-permute-start(bf16[384,1536]{1,0:T(8,128)(2,1)} %w0.1), channel_id=1, source_target_pairs={{0,2},{1,3},{2,0},{3,1},{4,6},{5,7},{6,4},{7,5},{8,10},{9,11},{10,... | collective-permute-start | bytes 3538952 | tf_op jit(solution)/shard_map/ppermute | solution.py:544
  19.1 3.3 %collective-permute-done.refs_1_ = bf16[2,512,128]{2,1,0:T(8,128)(2,1)S(1)} collective-permute-done((bf16[2,512,128]{2,1,0:T(8,128)(2,1)S(1)}, bf16[2,512,128]{2,1,0:T(8,128)(2,1)S(1)}, u32[]{:S(2)}, u32[]{:S(2)}) %collective-permute-start) | collective-permute-done | bytes 262176 | tf_op jit(solution)/shard_map/ppermute | solution.py:544
  24.0 3.6 %attend_open.2 = (f32[512,768]{1,0:T(8,128)S(1)}, f32[512,384]{1,0:T(8,128)S(1)}) custom-call(s32[10]{0:T(128)S(1)} %stack.39.left_ref.place_ref, bf16[512,384]{1,0:T(8,128)(2,1)S(1)} %query_projection.1.q_ref, bf16[2,512,128]{2,1,0:T(8,128)(2,1)S(1)} %get-tuple-element.55.refs_0_, bf16[2,512,128]{2,1,0:T(8,128)(2,1)S(1)} %collective-permute-done.refs_1_, ...), custom_call_target="tpu_custom_call" | custom-call | flops 7247757312 | bytes 786432 | tf_op jit(solution)/shard_map/attend_open/pallas_call | solution.py:218
  33.0 10.7 %collective-permute-done.6.t2 = bf16[512,384]{1,0:T(8,128)(2,1)S(1)} collective-permute-done((bf16[512,384]{1,0:T(8,128)(2,1)S(1)}, bf16[512,384]{1,0:T(8,128)(2,1)S(1)}, u32[]{:S(2)}, u32[]{:S(2)}) %collective-permute-start.6) | collective-permute-done | bytes 393248 | tf_op jit(solution)/shard_map/ppermute | solution.py:544
  43.7 3.1 %near_rows.1.sum_ref = f32[512,1536]{1,0:T(8,128)S(1)} custom-call(bf16[512,1536]{1,0:T(8,128)(2,1)S(1)} %bitcast.28, bf16[512,384]{1,0:T(8,128)(2,1)S(1)} %attend_close.2.t0, bf16[512,384]{1,0:T(8,128)(2,1)S(1)} %collective-permute-done.4.t1, bf16[384,1536]{1,0:T(8,128)(2,1)} %w0.1, bf16[384,1536]{1,0:T(8,128)(2,1)} %collective-permute-done.5.w1), custom_call_target="tpu_custom_call" | custom-call | flops 1207959552 | bytes 2359296 | tf_op jit(solution)/shard_map/near_rows/pallas_call | solution.py:248
  47.0 4.5 %hidden_rows.1 = (bf16[512,1536]{1,0:T(8,128)(2,1)S(1)}, bf16[512,512]{1,0:T(8,128)(2,1)}) custom-call(f32[512,1536]{1,0:T(8,128)S(1)} %near_rows.1.sum_ref, bf16[512,384]{1,0:T(8,128)(2,1)S(1)} %collective-permute-done.6.t2, bf16[512,384]{1,0:T(8,128)(2,1)S(1)} %collective-permute-done.7.t3, bf16[384,1536]{1,0:T(8,128)(2,1)} %collective-permute-done.3.w2, ...), custom_call_target="tpu_custom_call" | custom-call | flops 2415919104 | bytes 4718592 | tf_op jit(solution)/shard_map/hidden_rows/pallas_call | solution.py:286
  53.5 13.8 %collective-permute-done.10.e2 = bf16[512,512]{1,0:T(8,128)(2,1)} collective-permute-done((bf16[512,512]{1,0:T(8,128)(2,1)}, bf16[512,512]{1,0:T(8,128)(2,1)}, u32[]{:S(2)}, u32[]{:S(2)}) %collective-permute-start.10) | collective-permute-done | bytes 524320 | tf_op jit(solution)/shard_map/ppermute | solution.py:544
  69.6 2.7 %join_rows.1 = (bf16[2,512,128]{2,1,0:T(8,128)(2,1)S(1)}, f32[512,128]{1,0:T(8,128)S(1)}, bf16[512,2048]{1,0:T(8,128)(2,1)S(1)}) custom-call(s32[10]{0:T(128)S(1)} %stack.39.left_ref.place_ref, bf16[512,512]{1,0:T(8,128)(2,1)} %get-tuple-element.60.e0, bf16[512,512]{1,0:T(8,128)(2,1)} %collective-permute-done.9.e1, ...), custom_call_target="tpu_custom_call" | custom-call | flops 536870912 | bytes 4194304 | tf_op jit(solution)/shard_map/join_rows/pallas_call | solution.py:339
  72.3 3.3 %collective-permute-start.12 = (bf16[2,512,128]{2,1,0:T(8,128)(2,1)S(1)}, bf16[2,512,128]{2,1,0:T(8,128)(2,1)S(1)}, u32[]{:S(2)}, u32[]{:S(2)}) collective-permute-start(bf16[2,512,128]{2,1,0:T(8,128)(2,1)S(1)} %get-tuple-element.68.refs_0_), channel_id=1, source_target_pairs={{0,16},{8,24},{16,0},{24,8},{1,17},{9,25},{17,1},{25,9},{2,18},{10... | collective-permute-start | bytes 786440 | tf_op jit(solution)/shard_map/ppermute | solution.py:544
  84.3 3.6 %collective-permute-done.12.refs_1_ = bf16[2,512,128]{2,1,0:T(8,128)(2,1)S(1)} collective-permute-done((bf16[2,512,128]{2,1,0:T(8,128)(2,1)S(1)}, bf16[2,512,128]{2,1,0:T(8,128)(2,1)S(1)}, u32[]{:S(2)}, u32[]{:S(2)}) %collective-permute-start.12) | collective-permute-done | bytes 262176 | tf_op jit(solution)/shard_map/ppermute | solution.py:544
  88.6 4.9 %collective-permute-done.13.refs_2_ = bf16[2,512,128]{2,1,0:T(8,128)(2,1)S(1)} collective-permute-done((bf16[2,512,128]{2,1,0:T(8,128)(2,1)S(1)}, bf16[2,512,128]{2,1,0:T(8,128)(2,1)S(1)}, u32[]{:S(2)}, u32[]{:S(2)}) %collective-permute-start.13) | collective-permute-done | bytes 262176 | tf_op jit(solution)/shard_map/ppermute | solution.py:544
  93.5 4.8 %attend_open.3 = (f32[512,1024]{1,0:T(8,128)S(1)}, f32[512,512]{1,0:T(8,128)S(1)}) custom-call(s32[10]{0:T(128)S(1)} %stack.39.left_ref.place_ref, bf16[512,512]{1,0:T(8,128)(2,1)S(1)} %fusion.3.q_ref, bf16[2,512,128]{2,1,0:T(8,128)(2,1)S(1)} %get-tuple-element.68.refs_0_, bf16[2,512,128]{2,1,0:T(8,128)(2,1)S(1)} %collective-permute-done.12.refs_1_, ...), custom_call_target="tpu_custom_call" | custom-call | flops 9663676416 | bytes 1048576 | tf_op jit(solution)/shard_map/attend_open/pallas_call | solution.py:218
  100.0 4.1 %attend_close.3.att_ref = bf16[512,512]{1,0:T(8,128)(2,1)} custom-call(s32[10]{0:T(128)S(1)} %stack.39.left_ref.place_ref, bf16[512,512]{1,0:T(8,128)(2,1)S(1)} %fusion.3.q_ref, f32[512,1024]{1,0:T(8,128)S(1)} %get-tuple-element.76.wide_ref, f32[512,512]{1,0:T(8,128)S(1)} %get-tuple-element.77.top_ref, bf16[2,512,128]{2,1,0:T(8,128)(2,1)S(1)} %collective-permute-done.15.refs_0_), custom_call_target="tpu_custom_call" | custom-call | flops 134217728 | bytes 1048576 | tf_op jit(solution)/shard_map/attend_close/pallas_call | solution.py:218
  111.8 10.3 %collective-permute-done.34 = bf16[512,512]{1,0:T(8,128)(2,1)} collective-permute-done((bf16[512,512]{1,0:T(8,128)(2,1)}, bf16[512,512]{1,0:T(8,128)(2,1)}, u32[]{:S(2)}, u32[]{:S(2)}) %collective-permute-start.34) | collective-permute-done | bytes 524320 | tf_op jit(solution)/shard_map/ppermute | solution.py:544
  133.5 5.1 %collective-permute-done.19 = bf16[128,1024]{1,0:T(8,128)(2,1)S(1)} collective-permute-done((bf16[128,1024]{1,0:T(8,128)(2,1)S(1)}, bf16[128,1024]{1,0:T(8,128)(2,1)S(1)}, u32[]{:S(2)}, u32[]{:S(2)}) %collective-permute-start.19) | collective-permute-done | bytes 262176 | tf_op jit(solution)/shard_map/ppermute | solution.py:544
  142.4 4.1 %collective-permute-done.20 = bf16[128,1024]{1,0:T(8,128)(2,1)S(1)} collective-permute-done((bf16[128,1024]{1,0:T(8,128)(2,1)S(1)}, bf16[128,1024]{1,0:T(8,128)(2,1)S(1)}, u32[]{:S(2)}, u32[]{:S(2)}) %collective-permute-start.20) | collective-permute-done | bytes 262176 | tf_op jit(solution)/shard_map/ppermute | solution.py:544
  153.4 8.1 %collective-permute-done.36 = bf16[256,512]{1,0:T(8,128)(2,1)S(1)} collective-permute-done((bf16[256,512]{1,0:T(8,128)(2,1)S(1)}, bf16[256,512]{1,0:T(8,128)(2,1)S(1)}, u32[]{:S(2)}, u32[]{:S(2)}) %collective-permute-start.36) | collective-permute-done | bytes 262176 | tf_op jit(solution)/shard_map/ppermute | solution.py:544
  170.0 9.1 %collective-permute-done.35 = bf16[256,512]{1,0:T(8,128)(2,1)S(1)} collective-permute-done((bf16[256,512]{1,0:T(8,128)(2,1)S(1)}, bf16[256,512]{1,0:T(8,128)(2,1)S(1)}, u32[]{:S(2)}, u32[]{:S(2)}) %collective-permute-start.35) | collective-permute-done | bytes 262176 | tf_op jit(solution)/shard_map/ppermute | solution.py:544
  189.0 3.1 %collective-permute-start.40 = (bf16[128,512]{1,0:T(8,128)(2,1)S(1)}, bf16[128,512]{1,0:T(8,128)(2,1)S(1)}, u32[]{:S(2)}, u32[]{:S(2)}) collective-permute-start(bf16[128,512]{1,0:T(8,128)(2,1)S(1)} %fusion.16.refs_0_), channel_id=1, source_target_pairs={{0,16},{8,24},{16,0},{24,8},{1,17},{9,25},{17,1},{25,9},{2,18},{10... | collective-permute-start | bytes 393224 | tf_op jit(solution)/shard_map/ppermute | solution.py:544
  192.1 2.7 %collective-permute-start.48 = (bf16[128,512]{1,0:T(8,128)(2,1)S(1)}, bf16[128,512]{1,0:T(8,128)(2,1)S(1)}, u32[]{:S(2)}, u32[]{:S(2)}) collective-permute-start(bf16[128,512]{1,0:T(8,128)(2,1)S(1)} %collective-permute-done.39.refs_1_), channel_id=1, source_target_pairs={{0,8},{8,0},{16,24},{24,16},{1,9},{9,1},{17,25},{25,17},{2,10},{10... | collective-permute-start | bytes 393224 | tf_op jit(solution)/shard_map/ppermute | solution.py:544
  198.1 2.7 %collective-permute-start.41 = (bf16[128,512]{1,0:T(8,128)(2,1)S(1)}, bf16[128,512]{1,0:T(8,128)(2,1)S(1)}, u32[]{:S(2)}, u32[]{:S(2)}) collective-permute-start(bf16[128,512]{1,0:T(8,128)(2,1)S(1)} %fusion.16.refs_0_), channel_id=1, source_target_pairs={{0,8},{8,0},{16,24},{24,16},{1,9},{9,1},{17,25},{25,17},{2,10},{10... | collective-permute-start | bytes 393224 | tf_op jit(solution)/shard_map/ppermute | solution.py:544
  207.6 3.6 %assemble.3 = f32[384,1536]{1,0:T(8,128)} custom-call(s32[10]{0:T(128)S(1)} %stack.39.left_ref.place_ref, bf16[96,768]{1,0:T(8,128)(2,1)S(1)} %fusion.15.refs_0_, bf16[96,768]{1,0:T(8,128)(2,1)S(1)} %collective-permute-done.24.refs_1_, bf16[96,768]{1,0:T(8,128)(2,1)S(1)} %collective-permute-done.25.refs_2_, ...), custom_call_target="tpu_custom_call" | custom-call | flops 589824 | bytes 3538944 | tf_op jit(solution)/shard_map/assemble/pallas_call | solution.py:522
  211.2 3.4 %assemble.4.refs_8_ = f32[512,2048]{1,0:T(8,128)} custom-call(s32[10]{0:T(128)S(1)} %stack.39.left_ref.place_ref, bf16[128,512]{1,0:T(8,128)(2,1)S(1)} %fusion.17.refs_0_, bf16[128,512]{1,0:T(8,128)(2,1)S(1)} %collective-permute-done.39.refs_1_, bf16[128,512]{1,0:T(8,128)(2,1)S(1)} %collective-permute-done.47.refs_2_, ...), custom_call_target="tpu_custom_call" | custom-call | flops 1048576 | bytes 6291456 | tf_op jit(solution)/shard_map/assemble/pallas_call | solution.py:522
  216.0 3.4 %assemble.5 = f32[512,2048]{1,0:T(8,128)} custom-call(s32[10]{0:T(128)S(1)} %stack.39.left_ref.place_ref, bf16[128,512]{1,0:T(8,128)(2,1)S(1)} %fusion.16.refs_0_, bf16[128,512]{1,0:T(8,128)(2,1)S(1)} %collective-permute-done.40.refs_1_, bf16[128,512]{1,0:T(8,128)(2,1)S(1)} %collective-permute-done.41.refs_2_, ...), custom_call_target="tpu_custom_call", output_to_operand_aliasing={{}: (9, {})} | custom-call | flops 1048576 | bytes 6291456 | tf_op jit(solution)/shard_map/assemble/pallas_call | solution.py:522
  (186 shorter events, 93.4 us)
Async XLA Ops:
  0.6 31.5 %collective-permute-start.3 = (bf16[384,1536]{1,0:T(8,128)(2,1)}, bf16[384,1536]{1,0:T(8,128)(2,1)}, u32[]{:S(2)}, u32[]{:S(2)}) collective-permute-start(bf16[384,1536]{1,0:T(8,128)(2,1)} %w0.1), channel_id=1, source_target_pairs={{0,2},{1,3},{2,0},{3,1},{4,6},{5,7},{6,4},{7,5},{8,10},{9,11},{10,... | collective-permute-start | bytes 3538952 | tf_op jit(solution)/shard_map/ppermute | solution.py:544
  7.9 14.5 %collective-permute-start = (bf16[2,512,128]{2,1,0:T(8,128)(2,1)S(1)}, bf16[2,512,128]{2,1,0:T(8,128)(2,1)S(1)}, u32[]{:S(2)}, u32[]{:S(2)}) collective-permute-start(bf16[2,512,128]{2,1,0:T(8,128)(2,1)S(1)} %get-tuple-element.55.refs_0_), channel_id=1, source_target_pairs={{0,16},{8,24},{16,0},{24,8},{1,17},{9,25},{17,1},{25,9},{2,18},{10... | collective-permute-start | bytes 786440 | tf_op jit(solution)/shard_map/ppermute | solution.py:544
  11.9 12.1 %collective-permute-start.1 = (bf16[2,512,128]{2,1,0:T(8,128)(2,1)S(1)}, bf16[2,512,128]{2,1,0:T(8,128)(2,1)S(1)}, u32[]{:S(2)}, u32[]{:S(2)}) collective-permute-start(bf16[2,512,128]{2,1,0:T(8,128)(2,1)S(1)} %get-tuple-element.55.refs_0_), channel_id=1, source_target_pairs={{0,8},{8,0},{16,24},{24,16},{1,9},{9,1},{17,25},{25,17},{2,10},{10... | collective-permute-start | bytes 786440 | tf_op jit(solution)/shard_map/ppermute | solution.py:544
  13.5 30.2 %collective-permute-start.5 = (bf16[384,1536]{1,0:T(8,128)(2,1)}, bf16[384,1536]{1,0:T(8,128)(2,1)}, u32[]{:S(2)}, u32[]{:S(2)}) collective-permute-start(bf16[384,1536]{1,0:T(8,128)(2,1)} %w0.1), channel_id=1, source_target_pairs={{0,1},{1,0},{2,3},{3,2},{4,5},{5,4},{6,7},{7,6},{8,9},{9,8},{10,11... | collective-permute-start | bytes 3538952 | tf_op jit(solution)/shard_map/ppermute | solution.py:544
  32.1 14.8 %collective-permute-start.8 = (bf16[384,1536]{1,0:T(8,128)(2,1)}, bf16[384,1536]{1,0:T(8,128)(2,1)S(1)}, u32[]{:S(2)}, u32[]{:S(2)}) collective-permute-start(bf16[384,1536]{1,0:T(8,128)(2,1)} %collective-permute-done.3.w2), channel_id=1, source_target_pairs={{0,1},{1,0},{2,3},{3,2},{4,5},{5,4},{6,7},{7,6},{8,9},{9,8},{10,11... | collective-permute-start | bytes 3538952 | tf_op jit(solution)/shard_map/ppermute | solution.py:544
  32.2 11.5 %collective-permute-start.6 = (bf16[512,384]{1,0:T(8,128)(2,1)S(1)}, bf16[512,384]{1,0:T(8,128)(2,1)S(1)}, u32[]{:S(2)}, u32[]{:S(2)}) collective-permute-start(bf16[512,384]{1,0:T(8,128)(2,1)S(1)} %attend_close.2.t0), channel_id=1, source_target_pairs={{0,2},{1,3},{2,0},{3,1},{4,6},{5,7},{6,4},{7,5},{8,10},{9,11},{10,... | collective-permute-start | bytes 1179656 | tf_op jit(solution)/shard_map/ppermute | solution.py:544
  52.7 14.6 %collective-permute-start.10 = (bf16[512,512]{1,0:T(8,128)(2,1)}, bf16[512,512]{1,0:T(8,128)(2,1)}, u32[]{:S(2)}, u32[]{:S(2)}) collective-permute-start(bf16[512,512]{1,0:T(8,128)(2,1)} %get-tuple-element.60.e0), channel_id=1, source_target_pairs={{0,2},{1,3},{2,0},{3,1},{4,6},{5,7},{6,4},{7,5},{8,10},{9,11},{10,... | collective-permute-start | bytes 1572872 | tf_op jit(solution)/shard_map/ppermute | solution.py:544
  53.3 15.5 %collective-permute-start.9 = (bf16[512,512]{1,0:T(8,128)(2,1)}, bf16[512,512]{1,0:T(8,128)(2,1)}, u32[]{:S(2)}, u32[]{:S(2)}) collective-permute-start(bf16[512,512]{1,0:T(8,128)(2,1)} %get-tuple-element.60.e0), channel_id=1, source_target_pairs={{0,1},{1,0},{2,3},{3,2},{4,5},{5,4},{6,7},{7,6},{8,9},{9,8},{10,11... | collective-permute-start | bytes 1572872 | tf_op jit(solution)/shard_map/ppermute | solution.py:544
  72.3 15.6 %collective-permute-start.12 = (bf16[2,512,128]{2,1,0:T(8,128)(2,1)S(1)}, bf16[2,512,128]{2,1,0:T(8,128)(2,1)S(1)}, u32[]{:S(2)}, u32[]{:S(2)}) collective-permute-start(bf16[2,512,128]{2,1,0:T(8,128)(2,1)S(1)} %get-tuple-element.68.refs_0_), channel_id=1, source_target_pairs={{0,16},{8,24},{16,0},{24,8},{1,17},{9,25},{17,1},{25,9},{2,18},{10... | collective-permute-start | bytes 786440 | tf_op jit(solution)/shard_map/ppermute | solution.py:544
  79.0 20.1 %collective-permute-start.14 = (bf16[384,768]{1,0:T(8,128)(2,1)S(1)}, bf16[384,768]{1,0:T(8,128)(2,1)S(1)}, u32[]{:S(2)}, u32[]{:S(2)}) collective-permute-start(bf16[384,768]{1,0:T(8,128)(2,1)S(1)} %convolution_convert_fusion), channel_id=1, source_target_pairs={{0,4},{4,0},{1,5},{5,1},{2,6},{6,2},{3,7},{7,3},{8,12},{12,8},{9,1... | collective-permute-start | bytes 1769480 | tf_op jit(solution)/shard_map/ppermute | solution.py:544
  82.0 11.5 %collective-permute-start.13 = (bf16[2,512,128]{2,1,0:T(8,128)(2,1)S(1)}, bf16[2,512,128]{2,1,0:T(8,128)(2,1)S(1)}, u32[]{:S(2)}, u32[]{:S(2)}) collective-permute-start(bf16[2,512,128]{2,1,0:T(8,128)(2,1)S(1)} %get-tuple-element.68.refs_0_), channel_id=1, source_target_pairs={{0,8},{8,0},{16,24},{24,16},{1,9},{9,1},{17,25},{25,17},{2,10},{10... | collective-permute-start | bytes 786440 | tf_op jit(solution)/shard_map/ppermute | solution.py:544
  107.5 14.6 %collective-permute-start.34 = (bf16[512,512]{1,0:T(8,128)(2,1)}, bf16[512,512]{1,0:T(8,128)(2,1)}, u32[]{:S(2)}, u32[]{:S(2)}) collective-permute-start(bf16[512,512]{1,0:T(8,128)(2,1)} %attend_close.3.att_ref), channel_id=1, source_target_pairs={{0,4},{4,0},{1,5},{5,1},{2,6},{6,2},{3,7},{7,3},{8,12},{12,8},{9,1... | collective-permute-start | bytes 1572872 | tf_op jit(solution)/shard_map/ppermute | solution.py:544
  111.0 14.3 %collective-permute-start.17 = (bf16[128,2048]{1,0:T(8,128)(2,1)}, bf16[128,2048]{1,0:T(8,128)(2,1)}, u32[]{:S(2)}, u32[]{:S(2)}) collective-permute-start(bf16[128,2048]{1,0:T(8,128)(2,1)} %add_convert_fusion), channel_id=1, source_target_pairs={{0,2},{1,3},{2,0},{3,1},{4,6},{5,7},{6,4},{7,5},{8,10},{9,11},{10,... | collective-permute-start | bytes 1572872 | tf_op jit(solution)/shard_map/ppermute | solution.py:544
  111.7 11.6 %collective-permute-start.18 = (bf16[192,768]{1,0:T(8,128)(2,1)S(1)}, bf16[192,768]{1,0:T(8,128)(2,1)}, u32[]{:S(2)}, u32[]{:S(2)}) collective-permute-start(bf16[192,768]{1,0:T(8,128)(2,1)S(1)} %get-tuple-element.81), channel_id=1, source_target_pairs={{0,8},{8,0},{16,24},{24,16},{1,9},{9,1},{17,25},{25,17},{2,10},{10... | collective-permute-start | bytes 884744 | tf_op jit(solution)/shard_map/ppermute | solution.py:544
  129.2 11.4 %collective-permute-start.31 = (bf16[128,1024]{1,0:T(8,128)(2,1)S(1)}, bf16[128,1024]{1,0:T(8,128)(2,1)S(1)}, u32[]{:S(2)}, u32[]{:S(2)}) collective-permute-start(bf16[128,1024]{1,0:T(8,128)(2,1)S(1)} %get-tuple-element.93), channel_id=1, source_target_pairs={{0,2},{1,3},{2,0},{3,1},{4,6},{5,7},{6,4},{7,5},{8,10},{9,11},{10,... | collective-permute-start | bytes 786440 | tf_op jit(solution)/shard_map/ppermute | solution.py:544
  129.9 11.3 %collective-permute-start.32 = (bf16[128,1024]{1,0:T(8,128)(2,1)S(1)}, bf16[128,1024]{1,0:T(8,128)(2,1)S(1)}, u32[]{:S(2)}, u32[]{:S(2)}) collective-permute-start(bf16[128,1024]{1,0:T(8,128)(2,1)S(1)} %get-tuple-element.93), channel_id=1, source_target_pairs={{0,1},{1,0},{2,3},{3,2},{4,5},{5,4},{6,7},{7,6},{8,9},{9,8},{10,11... | collective-permute-start | bytes 786440 | tf_op jit(solution)/shard_map/ppermute | solution.py:544
  148.7 16.7 %collective-permute-start.24 = (bf16[96,768]{1,0:T(8,128)(2,1)S(1)}, bf16[96,768]{1,0:T(8,128)(2,1)S(1)}, u32[]{:S(2)}, u32[]{:S(2)}) collective-permute-start(bf16[96,768]{1,0:T(8,128)(2,1)S(1)} %fusion.15.refs_0_), channel_id=1, source_target_pairs={{0,16},{8,24},{16,0},{24,8},{1,17},{9,25},{17,1},{25,9},{2,18},{10... | collective-permute-start | bytes 442376 | tf_op jit(solution)/shard_map/ppermute | solution.py:544
  163.3 15.8 %collective-permute-start.35 = (bf16[256,512]{1,0:T(8,128)(2,1)S(1)}, bf16[256,512]{1,0:T(8,128)(2,1)S(1)}, u32[]{:S(2)}, u32[]{:S(2)}) collective-permute-start(bf16[256,512]{1,0:T(8,128)(2,1)S(1)} %get-tuple-element.96), channel_id=1, source_target_pairs={{0,8},{8,0},{16,24},{24,16},{1,9},{9,1},{17,25},{25,17},{2,10},{10... | collective-permute-start | bytes 786440 | tf_op jit(solution)/shard_map/ppermute | solution.py:544
  165.2 17.0 %collective-permute-start.25 = (bf16[96,768]{1,0:T(8,128)(2,1)S(1)}, bf16[96,768]{1,0:T(8,128)(2,1)S(1)}, u32[]{:S(2)}, u32[]{:S(2)}) collective-permute-start(bf16[96,768]{1,0:T(8,128)(2,1)S(1)} %fusion.15.refs_0_), channel_id=1, source_target_pairs={{0,8},{8,0},{16,24},{24,16},{1,9},{9,1},{17,25},{25,17},{2,10},{10... | collective-permute-start | bytes 442376 | tf_op jit(solution)/shard_map/ppermute | solution.py:544
  165.4 18.8 %collective-permute-start.26 = (bf16[96,768]{1,0:T(8,128)(2,1)S(1)}, bf16[96,768]{1,0:T(8,128)(2,1)S(1)}, u32[]{:S(2)}, u32[]{:S(2)}) collective-permute-start(bf16[96,768]{1,0:T(8,128)(2,1)S(1)} %collective-permute-done.24.refs_1_), channel_id=1, source_target_pairs={{0,8},{8,0},{16,24},{24,16},{1,9},{9,1},{17,25},{25,17},{2,10},{10... | collective-permute-start | bytes 442376 | tf_op jit(solution)/shard_map/ppermute | solution.py:544
  169.9 15.2 %collective-permute-start.39 = (bf16[128,512]{1,0:T(8,128)(2,1)S(1)}, bf16[128,512]{1,0:T(8,128)(2,1)S(1)}, u32[]{:S(2)}, u32[]{:S(2)}) collective-permute-start(bf16[128,512]{1,0:T(8,128)(2,1)S(1)} %fusion.17.refs_0_), channel_id=1, source_target_pairs={{0,16},{8,24},{16,0},{24,8},{1,17},{9,25},{17,1},{25,9},{2,18},{10... | collective-permute-start | bytes 393224 | tf_op jit(solution)/shard_map/ppermute | solution.py:544
  186.3 11.8 %collective-permute-start.49 = (bf16[128,512]{1,0:T(8,128)(2,1)S(1)}, bf16[128,512]{1,0:T(8,128)(2,1)S(1)}, u32[]{:S(2)}, u32[]{:S(2)}) collective-permute-start(bf16[128,512]{1,0:T(8,128)(2,1)S(1)} %fusion.17.refs_0_), channel_id=1, source_target_pairs={{0,4},{4,0},{1,5},{5,1},{2,6},{6,2},{3,7},{7,3},{8,12},{12,8},{9,1... | collective-permute-start | bytes 393224 | tf_op jit(solution)/shard_map/ppermute | solution.py:544
  189.0 11.9 %collective-permute-start.40 = (bf16[128,512]{1,0:T(8,128)(2,1)S(1)}, bf16[128,512]{1,0:T(8,128)(2,1)S(1)}, u32[]{:S(2)}, u32[]{:S(2)}) collective-permute-start(bf16[128,512]{1,0:T(8,128)(2,1)S(1)} %fusion.16.refs_0_), channel_id=1, source_target_pairs={{0,16},{8,24},{16,0},{24,8},{1,17},{9,25},{17,1},{25,9},{2,18},{10... | collective-permute-start | bytes 393224 | tf_op jit(solution)/shard_map/ppermute | solution.py:544
  201.8 12.7 %collective-permute-start.43 = (bf16[128,512]{1,0:T(8,128)(2,1)S(1)}, bf16[128,512]{1,0:T(8,128)(2,1)S(1)}, u32[]{:S(2)}, u32[]{:S(2)}) collective-permute-start(bf16[128,512]{1,0:T(8,128)(2,1)S(1)} %fusion.16.refs_0_), channel_id=1, source_target_pairs={{0,4},{4,0},{1,5},{5,1},{2,6},{6,2},{3,7},{7,3},{8,12},{12,8},{9,1... | collective-permute-start | bytes 393224 | tf_op jit(solution)/shard_map/ppermute | solution.py:544
  (52 other events, 456.0 us)

commit v7 on v6

--- a/solution.py
+++ b/solution.py
@@ -19,6 +19,7 @@
 TABLE = 6
 ROWS = (0, 2, 1, 3)
 LIMIT = 40 * 2**20
+HIGH = 56 * 2**20
 VMEM = pl.BlockSpec(memory_space=pltpu.VMEM)
 SMEM = pl.BlockSpec(memory_space=pltpu.SMEM)
 ANY = pl.BlockSpec(memory_space=pl.ANY)
@@ -86,7 +87,7 @@
             pltpu.VMEM((depth, 2 * width), BF16),
             pltpu.SemaphoreType.DMA((4,)),
         ],
-        compiler_params=pltpu.CompilerParams(vmem_limit_bytes=LIMIT),
+        compiler_params=pltpu.CompilerParams(vmem_limit_bytes=HIGH),
         cost_estimate=pl.CostEstimate(
             flops=4 * rows * depth * width, bytes_accessed=2 * rows * depth, transcendentals=0
         ),
@@ -113,7 +114,7 @@
             pltpu.VMEM((depth, width), BF16),
             pltpu.SemaphoreType.DMA((2,)),
         ],
-        compiler_params=pltpu.CompilerParams(vmem_limit_bytes=LIMIT),
+        compiler_params=pltpu.CompilerParams(vmem_limit_bytes=HIGH),
         cost_estimate=pl.CostEstimate(
             flops=2 * rows * depth * width, bytes_accessed=2 * rows * depth, transcendentals=0
         ),
@@ -395,17 +396,14 @@
 
 
 def mixed_kernel(
-    place_ref, emb_any, keep_ref, near_ref, got_ref, wv_ref, ret_ref,
-    value_ref, other_ref, own_ref, emb_ref, mixed_ref, sem,
+    place_ref, emb_ref, keep_ref, near_ref, got_ref, wv_ref, ret_ref,
+    value_ref, other_ref, own_ref, mixed_ref,
 ):
     rows, wide = got_ref.shape
     half = wide // 2
     block = 32
-    base = pl.multiple_of(place_ref[1] * rows, rows)
-    copy = pltpu.make_async_copy(emb_any.at[pl.ds(base, rows)], emb_ref, sem)
-    copy.start()
+    base = place_ref[1] * rows
     live_total = place_ref[4].astype(F32)
-    copy.wait()
 
     @pl.loop(0, rows // block)
     def _(i):
@@ -432,18 +430,14 @@
     rows, wide = got.shape
     return pl.pallas_call(
         mixed_kernel,
-        in_specs=[SMEM, ANY] + [VMEM] * 5,
+        in_specs=[SMEM] + [VMEM] * 6,
         out_specs=[VMEM] * 3,
         out_shape=[
             jax.ShapeDtypeStruct((rows, HEAD), F32),
             jax.ShapeDtypeStruct((rows, wide // 2), BF16),
             jax.ShapeDtypeStruct((rows, wide // 2), BF16),
         ],
-        scratch_shapes=[
-            pltpu.VMEM((rows, wide), BF16),
-            pltpu.VMEM((32, wide), F32),
-            pltpu.SemaphoreType.DMA,
-        ],
+        scratch_shapes=[pltpu.VMEM((32, wide), F32)],
         compiler_params=pltpu.CompilerParams(vmem_limit_bytes=LIMIT),
         cost_estimate=pl.CostEstimate(
             flops=10 * rows * wide, bytes_accessed=12 * rows * wide, transcendentals=0
@@ -621,6 +615,7 @@
     attended_far = swap(attended, "mdl", 2)
     attended_near = swap(attended, "mdl", 1)
     near_sum = near_rows(obs_in, [attended, attended_near], [a_out, swap(a_out, "mdl", 1)])
+    attended_far, near_sum = tied(attended_far, near_sum)
     hidden, embed_part = hidden_rows(
         near_sum,
         [attended_far, swap(attended_far, "mdl", 1)],
@@ -631,12 +626,12 @@
     embed_parts, _ = gather_parts(embed_part)
     critic_keyval, factor_c, embedded = join_rows(place, embed_parts, c_keyval)
     critic_queries = (dot(embedded, c_query) * (factor_c[:, :1] * score_scale)).astype(BF16)
-    late_keyval, critic_queries = tied(critic_keyval, critic_queries)
-    pieces_c = gather_blocks(critic_keyval, "rep", late_keyval)
 
     late_hidden, critic_keyval = tied(hidden, critic_keyval)
     source = late_hidden.astype(F32)
     factor_h = row_factor(source)
+    late_keyval, factor_h = tied(critic_keyval, factor_h)
+    pieces_c = gather_blocks(critic_keyval, "rep", late_keyval)
     logits = dot(late_hidden, w_policy) * factor_h
     log_probs = jax.nn.log_softmax(logits, axis=-1)
     onehot = (
@@ -662,8 +657,13 @@
 
     wide = w_value.shape[0]
     target = lax.dynamic_slice_in_dim(returns[0], mdl_index * value_rows, value_rows, 0)
-    critic_queries, own_a, w_row, target = tied(
-        critic_queries, own_a, w_value.reshape(1, wide), target.reshape(value_rows, 1)
+    emb_mine = lax.dynamic_slice_in_dim(embedded, mdl_index * value_rows, value_rows, 0)
+    critic_queries, own_a, w_row, target, emb_mine = tied(
+        critic_queries,
+        own_a,
+        w_value.reshape(1, wide),
+        target.reshape(value_rows, 1),
+        emb_mine,
     )
     state_c = attend_call(critic_queries, pieces_c[:-1], 0, place, [])
     *state_c, got_a, pieces_c[-1] = tied(*state_c, got_a, pieces_c[-1])
@@ -674,28 +674,30 @@
 
     send_m, keep_m, att_rows = part_rows(place, critic_attended, c_out)
     near_m = swap(send_m, "mdl", 1)
-    send_y = (keep_m[value_rows:] + near_m[value_rows:].astype(F32)).astype(BF16)
-    got_y = swap(send_y, "mdl", 2)
-    att_there = swap(critic_attended, "sec", 1)
-    got_y, moved_a = tied(got_y, moved_a)
-    value_wide, d_other, d_own = mixed_rows(
-        place, embedded, keep_m, near_m, got_y, w_row, target
-    )
-
-    d_there = swap(d_other, "sec", 1)
-    d_far = swap(d_own, "mdl", 2)
-    d_near = swap(d_own, "mdl", 1)
+    near_m, moved_a = tied(near_m, moved_a)
     bit = 2
     while bit < rep_count:
         keep_a, send_a = halve(keep_a, moved_a)
         moved_a = swap(send_a, "rep", bit)
         bit *= 2
-    there_far = swap(d_there, "mdl", 2)
-    there_near = swap(d_there, "mdl", 1)
-    own_rows = jnp.concatenate([d_own, d_far, d_near, swap(d_far, "mdl", 1)], axis=0)
-    there_far, moved_a = tied(there_far, moved_a)
+    send_y = (keep_m[value_rows:] + near_m[value_rows:].astype(F32)).astype(BF16)
+    got_y = swap(send_y, "mdl", 2)
+    att_there = swap(critic_attended, "sec", 1)
+    mine_a = gather_blocks((keep_a + moved_a.astype(F32)).astype(BF16), "rep")
+    got_y, *mine_a[1:-1] = tied(got_y, *mine_a[1:-1])
+    value_wide, d_other, d_own = mixed_rows(
+        place, emb_mine, keep_m, near_m, got_y, w_row, target
+    )
+
+    d_there = swap(d_other, "sec", 1)
+    d_far = swap(d_own, "mdl", 2)
+    there_far = swap(d_other, ("sec", "mdl"), mdl_count | 2)
+    d_far, mine_a[-1] = tied(d_far, mine_a[-1])
+    own_rows = jnp.concatenate(
+        [d_own, d_far, swap(d_own, "mdl", 1), swap(d_far, "mdl", 1)], axis=0
+    )
     there_rows = jnp.concatenate(
-        [d_there, there_far, there_near, swap(there_far, "mdl", 1)], axis=0
+        [d_there, there_far, swap(d_there, "mdl", 1), swap(there_far, "mdl", 1)], axis=0
     )
     att_there = jnp.concatenate(
         [
@@ -705,12 +707,11 @@
         axis=0,
     )
     value_part, there_rows = tied(value_wide[:, 0], there_rows)
-    mine_a = gather_blocks((keep_a + moved_a.astype(F32)).astype(BF16), "rep")
     theirs_a = [swap(block, "sec", 1) for block in mine_a]
     actor_summed = assemble(place, mine_a + theirs_a, rep_count, 0, 1, [])
 
     strip = d_own.shape[1] // CHUNKS
-    marks, result = [], []
+    chunks = []
     for c in range(CHUNKS):
         span = slice(c * strip, (c + 1) * strip)
         keep, send = split_sum(
@@ -719,22 +720,44 @@
             product(att_there, there_rows[:, span]),
             rep_count,
         )
-        bit, trail = 1, []
-        while bit < rep_count:
-            arrived = swap(send.astype(BF16), "rep", bit)
-            bit *= 2
-            if c > 0:
-                arrived, _ = tied(arrived, marks[min(len(trail) + 1, len(marks) - 1)])
-            if bit < rep_count:
-                keep, send = halve(keep, arrived)
-                trail.append(keep)
-        total = (keep + arrived.astype(F32)).astype(BF16)
-        trail.append(total)
-        mine = gather_blocks(total, "rep")
-        trail.append(mine[1])
-        marks = trail
-        theirs = [swap(block, "sec", 1) for block in mine]
-        result = [assemble(place, mine + theirs, rep_count, c, CHUNKS, result)]
+        chunks.append([keep, [swap(send.astype(BF16), "rep", 1)], [], [], []])
+    levels = rep_count.bit_length() - 1
+    for tick in range(2 * levels + CHUNKS - 1):
+        turn = [c for c in range(CHUNKS) if 0 <= tick - c < 2 * levels]
+        waited = [item for c in turn for item in chunks[c][1] + chunks[c][3]]
+        extra = []
+        if tick == 0:
+            extra = [chunks[c][0] for c in range(1, CHUNKS)] + theirs_a
+        if tick == levels:
+            extra = [actor_summed]
+        outs = list(tied(*waited, *extra))
+        if tick == 0:
+            for c in range(1, CHUNKS):
+                chunks[c][0] = outs[len(waited) + c - 1]
+        if tick == levels:
+            actor_summed = outs[-1]
+        for c in turn:
+            keep, pending, mine, crossing, theirs = chunks[c]
+            arrived, outs = outs[: len(pending)], outs[len(pending) :]
+            crossed, outs = outs[: len(crossing)], outs[len(crossing) :]
+            theirs = theirs + crossed
+            level = tick - c + 1
+            if level < levels:
+                keep, send = halve(keep, arrived[0])
+                pending = [swap(send, "rep", 1 << level)]
+            else:
+                fresh = arrived
+                if level == levels:
+                    fresh = [(keep + arrived[0].astype(F32)).astype(BF16)]
+                mine = mine + fresh
+                crossing = [swap(block, "sec", 1) for block in fresh]
+                bit = rep_count >> (level - levels + 1)
+                pending = [swap(block, "rep", bit) for block in mine] if bit else []
+            chunks[c] = [keep, pending, mine, crossing, theirs]
+    result = []
+    for c in range(CHUNKS):
+        _, _, mine, crossing, theirs = chunks[c]
+        result = [assemble(place, mine + theirs + crossing, rep_count, c, CHUNKS, result)]
 
     return (value_part[None, :], actor_summed, result[0])
 

time: 220 us -> 219 us (level)
  starting transfers between devices: 54.4 us -> 44.8 us
  Pallas kernels: 43.9 us -> 49.2 us
  waiting for transfers between devices: 94.4 us -> 99.2 us
    ppermute x53, starting transfers between devices: 54.4 us -> 44.8 us  [swap(): return lax.ppermute(block, axis, [(i, i ^ bit) for i in range(size)])]
    ppermute x53, waiting for transfers between devices: 94.4 us -> 99.2 us  [swap(): return lax.ppermute(block, axis, [(i, i ^ bit) for i in range(size)])]
    pallas_call x1, Pallas kernels: 1.34 us -> 4.46 us  [query_projection(): pl.pallas_call(functools.partial(query_kernel, scale), in_specs=[HBM, HBM...]
    unnamed x49 -> x47, local copies, waits for them, and re-layouts: 7.03 us -> 5.62 us
  transfers between devices with their start and end apart: 53 -> 53, of which waited for: 26 -> 30; matrix products, arithmetic and copies ran while one was open for 7% -> 7% of each run, Pallas kernels for 11% -> 15%
where the time goes in v7:
time: 219 us
  waiting for transfers between devices  99.2 us (45%)
  Pallas kernels  49.2 us (22%)
  starting transfers between devices  44.8 us (20%)
  local copies, waits for them, and re-layouts  12 us (5%)
  matrix products  5.64 us (3%)
  between operations  4.56 us (2%)
  other arithmetic  3.34 us (2%)
    ppermute x53, waiting for transfers between devices, swap(): return lax.ppermute(block, axis, [(i, i ^ bit) for i in range(size)])  99.2 us
    ppermute x53, starting transfers between devices, swap(): return lax.ppermute(block, axis, [(i, i ^ bit) for i in range(size)])  44.8 us
    pallas_call x4, Pallas kernels, attend_call(): pl.pallas_call(functools.partial(body, groups, units, TABLE + first), in_...  15 us
    pallas_call x3, Pallas kernels, assemble(): pl.pallas_call(functools.partial(assemble_kernel, gather_codes(count), ch...  10.1 us
    unnamed x47, local copies, waits for them, and re-layouts  5.62 us
    pallas_call x1, Pallas kernels, hidden_rows(): pl.pallas_call(hidden_kernel, in_specs=[VMEM] * 3 + [ANY] * 2 + [HBM], ou...  4.46 us
    pallas_call x1, Pallas kernels, query_projection(): pl.pallas_call(functools.partial(query_kernel, scale), in_specs=[HBM, HBM...  4.46 us
  transfers between devices with their start and end apart: 53, of which 30 were waited for; matrix products, arithmetic and copies ran while one was open for 7% of the time, Pallas kernels for 15%

profile of v7, /device:TPU:0, one launch (start us, length us, event | category | flops | bytes accessed | tf_op | source)
XLA Modules:
  0.0 218.8 jit_solution(13543304593870666735)
XLA Ops:
  0.6 3.0 %collective-permute-start.3 = (bf16[384,1536]{1,0:T(8,128)(2,1)}, bf16[384,1536]{1,0:T(8,128)(2,1)}, u32[]{:S(2)}, u32[]{:S(2)}) collective-permute-start(bf16[384,1536]{1,0:T(8,128)(2,1)} %w0.1), channel_id=1, source_target_pairs={{0,2},{1,3},{2,0},{3,1},{4,6},{5,7},{6,4},{7,5},{8,10},{9,11},{10,... | collective-permute-start | bytes 3538952 | tf_op jit(solution)/shard_map/ppermute | solution.py:538
  3.7 3.5 %first_projection.1 = (bf16[2,512,128]{2,1,0:T(8,128)(2,1)}, f32[512,128]{1,0:T(8,128)}) custom-call(bf16[512,1536]{1,0:T(8,128)(2,1)} %bitcast.30, bf16[2,1536,128]{2,1,0:T(8,128)(2,1)} %w_hbm.2), custom_call_target="tpu_custom_call" | custom-call | flops 402653184 | bytes 1572864 | tf_op jit(solution)/shard_map/first_projection/pallas_call | solution.py:77
  9.9 4.5 %query_projection.1.q_ref = bf16[512,384]{1,0:T(8,128)(2,1)} custom-call(bf16[512,1536]{1,0:T(8,128)(2,1)} %bitcast.31, bf16[1536,384]{1,0:T(8,128)(2,1)} %w_hbm.3, f32[512,128]{1,0:T(8,128)} %get-tuple-element.74.factor_ref), custom_call_target="tpu_custom_call" | custom-call | flops 603979776 | bytes 1572864 | tf_op jit(solution)/shard_map/query_projection/pallas_call | solution.py:107
  22.6 4.7 %collective-permute-done.1.refs_2_ = bf16[2,512,128]{2,1,0:T(8,128)(2,1)S(1)} collective-permute-done((bf16[2,512,128]{2,1,0:T(8,128)(2,1)S(1)}, bf16[2,512,128]{2,1,0:T(8,128)(2,1)S(1)}, u32[]{:S(2)}, u32[]{:S(2)}) %collective-permute-start.1) | collective-permute-done | bytes 262176 | tf_op jit(solution)/shard_map/ppermute | solution.py:538
  28.3 3.6 %attend_open.2 = (f32[512,768]{1,0:T(8,128)S(1)}, f32[512,384]{1,0:T(8,128)S(1)}) custom-call(s32[10]{0:T(128)S(1)} %stack.39.left_ref.place_ref, bf16[512,384]{1,0:T(8,128)(2,1)S(1)} %copy-done.8, bf16[2,512,128]{2,1,0:T(8,128)(2,1)S(1)} %copy-done.15, bf16[2,512,128]{2,1,0:T(8,128)(2,1)S(1)} %collective-permute-done.refs_1_, ...), custom_call_target="tpu_custom_call" | custom-call | flops 7247757312 | bytes 786432 | tf_op jit(solution)/shard_map/attend_open/pallas_call | solution.py:219
  37.7 3.1 %near_rows.1.sum_ref = f32[512,1536]{1,0:T(8,128)S(1)} custom-call(bf16[512,1536]{1,0:T(8,128)(2,1)S(1)} %bitcast.32, bf16[512,384]{1,0:T(8,128)(2,1)S(1)} %attend_close.2.t0, bf16[512,384]{1,0:T(8,128)(2,1)S(1)} %collective-permute-done.5.t1, bf16[384,1536]{1,0:T(8,128)(2,1)} %w0.1, bf16[384,1536]{1,0:T(8,128)(2,1)} %collective-permute-done.6.w1), custom_call_target="tpu_custom_call" | custom-call | flops 1207959552 | bytes 2359296 | tf_op jit(solution)/shard_map/near_rows/pallas_call | solution.py:249
  40.9 5.4 %collective-permute-done.4.t2 = bf16[512,384]{1,0:T(8,128)(2,1)S(1)} collective-permute-done((bf16[512,384]{1,0:T(8,128)(2,1)S(1)}, bf16[512,384]{1,0:T(8,128)(2,1)S(1)}, u32[]{:S(2)}, u32[]{:S(2)}) %collective-permute-start.4) | collective-permute-done | bytes 393248 | tf_op jit(solution)/shard_map/ppermute | solution.py:538
  47.9 4.5 %hidden_rows.1 = (bf16[512,1536]{1,0:T(8,128)(2,1)S(1)}, bf16[512,512]{1,0:T(8,128)(2,1)}) custom-call(f32[512,1536]{1,0:T(8,128)S(1)} %near_rows.1.sum_ref, bf16[512,384]{1,0:T(8,128)(2,1)S(1)} %collective-permute-done.4.t2, bf16[512,384]{1,0:T(8,128)(2,1)S(1)} %collective-permute-done.7.t3, bf16[384,1536]{1,0:T(8,128)(2,1)} %collective-permute-done.3.w2, ...), custom_call_target="tpu_custom_call" | custom-call | flops 2415919104 | bytes 4718592 | tf_op jit(solution)/shard_map/hidden_rows/pallas_call | solution.py:287
  54.1 13.7 %collective-permute-done.10.e2 = bf16[512,512]{1,0:T(8,128)(2,1)} collective-permute-done((bf16[512,512]{1,0:T(8,128)(2,1)}, bf16[512,512]{1,0:T(8,128)(2,1)}, u32[]{:S(2)}, u32[]{:S(2)}) %collective-permute-start.10) | collective-permute-done | bytes 524320 | tf_op jit(solution)/shard_map/ppermute | solution.py:538
  83.6 4.6 %collective-permute-done.12.refs_1_ = bf16[2,512,128]{2,1,0:T(8,128)(2,1)S(1)} collective-permute-done((bf16[2,512,128]{2,1,0:T(8,128)(2,1)S(1)}, bf16[2,512,128]{2,1,0:T(8,128)(2,1)S(1)}, u32[]{:S(2)}, u32[]{:S(2)}) %collective-permute-start.12) | collective-permute-done | bytes 262176 | tf_op jit(solution)/shard_map/ppermute | solution.py:538
  90.8 4.8 %attend_open.3 = (f32[512,1024]{1,0:T(8,128)S(1)}, f32[512,512]{1,0:T(8,128)S(1)}) custom-call(s32[10]{0:T(128)S(1)} %stack.39.left_ref.place_ref, bf16[512,512]{1,0:T(8,128)(2,1)S(1)} %fusion.3.q_ref, bf16[2,512,128]{2,1,0:T(8,128)(2,1)S(1)} %get-tuple-element.93.refs_0_, bf16[2,512,128]{2,1,0:T(8,128)(2,1)S(1)} %collective-permute-done.12.refs_1_, ...), custom_call_target="tpu_custom_call" | custom-call | flops 9663676416 | bytes 1048576 | tf_op jit(solution)/shard_map/attend_open/pallas_call | solution.py:219
  97.0 4.1 %attend_close.3.att_ref = bf16[512,512]{1,0:T(8,128)(2,1)} custom-call(s32[10]{0:T(128)S(1)} %stack.39.left_ref.place_ref, bf16[512,512]{1,0:T(8,128)(2,1)S(1)} %fusion.3.q_ref, f32[512,1024]{1,0:T(8,128)S(1)} %get-tuple-element.101.wide_ref, f32[512,512]{1,0:T(8,128)S(1)} %get-tuple-element.102.top_ref, bf16[2,512,128]{2,1,0:T(8,128)(2,1)S(1)} %collective-permute-done.15.refs_0_), custom_call_target="tpu_custom_call" | custom-call | flops 134217728 | bytes 1048576 | tf_op jit(solution)/shard_map/attend_close/pallas_call | solution.py:219
  104.1 9.1 %collective-permute-done.17 = bf16[192,768]{1,0:T(8,128)(2,1)S(1)} collective-permute-done((bf16[192,768]{1,0:T(8,128)(2,1)S(1)}, bf16[192,768]{1,0:T(8,128)(2,1)S(1)}, u32[]{:S(2)}, u32[]{:S(2)}) %collective-permute-start.17) | collective-permute-done | bytes 294944 | tf_op jit(solution)/shard_map/ppermute | solution.py:538
  116.7 5.8 %collective-permute-done.19 = bf16[96,768]{1,0:T(8,128)(2,1)S(1)} collective-permute-done((bf16[96,768]{1,0:T(8,128)(2,1)S(1)}, bf16[96,768]{1,0:T(8,128)(2,1)S(1)}, u32[]{:S(2)}, u32[]{:S(2)}) %collective-permute-start.19) | collective-permute-done | bytes 147488 | tf_op jit(solution)/shard_map/ppermute | solution.py:538
  124.8 5.6 %collective-permute-done.21.refs_2_ = bf16[96,768]{1,0:T(8,128)(2,1)S(1)} collective-permute-done((bf16[96,768]{1,0:T(8,128)(2,1)S(1)}, bf16[96,768]{1,0:T(8,128)(2,1)S(1)}, u32[]{:S(2)}, u32[]{:S(2)}) %collective-permute-start.21) | collective-permute-done | bytes 147488 | tf_op jit(solution)/shard_map/ppermute | solution.py:538
  133.8 3.0 %mixed_rows.1 = (f32[128,128]{1,0:T(8,128)S(1)}, bf16[128,1024]{1,0:T(8,128)(2,1)}, bf16[128,1024]{1,0:T(8,128)(2,1)S(1)}) custom-call(s32[10]{0:T(128)S(1)} %stack.39.left_ref.place_ref, bf16[128,2048]{1,0:T(8,128)(2,1)S(1)} %copy-done.5, f32[256,2048]{1,0:T(8,128)S(1)} %get-tuple-element.104.keep_ref, ...), custom_call_target="tpu_custom_call" | custom-call | flops 2621440 | bytes 3145728 | tf_op jit(solution)/shard_map/mixed_rows/pallas_call | solution.py:431
  143.8 4.6 %collective-permute-done.23 = bf16[128,1024]{1,0:T(8,128)(2,1)S(1)} collective-permute-done((bf16[128,1024]{1,0:T(8,128)(2,1)}, bf16[128,1024]{1,0:T(8,128)(2,1)S(1)}, u32[]{:S(2)}, u32[]{:S(2)}) %collective-permute-start.23) | collective-permute-done | bytes 262176 | tf_op jit(solution)/shard_map/ppermute | solution.py:538
  162.7 3.2 %collective-permute-done.34.refs_6_ = bf16[96,768]{1,0:T(8,128)(2,1)S(1)} collective-permute-done((bf16[96,768]{1,0:T(8,128)(2,1)S(1)}, bf16[96,768]{1,0:T(8,128)(2,1)S(1)}, u32[]{:S(2)}, u32[]{:S(2)}) %collective-permute-start.34) | collective-permute-done | bytes 147488 | tf_op jit(solution)/shard_map/ppermute | solution.py:538
  169.3 3.4 %collective-permute-done.37 = bf16[256,512]{1,0:T(8,128)(2,1)S(1)} collective-permute-done((bf16[256,512]{1,0:T(8,128)(2,1)S(1)}, bf16[256,512]{1,0:T(8,128)(2,1)S(1)}, u32[]{:S(2)}, u32[]{:S(2)}) %collective-permute-start.37) | collective-permute-done | bytes 262176 | tf_op jit(solution)/shard_map/ppermute | solution.py:538
  172.7 4.5 %collective-permute-done.36 = bf16[128,512]{1,0:T(8,128)(2,1)S(1)} collective-permute-done((bf16[128,512]{1,0:T(8,128)(2,1)S(1)}, bf16[128,512]{1,0:T(8,128)(2,1)S(1)}, u32[]{:S(2)}, u32[]{:S(2)}) %collective-permute-start.36) | collective-permute-done | bytes 131104 | tf_op jit(solution)/shard_map/ppermute | solution.py:538
  181.8 3.4 %assemble.3 = f32[384,1536]{1,0:T(8,128)} custom-call(s32[10]{0:T(128)S(1)} %stack.39.left_ref.place_ref, bf16[96,768]{1,0:T(8,128)(2,1)S(1)} %fusion.15.refs_0_, bf16[96,768]{1,0:T(8,128)(2,1)} %collective-permute-done.20.refs_1_, bf16[96,768]{1,0:T(8,128)(2,1)S(1)} %collective-permute-done.21.refs_2_, bf16[96,768]{1,0:T(8,128)(2,1)S(1)} %collective-permute-done.27.refs_3_, ...), custom_call_target="tpu_custom_call" | custom-call | flops 589824 | bytes 3538944 | tf_op jit(solution)/shard_map/assemble/pallas_call | solution.py:516
  203.2 3.5 %collective-permute-done.48.refs_5_ = bf16[128,512]{1,0:T(8,128)(2,1)S(1)} collective-permute-done((bf16[128,512]{1,0:T(8,128)(2,1)S(1)}, bf16[128,512]{1,0:T(8,128)(2,1)S(1)}, u32[]{:S(2)}, u32[]{:S(2)}) %collective-permute-start.48) | collective-permute-done | bytes 131104 | tf_op jit(solution)/shard_map/ppermute | solution.py:538
  211.8 3.4 %assemble.4.refs_8_ = f32[512,2048]{1,0:T(8,128)} custom-call(s32[10]{0:T(128)S(1)} %stack.39.left_ref.place_ref, bf16[128,512]{1,0:T(8,128)(2,1)S(1)} %fusion.17.refs_0_, bf16[128,512]{1,0:T(8,128)(2,1)S(1)} %collective-permute-done.38.refs_1_, bf16[128,512]{1,0:T(8,128)(2,1)S(1)} %collective-permute-done.41.refs_2_, ...), custom_call_target="tpu_custom_call" | custom-call | flops 1048576 | bytes 6291456 | tf_op jit(solution)/shard_map/assemble/pallas_call | solution.py:516
  215.2 3.4 %assemble.5 = f32[512,2048]{1,0:T(8,128)} custom-call(s32[10]{0:T(128)S(1)} %stack.39.left_ref.place_ref, bf16[128,512]{1,0:T(8,128)(2,1)S(1)} %fusion.16.refs_0_, bf16[128,512]{1,0:T(8,128)(2,1)S(1)} %collective-permute-done.44.refs_1_, bf16[128,512]{1,0:T(8,128)(2,1)S(1)} %collective-permute-done.46.refs_2_, ...), custom_call_target="tpu_custom_call", output_to_operand_aliasing={{}: (9, {})} | custom-call | flops 1048576 | bytes 6291456 | tf_op jit(solution)/shard_map/assemble/pallas_call | solution.py:516
  (186 shorter events, 102.1 us)
Async XLA Ops:
  0.6 33.9 %collective-permute-start.3 = (bf16[384,1536]{1,0:T(8,128)(2,1)}, bf16[384,1536]{1,0:T(8,128)(2,1)}, u32[]{:S(2)}, u32[]{:S(2)}) collective-permute-start(bf16[384,1536]{1,0:T(8,128)(2,1)} %w0.1), channel_id=1, source_target_pairs={{0,2},{1,3},{2,0},{3,1},{4,6},{5,7},{6,4},{7,5},{8,10},{9,11},{10,... | collective-permute-start | bytes 3538952 | tf_op jit(solution)/shard_map/ppermute | solution.py:538
  7.2 14.7 %collective-permute-start = (bf16[2,512,128]{2,1,0:T(8,128)(2,1)}, bf16[2,512,128]{2,1,0:T(8,128)(2,1)S(1)}, u32[]{:S(2)}, u32[]{:S(2)}) collective-permute-start(bf16[2,512,128]{2,1,0:T(8,128)(2,1)} %get-tuple-element.76.refs_0_), channel_id=1, source_target_pairs={{0,16},{8,24},{16,0},{24,8},{1,17},{9,25},{17,1},{25,9},{2,18},{10... | collective-permute-start | bytes 786440 | tf_op jit(solution)/shard_map/ppermute | solution.py:538
  14.3 12.9 %collective-permute-start.1 = (bf16[2,512,128]{2,1,0:T(8,128)(2,1)S(1)}, bf16[2,512,128]{2,1,0:T(8,128)(2,1)S(1)}, u32[]{:S(2)}, u32[]{:S(2)}) collective-permute-start(bf16[2,512,128]{2,1,0:T(8,128)(2,1)S(1)} %copy-done.15), channel_id=1, source_target_pairs={{0,8},{8,0},{16,24},{24,16},{1,9},{9,1},{17,25},{25,17},{2,10},{10... | collective-permute-start | bytes 786440 | tf_op jit(solution)/shard_map/ppermute | solution.py:538
  16.0 19.7 %collective-permute-start.6 = (bf16[384,1536]{1,0:T(8,128)(2,1)}, bf16[384,1536]{1,0:T(8,128)(2,1)}, u32[]{:S(2)}, u32[]{:S(2)}) collective-permute-start(bf16[384,1536]{1,0:T(8,128)(2,1)} %w0.1), channel_id=1, source_target_pairs={{0,1},{1,0},{2,3},{3,2},{4,5},{5,4},{6,7},{7,6},{8,9},{9,8},{10,11... | collective-permute-start | bytes 3538952 | tf_op jit(solution)/shard_map/ppermute | solution.py:538
  21.9 10.1 %collective-permute-start.2 = (bf16[2,512,128]{2,1,0:T(8,128)(2,1)S(1)}, bf16[2,512,128]{2,1,0:T(8,128)(2,1)S(1)}, u32[]{:S(2)}, u32[]{:S(2)}) collective-permute-start(bf16[2,512,128]{2,1,0:T(8,128)(2,1)S(1)} %collective-permute-done.refs_1_), channel_id=1, source_target_pairs={{0,8},{8,0},{16,24},{24,16},{1,9},{9,1},{17,25},{25,17},{2,10},{10... | collective-permute-start | bytes 786440 | tf_op jit(solution)/shard_map/ppermute | solution.py:538
  34.5 13.4 %collective-permute-start.8 = (bf16[384,1536]{1,0:T(8,128)(2,1)}, bf16[384,1536]{1,0:T(8,128)(2,1)S(1)}, u32[]{:S(2)}, u32[]{:S(2)}) collective-permute-start(bf16[384,1536]{1,0:T(8,128)(2,1)} %collective-permute-done.3.w2), channel_id=1, source_target_pairs={{0,1},{1,0},{2,3},{3,2},{4,5},{5,4},{6,7},{7,6},{8,9},{9,8},{10,11... | collective-permute-start | bytes 3538952 | tf_op jit(solution)/shard_map/ppermute | solution.py:538
  35.1 11.1 %collective-permute-start.4 = (bf16[512,384]{1,0:T(8,128)(2,1)S(1)}, bf16[512,384]{1,0:T(8,128)(2,1)S(1)}, u32[]{:S(2)}, u32[]{:S(2)}) collective-permute-start(bf16[512,384]{1,0:T(8,128)(2,1)S(1)} %attend_close.2.t0), channel_id=1, source_target_pairs={{0,2},{1,3},{2,0},{3,1},{4,6},{5,7},{6,4},{7,5},{8,10},{9,11},{10,... | collective-permute-start | bytes 1179656 | tf_op jit(solution)/shard_map/ppermute | solution.py:538
  53.6 14.3 %collective-permute-start.10 = (bf16[512,512]{1,0:T(8,128)(2,1)}, bf16[512,512]{1,0:T(8,128)(2,1)}, u32[]{:S(2)}, u32[]{:S(2)}) collective-permute-start(bf16[512,512]{1,0:T(8,128)(2,1)} %get-tuple-element.83.e0), channel_id=1, source_target_pairs={{0,2},{1,3},{2,0},{3,1},{4,6},{5,7},{6,4},{7,5},{8,10},{9,11},{10,... | collective-permute-start | bytes 1572872 | tf_op jit(solution)/shard_map/ppermute | solution.py:538
  54.1 15.1 %collective-permute-start.9 = (bf16[512,512]{1,0:T(8,128)(2,1)}, bf16[512,512]{1,0:T(8,128)(2,1)}, u32[]{:S(2)}, u32[]{:S(2)}) collective-permute-start(bf16[512,512]{1,0:T(8,128)(2,1)} %get-tuple-element.83.e0), channel_id=1, source_target_pairs={{0,1},{1,0},{2,3},{3,2},{4,5},{5,4},{6,7},{7,6},{8,9},{9,8},{10,11... | collective-permute-start | bytes 1572872 | tf_op jit(solution)/shard_map/ppermute | solution.py:538
  73.4 14.8 %collective-permute-start.12 = (bf16[2,512,128]{2,1,0:T(8,128)(2,1)S(1)}, bf16[2,512,128]{2,1,0:T(8,128)(2,1)S(1)}, u32[]{:S(2)}, u32[]{:S(2)}) collective-permute-start(bf16[2,512,128]{2,1,0:T(8,128)(2,1)S(1)} %get-tuple-element.93.refs_0_), channel_id=1, source_target_pairs={{0,16},{8,24},{16,0},{24,8},{1,17},{9,25},{17,1},{25,9},{2,18},{10... | collective-permute-start | bytes 786440 | tf_op jit(solution)/shard_map/ppermute | solution.py:538
  76.4 14.4 %collective-permute-start.13 = (bf16[2,512,128]{2,1,0:T(8,128)(2,1)S(1)}, bf16[2,512,128]{2,1,0:T(8,128)(2,1)S(1)}, u32[]{:S(2)}, u32[]{:S(2)}) collective-permute-start(bf16[2,512,128]{2,1,0:T(8,128)(2,1)S(1)} %get-tuple-element.93.refs_0_), channel_id=1, source_target_pairs={{0,8},{8,0},{16,24},{24,16},{1,9},{9,1},{17,25},{25,17},{2,10},{10... | collective-permute-start | bytes 786440 | tf_op jit(solution)/shard_map/ppermute | solution.py:538
  82.0 14.9 %collective-permute-start.14 = (bf16[384,768]{1,0:T(8,128)(2,1)S(1)}, bf16[384,768]{1,0:T(8,128)(2,1)S(1)}, u32[]{:S(2)}, u32[]{:S(2)}) collective-permute-start(bf16[384,768]{1,0:T(8,128)(2,1)S(1)} %convolution_convert_fusion), channel_id=1, source_target_pairs={{0,4},{4,0},{1,5},{5,1},{2,6},{6,2},{3,7},{7,3},{8,12},{12,8},{9,1... | collective-permute-start | bytes 1769480 | tf_op jit(solution)/shard_map/ppermute | solution.py:538
  114.6 18.2 %collective-permute-start.18 = (bf16[128,2048]{1,0:T(8,128)(2,1)}, bf16[128,2048]{1,0:T(8,128)(2,1)}, u32[]{:S(2)}, u32[]{:S(2)}) collective-permute-start(bf16[128,2048]{1,0:T(8,128)(2,1)} %add_convert_fusion), channel_id=1, source_target_pairs={{0,2},{1,3},{2,0},{3,1},{4,6},{5,7},{6,4},{7,5},{8,10},{9,11},{10,... | collective-permute-start | bytes 1572872 | tf_op jit(solution)/shard_map/ppermute | solution.py:538
  115.2 26.4 %collective-permute-start.30 = (bf16[512,512]{1,0:T(8,128)(2,1)}, bf16[512,512]{1,0:T(8,128)(2,1)}, u32[]{:S(2)}, u32[]{:S(2)}) collective-permute-start(bf16[512,512]{1,0:T(8,128)(2,1)} %attend_close.3.att_ref), channel_id=1, source_target_pairs={{0,4},{4,0},{1,5},{5,1},{2,6},{6,2},{3,7},{7,3},{8,12},{12,8},{9,1... | collective-permute-start | bytes 1572872 | tf_op jit(solution)/shard_map/ppermute | solution.py:538
  122.7 10.0 %collective-permute-start.20 = (bf16[96,768]{1,0:T(8,128)(2,1)S(1)}, bf16[96,768]{1,0:T(8,128)(2,1)}, u32[]{:S(2)}, u32[]{:S(2)}) collective-permute-start(bf16[96,768]{1,0:T(8,128)(2,1)S(1)} %fusion.15.refs_0_), channel_id=1, source_target_pairs={{0,16},{8,24},{16,0},{24,8},{1,17},{9,25},{17,1},{25,9},{2,18},{10... | collective-permute-start | bytes 442376 | tf_op jit(solution)/shard_map/ppermute | solution.py:538
  138.1 10.4 %collective-permute-start.23 = (bf16[128,1024]{1,0:T(8,128)(2,1)}, bf16[128,1024]{1,0:T(8,128)(2,1)S(1)}, u32[]{:S(2)}, u32[]{:S(2)}) collective-permute-start(bf16[128,1024]{1,0:T(8,128)(2,1)} %get-tuple-element.114), channel_id=1, source_target_pairs={{0,6},{1,7},{2,4},{3,5},{4,2},{5,3},{6,0},{7,1},{8,14},{9,15},{10,... | collective-permute-start | bytes 786440 | tf_op jit(solution)/shard_map/ppermute | solution.py:538
  139.7 11.8 %collective-permute-start.22 = (bf16[128,1024]{1,0:T(8,128)(2,1)}, bf16[128,1024]{1,0:T(8,128)(2,1)S(1)}, u32[]{:S(2)}, u32[]{:S(2)}) collective-permute-start(bf16[128,1024]{1,0:T(8,128)(2,1)} %get-tuple-element.114), channel_id=1, source_target_pairs={{0,4},{4,0},{1,5},{5,1},{2,6},{6,2},{3,7},{7,3},{8,12},{12,8},{9,1... | collective-permute-start | bytes 786440 | tf_op jit(solution)/shard_map/ppermute | solution.py:538
  140.2 14.2 %collective-permute-start.26 = (bf16[128,1024]{1,0:T(8,128)(2,1)}, bf16[128,1024]{1,0:T(8,128)(2,1)S(1)}, u32[]{:S(2)}, u32[]{:S(2)}) collective-permute-start(bf16[128,1024]{1,0:T(8,128)(2,1)} %copy-done.11), channel_id=1, source_target_pairs={{0,2},{1,3},{2,0},{3,1},{4,6},{5,7},{6,4},{7,5},{8,10},{9,11},{10,... | collective-permute-start | bytes 786440 | tf_op jit(solution)/shard_map/ppermute | solution.py:538
  142.7 10.2 %collective-permute-start.27 = (bf16[96,768]{1,0:T(8,128)(2,1)}, bf16[96,768]{1,0:T(8,128)(2,1)S(1)}, u32[]{:S(2)}, u32[]{:S(2)}) collective-permute-start(bf16[96,768]{1,0:T(8,128)(2,1)} %collective-permute-done.20.refs_1_), channel_id=1, source_target_pairs={{0,8},{8,0},{16,24},{24,16},{1,9},{9,1},{17,25},{25,17},{2,10},{10... | collective-permute-start | bytes 442376 | tf_op jit(solution)/shard_map/ppermute | solution.py:538
  142.8 11.9 %collective-permute-start.28 = (bf16[128,1024]{1,0:T(8,128)(2,1)}, bf16[128,1024]{1,0:T(8,128)(2,1)S(1)}, u32[]{:S(2)}, u32[]{:S(2)}) collective-permute-start(bf16[128,1024]{1,0:T(8,128)(2,1)} %copy-done.11), channel_id=1, source_target_pairs={{0,1},{1,0},{2,3},{3,2},{4,5},{5,4},{6,7},{7,6},{8,9},{9,8},{10,11... | collective-permute-start | bytes 786440 | tf_op jit(solution)/shard_map/ppermute | solution.py:538
  155.3 10.6 %collective-permute-start.34 = (bf16[96,768]{1,0:T(8,128)(2,1)S(1)}, bf16[96,768]{1,0:T(8,128)(2,1)S(1)}, u32[]{:S(2)}, u32[]{:S(2)}) collective-permute-start(bf16[96,768]{1,0:T(8,128)(2,1)S(1)} %collective-permute-done.21.refs_2_), channel_id=1, source_target_pairs={{0,4},{4,0},{1,5},{5,1},{2,6},{6,2},{3,7},{7,3},{8,12},{12,8},{9,1... | collective-permute-start | bytes 442376 | tf_op jit(solution)/shard_map/ppermute | solution.py:538
  156.8 11.8 %collective-permute-start.35 = (bf16[96,768]{1,0:T(8,128)(2,1)S(1)}, bf16[96,768]{1,0:T(8,128)(2,1)S(1)}, u32[]{:S(2)}, u32[]{:S(2)}) collective-permute-start(bf16[96,768]{1,0:T(8,128)(2,1)S(1)} %collective-permute-done.27.refs_3_), channel_id=1, source_target_pairs={{0,4},{4,0},{1,5},{5,1},{2,6},{6,2},{3,7},{7,3},{8,12},{12,8},{9,1... | collective-permute-start | bytes 442376 | tf_op jit(solution)/shard_map/ppermute | solution.py:538
  159.7 13.0 %collective-permute-start.37 = (bf16[256,512]{1,0:T(8,128)(2,1)S(1)}, bf16[256,512]{1,0:T(8,128)(2,1)S(1)}, u32[]{:S(2)}, u32[]{:S(2)}) collective-permute-start(bf16[256,512]{1,0:T(8,128)(2,1)S(1)} %get-tuple-element.127), channel_id=1, source_target_pairs={{0,8},{8,0},{16,24},{24,16},{1,9},{9,1},{17,25},{25,17},{2,10},{10... | collective-permute-start | bytes 786440 | tf_op jit(solution)/shard_map/ppermute | solution.py:538
  179.0 10.1 %collective-permute-start.38 = (bf16[128,512]{1,0:T(8,128)(2,1)S(1)}, bf16[128,512]{1,0:T(8,128)(2,1)S(1)}, u32[]{:S(2)}, u32[]{:S(2)}) collective-permute-start(bf16[128,512]{1,0:T(8,128)(2,1)S(1)} %fusion.17.refs_0_), channel_id=1, source_target_pairs={{0,16},{8,24},{16,0},{24,8},{1,17},{9,25},{17,1},{25,9},{2,18},{10... | collective-permute-start | bytes 393224 | tf_op jit(solution)/shard_map/ppermute | solution.py:538
  (51 other events, 446.0 us)

commit v8 on v7

--- a/solution.py
+++ b/solution.py
@@ -114,7 +114,7 @@
             pltpu.VMEM((depth, width), BF16),
             pltpu.SemaphoreType.DMA((2,)),
         ],
-        compiler_params=pltpu.CompilerParams(vmem_limit_bytes=HIGH),
+        compiler_params=pltpu.CompilerParams(vmem_limit_bytes=LIMIT),
         cost_estimate=pl.CostEstimate(
             flops=2 * rows * depth * width, bytes_accessed=2 * rows * depth, transcendentals=0
         ),
@@ -486,35 +486,31 @@
     )(index, own, got)
 
 
-def assemble_kernel(codes, chunk, chunks, place_ref, *refs):
-    parts = refs[: len(codes) * 2]
+def assemble_kernel(spots, chunks, place_ref, *refs):
+    parts = refs[: len(spots)]
     out, got_ref, wide_ref, got_sems, sems = refs[-5:]
     block, strip = parts[0].shape
     got = start_copies([(part, got_ref.at[i]) for i, part in enumerate(parts)], got_sems)
     copies = []
-    for side in range(2):
-        for k, code in enumerate(codes):
-            at = side * len(codes) + k
-            row = pl.multiple_of((place_ref[5] ^ code) * block, block)
-            column = pl.multiple_of(((place_ref[0] ^ side) * chunks + chunk) * strip, strip)
-            got[at].wait()
-            wide_ref[at] = got_ref[at].astype(F32)
-            copy = pltpu.make_async_copy(
-                wide_ref.at[at],
-                out.at[pl.ds(row, block), pl.ds(column, strip)],
-                sems.at[at],
-            )
-            copy.start()
-            copies.append(copy)
+    for i, (chunk, side, code) in enumerate(spots):
+        row = pl.multiple_of((place_ref[5] ^ code) * block, block)
+        column = pl.multiple_of(((place_ref[0] ^ side) * chunks + chunk) * strip, strip)
+        got[i].wait()
+        wide_ref[i] = got_ref[i].astype(F32)
+        copy = pltpu.make_async_copy(
+            wide_ref.at[i], out.at[pl.ds(row, block), pl.ds(column, strip)], sems.at[i]
+        )
+        copy.start()
+        copies.append(copy)
     for copy in copies:
         copy.wait()
 
 
-def assemble(place, parts, count, chunk, chunks, before):
+def assemble(place, parts, spots, count, chunks, before):
     block, strip = parts[0].shape
     rows, wide = block * count, strip * 2 * chunks
     return pl.pallas_call(
-        functools.partial(assemble_kernel, gather_codes(count), chunk, chunks),
+        functools.partial(assemble_kernel, spots, chunks),
         in_specs=[SMEM] + [ANY] * (len(parts) + len(before)),
         out_specs=ANY,
         out_shape=jax.ShapeDtypeStruct((rows, wide), F32),
@@ -674,17 +670,15 @@
 
     send_m, keep_m, att_rows = part_rows(place, critic_attended, c_out)
     near_m = swap(send_m, "mdl", 1)
-    near_m, moved_a = tied(near_m, moved_a)
+    send_y = (keep_m[value_rows:] + near_m[value_rows:].astype(F32)).astype(BF16)
+    got_y = swap(send_y, "mdl", 2)
+    att_there = swap(critic_attended, "sec", 1)
+    got_y, moved_a = tied(got_y, moved_a)
     bit = 2
     while bit < rep_count:
         keep_a, send_a = halve(keep_a, moved_a)
         moved_a = swap(send_a, "rep", bit)
         bit *= 2
-    send_y = (keep_m[value_rows:] + near_m[value_rows:].astype(F32)).astype(BF16)
-    got_y = swap(send_y, "mdl", 2)
-    att_there = swap(critic_attended, "sec", 1)
-    mine_a = gather_blocks((keep_a + moved_a.astype(F32)).astype(BF16), "rep")
-    got_y, *mine_a[1:-1] = tied(got_y, *mine_a[1:-1])
     value_wide, d_other, d_own = mixed_rows(
         place, emb_mine, keep_m, near_m, got_y, w_row, target
     )
@@ -692,7 +686,9 @@
     d_there = swap(d_other, "sec", 1)
     d_far = swap(d_own, "mdl", 2)
     there_far = swap(d_other, ("sec", "mdl"), mdl_count | 2)
-    d_far, mine_a[-1] = tied(d_far, mine_a[-1])
+    d_far, moved_a = tied(d_far, moved_a)
+    mine_a = gather_blocks((keep_a + moved_a.astype(F32)).astype(BF16), "rep")
+    d_there, *mine_a[1:-1] = tied(d_there, *mine_a[1:-1])
     own_rows = jnp.concatenate(
         [d_own, d_far, swap(d_own, "mdl", 1), swap(d_far, "mdl", 1)], axis=0
     )
@@ -708,7 +704,9 @@
     )
     value_part, there_rows = tied(value_wide[:, 0], there_rows)
     theirs_a = [swap(block, "sec", 1) for block in mine_a]
-    actor_summed = assemble(place, mine_a + theirs_a, rep_count, 0, 1, [])
+    codes = gather_codes(rep_count)
+    spots = [(0, side, code) for side in range(2) for code in codes]
+    actor_summed = assemble(place, mine_a + theirs_a, spots, rep_count, 1, [])
 
     strip = d_own.shape[1] // CHUNKS
     chunks = []
@@ -727,15 +725,29 @@
         waited = [item for c in turn for item in chunks[c][1] + chunks[c][3]]
         extra = []
         if tick == 0:
-            extra = [chunks[c][0] for c in range(1, CHUNKS)] + theirs_a
-        if tick == levels:
+            extra = [chunks[c][0] for c in range(1, CHUNKS)]
+        if tick == 1:
+            extra = mine_a[-1:]
+        if tick == 2:
+            extra = theirs_a
+        if tick == 2 * levels - 1:
             extra = [actor_summed]
+        if tick == 2 * levels + CHUNKS - 2:
+            done = [
+                (item, (c, side, code))
+                for c in range(CHUNKS)
+                for side in range(2)
+                for item, code in zip(chunks[c][2 + 2 * side], codes)
+            ]
+            extra = [assemble(place, *zip(*done), rep_count, CHUNKS, [])]
         outs = list(tied(*waited, *extra))
         if tick == 0:
             for c in range(1, CHUNKS):
                 chunks[c][0] = outs[len(waited) + c - 1]
-        if tick == levels:
+        if tick == 2 * levels - 1:
             actor_summed = outs[-1]
+        if tick == 2 * levels + CHUNKS - 2:
+            result = outs[-1]
         for c in turn:
             keep, pending, mine, crossing, theirs = chunks[c]
             arrived, outs = outs[: len(pending)], outs[len(pending) :]
@@ -754,12 +766,16 @@
                 bit = rep_count >> (level - levels + 1)
                 pending = [swap(block, "rep", bit) for block in mine] if bit else []
             chunks[c] = [keep, pending, mine, crossing, theirs]
-    result = []
-    for c in range(CHUNKS):
-        _, _, mine, crossing, theirs = chunks[c]
-        result = [assemble(place, mine + theirs + crossing, rep_count, c, CHUNKS, result)]
-
-    return (value_part[None, :], actor_summed, result[0])
+    rest = [
+        (item, (c, side, code))
+        for c in range(CHUNKS)
+        for side, group in enumerate((chunks[c][2], chunks[c][4] + chunks[c][3]))
+        for item, code in zip(group, codes)
+        if (c, side, code) not in [spot for _, spot in done]
+    ]
+    result = assemble(place, *zip(*rest), rep_count, CHUNKS, [result])
+
+    return (value_part[None, :], actor_summed, result)
 
 
 def solution(mesh):

time: 219 us -> 218 us (level)
  Pallas kernels: 49.2 us -> 45.6 us
    pallas_call x1, Pallas kernels: 4.46 us -> 1.34 us  [query_projection(): pl.pallas_call(functools.partial(query_kernel, scale), in_specs=[HBM, HBM...]
    unnamed x47 -> x49, local copies, waits for them, and re-layouts: 5.62 us -> 6.17 us
  transfers between devices with their start and end apart: 53 -> 53, of which waited for: 30 -> 30; matrix products, arithmetic and copies ran while one was open for 7% -> 7% of each run, Pallas kernels for 15% -> 12%
where the time goes in v8:
time: 218 us; the launch traced here: 217 us
  waiting for transfers between devices  99.1 us (45%)
  Pallas kernels  45.6 us (21%)
  starting transfers between devices  45.4 us (21%)
  local copies, waits for them, and re-layouts  11.9 us (5%)
  matrix products  5.59 us (3%)
  between operations  4.87 us (2%)
  other arithmetic  4.46 us (2%)
    ppermute x53, waiting for transfers between devices, swap(): return lax.ppermute(block, axis, [(i, i ^ bit) for i in range(size)])  99.1 us
    ppermute x53, starting transfers between devices, swap(): return lax.ppermute(block, axis, [(i, i ^ bit) for i in range(size)])  45.4 us
    pallas_call x4, Pallas kernels, attend_call(): pl.pallas_call(functools.partial(body, groups, units, TABLE + first), in_...  15 us
    pallas_call x3, Pallas kernels, assemble(): pl.pallas_call(functools.partial(assemble_kernel, spots, chunks), in_spec...  10.3 us
    unnamed x49, local copies, waits for them, and re-layouts  6.17 us
    pallas_call x1, Pallas kernels, hidden_rows(): pl.pallas_call(hidden_kernel, in_specs=[VMEM] * 3 + [ANY] * 2 + [HBM], ou...  4.46 us
  transfers between devices with their start and end apart: 53, of which 30 were waited for; matrix products, arithmetic and copies ran while one was open for 7% of the time, Pallas kernels for 12%

profile of v8, /device:TPU:0, one launch (start us, length us, event | category | flops | bytes accessed | tf_op | source)
XLA Modules:
  0.0 216.9 jit_solution(5796202947875757513)
XLA Ops:
  0.7 3.0 %collective-permute-start.3 = (bf16[384,1536]{1,0:T(8,128)(2,1)}, bf16[384,1536]{1,0:T(8,128)(2,1)}, u32[]{:S(2)}, u32[]{:S(2)}) collective-permute-start(bf16[384,1536]{1,0:T(8,128)(2,1)} %w0.1), channel_id=1, source_target_pairs={{0,2},{1,3},{2,0},{3,1},{4,6},{5,7},{6,4},{7,5},{8,10},{9,11},{10,... | collective-permute-start | bytes 3538952 | tf_op jit(solution)/shard_map/ppermute | solution.py:534
  3.7 3.5 %first_projection.1 = (bf16[2,512,128]{2,1,0:T(8,128)(2,1)}, f32[512,128]{1,0:T(8,128)}) custom-call(bf16[512,1536]{1,0:T(8,128)(2,1)} %bitcast.30, bf16[2,1536,128]{2,1,0:T(8,128)(2,1)} %w_hbm.2), custom_call_target="tpu_custom_call" | custom-call | flops 402653184 | bytes 1572864 | tf_op jit(solution)/shard_map/first_projection/pallas_call | solution.py:77
  7.2 2.7 %collective-permute-start = (bf16[2,512,128]{2,1,0:T(8,128)(2,1)}, bf16[2,512,128]{2,1,0:T(8,128)(2,1)S(1)}, u32[]{:S(2)}, u32[]{:S(2)}) collective-permute-start(bf16[2,512,128]{2,1,0:T(8,128)(2,1)} %get-tuple-element.77.refs_0_), channel_id=1, source_target_pairs={{0,16},{8,24},{16,0},{24,8},{1,17},{9,25},{17,1},{25,9},{2,18},{10... | collective-permute-start | bytes 786440 | tf_op jit(solution)/shard_map/ppermute | solution.py:534
  22.6 4.1 %collective-permute-done.1.refs_2_ = bf16[2,512,128]{2,1,0:T(8,128)(2,1)S(1)} collective-permute-done((bf16[2,512,128]{2,1,0:T(8,128)(2,1)S(1)}, bf16[2,512,128]{2,1,0:T(8,128)(2,1)S(1)}, u32[]{:S(2)}, u32[]{:S(2)}) %collective-permute-start.1) | collective-permute-done | bytes 262176 | tf_op jit(solution)/shard_map/ppermute | solution.py:534
  26.7 3.6 %attend_open.2 = (f32[512,768]{1,0:T(8,128)S(1)}, f32[512,384]{1,0:T(8,128)S(1)}) custom-call(s32[10]{0:T(128)S(1)} %stack.39.left_ref.place_ref, bf16[512,384]{1,0:T(8,128)(2,1)S(1)} %query_projection.1.q_ref, bf16[2,512,128]{2,1,0:T(8,128)(2,1)S(1)} %copy-done.16, bf16[2,512,128]{2,1,0:T(8,128)(2,1)S(1)} %collective-permute-done.refs_1_, ...), custom_call_target="tpu_custom_call" | custom-call | flops 7247757312 | bytes 786432 | tf_op jit(solution)/shard_map/attend_open/pallas_call | solution.py:219
  36.8 3.1 %near_rows.1.sum_ref = f32[512,1536]{1,0:T(8,128)S(1)} custom-call(bf16[512,1536]{1,0:T(8,128)(2,1)S(1)} %bitcast.32, bf16[512,384]{1,0:T(8,128)(2,1)S(1)} %attend_close.2.t0, bf16[512,384]{1,0:T(8,128)(2,1)S(1)} %collective-permute-done.5.t1, bf16[384,1536]{1,0:T(8,128)(2,1)} %w0.1, bf16[384,1536]{1,0:T(8,128)(2,1)} %collective-permute-done.6.w1), custom_call_target="tpu_custom_call" | custom-call | flops 1207959552 | bytes 2359296 | tf_op jit(solution)/shard_map/near_rows/pallas_call | solution.py:249
  40.0 5.4 %collective-permute-done.4.t2 = bf16[512,384]{1,0:T(8,128)(2,1)S(1)} collective-permute-done((bf16[512,384]{1,0:T(8,128)(2,1)S(1)}, bf16[512,384]{1,0:T(8,128)(2,1)S(1)}, u32[]{:S(2)}, u32[]{:S(2)}) %collective-permute-start.4) | collective-permute-done | bytes 393248 | tf_op jit(solution)/shard_map/ppermute | solution.py:534
  47.1 4.5 %hidden_rows.1 = (bf16[512,1536]{1,0:T(8,128)(2,1)S(1)}, bf16[512,512]{1,0:T(8,128)(2,1)}) custom-call(f32[512,1536]{1,0:T(8,128)S(1)} %near_rows.1.sum_ref, bf16[512,384]{1,0:T(8,128)(2,1)S(1)} %collective-permute-done.4.t2, bf16[512,384]{1,0:T(8,128)(2,1)S(1)} %collective-permute-done.7.t3, bf16[384,1536]{1,0:T(8,128)(2,1)} %collective-permute-done.3.w2, ...), custom_call_target="tpu_custom_call" | custom-call | flops 2415919104 | bytes 4718592 | tf_op jit(solution)/shard_map/hidden_rows/pallas_call | solution.py:287
  53.5 13.5 %collective-permute-done.10.e2 = bf16[512,512]{1,0:T(8,128)(2,1)} collective-permute-done((bf16[512,512]{1,0:T(8,128)(2,1)}, bf16[512,512]{1,0:T(8,128)(2,1)}, u32[]{:S(2)}, u32[]{:S(2)}) %collective-permute-start.10) | collective-permute-done | bytes 524320 | tf_op jit(solution)/shard_map/ppermute | solution.py:534
  69.2 2.7 %join_rows.1 = (bf16[2,512,128]{2,1,0:T(8,128)(2,1)S(1)}, f32[512,128]{1,0:T(8,128)S(1)}, bf16[512,2048]{1,0:T(8,128)(2,1)S(1)}) custom-call(s32[10]{0:T(128)S(1)} %stack.39.left_ref.place_ref, bf16[512,512]{1,0:T(8,128)(2,1)} %get-tuple-element.84.e0, bf16[512,512]{1,0:T(8,128)(2,1)} %collective-permute-done.9.e1, ...), custom_call_target="tpu_custom_call" | custom-call | flops 536870912 | bytes 4194304 | tf_op jit(solution)/shard_map/join_rows/pallas_call | solution.py:340
  82.8 4.5 %collective-permute-done.12.refs_1_ = bf16[2,512,128]{2,1,0:T(8,128)(2,1)S(1)} collective-permute-done((bf16[2,512,128]{2,1,0:T(8,128)(2,1)S(1)}, bf16[2,512,128]{2,1,0:T(8,128)(2,1)S(1)}, u32[]{:S(2)}, u32[]{:S(2)}) %collective-permute-start.12) | collective-permute-done | bytes 262176 | tf_op jit(solution)/shard_map/ppermute | solution.py:534
  87.3 2.7 %collective-permute-done.13.refs_2_ = bf16[2,512,128]{2,1,0:T(8,128)(2,1)S(1)} collective-permute-done((bf16[2,512,128]{2,1,0:T(8,128)(2,1)S(1)}, bf16[2,512,128]{2,1,0:T(8,128)(2,1)S(1)}, u32[]{:S(2)}, u32[]{:S(2)}) %collective-permute-start.13) | collective-permute-done | bytes 262176 | tf_op jit(solution)/shard_map/ppermute | solution.py:534
  90.0 4.8 %attend_open.3 = (f32[512,1024]{1,0:T(8,128)S(1)}, f32[512,512]{1,0:T(8,128)S(1)}) custom-call(s32[10]{0:T(128)S(1)} %stack.39.left_ref.place_ref, bf16[512,512]{1,0:T(8,128)(2,1)S(1)} %fusion.3.q_ref, bf16[2,512,128]{2,1,0:T(8,128)(2,1)S(1)} %get-tuple-element.94.refs_0_, bf16[2,512,128]{2,1,0:T(8,128)(2,1)S(1)} %collective-permute-done.12.refs_1_, ...), custom_call_target="tpu_custom_call" | custom-call | flops 9663676416 | bytes 1048576 | tf_op jit(solution)/shard_map/attend_open/pallas_call | solution.py:219
  97.0 4.1 %attend_close.3.att_ref = bf16[512,512]{1,0:T(8,128)(2,1)} custom-call(s32[10]{0:T(128)S(1)} %stack.39.left_ref.place_ref, bf16[512,512]{1,0:T(8,128)(2,1)S(1)} %fusion.3.q_ref, f32[512,1024]{1,0:T(8,128)S(1)} %get-tuple-element.102.wide_ref, f32[512,512]{1,0:T(8,128)S(1)} %get-tuple-element.103.top_ref, bf16[2,512,128]{2,1,0:T(8,128)(2,1)S(1)} %collective-permute-done.15.refs_0_), custom_call_target="tpu_custom_call" | custom-call | flops 134217728 | bytes 1048576 | tf_op jit(solution)/shard_map/attend_close/pallas_call | solution.py:219
  101.1 2.6 %part_rows.1 = (bf16[256,2048]{1,0:T(8,128)(2,1)S(1)}, f32[256,2048]{1,0:T(8,128)S(1)}, bf16[512,512]{1,0:T(8,128)(2,1)S(1)}) custom-call(s32[10]{0:T(128)S(1)} %stack.39.left_ref.place_ref, bf16[512,512]{1,0:T(8,128)(2,1)} %attend_close.3.att_ref, bf16[512,2048]{1,0:T(8,128)(2,1)S(1)} %copy-done.14), custom_call_target="tpu_custom_call" | custom-call | flops 1073741824 | bytes 8388608 | tf_op jit(solution)/shard_map/part_rows/pallas_call | solution.py:380
  109.3 9.9 %collective-permute-done.29 = bf16[512,512]{1,0:T(8,128)(2,1)} collective-permute-done((bf16[512,512]{1,0:T(8,128)(2,1)}, bf16[512,512]{1,0:T(8,128)(2,1)}, u32[]{:S(2)}, u32[]{:S(2)}) %collective-permute-start.29) | collective-permute-done | bytes 524320 | tf_op jit(solution)/shard_map/ppermute | solution.py:534
  131.6 8.6 %collective-permute-done.21 = bf16[96,768]{1,0:T(8,128)(2,1)S(1)} collective-permute-done((bf16[96,768]{1,0:T(8,128)(2,1)S(1)}, bf16[96,768]{1,0:T(8,128)(2,1)S(1)}, u32[]{:S(2)}, u32[]{:S(2)}) %collective-permute-start.21) | collective-permute-done | bytes 147488 | tf_op jit(solution)/shard_map/ppermute | solution.py:534
  142.8 6.0 %collective-permute-done.23.refs_2_ = bf16[96,768]{1,0:T(8,128)(2,1)S(1)} collective-permute-done((bf16[96,768]{1,0:T(8,128)(2,1)S(1)}, bf16[96,768]{1,0:T(8,128)(2,1)S(1)}, u32[]{:S(2)}, u32[]{:S(2)}) %collective-permute-start.23) | collective-permute-done | bytes 147488 | tf_op jit(solution)/shard_map/ppermute | solution.py:534
  156.2 6.4 %collective-permute-done.30 = bf16[256,512]{1,0:T(8,128)(2,1)S(1)} collective-permute-done((bf16[256,512]{1,0:T(8,128)(2,1)S(1)}, bf16[256,512]{1,0:T(8,128)(2,1)S(1)}, u32[]{:S(2)}, u32[]{:S(2)}) %collective-permute-start.30) | collective-permute-done | bytes 262176 | tf_op jit(solution)/shard_map/ppermute | solution.py:534
  168.7 4.7 %collective-permute-done.32 = bf16[256,512]{1,0:T(8,128)(2,1)S(1)} collective-permute-done((bf16[256,512]{1,0:T(8,128)(2,1)S(1)}, bf16[256,512]{1,0:T(8,128)(2,1)S(1)}, u32[]{:S(2)}, u32[]{:S(2)}) %collective-permute-start.32) | collective-permute-done | bytes 262176 | tf_op jit(solution)/shard_map/ppermute | solution.py:534
  179.9 5.9 %collective-permute-done.37 = bf16[128,512]{1,0:T(8,128)(2,1)S(1)} collective-permute-done((bf16[128,512]{1,0:T(8,128)(2,1)S(1)}, bf16[128,512]{1,0:T(8,128)(2,1)S(1)}, u32[]{:S(2)}, u32[]{:S(2)}) %collective-permute-start.37) | collective-permute-done | bytes 131104 | tf_op jit(solution)/shard_map/ppermute | solution.py:534
  192.7 3.6 %assemble.3 = f32[384,1536]{1,0:T(8,128)} custom-call(s32[10]{0:T(128)S(1)} %stack.39.left_ref.place_ref, bf16[96,768]{1,0:T(8,128)(2,1)S(1)} %fusion.15.refs_0_, bf16[96,768]{1,0:T(8,128)(2,1)S(1)} %collective-permute-done.22.refs_1_, bf16[96,768]{1,0:T(8,128)(2,1)S(1)} %collective-permute-done.23.refs_2_, ...), custom_call_target="tpu_custom_call" | custom-call | flops 589824 | bytes 3538944 | tf_op jit(solution)/shard_map/assemble/pallas_call | solution.py:512
  202.4 3.6 %assemble.4.refs_7_ = f32[512,2048]{1,0:T(8,128)} custom-call(s32[10]{0:T(128)S(1)} %stack.39.left_ref.place_ref, bf16[128,512]{1,0:T(8,128)(2,1)S(1)} %fusion.17.refs_0_, bf16[128,512]{1,0:T(8,128)(2,1)S(1)} %collective-permute-done.35.refs_1_, bf16[128,512]{1,0:T(8,128)(2,1)S(1)} %collective-permute-done.34.refs_2_, ...), custom_call_target="tpu_custom_call" | custom-call | flops 1048576 | bytes 6291456 | tf_op jit(solution)/shard_map/assemble/pallas_call | solution.py:512
  213.7 3.1 %assemble.5 = f32[512,2048]{1,0:T(8,128)} custom-call(s32[10]{0:T(128)S(1)} %stack.39.left_ref.place_ref, bf16[128,512]{1,0:T(8,128)(2,1)S(1)} %collective-permute-done.46.refs_0_, bf16[128,512]{1,0:T(8,128)(2,1)S(1)} %collective-permute-done.47.refs_1_, bf16[128,512]{1,0:T(8,128)(2,1)S(1)} %collective-permute-done.48.refs_2_, ...), custom_call_target="tpu_custom_call", output_to_operand_aliasing={{}: (8, {})} | custom-call | flops 1048576 | bytes 6291456 | tf_op jit(solution)/shard_map/assemble/pallas_call | solution.py:512
  (188 shorter events, 95.6 us)
Async XLA Ops:
  0.7 33.0 %collective-permute-start.3 = (bf16[384,1536]{1,0:T(8,128)(2,1)}, bf16[384,1536]{1,0:T(8,128)(2,1)}, u32[]{:S(2)}, u32[]{:S(2)}) collective-permute-start(bf16[384,1536]{1,0:T(8,128)(2,1)} %w0.1), channel_id=1, source_target_pairs={{0,2},{1,3},{2,0},{3,1},{4,6},{5,7},{6,4},{7,5},{8,10},{9,11},{10,... | collective-permute-start | bytes 3538952 | tf_op jit(solution)/shard_map/ppermute | solution.py:534
  7.2 14.7 %collective-permute-start = (bf16[2,512,128]{2,1,0:T(8,128)(2,1)}, bf16[2,512,128]{2,1,0:T(8,128)(2,1)S(1)}, u32[]{:S(2)}, u32[]{:S(2)}) collective-permute-start(bf16[2,512,128]{2,1,0:T(8,128)(2,1)} %get-tuple-element.77.refs_0_), channel_id=1, source_target_pairs={{0,16},{8,24},{16,0},{24,8},{1,17},{9,25},{17,1},{25,9},{2,18},{10... | collective-permute-start | bytes 786440 | tf_op jit(solution)/shard_map/ppermute | solution.py:534
  13.4 13.2 %collective-permute-start.1 = (bf16[2,512,128]{2,1,0:T(8,128)(2,1)S(1)}, bf16[2,512,128]{2,1,0:T(8,128)(2,1)S(1)}, u32[]{:S(2)}, u32[]{:S(2)}) collective-permute-start(bf16[2,512,128]{2,1,0:T(8,128)(2,1)S(1)} %copy-done.16), channel_id=1, source_target_pairs={{0,8},{8,0},{16,24},{24,16},{1,9},{9,1},{17,25},{25,17},{2,10},{10... | collective-permute-start | bytes 786440 | tf_op jit(solution)/shard_map/ppermute | solution.py:534
  15.1 19.9 %collective-permute-start.6 = (bf16[384,1536]{1,0:T(8,128)(2,1)}, bf16[384,1536]{1,0:T(8,128)(2,1)}, u32[]{:S(2)}, u32[]{:S(2)}) collective-permute-start(bf16[384,1536]{1,0:T(8,128)(2,1)} %w0.1), channel_id=1, source_target_pairs={{0,1},{1,0},{2,3},{3,2},{4,5},{5,4},{6,7},{7,6},{8,9},{9,8},{10,11... | collective-permute-start | bytes 3538952 | tf_op jit(solution)/shard_map/ppermute | solution.py:534
  33.7 13.4 %collective-permute-start.8 = (bf16[384,1536]{1,0:T(8,128)(2,1)}, bf16[384,1536]{1,0:T(8,128)(2,1)S(1)}, u32[]{:S(2)}, u32[]{:S(2)}) collective-permute-start(bf16[384,1536]{1,0:T(8,128)(2,1)} %collective-permute-done.3.w2), channel_id=1, source_target_pairs={{0,1},{1,0},{2,3},{3,2},{4,5},{5,4},{6,7},{7,6},{8,9},{9,8},{10,11... | collective-permute-start | bytes 3538952 | tf_op jit(solution)/shard_map/ppermute | solution.py:534
  52.7 14.3 %collective-permute-start.10 = (bf16[512,512]{1,0:T(8,128)(2,1)}, bf16[512,512]{1,0:T(8,128)(2,1)}, u32[]{:S(2)}, u32[]{:S(2)}) collective-permute-start(bf16[512,512]{1,0:T(8,128)(2,1)} %get-tuple-element.84.e0), channel_id=1, source_target_pairs={{0,2},{1,3},{2,0},{3,1},{4,6},{5,7},{6,4},{7,5},{8,10},{9,11},{10,... | collective-permute-start | bytes 1572872 | tf_op jit(solution)/shard_map/ppermute | solution.py:534
  53.4 15.0 %collective-permute-start.9 = (bf16[512,512]{1,0:T(8,128)(2,1)}, bf16[512,512]{1,0:T(8,128)(2,1)}, u32[]{:S(2)}, u32[]{:S(2)}) collective-permute-start(bf16[512,512]{1,0:T(8,128)(2,1)} %get-tuple-element.84.e0), channel_id=1, source_target_pairs={{0,1},{1,0},{2,3},{3,2},{4,5},{5,4},{6,7},{7,6},{8,9},{9,8},{10,11... | collective-permute-start | bytes 1572872 | tf_op jit(solution)/shard_map/ppermute | solution.py:534
  72.5 14.8 %collective-permute-start.12 = (bf16[2,512,128]{2,1,0:T(8,128)(2,1)S(1)}, bf16[2,512,128]{2,1,0:T(8,128)(2,1)S(1)}, u32[]{:S(2)}, u32[]{:S(2)}) collective-permute-start(bf16[2,512,128]{2,1,0:T(8,128)(2,1)S(1)} %get-tuple-element.94.refs_0_), channel_id=1, source_target_pairs={{0,16},{8,24},{16,0},{24,8},{1,17},{9,25},{17,1},{25,9},{2,18},{10... | collective-permute-start | bytes 786440 | tf_op jit(solution)/shard_map/ppermute | solution.py:534
  76.3 13.7 %collective-permute-start.13 = (bf16[2,512,128]{2,1,0:T(8,128)(2,1)S(1)}, bf16[2,512,128]{2,1,0:T(8,128)(2,1)S(1)}, u32[]{:S(2)}, u32[]{:S(2)}) collective-permute-start(bf16[2,512,128]{2,1,0:T(8,128)(2,1)S(1)} %get-tuple-element.94.refs_0_), channel_id=1, source_target_pairs={{0,8},{8,0},{16,24},{24,16},{1,9},{9,1},{17,25},{25,17},{2,10},{10... | collective-permute-start | bytes 786440 | tf_op jit(solution)/shard_map/ppermute | solution.py:534
  81.2 14.9 %collective-permute-start.14 = (bf16[384,768]{1,0:T(8,128)(2,1)S(1)}, bf16[384,768]{1,0:T(8,128)(2,1)S(1)}, u32[]{:S(2)}, u32[]{:S(2)}) collective-permute-start(bf16[384,768]{1,0:T(8,128)(2,1)S(1)} %convolution_convert_fusion), channel_id=1, source_target_pairs={{0,4},{4,0},{1,5},{5,1},{2,6},{6,2},{3,7},{7,3},{8,12},{12,8},{9,1... | collective-permute-start | bytes 1769480 | tf_op jit(solution)/shard_map/ppermute | solution.py:534
  104.5 14.7 %collective-permute-start.29 = (bf16[512,512]{1,0:T(8,128)(2,1)}, bf16[512,512]{1,0:T(8,128)(2,1)}, u32[]{:S(2)}, u32[]{:S(2)}) collective-permute-start(bf16[512,512]{1,0:T(8,128)(2,1)} %attend_close.3.att_ref), channel_id=1, source_target_pairs={{0,4},{4,0},{1,5},{5,1},{2,6},{6,2},{3,7},{7,3},{8,12},{12,8},{9,1... | collective-permute-start | bytes 1572872 | tf_op jit(solution)/shard_map/ppermute | solution.py:534
  108.1 14.3 %collective-permute-start.17 = (bf16[128,2048]{1,0:T(8,128)(2,1)}, bf16[128,2048]{1,0:T(8,128)(2,1)}, u32[]{:S(2)}, u32[]{:S(2)}) collective-permute-start(bf16[128,2048]{1,0:T(8,128)(2,1)} %add_convert_fusion), channel_id=1, source_target_pairs={{0,2},{1,3},{2,0},{3,1},{4,6},{5,7},{6,4},{7,5},{8,10},{9,11},{10,... | collective-permute-start | bytes 1572872 | tf_op jit(solution)/shard_map/ppermute | solution.py:534
  108.9 11.5 %collective-permute-start.18 = (bf16[192,768]{1,0:T(8,128)(2,1)S(1)}, bf16[192,768]{1,0:T(8,128)(2,1)}, u32[]{:S(2)}, u32[]{:S(2)}) collective-permute-start(bf16[192,768]{1,0:T(8,128)(2,1)S(1)} %get-tuple-element.107), channel_id=1, source_target_pairs={{0,8},{8,0},{16,24},{24,16},{1,9},{9,1},{17,25},{25,17},{2,10},{10... | collective-permute-start | bytes 884744 | tf_op jit(solution)/shard_map/ppermute | solution.py:534
  125.7 14.7 %collective-permute-start.24 = (bf16[128,1024]{1,0:T(8,128)(2,1)S(1)}, bf16[128,1024]{1,0:T(8,128)(2,1)S(1)}, u32[]{:S(2)}, u32[]{:S(2)}) collective-permute-start(bf16[128,1024]{1,0:T(8,128)(2,1)S(1)} %get-tuple-element.112), channel_id=1, source_target_pairs={{0,6},{1,7},{2,4},{3,5},{4,2},{5,3},{6,0},{7,1},{8,14},{9,15},{10,... | collective-permute-start | bytes 786440 | tf_op jit(solution)/shard_map/ppermute | solution.py:534
  127.4 15.3 %collective-permute-start.19 = (bf16[128,1024]{1,0:T(8,128)(2,1)S(1)}, bf16[128,1024]{1,0:T(8,128)(2,1)S(1)}, u32[]{:S(2)}, u32[]{:S(2)}) collective-permute-start(bf16[128,1024]{1,0:T(8,128)(2,1)S(1)} %get-tuple-element.112), channel_id=1, source_target_pairs={{0,4},{4,0},{1,5},{5,1},{2,6},{6,2},{3,7},{7,3},{8,12},{12,8},{9,1... | collective-permute-start | bytes 786440 | tf_op jit(solution)/shard_map/ppermute | solution.py:534
  128.0 14.7 %collective-permute-start.27 = (bf16[128,1024]{1,0:T(8,128)(2,1)S(1)}, bf16[128,1024]{1,0:T(8,128)(2,1)S(1)}, u32[]{:S(2)}, u32[]{:S(2)}) collective-permute-start(bf16[128,1024]{1,0:T(8,128)(2,1)S(1)} %get-tuple-element.115), channel_id=1, source_target_pairs={{0,1},{1,0},{2,3},{3,2},{4,5},{5,4},{6,7},{7,6},{8,9},{9,8},{10,11... | collective-permute-start | bytes 786440 | tf_op jit(solution)/shard_map/ppermute | solution.py:534
  128.0 12.2 %collective-permute-start.20 = (bf16[128,1024]{1,0:T(8,128)(2,1)S(1)}, bf16[128,1024]{1,0:T(8,128)(2,1)S(1)}, u32[]{:S(2)}, u32[]{:S(2)}) collective-permute-start(bf16[128,1024]{1,0:T(8,128)(2,1)S(1)} %get-tuple-element.115), channel_id=1, source_target_pairs={{0,2},{1,3},{2,0},{3,1},{4,6},{5,7},{6,4},{7,5},{8,10},{9,11},{10,... | collective-permute-start | bytes 786440 | tf_op jit(solution)/shard_map/ppermute | solution.py:534
  153.9 13.2 %collective-permute-start.33 = (bf16[96,768]{1,0:T(8,128)(2,1)S(1)}, bf16[96,768]{1,0:T(8,128)(2,1)S(1)}, u32[]{:S(2)}, u32[]{:S(2)}) collective-permute-start(bf16[96,768]{1,0:T(8,128)(2,1)S(1)} %collective-permute-done.22.refs_1_), channel_id=1, source_target_pairs={{0,8},{8,0},{16,24},{24,16},{1,9},{9,1},{17,25},{25,17},{2,10},{10... | collective-permute-start | bytes 442376 | tf_op jit(solution)/shard_map/ppermute | solution.py:534
  156.1 17.3 %collective-permute-start.32 = (bf16[256,512]{1,0:T(8,128)(2,1)S(1)}, bf16[256,512]{1,0:T(8,128)(2,1)S(1)}, u32[]{:S(2)}, u32[]{:S(2)}) collective-permute-start(bf16[256,512]{1,0:T(8,128)(2,1)S(1)} %get-tuple-element.126), channel_id=1, source_target_pairs={{0,8},{8,0},{16,24},{24,16},{1,9},{9,1},{17,25},{25,17},{2,10},{10... | collective-permute-start | bytes 786440 | tf_op jit(solution)/shard_map/ppermute | solution.py:534
  162.7 12.2 %collective-permute-start.31 = (bf16[128,512]{1,0:T(8,128)(2,1)S(1)}, bf16[128,512]{1,0:T(8,128)(2,1)S(1)}, u32[]{:S(2)}, u32[]{:S(2)}) collective-permute-start(bf16[128,512]{1,0:T(8,128)(2,1)S(1)} %slice.94), channel_id=1, source_target_pairs={{0,16},{8,24},{16,0},{24,8},{1,17},{9,25},{17,1},{25,9},{2,18},{10... | collective-permute-start | bytes 393224 | tf_op jit(solution)/shard_map/ppermute | solution.py:534
  163.0 12.1 %collective-permute-start.38 = (bf16[96,768]{1,0:T(8,128)(2,1)S(1)}, bf16[96,768]{1,0:T(8,128)(2,1)S(1)}, u32[]{:S(2)}, u32[]{:S(2)}) collective-permute-start(bf16[96,768]{1,0:T(8,128)(2,1)S(1)} %fusion.15.refs_0_), channel_id=1, source_target_pairs={{0,4},{4,0},{1,5},{5,1},{2,6},{6,2},{3,7},{7,3},{8,12},{12,8},{9,1... | collective-permute-start | bytes 442376 | tf_op jit(solution)/shard_map/ppermute | solution.py:534
  164.5 11.8 %collective-permute-start.39 = (bf16[96,768]{1,0:T(8,128)(2,1)S(1)}, bf16[96,768]{1,0:T(8,128)(2,1)S(1)}, u32[]{:S(2)}, u32[]{:S(2)}) collective-permute-start(bf16[96,768]{1,0:T(8,128)(2,1)S(1)} %collective-permute-done.22.refs_1_), channel_id=1, source_target_pairs={{0,4},{4,0},{1,5},{5,1},{2,6},{6,2},{3,7},{7,3},{8,12},{12,8},{9,1... | collective-permute-start | bytes 442376 | tf_op jit(solution)/shard_map/ppermute | solution.py:534
  176.3 11.8 %collective-permute-start.35 = (bf16[128,512]{1,0:T(8,128)(2,1)S(1)}, bf16[128,512]{1,0:T(8,128)(2,1)S(1)}, u32[]{:S(2)}, u32[]{:S(2)}) collective-permute-start(bf16[128,512]{1,0:T(8,128)(2,1)S(1)} %fusion.17.refs_0_), channel_id=1, source_target_pairs={{0,16},{8,24},{16,0},{24,8},{1,17},{9,25},{17,1},{25,9},{2,18},{10... | collective-permute-start | bytes 393224 | tf_op jit(solution)/shard_map/ppermute | solution.py:534
  178.6 17.8 %collective-permute-start.34 = (bf16[128,512]{1,0:T(8,128)(2,1)S(1)}, bf16[128,512]{1,0:T(8,128)(2,1)S(1)}, u32[]{:S(2)}, u32[]{:S(2)}) collective-permute-start(bf16[128,512]{1,0:T(8,128)(2,1)S(1)} %fusion.17.refs_0_), channel_id=1, source_target_pairs={{0,8},{8,0},{16,24},{24,16},{1,9},{9,1},{17,25},{25,17},{2,10},{10... | collective-permute-start | bytes 393224 | tf_op jit(solution)/shard_map/ppermute | solution.py:534
  (52 other events, 456.4 us)

commit v9 on v8

--- a/solution.py
+++ b/solution.py
@@ -619,16 +619,9 @@
         c_in,
     )
 
-    embed_parts, _ = gather_parts(embed_part)
-    critic_keyval, factor_c, embedded = join_rows(place, embed_parts, c_keyval)
-    critic_queries = (dot(embedded, c_query) * (factor_c[:, :1] * score_scale)).astype(BF16)
-
-    late_hidden, critic_keyval = tied(hidden, critic_keyval)
-    source = late_hidden.astype(F32)
+    source = hidden.astype(F32)
     factor_h = row_factor(source)
-    late_keyval, factor_h = tied(critic_keyval, factor_h)
-    pieces_c = gather_blocks(critic_keyval, "rep", late_keyval)
-    logits = dot(late_hidden, w_policy) * factor_h
+    logits = dot(hidden, w_policy) * factor_h
     log_probs = jax.nn.log_softmax(logits, axis=-1)
     onehot = (
         actions[0][:, None] == lax.broadcasted_iota(jnp.int32, logits.shape, 1)
@@ -643,42 +636,47 @@
     dnormed = dot(dlogits.astype(BF16), w_policy.T)
     dhidden = (factor_h * (dnormed - source * (factor_h * along))).astype(BF16)
     half_a = dhidden.shape[1] // 2
-    got_a = swap(
-        product(attended, lax.dynamic_slice_in_dim(dhidden, (1 - batch_index) * half_a, half_a, 1))
-        .astype(BF16),
-        "sec",
-        1,
-    )
-    own_a = product(attended, lax.dynamic_slice_in_dim(dhidden, batch_index * half_a, half_a, 1))
+    send_a, own_a = [
+        product(attended, lax.dynamic_slice_in_dim(dhidden, side * half_a, half_a, 1))
+        for side in (1 - batch_index, batch_index)
+    ]
+
+    embed_far = swap(embed_part, "mdl", 2)
+    embed_far, own_a = tied(embed_far, own_a)
+    got_a = swap(send_a.astype(BF16), "sec", 1)
+    embed_parts = [embed_part, swap(embed_part, "mdl", 1), embed_far, swap(embed_far, "mdl", 1)]
+    critic_keyval, factor_c, embedded = join_rows(place, embed_parts, c_keyval)
+    pieces_c = gather_blocks(critic_keyval, "rep")
+    critic_queries = (dot(embedded, c_query) * (factor_c[:, :1] * score_scale)).astype(BF16)
+    critic_queries, got_a = tied(critic_queries, got_a)
+    keep_a, send_a = split_sum(rep_place, own_a, got_a, rep_count)
+    moved_a = swap(send_a.astype(BF16), "rep", 1)
 
     wide = w_value.shape[0]
     target = lax.dynamic_slice_in_dim(returns[0], mdl_index * value_rows, value_rows, 0)
     emb_mine = lax.dynamic_slice_in_dim(embedded, mdl_index * value_rows, value_rows, 0)
-    critic_queries, own_a, w_row, target, emb_mine = tied(
+    critic_queries, w_row, target, emb_mine = tied(
         critic_queries,
-        own_a,
         w_value.reshape(1, wide),
         target.reshape(value_rows, 1),
         emb_mine,
     )
     state_c = attend_call(critic_queries, pieces_c[:-1], 0, place, [])
-    *state_c, got_a, pieces_c[-1] = tied(*state_c, got_a, pieces_c[-1])
-    keep_a, send_a = split_sum(rep_place, own_a, got_a, rep_count)
-    *state_c, send_a = tied(*state_c, send_a)
-    moved_a = swap(send_a.astype(BF16), "rep", 1)
     critic_attended = attend_call(critic_queries, pieces_c[-1:], rep_count - 1, place, state_c)
 
     send_m, keep_m, att_rows = part_rows(place, critic_attended, c_out)
     near_m = swap(send_m, "mdl", 1)
-    send_y = (keep_m[value_rows:] + near_m[value_rows:].astype(F32)).astype(BF16)
-    got_y = swap(send_y, "mdl", 2)
-    att_there = swap(critic_attended, "sec", 1)
-    got_y, moved_a = tied(got_y, moved_a)
+    near_m, moved_a = tied(near_m, moved_a)
     bit = 2
     while bit < rep_count:
         keep_a, send_a = halve(keep_a, moved_a)
         moved_a = swap(send_a, "rep", bit)
         bit *= 2
+    send_y = (keep_m[value_rows:] + near_m[value_rows:].astype(F32)).astype(BF16)
+    got_y = swap(send_y, "mdl", 2)
+    att_there = swap(critic_attended, "sec", 1)
+    got_y, moved_a = tied(got_y, moved_a)
+    mine_a = gather_blocks((keep_a + moved_a.astype(F32)).astype(BF16), "rep")
     value_wide, d_other, d_own = mixed_rows(
         place, emb_mine, keep_m, near_m, got_y, w_row, target
     )
@@ -686,8 +684,6 @@
     d_there = swap(d_other, "sec", 1)
     d_far = swap(d_own, "mdl", 2)
     there_far = swap(d_other, ("sec", "mdl"), mdl_count | 2)
-    d_far, moved_a = tied(d_far, moved_a)
-    mine_a = gather_blocks((keep_a + moved_a.astype(F32)).astype(BF16), "rep")
     d_there, *mine_a[1:-1] = tied(d_there, *mine_a[1:-1])
     own_rows = jnp.concatenate(
         [d_own, d_far, swap(d_own, "mdl", 1), swap(d_far, "mdl", 1)], axis=0
@@ -725,10 +721,8 @@
         waited = [item for c in turn for item in chunks[c][1] + chunks[c][3]]
         extra = []
         if tick == 0:
-            extra = [chunks[c][0] for c in range(1, CHUNKS)]
+            extra = [chunks[c][0] for c in range(1, CHUNKS)] + mine_a[-1:]
         if tick == 1:
-            extra = mine_a[-1:]
-        if tick == 2:
             extra = theirs_a
         if tick == 2 * levels - 1:
             extra = [actor_summed]

time: 218 us -> 217 us (level)
  waiting for transfers between devices: 99.1 us -> 82.8 us
  starting transfers between devices: 45.4 us -> 54.9 us
  local copies, waits for them, and re-layouts: 11.9 us -> 17.7 us
    ppermute x53, waiting for transfers between devices: 99.1 us -> 82.8 us  [swap(): return lax.ppermute(block, axis, [(i, i ^ bit) for i in range(size)])]
    ppermute x53, starting transfers between devices: 45.4 us -> 54.9 us  [swap(): return lax.ppermute(block, axis, [(i, i ^ bit) for i in range(size)])]
    unnamed x49 -> x59, local copies, waits for them, and re-layouts: 6.17 us -> 11.6 us
  transfers between devices with their start and end apart: 53 -> 53, of which waited for: 30 -> 24; matrix products, arithmetic and copies ran while one was open for 7% -> 8% of each run, Pallas kernels for 12% -> 15%
where the time goes in v9:
time: 217 us; the launch traced here: 216 us
  waiting for transfers between devices  82.8 us (38%)
  starting transfers between devices  54.9 us (25%)
  Pallas kernels  46.7 us (22%)
  local copies, waits for them, and re-layouts  17.7 us (8%)
  matrix products  6.89 us (3%)
  between operations  4.52 us (2%)
  other arithmetic  2.53 us (1%)
    ppermute x53, waiting for transfers between devices, swap(): return lax.ppermute(block, axis, [(i, i ^ bit) for i in range(size)])  82.8 us
    ppermute x53, starting transfers between devices, swap(): return lax.ppermute(block, axis, [(i, i ^ bit) for i in range(size)])  54.9 us
    pallas_call x4, Pallas kernels, attend_call(): pl.pallas_call(functools.partial(body, groups, units, TABLE + first), in_...  14.7 us
    unnamed x59, local copies, waits for them, and re-layouts  11.6 us
    pallas_call x3, Pallas kernels, assemble(): pl.pallas_call(functools.partial(assemble_kernel, spots, chunks), in_spec...  10.3 us
    pallas_call x1, Pallas kernels, hidden_rows(): pl.pallas_call(hidden_kernel, in_specs=[VMEM] * 3 + [ANY] * 2 + [HBM], ou...  5.62 us
  transfers between devices with their start and end apart: 53, of which 24 were waited for; matrix products, arithmetic and copies ran while one was open for 8% of the time, Pallas kernels for 15%

profile of v9, /device:TPU:0, one launch (start us, length us, event | category | flops | bytes accessed | tf_op | source)
XLA Modules:
  0.0 216.0 jit_solution(7556743498613197446)
XLA Ops:
  0.7 3.0 %collective-permute-start.3 = (bf16[384,1536]{1,0:T(8,128)(2,1)}, bf16[384,1536]{1,0:T(8,128)(2,1)}, u32[]{:S(2)}, u32[]{:S(2)}) collective-permute-start(bf16[384,1536]{1,0:T(8,128)(2,1)} %w0.1), channel_id=1, source_target_pairs={{0,2},{1,3},{2,0},{3,1},{4,6},{5,7},{6,4},{7,5},{8,10},{9,11},{10,... | collective-permute-start | bytes 3538952 | tf_op jit(solution)/shard_map/ppermute | solution.py:534
  3.7 3.5 %first_projection.1 = (bf16[2,512,128]{2,1,0:T(8,128)(2,1)}, f32[512,128]{1,0:T(8,128)}) custom-call(bf16[512,1536]{1,0:T(8,128)(2,1)} %bitcast.26, bf16[2,1536,128]{2,1,0:T(8,128)(2,1)} %w_hbm.2), custom_call_target="tpu_custom_call" | custom-call | flops 402653184 | bytes 1572864 | tf_op jit(solution)/shard_map/first_projection/pallas_call | solution.py:77
  22.6 4.1 %collective-permute-done.1.refs_2_ = bf16[2,512,128]{2,1,0:T(8,128)(2,1)S(1)} collective-permute-done((bf16[2,512,128]{2,1,0:T(8,128)(2,1)S(1)}, bf16[2,512,128]{2,1,0:T(8,128)(2,1)S(1)}, u32[]{:S(2)}, u32[]{:S(2)}) %collective-permute-start.1) | collective-permute-done | bytes 262176 | tf_op jit(solution)/shard_map/ppermute | solution.py:534
  26.7 3.6 %attend_open.2 = (f32[512,768]{1,0:T(8,128)S(1)}, f32[512,384]{1,0:T(8,128)S(1)}) custom-call(s32[10]{0:T(128)S(1)} %stack.39.left_ref.place_ref, bf16[512,384]{1,0:T(8,128)(2,1)S(1)} %query_projection.1.q_ref, bf16[2,512,128]{2,1,0:T(8,128)(2,1)S(1)} %copy-done.20, bf16[2,512,128]{2,1,0:T(8,128)(2,1)S(1)} %collective-permute-done.refs_1_, ...), custom_call_target="tpu_custom_call" | custom-call | flops 7247757312 | bytes 786432 | tf_op jit(solution)/shard_map/attend_open/pallas_call | solution.py:219
  36.8 3.1 %near_rows.1.sum_ref = f32[512,1536]{1,0:T(8,128)S(1)} custom-call(bf16[512,1536]{1,0:T(8,128)(2,1)S(1)} %bitcast.28, bf16[512,384]{1,0:T(8,128)(2,1)S(1)} %attend_close.2.t0, bf16[512,384]{1,0:T(8,128)(2,1)S(1)} %collective-permute-done.5.t1, bf16[384,1536]{1,0:T(8,128)(2,1)} %w0.1, bf16[384,1536]{1,0:T(8,128)(2,1)} %collective-permute-done.6.w1), custom_call_target="tpu_custom_call" | custom-call | flops 1207959552 | bytes 2359296 | tf_op jit(solution)/shard_map/near_rows/pallas_call | solution.py:249
  41.6 3.8 %collective-permute-done.4.t2 = bf16[512,384]{1,0:T(8,128)(2,1)} collective-permute-done((bf16[512,384]{1,0:T(8,128)(2,1)S(1)}, bf16[512,384]{1,0:T(8,128)(2,1)}, u32[]{:S(2)}, u32[]{:S(2)}) %collective-permute-start.4) | collective-permute-done | bytes 393248 | tf_op jit(solution)/shard_map/ppermute | solution.py:534
  50.8 5.6 %hidden_rows.1 = (bf16[512,1536]{1,0:T(8,128)(2,1)S(1)}, bf16[512,512]{1,0:T(8,128)(2,1)}) custom-call(f32[512,1536]{1,0:T(8,128)S(1)} %copy-done.7, bf16[512,384]{1,0:T(8,128)(2,1)} %collective-permute-done.4.t2, bf16[512,384]{1,0:T(8,128)(2,1)} %collective-permute-done.7.t3, bf16[384,1536]{1,0:T(8,128)(2,1)} %collective-permute-done.3.w2, ...), custom_call_target="tpu_custom_call" | custom-call | flops 2415919104 | bytes 4718592 | tf_op jit(solution)/shard_map/hidden_rows/pallas_call | solution.py:287
  61.3 9.5 %collective-permute-done.10.e2 = bf16[512,512]{1,0:T(8,128)(2,1)} collective-permute-done((bf16[512,512]{1,0:T(8,128)(2,1)}, bf16[512,512]{1,0:T(8,128)(2,1)}, u32[]{:S(2)}, u32[]{:S(2)}) %collective-permute-start.10) | collective-permute-done | bytes 524320 | tf_op jit(solution)/shard_map/ppermute | solution.py:534
  77.7 2.9 %collective-permute-start.13 = (bf16[2,512,128]{2,1,0:T(8,128)(2,1)S(1)}, bf16[2,512,128]{2,1,0:T(8,128)(2,1)S(1)}, u32[]{:S(2)}, u32[]{:S(2)}) collective-permute-start(bf16[2,512,128]{2,1,0:T(8,128)(2,1)S(1)} %get-tuple-element.84.refs_0_), channel_id=1, source_target_pairs={{0,16},{8,24},{16,0},{24,8},{1,17},{9,25},{17,1},{25,9},{2,18},{10... | collective-permute-start | bytes 786440 | tf_op jit(solution)/shard_map/ppermute | solution.py:534
  82.1 6.4 %collective-permute-done.12.got_ref = bf16[384,768]{1,0:T(8,128)(2,1)S(1)} collective-permute-done((bf16[384,768]{1,0:T(8,128)(2,1)S(1)}, bf16[384,768]{1,0:T(8,128)(2,1)S(1)}, u32[]{:S(2)}, u32[]{:S(2)}) %collective-permute-start.12) | collective-permute-done | bytes 589856 | tf_op jit(solution)/shard_map/ppermute | solution.py:534
  89.3 3.5 %collective-permute-done.13.refs_1_ = bf16[2,512,128]{2,1,0:T(8,128)(2,1)S(1)} collective-permute-done((bf16[2,512,128]{2,1,0:T(8,128)(2,1)S(1)}, bf16[2,512,128]{2,1,0:T(8,128)(2,1)S(1)}, u32[]{:S(2)}, u32[]{:S(2)}) %collective-permute-start.13) | collective-permute-done | bytes 262176 | tf_op jit(solution)/shard_map/ppermute | solution.py:534
  93.1 4.6 %attend_open.3 = (f32[512,1024]{1,0:T(8,128)S(1)}, f32[512,512]{1,0:T(8,128)S(1)}) custom-call(s32[10]{0:T(128)S(1)} %stack.39.left_ref.place_ref, bf16[512,512]{1,0:T(8,128)(2,1)S(1)} %fusion.4.q_ref, bf16[2,512,128]{2,1,0:T(8,128)(2,1)S(1)} %get-tuple-element.84.refs_0_, bf16[2,512,128]{2,1,0:T(8,128)(2,1)S(1)} %collective-permute-done.13.refs_1_, ...), custom_call_target="tpu_custom_call" | custom-call | flops 9663676416 | bytes 1048576 | tf_op jit(solution)/shard_map/attend_open/pallas_call | solution.py:219
  99.1 4.0 %attend_close.3.att_ref = bf16[512,512]{1,0:T(8,128)(2,1)} custom-call(s32[10]{0:T(128)S(1)} %stack.39.left_ref.place_ref, bf16[512,512]{1,0:T(8,128)(2,1)S(1)} %fusion.4.q_ref, f32[512,1024]{1,0:T(8,128)S(1)} %get-tuple-element.85.wide_ref, f32[512,512]{1,0:T(8,128)S(1)} %get-tuple-element.86.top_ref, bf16[2,512,128]{2,1,0:T(8,128)(2,1)S(1)} %collective-permute-done.15.refs_0_), custom_call_target="tpu_custom_call" | custom-call | flops 134217728 | bytes 1048576 | tf_op jit(solution)/shard_map/attend_close/pallas_call | solution.py:219
  107.4 7.9 %collective-permute-done.17 = bf16[192,768]{1,0:T(8,128)(2,1)S(1)} collective-permute-done((bf16[192,768]{1,0:T(8,128)(2,1)S(1)}, bf16[192,768]{1,0:T(8,128)(2,1)S(1)}, u32[]{:S(2)}, u32[]{:S(2)}) %collective-permute-start.17) | collective-permute-done | bytes 294944 | tf_op jit(solution)/shard_map/ppermute | solution.py:534
  119.3 6.7 %collective-permute-done.19 = bf16[96,768]{1,0:T(8,128)(2,1)S(1)} collective-permute-done((bf16[96,768]{1,0:T(8,128)(2,1)S(1)}, bf16[96,768]{1,0:T(8,128)(2,1)S(1)}, u32[]{:S(2)}, u32[]{:S(2)}) %collective-permute-start.19) | collective-permute-done | bytes 147488 | tf_op jit(solution)/shard_map/ppermute | solution.py:534
  126.0 3.1 %collective-permute-done.18.got_ref = bf16[128,2048]{1,0:T(8,128)(2,1)S(1)} collective-permute-done((bf16[128,2048]{1,0:T(8,128)(2,1)S(1)}, bf16[128,2048]{1,0:T(8,128)(2,1)S(1)}, u32[]{:S(2)}, u32[]{:S(2)}) %collective-permute-start.18) | collective-permute-done | bytes 524320 | tf_op jit(solution)/shard_map/ppermute | solution.py:534
  146.4 3.1 %collective-permute-done.23 = bf16[128,1024]{1,0:T(8,128)(2,1)S(1)} collective-permute-done((bf16[128,1024]{1,0:T(8,128)(2,1)}, bf16[128,1024]{1,0:T(8,128)(2,1)S(1)}, u32[]{:S(2)}, u32[]{:S(2)}) %collective-permute-start.23) | collective-permute-done | bytes 262176 | tf_op jit(solution)/shard_map/ppermute | solution.py:534
  159.3 5.1 %collective-permute-done.30 = bf16[256,512]{1,0:T(8,128)(2,1)S(1)} collective-permute-done((bf16[256,512]{1,0:T(8,128)(2,1)S(1)}, bf16[256,512]{1,0:T(8,128)(2,1)S(1)}, u32[]{:S(2)}, u32[]{:S(2)}) %collective-permute-start.30) | collective-permute-done | bytes 262176 | tf_op jit(solution)/shard_map/ppermute | solution.py:534
  168.4 5.7 %collective-permute-done.33 = bf16[256,512]{1,0:T(8,128)(2,1)S(1)} collective-permute-done((bf16[256,512]{1,0:T(8,128)(2,1)S(1)}, bf16[256,512]{1,0:T(8,128)(2,1)S(1)}, u32[]{:S(2)}, u32[]{:S(2)}) %collective-permute-start.33) | collective-permute-done | bytes 262176 | tf_op jit(solution)/shard_map/ppermute | solution.py:534
  179.4 5.8 %collective-permute-done.41 = bf16[128,512]{1,0:T(8,128)(2,1)S(1)} collective-permute-done((bf16[128,512]{1,0:T(8,128)(2,1)S(1)}, bf16[128,512]{1,0:T(8,128)(2,1)S(1)}, u32[]{:S(2)}, u32[]{:S(2)}) %collective-permute-start.41) | collective-permute-done | bytes 131104 | tf_op jit(solution)/shard_map/ppermute | solution.py:534
  188.8 4.1 %collective-permute-start.42 = (bf16[128,512]{1,0:T(8,128)(2,1)S(1)}, bf16[128,512]{1,0:T(8,128)(2,1)S(1)}, u32[]{:S(2)}, u32[]{:S(2)}) collective-permute-start(bf16[128,512]{1,0:T(8,128)(2,1)S(1)} %collective-permute-done.39.refs_1_), channel_id=1, source_target_pairs={{0,8},{8,0},{16,24},{24,16},{1,9},{9,1},{17,25},{25,17},{2,10},{10... | collective-permute-start | bytes 393224 | tf_op jit(solution)/shard_map/ppermute | solution.py:534
  192.8 3.6 %assemble.3 = f32[384,1536]{1,0:T(8,128)} custom-call(s32[10]{0:T(128)S(1)} %stack.39.left_ref.place_ref, bf16[96,768]{1,0:T(8,128)(2,1)S(1)} %fusion.16.refs_0_, bf16[96,768]{1,0:T(8,128)(2,1)S(1)} %collective-permute-done.21.refs_1_, bf16[96,768]{1,0:T(8,128)(2,1)S(1)} %collective-permute-done.22.refs_2_, ...), custom_call_target="tpu_custom_call" | custom-call | flops 589824 | bytes 3538944 | tf_op jit(solution)/shard_map/assemble/pallas_call | solution.py:512
  201.2 3.6 %assemble.4.refs_7_ = f32[512,2048]{1,0:T(8,128)} custom-call(s32[10]{0:T(128)S(1)} %stack.39.left_ref.place_ref, bf16[128,512]{1,0:T(8,128)(2,1)S(1)} %fusion.18.refs_0_, bf16[128,512]{1,0:T(8,128)(2,1)S(1)} %collective-permute-done.39.refs_1_, bf16[128,512]{1,0:T(8,128)(2,1)S(1)} %collective-permute-done.38.refs_2_, ...), custom_call_target="tpu_custom_call" | custom-call | flops 1048576 | bytes 6291456 | tf_op jit(solution)/shard_map/assemble/pallas_call | solution.py:512
  212.7 3.1 %assemble.5 = f32[512,2048]{1,0:T(8,128)} custom-call(s32[10]{0:T(128)S(1)} %stack.39.left_ref.place_ref, bf16[128,512]{1,0:T(8,128)(2,1)S(1)} %collective-permute-done.46.refs_0_, bf16[128,512]{1,0:T(8,128)(2,1)S(1)} %collective-permute-done.47.refs_1_, bf16[128,512]{1,0:T(8,128)(2,1)S(1)} %collective-permute-done.48.refs_2_, ...), custom_call_target="tpu_custom_call", output_to_operand_aliasing={{}: (8, {})} | custom-call | flops 1048576 | bytes 6291456 | tf_op jit(solution)/shard_map/assemble/pallas_call | solution.py:512
  (197 shorter events, 101.9 us)
Async XLA Ops:
  0.7 33.0 %collective-permute-start.3 = (bf16[384,1536]{1,0:T(8,128)(2,1)}, bf16[384,1536]{1,0:T(8,128)(2,1)}, u32[]{:S(2)}, u32[]{:S(2)}) collective-permute-start(bf16[384,1536]{1,0:T(8,128)(2,1)} %w0.1), channel_id=1, source_target_pairs={{0,2},{1,3},{2,0},{3,1},{4,6},{5,7},{6,4},{7,5},{8,10},{9,11},{10,... | collective-permute-start | bytes 3538952 | tf_op jit(solution)/shard_map/ppermute | solution.py:534
  7.2 14.7 %collective-permute-start = (bf16[2,512,128]{2,1,0:T(8,128)(2,1)}, bf16[2,512,128]{2,1,0:T(8,128)(2,1)S(1)}, u32[]{:S(2)}, u32[]{:S(2)}) collective-permute-start(bf16[2,512,128]{2,1,0:T(8,128)(2,1)} %get-tuple-element.69.refs_0_), channel_id=1, source_target_pairs={{0,16},{8,24},{16,0},{24,8},{1,17},{9,25},{17,1},{25,9},{2,18},{10... | collective-permute-start | bytes 786440 | tf_op jit(solution)/shard_map/ppermute | solution.py:534
  13.4 13.2 %collective-permute-start.1 = (bf16[2,512,128]{2,1,0:T(8,128)(2,1)S(1)}, bf16[2,512,128]{2,1,0:T(8,128)(2,1)S(1)}, u32[]{:S(2)}, u32[]{:S(2)}) collective-permute-start(bf16[2,512,128]{2,1,0:T(8,128)(2,1)S(1)} %copy-done.20), channel_id=1, source_target_pairs={{0,8},{8,0},{16,24},{24,16},{1,9},{9,1},{17,25},{25,17},{2,10},{10... | collective-permute-start | bytes 786440 | tf_op jit(solution)/shard_map/ppermute | solution.py:534
  15.1 19.9 %collective-permute-start.6 = (bf16[384,1536]{1,0:T(8,128)(2,1)}, bf16[384,1536]{1,0:T(8,128)(2,1)}, u32[]{:S(2)}, u32[]{:S(2)}) collective-permute-start(bf16[384,1536]{1,0:T(8,128)(2,1)} %w0.1), channel_id=1, source_target_pairs={{0,1},{1,0},{2,3},{3,2},{4,5},{5,4},{6,7},{7,6},{8,9},{9,8},{10,11... | collective-permute-start | bytes 3538952 | tf_op jit(solution)/shard_map/ppermute | solution.py:534
  33.7 13.8 %collective-permute-start.8 = (bf16[384,1536]{1,0:T(8,128)(2,1)}, bf16[384,1536]{1,0:T(8,128)(2,1)S(1)}, u32[]{:S(2)}, u32[]{:S(2)}) collective-permute-start(bf16[384,1536]{1,0:T(8,128)(2,1)} %collective-permute-done.3.w2), channel_id=1, source_target_pairs={{0,1},{1,0},{2,3},{3,2},{4,5},{5,4},{6,7},{7,6},{8,9},{9,8},{10,11... | collective-permute-start | bytes 3538952 | tf_op jit(solution)/shard_map/ppermute | solution.py:534
  34.2 11.2 %collective-permute-start.4 = (bf16[512,384]{1,0:T(8,128)(2,1)S(1)}, bf16[512,384]{1,0:T(8,128)(2,1)}, u32[]{:S(2)}, u32[]{:S(2)}) collective-permute-start(bf16[512,384]{1,0:T(8,128)(2,1)S(1)} %attend_close.2.t0), channel_id=1, source_target_pairs={{0,2},{1,3},{2,0},{3,1},{4,6},{5,7},{6,4},{7,5},{8,10},{9,11},{10,... | collective-permute-start | bytes 1179656 | tf_op jit(solution)/shard_map/ppermute | solution.py:534
  56.5 14.3 %collective-permute-start.10 = (bf16[512,512]{1,0:T(8,128)(2,1)}, bf16[512,512]{1,0:T(8,128)(2,1)}, u32[]{:S(2)}, u32[]{:S(2)}) collective-permute-start(bf16[512,512]{1,0:T(8,128)(2,1)} %get-tuple-element.76.e0), channel_id=1, source_target_pairs={{0,2},{1,3},{2,0},{3,1},{4,6},{5,7},{6,4},{7,5},{8,10},{9,11},{10,... | collective-permute-start | bytes 1572872 | tf_op jit(solution)/shard_map/ppermute | solution.py:534
  57.3 17.6 %collective-permute-start.9 = (bf16[512,512]{1,0:T(8,128)(2,1)}, bf16[512,512]{1,0:T(8,128)(2,1)}, u32[]{:S(2)}, u32[]{:S(2)}) collective-permute-start(bf16[512,512]{1,0:T(8,128)(2,1)} %get-tuple-element.76.e0), channel_id=1, source_target_pairs={{0,1},{1,0},{2,3},{3,2},{4,5},{5,4},{6,7},{7,6},{8,9},{9,8},{10,11... | collective-permute-start | bytes 1572872 | tf_op jit(solution)/shard_map/ppermute | solution.py:534
  72.7 15.8 %collective-permute-start.12 = (bf16[384,768]{1,0:T(8,128)(2,1)S(1)}, bf16[384,768]{1,0:T(8,128)(2,1)S(1)}, u32[]{:S(2)}, u32[]{:S(2)}) collective-permute-start(bf16[384,768]{1,0:T(8,128)(2,1)S(1)} %convolution_convert_fusion), channel_id=1, source_target_pairs={{0,4},{4,0},{1,5},{5,1},{2,6},{6,2},{3,7},{7,3},{8,12},{12,8},{9,1... | collective-permute-start | bytes 1769480 | tf_op jit(solution)/shard_map/ppermute | solution.py:534
  77.6 15.4 %collective-permute-start.14 = (bf16[2,512,128]{2,1,0:T(8,128)(2,1)S(1)}, bf16[2,512,128]{2,1,0:T(8,128)(2,1)S(1)}, u32[]{:S(2)}, u32[]{:S(2)}) collective-permute-start(bf16[2,512,128]{2,1,0:T(8,128)(2,1)S(1)} %get-tuple-element.84.refs_0_), channel_id=1, source_target_pairs={{0,8},{8,0},{16,24},{24,16},{1,9},{9,1},{17,25},{25,17},{2,10},{10... | collective-permute-start | bytes 786440 | tf_op jit(solution)/shard_map/ppermute | solution.py:534
  77.7 15.1 %collective-permute-start.13 = (bf16[2,512,128]{2,1,0:T(8,128)(2,1)S(1)}, bf16[2,512,128]{2,1,0:T(8,128)(2,1)S(1)}, u32[]{:S(2)}, u32[]{:S(2)}) collective-permute-start(bf16[2,512,128]{2,1,0:T(8,128)(2,1)S(1)} %get-tuple-element.84.refs_0_), channel_id=1, source_target_pairs={{0,16},{8,24},{16,0},{24,8},{1,17},{9,25},{17,1},{25,9},{2,18},{10... | collective-permute-start | bytes 786440 | tf_op jit(solution)/shard_map/ppermute | solution.py:534
  115.5 13.6 %collective-permute-start.18 = (bf16[128,2048]{1,0:T(8,128)(2,1)S(1)}, bf16[128,2048]{1,0:T(8,128)(2,1)S(1)}, u32[]{:S(2)}, u32[]{:S(2)}) collective-permute-start(bf16[128,2048]{1,0:T(8,128)(2,1)S(1)} %add_convert_fusion), channel_id=1, source_target_pairs={{0,2},{1,3},{2,0},{3,1},{4,6},{5,7},{6,4},{7,5},{8,10},{9,11},{10,... | collective-permute-start | bytes 1572872 | tf_op jit(solution)/shard_map/ppermute | solution.py:534
  116.4 24.2 %collective-permute-start.29 = (bf16[512,512]{1,0:T(8,128)(2,1)}, bf16[512,512]{1,0:T(8,128)(2,1)}, u32[]{:S(2)}, u32[]{:S(2)}) collective-permute-start(bf16[512,512]{1,0:T(8,128)(2,1)} %attend_close.3.att_ref), channel_id=1, source_target_pairs={{0,4},{4,0},{1,5},{5,1},{2,6},{6,2},{3,7},{7,3},{8,12},{12,8},{9,1... | collective-permute-start | bytes 1572872 | tf_op jit(solution)/shard_map/ppermute | solution.py:534
  129.1 13.8 %collective-permute-start.22 = (bf16[96,768]{1,0:T(8,128)(2,1)S(1)}, bf16[96,768]{1,0:T(8,128)(2,1)S(1)}, u32[]{:S(2)}, u32[]{:S(2)}) collective-permute-start(bf16[96,768]{1,0:T(8,128)(2,1)S(1)} %fusion.16.refs_0_), channel_id=1, source_target_pairs={{0,8},{8,0},{16,24},{24,16},{1,9},{9,1},{17,25},{25,17},{2,10},{10... | collective-permute-start | bytes 442376 | tf_op jit(solution)/shard_map/ppermute | solution.py:534
  135.8 10.6 %collective-permute-start.20 = (bf16[128,1024]{1,0:T(8,128)(2,1)}, bf16[128,1024]{1,0:T(8,128)(2,1)S(1)}, u32[]{:S(2)}, u32[]{:S(2)}) collective-permute-start(bf16[128,1024]{1,0:T(8,128)(2,1)} %get-tuple-element.99), channel_id=1, source_target_pairs={{0,4},{4,0},{1,5},{5,1},{2,6},{6,2},{3,7},{7,3},{8,12},{12,8},{9,1... | collective-permute-start | bytes 786440 | tf_op jit(solution)/shard_map/ppermute | solution.py:534
  136.3 13.2 %collective-permute-start.23 = (bf16[128,1024]{1,0:T(8,128)(2,1)}, bf16[128,1024]{1,0:T(8,128)(2,1)S(1)}, u32[]{:S(2)}, u32[]{:S(2)}) collective-permute-start(bf16[128,1024]{1,0:T(8,128)(2,1)} %get-tuple-element.99), channel_id=1, source_target_pairs={{0,6},{1,7},{2,4},{3,5},{4,2},{5,3},{6,0},{7,1},{8,14},{9,15},{10,... | collective-permute-start | bytes 786440 | tf_op jit(solution)/shard_map/ppermute | solution.py:534
  140.6 11.6 %collective-permute-start.26 = (bf16[128,1024]{1,0:T(8,128)(2,1)}, bf16[128,1024]{1,0:T(8,128)(2,1)S(1)}, u32[]{:S(2)}, u32[]{:S(2)}) collective-permute-start(bf16[128,1024]{1,0:T(8,128)(2,1)} %copy-done.15), channel_id=1, source_target_pairs={{0,2},{1,3},{2,0},{3,1},{4,6},{5,7},{6,4},{7,5},{8,10},{9,11},{10,... | collective-permute-start | bytes 786440 | tf_op jit(solution)/shard_map/ppermute | solution.py:534
  145.9 20.2 %collective-permute-start.34 = (bf16[96,768]{1,0:T(8,128)(2,1)S(1)}, bf16[96,768]{1,0:T(8,128)(2,1)S(1)}, u32[]{:S(2)}, u32[]{:S(2)}) collective-permute-start(bf16[96,768]{1,0:T(8,128)(2,1)S(1)} %fusion.16.refs_0_), channel_id=1, source_target_pairs={{0,4},{4,0},{1,5},{5,1},{2,6},{6,2},{3,7},{7,3},{8,12},{12,8},{9,1... | collective-permute-start | bytes 442376 | tf_op jit(solution)/shard_map/ppermute | solution.py:534
  153.0 15.4 %collective-permute-start.35 = (bf16[96,768]{1,0:T(8,128)(2,1)S(1)}, bf16[96,768]{1,0:T(8,128)(2,1)S(1)}, u32[]{:S(2)}, u32[]{:S(2)}) collective-permute-start(bf16[96,768]{1,0:T(8,128)(2,1)S(1)} %collective-permute-done.21.refs_1_), channel_id=1, source_target_pairs={{0,4},{4,0},{1,5},{5,1},{2,6},{6,2},{3,7},{7,3},{8,12},{12,8},{9,1... | collective-permute-start | bytes 442376 | tf_op jit(solution)/shard_map/ppermute | solution.py:534
  153.5 14.9 %collective-permute-start.36 = (bf16[96,768]{1,0:T(8,128)(2,1)S(1)}, bf16[96,768]{1,0:T(8,128)(2,1)S(1)}, u32[]{:S(2)}, u32[]{:S(2)}) collective-permute-start(bf16[96,768]{1,0:T(8,128)(2,1)S(1)} %collective-permute-done.22.refs_2_), channel_id=1, source_target_pairs={{0,4},{4,0},{1,5},{5,1},{2,6},{6,2},{3,7},{7,3},{8,12},{12,8},{9,1... | collective-permute-start | bytes 442376 | tf_op jit(solution)/shard_map/ppermute | solution.py:534
  158.6 9.7 %collective-permute-start.37 = (bf16[96,768]{1,0:T(8,128)(2,1)S(1)}, bf16[96,768]{1,0:T(8,128)(2,1)S(1)}, u32[]{:S(2)}, u32[]{:S(2)}) collective-permute-start(bf16[96,768]{1,0:T(8,128)(2,1)S(1)} %collective-permute-done.31.refs_3_), channel_id=1, source_target_pairs={{0,4},{4,0},{1,5},{5,1},{2,6},{6,2},{3,7},{7,3},{8,12},{12,8},{9,1... | collective-permute-start | bytes 442376 | tf_op jit(solution)/shard_map/ppermute | solution.py:534
  174.2 11.0 %collective-permute-start.41 = (bf16[128,512]{1,0:T(8,128)(2,1)S(1)}, bf16[128,512]{1,0:T(8,128)(2,1)S(1)}, u32[]{:S(2)}, u32[]{:S(2)}) collective-permute-start(bf16[128,512]{1,0:T(8,128)(2,1)S(1)} %slice.92), channel_id=1, source_target_pairs={{0,16},{8,24},{16,0},{24,8},{1,17},{9,25},{17,1},{25,9},{2,18},{10... | collective-permute-start | bytes 393224 | tf_op jit(solution)/shard_map/ppermute | solution.py:534
  177.7 18.7 %collective-permute-start.38 = (bf16[128,512]{1,0:T(8,128)(2,1)S(1)}, bf16[128,512]{1,0:T(8,128)(2,1)S(1)}, u32[]{:S(2)}, u32[]{:S(2)}) collective-permute-start(bf16[128,512]{1,0:T(8,128)(2,1)S(1)} %fusion.18.refs_0_), channel_id=1, source_target_pairs={{0,8},{8,0},{16,24},{24,16},{1,9},{9,1},{17,25},{25,17},{2,10},{10... | collective-permute-start | bytes 393224 | tf_op jit(solution)/shard_map/ppermute | solution.py:534
  186.7 9.9 %collective-permute-start.45 = (bf16[128,512]{1,0:T(8,128)(2,1)S(1)}, bf16[128,512]{1,0:T(8,128)(2,1)S(1)}, u32[]{:S(2)}, u32[]{:S(2)}) collective-permute-start(bf16[128,512]{1,0:T(8,128)(2,1)S(1)} %fusion.17.refs_6_), channel_id=1, source_target_pairs={{0,4},{4,0},{1,5},{5,1},{2,6},{6,2},{3,7},{7,3},{8,12},{12,8},{9,1... | collective-permute-start | bytes 393224 | tf_op jit(solution)/shard_map/ppermute | solution.py:534
  (57 other events, 424.3 us)

commit v10 on v8

--- a/solution.py
+++ b/solution.py
@@ -686,9 +686,8 @@
     d_there = swap(d_other, "sec", 1)
     d_far = swap(d_own, "mdl", 2)
     there_far = swap(d_other, ("sec", "mdl"), mdl_count | 2)
-    d_far, moved_a = tied(d_far, moved_a)
-    mine_a = gather_blocks((keep_a + moved_a.astype(F32)).astype(BF16), "rep")
-    d_there, *mine_a[1:-1] = tied(d_there, *mine_a[1:-1])
+    d_there, moved_a = tied(d_there, moved_a)
+    total_a = (keep_a + moved_a.astype(F32)).astype(BF16)
     own_rows = jnp.concatenate(
         [d_own, d_far, swap(d_own, "mdl", 1), swap(d_far, "mdl", 1)], axis=0
     )
@@ -703,10 +702,7 @@
         axis=0,
     )
     value_part, there_rows = tied(value_wide[:, 0], there_rows)
-    theirs_a = [swap(block, "sec", 1) for block in mine_a]
     codes = gather_codes(rep_count)
-    spots = [(0, side, code) for side in range(2) for code in codes]
-    actor_summed = assemble(place, mine_a + theirs_a, spots, rep_count, 1, [])
 
     strip = d_own.shape[1] // CHUNKS
     chunks = []
@@ -720,19 +716,23 @@
         )
         chunks.append([keep, [swap(send.astype(BF16), "rep", 1)], [], [], []])
     levels = rep_count.bit_length() - 1
-    for tick in range(2 * levels + CHUNKS - 1):
-        turn = [c for c in range(CHUNKS) if 0 <= tick - c < 2 * levels]
+    last = 2 * levels + CHUNKS - 2
+    first_swap = [swap(total_a, "rep", rep_count // 2)]
+    chunks.append([None, first_swap, [total_a], [swap(total_a, "sec", 1)], []])
+    starts = list(range(CHUNKS)) + [-levels]
+    for tick in range(last + 1):
+        turn = [c for c, start in enumerate(starts) if 0 <= tick - start < 2 * levels]
         waited = [item for c in turn for item in chunks[c][1] + chunks[c][3]]
         extra = []
         if tick == 0:
             extra = [chunks[c][0] for c in range(1, CHUNKS)]
-        if tick == 1:
-            extra = mine_a[-1:]
-        if tick == 2:
-            extra = theirs_a
+        if tick == levels:
+            extra = chunks[CHUNKS][3]
         if tick == 2 * levels - 1:
-            extra = [actor_summed]
-        if tick == 2 * levels + CHUNKS - 2:
+            _, _, mine, crossing, theirs = chunks[CHUNKS]
+            spots = [(0, side, code) for side in range(2) for code in codes]
+            extra = [assemble(place, mine + theirs + crossing, spots, rep_count, 1, [])]
+        if tick == last:
             done = [
                 (item, (c, side, code))
                 for c in range(CHUNKS)
@@ -744,16 +744,18 @@
         if tick == 0:
             for c in range(1, CHUNKS):
                 chunks[c][0] = outs[len(waited) + c - 1]
+        if tick == levels:
+            chunks[CHUNKS][3] = outs[len(waited) :]
         if tick == 2 * levels - 1:
             actor_summed = outs[-1]
-        if tick == 2 * levels + CHUNKS - 2:
+        if tick == last:
             result = outs[-1]
         for c in turn:
             keep, pending, mine, crossing, theirs = chunks[c]
             arrived, outs = outs[: len(pending)], outs[len(pending) :]
             crossed, outs = outs[: len(crossing)], outs[len(crossing) :]
             theirs = theirs + crossed
-            level = tick - c + 1
+            level = tick - starts[c] + 1
             if level < levels:
                 keep, send = halve(keep, arrived[0])
                 pending = [swap(send, "rep", 1 << level)]

time: 218 us -> 214 us (0.982)
  waiting for transfers between devices: 99.1 us -> 96.2 us
    ppermute x53, waiting for transfers between devices: 99.1 us -> 96.2 us  [swap(): return lax.ppermute(block, axis, [(i, i ^ bit) for i in range(size)])]
where the time goes in v10:
time: 214 us
  waiting for transfers between devices  96.2 us (45%)
  Pallas kernels  45.6 us (21%)
  starting transfers between devices  45.3 us (21%)
  local copies, waits for them, and re-layouts  11.9 us (6%)
  matrix products  5.6 us (3%)
  between operations  4.84 us (2%)
  other arithmetic  4.41 us (2%)
    ppermute x53, waiting for transfers between devices, swap(): return lax.ppermute(block, axis, [(i, i ^ bit) for i in range(size)])  96.2 us
    ppermute x53, starting transfers between devices, swap(): return lax.ppermute(block, axis, [(i, i ^ bit) for i in range(size)])  45.3 us
    pallas_call x4, Pallas kernels, attend_call(): pl.pallas_call(functools.partial(body, groups, units, TABLE + first), in_...  15 us
    pallas_call x3, Pallas kernels, assemble(): pl.pallas_call(functools.partial(assemble_kernel, spots, chunks), in_spec...  10.3 us
    unnamed x49, local copies, waits for them, and re-layouts  6.17 us
    pallas_call x1, Pallas kernels, hidden_rows(): pl.pallas_call(hidden_kernel, in_specs=[VMEM] * 3 + [ANY] * 2 + [HBM], ou...  4.46 us
  transfers between devices with their start and end apart: 53, of which 30 were waited for; matrix products, arithmetic and copies ran while one was open for 7% of the time, Pallas kernels for 12%

profile of v10, /device:TPU:0, one launch (start us, length us, event | category | flops | bytes accessed | tf_op | source)
XLA Modules:
  0.0 213.9 jit_solution(4051878156106245931)
XLA Ops:
  0.7 3.0 %collective-permute-start.3 = (bf16[384,1536]{1,0:T(8,128)(2,1)}, bf16[384,1536]{1,0:T(8,128)(2,1)}, u32[]{:S(2)}, u32[]{:S(2)}) collective-permute-start(bf16[384,1536]{1,0:T(8,128)(2,1)} %w0.1), channel_id=1, source_target_pairs={{0,2},{1,3},{2,0},{3,1},{4,6},{5,7},{6,4},{7,5},{8,10},{9,11},{10,... | collective-permute-start | bytes 3538952 | tf_op jit(solution)/shard_map/ppermute | solution.py:534
  3.7 3.5 %first_projection.1 = (bf16[2,512,128]{2,1,0:T(8,128)(2,1)}, f32[512,128]{1,0:T(8,128)}) custom-call(bf16[512,1536]{1,0:T(8,128)(2,1)} %bitcast.30, bf16[2,1536,128]{2,1,0:T(8,128)(2,1)} %w_hbm.2), custom_call_target="tpu_custom_call" | custom-call | flops 402653184 | bytes 1572864 | tf_op jit(solution)/shard_map/first_projection/pallas_call | solution.py:77
  22.6 4.1 %collective-permute-done.1.refs_2_ = bf16[2,512,128]{2,1,0:T(8,128)(2,1)S(1)} collective-permute-done((bf16[2,512,128]{2,1,0:T(8,128)(2,1)S(1)}, bf16[2,512,128]{2,1,0:T(8,128)(2,1)S(1)}, u32[]{:S(2)}, u32[]{:S(2)}) %collective-permute-start.1) | collective-permute-done | bytes 262176 | tf_op jit(solution)/shard_map/ppermute | solution.py:534
  26.7 3.6 %attend_open.2 = (f32[512,768]{1,0:T(8,128)S(1)}, f32[512,384]{1,0:T(8,128)S(1)}) custom-call(s32[10]{0:T(128)S(1)} %stack.39.left_ref.place_ref, bf16[512,384]{1,0:T(8,128)(2,1)S(1)} %query_projection.1.q_ref, bf16[2,512,128]{2,1,0:T(8,128)(2,1)S(1)} %copy-done.16, bf16[2,512,128]{2,1,0:T(8,128)(2,1)S(1)} %collective-permute-done.refs_1_, ...), custom_call_target="tpu_custom_call" | custom-call | flops 7247757312 | bytes 786432 | tf_op jit(solution)/shard_map/attend_open/pallas_call | solution.py:219
  36.8 3.1 %near_rows.1.sum_ref = f32[512,1536]{1,0:T(8,128)S(1)} custom-call(bf16[512,1536]{1,0:T(8,128)(2,1)S(1)} %bitcast.32, bf16[512,384]{1,0:T(8,128)(2,1)S(1)} %attend_close.2.t0, bf16[512,384]{1,0:T(8,128)(2,1)S(1)} %collective-permute-done.5.t1, bf16[384,1536]{1,0:T(8,128)(2,1)} %w0.1, bf16[384,1536]{1,0:T(8,128)(2,1)} %collective-permute-done.6.w1), custom_call_target="tpu_custom_call" | custom-call | flops 1207959552 | bytes 2359296 | tf_op jit(solution)/shard_map/near_rows/pallas_call | solution.py:249
  40.0 5.4 %collective-permute-done.4.t2 = bf16[512,384]{1,0:T(8,128)(2,1)S(1)} collective-permute-done((bf16[512,384]{1,0:T(8,128)(2,1)S(1)}, bf16[512,384]{1,0:T(8,128)(2,1)S(1)}, u32[]{:S(2)}, u32[]{:S(2)}) %collective-permute-start.4) | collective-permute-done | bytes 393248 | tf_op jit(solution)/shard_map/ppermute | solution.py:534
  47.1 4.5 %hidden_rows.1 = (bf16[512,1536]{1,0:T(8,128)(2,1)S(1)}, bf16[512,512]{1,0:T(8,128)(2,1)}) custom-call(f32[512,1536]{1,0:T(8,128)S(1)} %near_rows.1.sum_ref, bf16[512,384]{1,0:T(8,128)(2,1)S(1)} %collective-permute-done.4.t2, bf16[512,384]{1,0:T(8,128)(2,1)S(1)} %collective-permute-done.7.t3, bf16[384,1536]{1,0:T(8,128)(2,1)} %collective-permute-done.3.w2, ...), custom_call_target="tpu_custom_call" | custom-call | flops 2415919104 | bytes 4718592 | tf_op jit(solution)/shard_map/hidden_rows/pallas_call | solution.py:287
  53.5 13.5 %collective-permute-done.10.e2 = bf16[512,512]{1,0:T(8,128)(2,1)} collective-permute-done((bf16[512,512]{1,0:T(8,128)(2,1)}, bf16[512,512]{1,0:T(8,128)(2,1)}, u32[]{:S(2)}, u32[]{:S(2)}) %collective-permute-start.10) | collective-permute-done | bytes 524320 | tf_op jit(solution)/shard_map/ppermute | solution.py:534
  69.2 2.7 %join_rows.1 = (bf16[2,512,128]{2,1,0:T(8,128)(2,1)S(1)}, f32[512,128]{1,0:T(8,128)S(1)}, bf16[512,2048]{1,0:T(8,128)(2,1)S(1)}) custom-call(s32[10]{0:T(128)S(1)} %stack.39.left_ref.place_ref, bf16[512,512]{1,0:T(8,128)(2,1)} %get-tuple-element.88.e0, bf16[512,512]{1,0:T(8,128)(2,1)} %collective-permute-done.9.e1, ...), custom_call_target="tpu_custom_call" | custom-call | flops 536870912 | bytes 4194304 | tf_op jit(solution)/shard_map/join_rows/pallas_call | solution.py:340
  82.8 4.5 %collective-permute-done.12.refs_1_ = bf16[2,512,128]{2,1,0:T(8,128)(2,1)S(1)} collective-permute-done((bf16[2,512,128]{2,1,0:T(8,128)(2,1)S(1)}, bf16[2,512,128]{2,1,0:T(8,128)(2,1)S(1)}, u32[]{:S(2)}, u32[]{:S(2)}) %collective-permute-start.12) | collective-permute-done | bytes 262176 | tf_op jit(solution)/shard_map/ppermute | solution.py:534
  87.3 2.7 %collective-permute-done.13.refs_2_ = bf16[2,512,128]{2,1,0:T(8,128)(2,1)S(1)} collective-permute-done((bf16[2,512,128]{2,1,0:T(8,128)(2,1)S(1)}, bf16[2,512,128]{2,1,0:T(8,128)(2,1)S(1)}, u32[]{:S(2)}, u32[]{:S(2)}) %collective-permute-start.13) | collective-permute-done | bytes 262176 | tf_op jit(solution)/shard_map/ppermute | solution.py:534
  90.0 4.8 %attend_open.3 = (f32[512,1024]{1,0:T(8,128)S(1)}, f32[512,512]{1,0:T(8,128)S(1)}) custom-call(s32[10]{0:T(128)S(1)} %stack.39.left_ref.place_ref, bf16[512,512]{1,0:T(8,128)(2,1)S(1)} %fusion.3.q_ref, bf16[2,512,128]{2,1,0:T(8,128)(2,1)S(1)} %get-tuple-element.98.refs_0_, bf16[2,512,128]{2,1,0:T(8,128)(2,1)S(1)} %collective-permute-done.12.refs_1_, ...), custom_call_target="tpu_custom_call" | custom-call | flops 9663676416 | bytes 1048576 | tf_op jit(solution)/shard_map/attend_open/pallas_call | solution.py:219
  97.0 4.1 %attend_close.3.att_ref = bf16[512,512]{1,0:T(8,128)(2,1)} custom-call(s32[10]{0:T(128)S(1)} %stack.39.left_ref.place_ref, bf16[512,512]{1,0:T(8,128)(2,1)S(1)} %fusion.3.q_ref, f32[512,1024]{1,0:T(8,128)S(1)} %get-tuple-element.106.wide_ref, f32[512,512]{1,0:T(8,128)S(1)} %get-tuple-element.107.top_ref, bf16[2,512,128]{2,1,0:T(8,128)(2,1)S(1)} %collective-permute-done.15.refs_0_), custom_call_target="tpu_custom_call" | custom-call | flops 134217728 | bytes 1048576 | tf_op jit(solution)/shard_map/attend_close/pallas_call | solution.py:219
  109.3 9.9 %collective-permute-done.27 = bf16[512,512]{1,0:T(8,128)(2,1)} collective-permute-done((bf16[512,512]{1,0:T(8,128)(2,1)}, bf16[512,512]{1,0:T(8,128)(2,1)}, u32[]{:S(2)}, u32[]{:S(2)}) %collective-permute-start.27) | collective-permute-done | bytes 524320 | tf_op jit(solution)/shard_map/ppermute | solution.py:534
  131.6 8.6 %collective-permute-done.20 = bf16[96,768]{1,0:T(8,128)(2,1)S(1)} collective-permute-done((bf16[96,768]{1,0:T(8,128)(2,1)S(1)}, bf16[96,768]{1,0:T(8,128)(2,1)S(1)}, u32[]{:S(2)}, u32[]{:S(2)}) %collective-permute-start.20) | collective-permute-done | bytes 147488 | tf_op jit(solution)/shard_map/ppermute | solution.py:534
  149.1 2.7 %collective-permute-done.29.refs_1_ = bf16[96,768]{1,0:T(8,128)(2,1)S(1)} collective-permute-done((bf16[96,768]{1,0:T(8,128)(2,1)S(1)}, bf16[96,768]{1,0:T(8,128)(2,1)S(1)}, u32[]{:S(2)}, u32[]{:S(2)}) %collective-permute-start.29) | collective-permute-done | bytes 147488 | tf_op jit(solution)/shard_map/ppermute | solution.py:534
  151.8 5.6 %collective-permute-done.28 = bf16[256,512]{1,0:T(8,128)(2,1)S(1)} collective-permute-done((bf16[256,512]{1,0:T(8,128)(2,1)S(1)}, bf16[256,512]{1,0:T(8,128)(2,1)S(1)}, u32[]{:S(2)}, u32[]{:S(2)}) %collective-permute-start.28) | collective-permute-done | bytes 262176 | tf_op jit(solution)/shard_map/ppermute | solution.py:534
  162.0 7.0 %collective-permute-done.32 = bf16[256,512]{1,0:T(8,128)(2,1)S(1)} collective-permute-done((bf16[256,512]{1,0:T(8,128)(2,1)S(1)}, bf16[256,512]{1,0:T(8,128)(2,1)S(1)}, u32[]{:S(2)}, u32[]{:S(2)}) %collective-permute-start.32) | collective-permute-done | bytes 262176 | tf_op jit(solution)/shard_map/ppermute | solution.py:534
  174.4 2.8 %collective-permute-start.37 = (bf16[128,512]{1,0:T(8,128)(2,1)S(1)}, bf16[128,512]{1,0:T(8,128)(2,1)S(1)}, u32[]{:S(2)}, u32[]{:S(2)}) collective-permute-start(bf16[128,512]{1,0:T(8,128)(2,1)S(1)} %fusion.17.refs_0_), channel_id=1, source_target_pairs={{0,16},{8,24},{16,0},{24,8},{1,17},{9,25},{17,1},{25,9},{2,18},{10... | collective-permute-start | bytes 393224 | tf_op jit(solution)/shard_map/ppermute | solution.py:534
  177.3 4.9 %collective-permute-done.39 = bf16[128,512]{1,0:T(8,128)(2,1)S(1)} collective-permute-done((bf16[128,512]{1,0:T(8,128)(2,1)S(1)}, bf16[128,512]{1,0:T(8,128)(2,1)S(1)}, u32[]{:S(2)}, u32[]{:S(2)}) %collective-permute-start.39) | collective-permute-done | bytes 131104 | tf_op jit(solution)/shard_map/ppermute | solution.py:534
  189.8 3.6 %assemble.3 = f32[384,1536]{1,0:T(8,128)} custom-call(s32[10]{0:T(128)S(1)} %stack.39.left_ref.place_ref, bf16[96,768]{1,0:T(8,128)(2,1)S(1)} %fusion.15.refs_0_, bf16[96,768]{1,0:T(8,128)(2,1)S(1)} %collective-permute-done.29.refs_1_, bf16[96,768]{1,0:T(8,128)(2,1)S(1)} %collective-permute-done.33.refs_2_, ...), custom_call_target="tpu_custom_call" | custom-call | flops 589824 | bytes 3538944 | tf_op jit(solution)/shard_map/assemble/pallas_call | solution.py:512
  198.5 3.6 %assemble.4.refs_7_ = f32[512,2048]{1,0:T(8,128)} custom-call(s32[10]{0:T(128)S(1)} %stack.39.left_ref.place_ref, bf16[128,512]{1,0:T(8,128)(2,1)S(1)} %fusion.17.refs_0_, bf16[128,512]{1,0:T(8,128)(2,1)S(1)} %collective-permute-done.37.refs_1_, bf16[128,512]{1,0:T(8,128)(2,1)S(1)} %collective-permute-done.36.refs_2_, ...), custom_call_target="tpu_custom_call" | custom-call | flops 1048576 | bytes 6291456 | tf_op jit(solution)/shard_map/assemble/pallas_call | solution.py:512
  204.2 2.7 %collective-permute-done.47.refs_1_ = bf16[128,512]{1,0:T(8,128)(2,1)S(1)} collective-permute-done((bf16[128,512]{1,0:T(8,128)(2,1)S(1)}, bf16[128,512]{1,0:T(8,128)(2,1)S(1)}, u32[]{:S(2)}, u32[]{:S(2)}) %collective-permute-start.47) | collective-permute-done | bytes 131104 | tf_op jit(solution)/shard_map/ppermute | solution.py:534
  210.6 3.1 %assemble.5 = f32[512,2048]{1,0:T(8,128)} custom-call(s32[10]{0:T(128)S(1)} %stack.39.left_ref.place_ref, bf16[128,512]{1,0:T(8,128)(2,1)S(1)} %collective-permute-done.46.refs_0_, bf16[128,512]{1,0:T(8,128)(2,1)S(1)} %collective-permute-done.47.refs_1_, bf16[128,512]{1,0:T(8,128)(2,1)S(1)} %collective-permute-done.48.refs_2_, ...), custom_call_target="tpu_custom_call", output_to_operand_aliasing={{}: (8, {})} | custom-call | flops 1048576 | bytes 6291456 | tf_op jit(solution)/shard_map/assemble/pallas_call | solution.py:512
  (188 shorter events, 95.0 us)
Async XLA Ops:
  0.7 33.0 %collective-permute-start.3 = (bf16[384,1536]{1,0:T(8,128)(2,1)}, bf16[384,1536]{1,0:T(8,128)(2,1)}, u32[]{:S(2)}, u32[]{:S(2)}) collective-permute-start(bf16[384,1536]{1,0:T(8,128)(2,1)} %w0.1), channel_id=1, source_target_pairs={{0,2},{1,3},{2,0},{3,1},{4,6},{5,7},{6,4},{7,5},{8,10},{9,11},{10,... | collective-permute-start | bytes 3538952 | tf_op jit(solution)/shard_map/ppermute | solution.py:534
  7.2 14.7 %collective-permute-start = (bf16[2,512,128]{2,1,0:T(8,128)(2,1)}, bf16[2,512,128]{2,1,0:T(8,128)(2,1)S(1)}, u32[]{:S(2)}, u32[]{:S(2)}) collective-permute-start(bf16[2,512,128]{2,1,0:T(8,128)(2,1)} %get-tuple-element.81.refs_0_), channel_id=1, source_target_pairs={{0,16},{8,24},{16,0},{24,8},{1,17},{9,25},{17,1},{25,9},{2,18},{10... | collective-permute-start | bytes 786440 | tf_op jit(solution)/shard_map/ppermute | solution.py:534
  13.4 13.2 %collective-permute-start.1 = (bf16[2,512,128]{2,1,0:T(8,128)(2,1)S(1)}, bf16[2,512,128]{2,1,0:T(8,128)(2,1)S(1)}, u32[]{:S(2)}, u32[]{:S(2)}) collective-permute-start(bf16[2,512,128]{2,1,0:T(8,128)(2,1)S(1)} %copy-done.16), channel_id=1, source_target_pairs={{0,8},{8,0},{16,24},{24,16},{1,9},{9,1},{17,25},{25,17},{2,10},{10... | collective-permute-start | bytes 786440 | tf_op jit(solution)/shard_map/ppermute | solution.py:534
  15.1 19.9 %collective-permute-start.6 = (bf16[384,1536]{1,0:T(8,128)(2,1)}, bf16[384,1536]{1,0:T(8,128)(2,1)}, u32[]{:S(2)}, u32[]{:S(2)}) collective-permute-start(bf16[384,1536]{1,0:T(8,128)(2,1)} %w0.1), channel_id=1, source_target_pairs={{0,1},{1,0},{2,3},{3,2},{4,5},{5,4},{6,7},{7,6},{8,9},{9,8},{10,11... | collective-permute-start | bytes 3538952 | tf_op jit(solution)/shard_map/ppermute | solution.py:534
  33.7 13.4 %collective-permute-start.8 = (bf16[384,1536]{1,0:T(8,128)(2,1)}, bf16[384,1536]{1,0:T(8,128)(2,1)S(1)}, u32[]{:S(2)}, u32[]{:S(2)}) collective-permute-start(bf16[384,1536]{1,0:T(8,128)(2,1)} %collective-permute-done.3.w2), channel_id=1, source_target_pairs={{0,1},{1,0},{2,3},{3,2},{4,5},{5,4},{6,7},{7,6},{8,9},{9,8},{10,11... | collective-permute-start | bytes 3538952 | tf_op jit(solution)/shard_map/ppermute | solution.py:534
  52.7 14.3 %collective-permute-start.10 = (bf16[512,512]{1,0:T(8,128)(2,1)}, bf16[512,512]{1,0:T(8,128)(2,1)}, u32[]{:S(2)}, u32[]{:S(2)}) collective-permute-start(bf16[512,512]{1,0:T(8,128)(2,1)} %get-tuple-element.88.e0), channel_id=1, source_target_pairs={{0,2},{1,3},{2,0},{3,1},{4,6},{5,7},{6,4},{7,5},{8,10},{9,11},{10,... | collective-permute-start | bytes 1572872 | tf_op jit(solution)/shard_map/ppermute | solution.py:534
  53.4 15.0 %collective-permute-start.9 = (bf16[512,512]{1,0:T(8,128)(2,1)}, bf16[512,512]{1,0:T(8,128)(2,1)}, u32[]{:S(2)}, u32[]{:S(2)}) collective-permute-start(bf16[512,512]{1,0:T(8,128)(2,1)} %get-tuple-element.88.e0), channel_id=1, source_target_pairs={{0,1},{1,0},{2,3},{3,2},{4,5},{5,4},{6,7},{7,6},{8,9},{9,8},{10,11... | collective-permute-start | bytes 1572872 | tf_op jit(solution)/shard_map/ppermute | solution.py:534
  72.5 14.8 %collective-permute-start.12 = (bf16[2,512,128]{2,1,0:T(8,128)(2,1)S(1)}, bf16[2,512,128]{2,1,0:T(8,128)(2,1)S(1)}, u32[]{:S(2)}, u32[]{:S(2)}) collective-permute-start(bf16[2,512,128]{2,1,0:T(8,128)(2,1)S(1)} %get-tuple-element.98.refs_0_), channel_id=1, source_target_pairs={{0,16},{8,24},{16,0},{24,8},{1,17},{9,25},{17,1},{25,9},{2,18},{10... | collective-permute-start | bytes 786440 | tf_op jit(solution)/shard_map/ppermute | solution.py:534
  76.3 13.7 %collective-permute-start.13 = (bf16[2,512,128]{2,1,0:T(8,128)(2,1)S(1)}, bf16[2,512,128]{2,1,0:T(8,128)(2,1)S(1)}, u32[]{:S(2)}, u32[]{:S(2)}) collective-permute-start(bf16[2,512,128]{2,1,0:T(8,128)(2,1)S(1)} %get-tuple-element.98.refs_0_), channel_id=1, source_target_pairs={{0,8},{8,0},{16,24},{24,16},{1,9},{9,1},{17,25},{25,17},{2,10},{10... | collective-permute-start | bytes 786440 | tf_op jit(solution)/shard_map/ppermute | solution.py:534
  81.2 14.9 %collective-permute-start.14 = (bf16[384,768]{1,0:T(8,128)(2,1)S(1)}, bf16[384,768]{1,0:T(8,128)(2,1)S(1)}, u32[]{:S(2)}, u32[]{:S(2)}) collective-permute-start(bf16[384,768]{1,0:T(8,128)(2,1)S(1)} %convolution_convert_fusion), channel_id=1, source_target_pairs={{0,4},{4,0},{1,5},{5,1},{2,6},{6,2},{3,7},{7,3},{8,12},{12,8},{9,1... | collective-permute-start | bytes 1769480 | tf_op jit(solution)/shard_map/ppermute | solution.py:534
  104.5 14.7 %collective-permute-start.27 = (bf16[512,512]{1,0:T(8,128)(2,1)}, bf16[512,512]{1,0:T(8,128)(2,1)}, u32[]{:S(2)}, u32[]{:S(2)}) collective-permute-start(bf16[512,512]{1,0:T(8,128)(2,1)} %attend_close.3.att_ref), channel_id=1, source_target_pairs={{0,4},{4,0},{1,5},{5,1},{2,6},{6,2},{3,7},{7,3},{8,12},{12,8},{9,1... | collective-permute-start | bytes 1572872 | tf_op jit(solution)/shard_map/ppermute | solution.py:534
  108.1 14.3 %collective-permute-start.17 = (bf16[128,2048]{1,0:T(8,128)(2,1)}, bf16[128,2048]{1,0:T(8,128)(2,1)}, u32[]{:S(2)}, u32[]{:S(2)}) collective-permute-start(bf16[128,2048]{1,0:T(8,128)(2,1)} %add_convert_fusion), channel_id=1, source_target_pairs={{0,2},{1,3},{2,0},{3,1},{4,6},{5,7},{6,4},{7,5},{8,10},{9,11},{10,... | collective-permute-start | bytes 1572872 | tf_op jit(solution)/shard_map/ppermute | solution.py:534
  108.9 11.5 %collective-permute-start.18 = (bf16[192,768]{1,0:T(8,128)(2,1)S(1)}, bf16[192,768]{1,0:T(8,128)(2,1)}, u32[]{:S(2)}, u32[]{:S(2)}) collective-permute-start(bf16[192,768]{1,0:T(8,128)(2,1)S(1)} %get-tuple-element.111), channel_id=1, source_target_pairs={{0,8},{8,0},{16,24},{24,16},{1,9},{9,1},{17,25},{25,17},{2,10},{10... | collective-permute-start | bytes 884744 | tf_op jit(solution)/shard_map/ppermute | solution.py:534
  125.7 14.5 %collective-permute-start.21 = (bf16[128,1024]{1,0:T(8,128)(2,1)S(1)}, bf16[128,1024]{1,0:T(8,128)(2,1)S(1)}, u32[]{:S(2)}, u32[]{:S(2)}) collective-permute-start(bf16[128,1024]{1,0:T(8,128)(2,1)S(1)} %get-tuple-element.116), channel_id=1, source_target_pairs={{0,6},{1,7},{2,4},{3,5},{4,2},{5,3},{6,0},{7,1},{8,14},{9,15},{10,... | collective-permute-start | bytes 786440 | tf_op jit(solution)/shard_map/ppermute | solution.py:534
  127.4 12.7 %collective-permute-start.19 = (bf16[128,1024]{1,0:T(8,128)(2,1)S(1)}, bf16[128,1024]{1,0:T(8,128)(2,1)S(1)}, u32[]{:S(2)}, u32[]{:S(2)}) collective-permute-start(bf16[128,1024]{1,0:T(8,128)(2,1)S(1)} %get-tuple-element.116), channel_id=1, source_target_pairs={{0,4},{4,0},{1,5},{5,1},{2,6},{6,2},{3,7},{7,3},{8,12},{12,8},{9,1... | collective-permute-start | bytes 786440 | tf_op jit(solution)/shard_map/ppermute | solution.py:534
  128.0 14.3 %collective-permute-start.25 = (bf16[128,1024]{1,0:T(8,128)(2,1)S(1)}, bf16[128,1024]{1,0:T(8,128)(2,1)S(1)}, u32[]{:S(2)}, u32[]{:S(2)}) collective-permute-start(bf16[128,1024]{1,0:T(8,128)(2,1)S(1)} %get-tuple-element.122), channel_id=1, source_target_pairs={{0,1},{1,0},{2,3},{3,2},{4,5},{5,4},{6,7},{7,6},{8,9},{9,8},{10,11... | collective-permute-start | bytes 786440 | tf_op jit(solution)/shard_map/ppermute | solution.py:534
  128.0 14.2 %collective-permute-start.24 = (bf16[128,1024]{1,0:T(8,128)(2,1)S(1)}, bf16[128,1024]{1,0:T(8,128)(2,1)S(1)}, u32[]{:S(2)}, u32[]{:S(2)}) collective-permute-start(bf16[128,1024]{1,0:T(8,128)(2,1)S(1)} %get-tuple-element.122), channel_id=1, source_target_pairs={{0,2},{1,3},{2,0},{3,1},{4,6},{5,7},{6,4},{7,5},{8,10},{9,11},{10,... | collective-permute-start | bytes 786440 | tf_op jit(solution)/shard_map/ppermute | solution.py:534
  145.3 12.1 %collective-permute-start.28 = (bf16[256,512]{1,0:T(8,128)(2,1)S(1)}, bf16[256,512]{1,0:T(8,128)(2,1)S(1)}, u32[]{:S(2)}, u32[]{:S(2)}) collective-permute-start(bf16[256,512]{1,0:T(8,128)(2,1)S(1)} %get-tuple-element.125), channel_id=1, source_target_pairs={{0,8},{8,0},{16,24},{24,16},{1,9},{9,1},{17,25},{25,17},{2,10},{10... | collective-permute-start | bytes 786440 | tf_op jit(solution)/shard_map/ppermute | solution.py:534
  146.8 15.2 %collective-permute-start.33 = (bf16[96,768]{1,0:T(8,128)(2,1)S(1)}, bf16[96,768]{1,0:T(8,128)(2,1)S(1)}, u32[]{:S(2)}, u32[]{:S(2)}) collective-permute-start(bf16[96,768]{1,0:T(8,128)(2,1)S(1)} %fusion.15.refs_0_), channel_id=1, source_target_pairs={{0,8},{8,0},{16,24},{24,16},{1,9},{9,1},{17,25},{25,17},{2,10},{10... | collective-permute-start | bytes 442376 | tf_op jit(solution)/shard_map/ppermute | solution.py:534
  148.0 21.0 %collective-permute-start.32 = (bf16[256,512]{1,0:T(8,128)(2,1)S(1)}, bf16[256,512]{1,0:T(8,128)(2,1)S(1)}, u32[]{:S(2)}, u32[]{:S(2)}) collective-permute-start(bf16[256,512]{1,0:T(8,128)(2,1)S(1)} %get-tuple-element.129), channel_id=1, source_target_pairs={{0,8},{8,0},{16,24},{24,16},{1,9},{9,1},{17,25},{25,17},{2,10},{10... | collective-permute-start | bytes 786440 | tf_op jit(solution)/shard_map/ppermute | solution.py:534
  157.4 11.6 %collective-permute-start.35 = (bf16[96,768]{1,0:T(8,128)(2,1)S(1)}, bf16[96,768]{1,0:T(8,128)(2,1)S(1)}, u32[]{:S(2)}, u32[]{:S(2)}) collective-permute-start(bf16[96,768]{1,0:T(8,128)(2,1)S(1)} %collective-permute-done.29.refs_1_), channel_id=1, source_target_pairs={{0,4},{4,0},{1,5},{5,1},{2,6},{6,2},{3,7},{7,3},{8,12},{12,8},{9,1... | collective-permute-start | bytes 442376 | tf_op jit(solution)/shard_map/ppermute | solution.py:534
  158.0 13.6 %collective-permute-start.34 = (bf16[96,768]{1,0:T(8,128)(2,1)S(1)}, bf16[96,768]{1,0:T(8,128)(2,1)S(1)}, u32[]{:S(2)}, u32[]{:S(2)}) collective-permute-start(bf16[96,768]{1,0:T(8,128)(2,1)S(1)} %collective-permute-done.29.refs_1_), channel_id=1, source_target_pairs={{0,8},{8,0},{16,24},{24,16},{1,9},{9,1},{17,25},{25,17},{2,10},{10... | collective-permute-start | bytes 442376 | tf_op jit(solution)/shard_map/ppermute | solution.py:534
  171.7 13.3 %collective-permute-start.40 = (bf16[96,768]{1,0:T(8,128)(2,1)S(1)}, bf16[96,768]{1,0:T(8,128)(2,1)S(1)}, u32[]{:S(2)}, u32[]{:S(2)}) collective-permute-start(bf16[96,768]{1,0:T(8,128)(2,1)S(1)} %collective-permute-done.33.refs_2_), channel_id=1, source_target_pairs={{0,4},{4,0},{1,5},{5,1},{2,6},{6,2},{3,7},{7,3},{8,12},{12,8},{9,1... | collective-permute-start | bytes 442376 | tf_op jit(solution)/shard_map/ppermute | solution.py:534
  172.3 12.7 %collective-permute-start.41 = (bf16[96,768]{1,0:T(8,128)(2,1)S(1)}, bf16[96,768]{1,0:T(8,128)(2,1)S(1)}, u32[]{:S(2)}, u32[]{:S(2)}) collective-permute-start(bf16[96,768]{1,0:T(8,128)(2,1)S(1)} %collective-permute-done.34.refs_3_), channel_id=1, source_target_pairs={{0,4},{4,0},{1,5},{5,1},{2,6},{6,2},{3,7},{7,3},{8,12},{12,8},{9,1... | collective-permute-start | bytes 442376 | tf_op jit(solution)/shard_map/ppermute | solution.py:534
  (52 other events, 435.6 us)

commit v11 on v10

--- a/solution.py
+++ b/solution.py
@@ -15,7 +15,7 @@
 LOG2E = 1.4426950408889634
 F32 = jnp.float32
 BF16 = jnp.bfloat16
-CHUNKS = 2
+CHUNKS = 1
 TABLE = 6
 ROWS = (0, 2, 1, 3)
 LIMIT = 40 * 2**20
@@ -717,7 +717,8 @@
         chunks.append([keep, [swap(send.astype(BF16), "rep", 1)], [], [], []])
     levels = rep_count.bit_length() - 1
     last = 2 * levels + CHUNKS - 2
-    first_swap = [swap(total_a, "rep", rep_count // 2)]
+    eager = rep_count == 4
+    first_swap = [swap(total_a, "rep", bit) for bit in ([2, 1] if eager else [rep_count // 2])]
     chunks.append([None, first_swap, [total_a], [swap(total_a, "sec", 1)], []])
     starts = list(range(CHUNKS)) + [-levels]
     for tick in range(last + 1):
@@ -731,7 +732,7 @@
         if tick == 2 * levels - 1:
             _, _, mine, crossing, theirs = chunks[CHUNKS]
             spots = [(0, side, code) for side in range(2) for code in codes]
-            extra = [assemble(place, mine + theirs + crossing, spots, rep_count, 1, [])]
+            extra = extra + [assemble(place, mine + theirs + crossing, spots, rep_count, 1, [])]
         if tick == last:
             done = [
                 (item, (c, side, code))
@@ -739,7 +740,7 @@
                 for side in range(2)
                 for item, code in zip(chunks[c][2 + 2 * side], codes)
             ]
-            extra = [assemble(place, *zip(*done), rep_count, CHUNKS, [])]
+            extra = extra + [assemble(place, *zip(*done), rep_count, CHUNKS, [])]
         outs = list(tied(*waited, *extra))
         if tick == 0:
             for c in range(1, CHUNKS):
@@ -747,7 +748,7 @@
         if tick == levels:
             chunks[CHUNKS][3] = outs[len(waited) :]
         if tick == 2 * levels - 1:
-            actor_summed = outs[-1]
+            actor_summed = outs[len(waited)]
         if tick == last:
             result = outs[-1]
         for c in turn:
@@ -766,7 +767,12 @@
                 mine = mine + fresh
                 crossing = [swap(block, "sec", 1) for block in fresh]
                 bit = rep_count >> (level - levels + 1)
-                pending = [swap(block, "rep", bit) for block in mine] if bit else []
+                if eager and level == levels:
+                    pending = [swap(mine[0], "rep", 2), swap(mine[0], "rep", 1)]
+                elif eager and bit:
+                    pending = [swap(mine[1], "rep", bit)]
+                else:
+                    pending = [swap(block, "rep", bit) for block in mine] if bit else []
             chunks[c] = [keep, pending, mine, crossing, theirs]
     rest = [
         (item, (c, side, code))

time: 214 us -> 218 us (1.019)
  waiting for transfers between devices: 96.2 us -> 109 us
  starting transfers between devices: 45.3 us -> 38.7 us
  Pallas kernels: 45.6 us -> 43.1 us
    ppermute x53 -> x44, waiting for transfers between devices: 96.2 us -> 109 us  [swap(): return lax.ppermute(block, axis, [(i, i ^ bit) for i in range(size)])]
    ppermute x53 -> x44, starting transfers between devices: 45.3 us -> 38.7 us  [swap(): return lax.ppermute(block, axis, [(i, i ^ bit) for i in range(size)])]
    pallas_call x3, Pallas kernels: 10.3 us -> 7.68 us  [assemble(): pl.pallas_call(functools.partial(assemble_kernel, spots, chunks), in_spec...]
    unnamed x49 -> x46, local copies, waits for them, and re-layouts: 6.17 us -> 6.1 us
  transfers between devices with their start and end apart: 53 -> 44, of which waited for: 30 -> 30; matrix products, arithmetic and copies ran while one was open for 7% -> 6% of each run, Pallas kernels for 12% -> 12%
where the time goes in v11:
time: 218 us; the launch traced here: 217 us
  waiting for transfers between devices  109 us (50%)
  Pallas kernels  43.1 us (20%)
  starting transfers between devices  38.7 us (18%)
  local copies, waits for them, and re-layouts  11.5 us (5%)
  matrix products  6.19 us (3%)
  other arithmetic  4.25 us (2%)
  between operations  4.2 us (2%)
    ppermute x44, waiting for transfers between devices, swap(): return lax.ppermute(block, axis, [(i, i ^ bit) for i in range(size)])  109 us
    ppermute x44, starting transfers between devices, swap(): return lax.ppermute(block, axis, [(i, i ^ bit) for i in range(size)])  38.7 us
    pallas_call x4, Pallas kernels, attend_call(): pl.pallas_call(functools.partial(body, groups, units, TABLE + first), in_...  15 us
    pallas_call x3, Pallas kernels, assemble(): pl.pallas_call(functools.partial(assemble_kernel, spots, chunks), in_spec...  7.68 us
    unnamed x46, local copies, waits for them, and re-layouts  6.1 us
    pallas_call x1, Pallas kernels, hidden_rows(): pl.pallas_call(hidden_kernel, in_specs=[VMEM] * 3 + [ANY] * 2 + [HBM], ou...  4.49 us
  transfers between devices with their start and end apart: 44, of which 30 were waited for; matrix products, arithmetic and copies ran while one was open for 6% of the time, Pallas kernels for 12%

profile of v11, /device:TPU:0, one launch (start us, length us, event | category | flops | bytes accessed | tf_op | source)
XLA Modules:
  0.0 217.1 jit_solution(12548137043408886461)
XLA Ops:
  0.7 3.0 %collective-permute-start.3 = (bf16[384,1536]{1,0:T(8,128)(2,1)}, bf16[384,1536]{1,0:T(8,128)(2,1)}, u32[]{:S(2)}, u32[]{:S(2)}) collective-permute-start(bf16[384,1536]{1,0:T(8,128)(2,1)} %w0.1), channel_id=1, source_target_pairs={{0,2},{1,3},{2,0},{3,1},{4,6},{5,7},{6,4},{7,5},{8,10},{9,11},{10,... | collective-permute-start | bytes 3538952 | tf_op jit(solution)/shard_map/ppermute | solution.py:534
  3.7 3.5 %first_projection.1 = (bf16[2,512,128]{2,1,0:T(8,128)(2,1)}, f32[512,128]{1,0:T(8,128)}) custom-call(bf16[512,1536]{1,0:T(8,128)(2,1)} %bitcast.30, bf16[2,1536,128]{2,1,0:T(8,128)(2,1)} %w_hbm.2), custom_call_target="tpu_custom_call" | custom-call | flops 402653184 | bytes 1572864 | tf_op jit(solution)/shard_map/first_projection/pallas_call | solution.py:77
  22.6 4.1 %collective-permute-done.1.refs_2_ = bf16[2,512,128]{2,1,0:T(8,128)(2,1)S(1)} collective-permute-done((bf16[2,512,128]{2,1,0:T(8,128)(2,1)S(1)}, bf16[2,512,128]{2,1,0:T(8,128)(2,1)S(1)}, u32[]{:S(2)}, u32[]{:S(2)}) %collective-permute-start.1) | collective-permute-done | bytes 262176 | tf_op jit(solution)/shard_map/ppermute | solution.py:534
  26.7 3.8 %attend_open.2 = (f32[512,768]{1,0:T(8,128)S(1)}, f32[512,384]{1,0:T(8,128)S(1)}) custom-call(s32[10]{0:T(128)S(1)} %stack.39.left_ref.place_ref, bf16[512,384]{1,0:T(8,128)(2,1)S(1)} %query_projection.1.q_ref, bf16[2,512,128]{2,1,0:T(8,128)(2,1)S(1)} %copy-done.14, bf16[2,512,128]{2,1,0:T(8,128)(2,1)S(1)} %collective-permute-done.refs_1_, ...), custom_call_target="tpu_custom_call" | custom-call | flops 7247757312 | bytes 786432 | tf_op jit(solution)/shard_map/attend_open/pallas_call | solution.py:219
  36.8 3.2 %near_rows.1.sum_ref = f32[512,1536]{1,0:T(8,128)S(1)} custom-call(bf16[512,1536]{1,0:T(8,128)(2,1)S(1)} %bitcast.32, bf16[512,384]{1,0:T(8,128)(2,1)S(1)} %attend_close.2.t0, bf16[512,384]{1,0:T(8,128)(2,1)S(1)} %collective-permute-done.5.t1, bf16[384,1536]{1,0:T(8,128)(2,1)} %w0.1, bf16[384,1536]{1,0:T(8,128)(2,1)} %collective-permute-done.6.w1), custom_call_target="tpu_custom_call" | custom-call | flops 1207959552 | bytes 2359296 | tf_op jit(solution)/shard_map/near_rows/pallas_call | solution.py:249
  40.0 5.3 %collective-permute-done.4.t2 = bf16[512,384]{1,0:T(8,128)(2,1)S(1)} collective-permute-done((bf16[512,384]{1,0:T(8,128)(2,1)S(1)}, bf16[512,384]{1,0:T(8,128)(2,1)S(1)}, u32[]{:S(2)}, u32[]{:S(2)}) %collective-permute-start.4) | collective-permute-done | bytes 393248 | tf_op jit(solution)/shard_map/ppermute | solution.py:534
  47.1 4.5 %hidden_rows.1 = (bf16[512,1536]{1,0:T(8,128)(2,1)S(1)}, bf16[512,512]{1,0:T(8,128)(2,1)}) custom-call(f32[512,1536]{1,0:T(8,128)S(1)} %near_rows.1.sum_ref, bf16[512,384]{1,0:T(8,128)(2,1)S(1)} %collective-permute-done.4.t2, bf16[512,384]{1,0:T(8,128)(2,1)S(1)} %collective-permute-done.7.t3, bf16[384,1536]{1,0:T(8,128)(2,1)} %collective-permute-done.3.w2, ...), custom_call_target="tpu_custom_call" | custom-call | flops 2415919104 | bytes 4718592 | tf_op jit(solution)/shard_map/hidden_rows/pallas_call | solution.py:287
  53.5 13.5 %collective-permute-done.10.e2 = bf16[512,512]{1,0:T(8,128)(2,1)} collective-permute-done((bf16[512,512]{1,0:T(8,128)(2,1)}, bf16[512,512]{1,0:T(8,128)(2,1)}, u32[]{:S(2)}, u32[]{:S(2)}) %collective-permute-start.10) | collective-permute-done | bytes 524320 | tf_op jit(solution)/shard_map/ppermute | solution.py:534
  69.3 2.7 %join_rows.1 = (bf16[2,512,128]{2,1,0:T(8,128)(2,1)S(1)}, f32[512,128]{1,0:T(8,128)S(1)}, bf16[512,2048]{1,0:T(8,128)(2,1)S(1)}) custom-call(s32[10]{0:T(128)S(1)} %stack.39.left_ref.place_ref, bf16[512,512]{1,0:T(8,128)(2,1)} %get-tuple-element.79.e0, bf16[512,512]{1,0:T(8,128)(2,1)} %collective-permute-done.9.e1, ...), custom_call_target="tpu_custom_call" | custom-call | flops 536870912 | bytes 4194304 | tf_op jit(solution)/shard_map/join_rows/pallas_call | solution.py:340
  82.8 4.6 %collective-permute-done.12.refs_1_ = bf16[2,512,128]{2,1,0:T(8,128)(2,1)S(1)} collective-permute-done((bf16[2,512,128]{2,1,0:T(8,128)(2,1)S(1)}, bf16[2,512,128]{2,1,0:T(8,128)(2,1)S(1)}, u32[]{:S(2)}, u32[]{:S(2)}) %collective-permute-start.12) | collective-permute-done | bytes 262176 | tf_op jit(solution)/shard_map/ppermute | solution.py:534
  89.9 4.7 %attend_open.3 = (f32[512,1024]{1,0:T(8,128)S(1)}, f32[512,512]{1,0:T(8,128)S(1)}) custom-call(s32[10]{0:T(128)S(1)} %stack.39.left_ref.place_ref, bf16[512,512]{1,0:T(8,128)(2,1)S(1)} %fusion.3.q_ref, bf16[2,512,128]{2,1,0:T(8,128)(2,1)S(1)} %get-tuple-element.89.refs_0_, bf16[2,512,128]{2,1,0:T(8,128)(2,1)S(1)} %collective-permute-done.12.refs_1_, ...), custom_call_target="tpu_custom_call" | custom-call | flops 9663676416 | bytes 1048576 | tf_op jit(solution)/shard_map/attend_open/pallas_call | solution.py:219
  97.0 4.0 %attend_close.3.att_ref = bf16[512,512]{1,0:T(8,128)(2,1)} custom-call(s32[10]{0:T(128)S(1)} %stack.39.left_ref.place_ref, bf16[512,512]{1,0:T(8,128)(2,1)S(1)} %fusion.3.q_ref, f32[512,1024]{1,0:T(8,128)S(1)} %get-tuple-element.97.wide_ref, f32[512,512]{1,0:T(8,128)S(1)} %get-tuple-element.98.top_ref, bf16[2,512,128]{2,1,0:T(8,128)(2,1)S(1)} %collective-permute-done.15.refs_0_), custom_call_target="tpu_custom_call" | custom-call | flops 134217728 | bytes 1048576 | tf_op jit(solution)/shard_map/attend_close/pallas_call | solution.py:219
  104.4 2.7 %collective-permute-done.16.near_ref = bf16[256,2048]{1,0:T(8,128)(2,1)S(1)} collective-permute-done((bf16[256,2048]{1,0:T(8,128)(2,1)S(1)}, bf16[256,2048]{1,0:T(8,128)(2,1)S(1)}, u32[]{:S(2)}, u32[]{:S(2)}) %collective-permute-start.16) | collective-permute-done | bytes 1048608 | tf_op jit(solution)/shard_map/ppermute | solution.py:534
  110.7 7.0 %collective-permute-done.18 = bf16[192,768]{1,0:T(8,128)(2,1)} collective-permute-done((bf16[192,768]{1,0:T(8,128)(2,1)S(1)}, bf16[192,768]{1,0:T(8,128)(2,1)}, u32[]{:S(2)}, u32[]{:S(2)}) %collective-permute-start.18) | collective-permute-done | bytes 294944 | tf_op jit(solution)/shard_map/ppermute | solution.py:534
  117.6 4.6 %collective-permute-done.17.got_ref = bf16[128,2048]{1,0:T(8,128)(2,1)} collective-permute-done((bf16[128,2048]{1,0:T(8,128)(2,1)}, bf16[128,2048]{1,0:T(8,128)(2,1)}, u32[]{:S(2)}, u32[]{:S(2)}) %collective-permute-start.17) | collective-permute-done | bytes 524320 | tf_op jit(solution)/shard_map/ppermute | solution.py:534
  131.0 6.4 %collective-permute-done.20 = bf16[96,768]{1,0:T(8,128)(2,1)S(1)} collective-permute-done((bf16[96,768]{1,0:T(8,128)(2,1)S(1)}, bf16[96,768]{1,0:T(8,128)(2,1)S(1)}, u32[]{:S(2)}, u32[]{:S(2)}) %collective-permute-start.20) | collective-permute-done | bytes 147488 | tf_op jit(solution)/shard_map/ppermute | solution.py:534
  151.5 14.3 %collective-permute-done.30.refs_2_ = bf16[96,768]{1,0:T(8,128)(2,1)S(1)} collective-permute-done((bf16[96,768]{1,0:T(8,128)(2,1)S(1)}, bf16[96,768]{1,0:T(8,128)(2,1)S(1)}, u32[]{:S(2)}, u32[]{:S(2)}) %collective-permute-start.30) | collective-permute-done | bytes 147488 | tf_op jit(solution)/shard_map/ppermute | solution.py:534
  170.5 3.4 %collective-permute-done.35.refs_6_ = bf16[96,768]{1,0:T(8,128)(2,1)S(1)} collective-permute-done((bf16[96,768]{1,0:T(8,128)(2,1)S(1)}, bf16[96,768]{1,0:T(8,128)(2,1)S(1)}, u32[]{:S(2)}, u32[]{:S(2)}) %collective-permute-start.35) | collective-permute-done | bytes 147488 | tf_op jit(solution)/shard_map/ppermute | solution.py:534
  175.8 4.6 %collective-permute-done.32 = bf16[128,1024]{1,0:T(8,128)(2,1)S(1)} collective-permute-done((bf16[128,1024]{1,0:T(8,128)(2,1)S(1)}, bf16[128,1024]{1,0:T(8,128)(2,1)S(1)}, u32[]{:S(2)}, u32[]{:S(2)}) %collective-permute-start.32) | collective-permute-done | bytes 262176 | tf_op jit(solution)/shard_map/ppermute | solution.py:534
  184.9 6.8 %collective-permute-done.39.refs_7_ = bf16[96,768]{1,0:T(8,128)(2,1)S(1)} collective-permute-done((bf16[96,768]{1,0:T(8,128)(2,1)S(1)}, bf16[96,768]{1,0:T(8,128)(2,1)S(1)}, u32[]{:S(2)}, u32[]{:S(2)}) %collective-permute-start.39) | collective-permute-done | bytes 147488 | tf_op jit(solution)/shard_map/ppermute | solution.py:534
  191.7 2.8 %collective-permute-done.37.refs_2_ = bf16[128,1024]{1,0:T(8,128)(2,1)S(1)} collective-permute-done((bf16[128,1024]{1,0:T(8,128)(2,1)S(1)}, bf16[128,1024]{1,0:T(8,128)(2,1)S(1)}, u32[]{:S(2)}, u32[]{:S(2)}) %collective-permute-start.37) | collective-permute-done | bytes 262176 | tf_op jit(solution)/shard_map/ppermute | solution.py:534
  198.4 3.6 %assemble.3 = f32[384,1536]{1,0:T(8,128)} custom-call(s32[10]{0:T(128)S(1)} %stack.39.left_ref.place_ref, bf16[96,768]{1,0:T(8,128)(2,1)S(1)} %fusion.24.refs_0_, bf16[96,768]{1,0:T(8,128)(2,1)S(1)} %collective-permute-done.29.refs_1_, bf16[96,768]{1,0:T(8,128)(2,1)S(1)} %collective-permute-done.30.refs_2_, ...), custom_call_target="tpu_custom_call" | custom-call | flops 589824 | bytes 3538944 | tf_op jit(solution)/shard_map/assemble/pallas_call | solution.py:512
  204.7 3.8 %collective-permute-done.41.refs_1_ = bf16[128,1024]{1,0:T(8,128)(2,1)S(1)} collective-permute-done((bf16[128,1024]{1,0:T(8,128)(2,1)S(1)}, bf16[128,1024]{1,0:T(8,128)(2,1)S(1)}, u32[]{:S(2)}, u32[]{:S(2)}) %collective-permute-start.41) | collective-permute-done | bytes 262176 | tf_op jit(solution)/shard_map/ppermute | solution.py:534
  209.0 5.8 %collective-permute-done.43.refs_3_ = bf16[128,1024]{1,0:T(8,128)(2,1)S(1)} collective-permute-done((bf16[128,1024]{1,0:T(8,128)(2,1)S(1)}, bf16[128,1024]{1,0:T(8,128)(2,1)S(1)}, u32[]{:S(2)}, u32[]{:S(2)}) %collective-permute-start.43) | collective-permute-done | bytes 262176 | tf_op jit(solution)/shard_map/ppermute | solution.py:534
  (160 shorter events, 90.2 us)
Async XLA Ops:
  0.7 33.0 %collective-permute-start.3 = (bf16[384,1536]{1,0:T(8,128)(2,1)}, bf16[384,1536]{1,0:T(8,128)(2,1)}, u32[]{:S(2)}, u32[]{:S(2)}) collective-permute-start(bf16[384,1536]{1,0:T(8,128)(2,1)} %w0.1), channel_id=1, source_target_pairs={{0,2},{1,3},{2,0},{3,1},{4,6},{5,7},{6,4},{7,5},{8,10},{9,11},{10,... | collective-permute-start | bytes 3538952 | tf_op jit(solution)/shard_map/ppermute | solution.py:534
  7.2 14.7 %collective-permute-start = (bf16[2,512,128]{2,1,0:T(8,128)(2,1)}, bf16[2,512,128]{2,1,0:T(8,128)(2,1)S(1)}, u32[]{:S(2)}, u32[]{:S(2)}) collective-permute-start(bf16[2,512,128]{2,1,0:T(8,128)(2,1)} %get-tuple-element.72.refs_0_), channel_id=1, source_target_pairs={{0,16},{8,24},{16,0},{24,8},{1,17},{9,25},{17,1},{25,9},{2,18},{10... | collective-permute-start | bytes 786440 | tf_op jit(solution)/shard_map/ppermute | solution.py:534
  13.4 13.2 %collective-permute-start.1 = (bf16[2,512,128]{2,1,0:T(8,128)(2,1)S(1)}, bf16[2,512,128]{2,1,0:T(8,128)(2,1)S(1)}, u32[]{:S(2)}, u32[]{:S(2)}) collective-permute-start(bf16[2,512,128]{2,1,0:T(8,128)(2,1)S(1)} %copy-done.14), channel_id=1, source_target_pairs={{0,8},{8,0},{16,24},{24,16},{1,9},{9,1},{17,25},{25,17},{2,10},{10... | collective-permute-start | bytes 786440 | tf_op jit(solution)/shard_map/ppermute | solution.py:534
  15.1 19.9 %collective-permute-start.6 = (bf16[384,1536]{1,0:T(8,128)(2,1)}, bf16[384,1536]{1,0:T(8,128)(2,1)}, u32[]{:S(2)}, u32[]{:S(2)}) collective-permute-start(bf16[384,1536]{1,0:T(8,128)(2,1)} %w0.1), channel_id=1, source_target_pairs={{0,1},{1,0},{2,3},{3,2},{4,5},{5,4},{6,7},{7,6},{8,9},{9,8},{10,11... | collective-permute-start | bytes 3538952 | tf_op jit(solution)/shard_map/ppermute | solution.py:534
  33.7 13.4 %collective-permute-start.8 = (bf16[384,1536]{1,0:T(8,128)(2,1)}, bf16[384,1536]{1,0:T(8,128)(2,1)S(1)}, u32[]{:S(2)}, u32[]{:S(2)}) collective-permute-start(bf16[384,1536]{1,0:T(8,128)(2,1)} %collective-permute-done.3.w2), channel_id=1, source_target_pairs={{0,1},{1,0},{2,3},{3,2},{4,5},{5,4},{6,7},{7,6},{8,9},{9,8},{10,11... | collective-permute-start | bytes 3538952 | tf_op jit(solution)/shard_map/ppermute | solution.py:534
  34.3 11.1 %collective-permute-start.4 = (bf16[512,384]{1,0:T(8,128)(2,1)S(1)}, bf16[512,384]{1,0:T(8,128)(2,1)S(1)}, u32[]{:S(2)}, u32[]{:S(2)}) collective-permute-start(bf16[512,384]{1,0:T(8,128)(2,1)S(1)} %attend_close.2.t0), channel_id=1, source_target_pairs={{0,2},{1,3},{2,0},{3,1},{4,6},{5,7},{6,4},{7,5},{8,10},{9,11},{10,... | collective-permute-start | bytes 1179656 | tf_op jit(solution)/shard_map/ppermute | solution.py:534
  52.7 14.3 %collective-permute-start.10 = (bf16[512,512]{1,0:T(8,128)(2,1)}, bf16[512,512]{1,0:T(8,128)(2,1)}, u32[]{:S(2)}, u32[]{:S(2)}) collective-permute-start(bf16[512,512]{1,0:T(8,128)(2,1)} %get-tuple-element.79.e0), channel_id=1, source_target_pairs={{0,2},{1,3},{2,0},{3,1},{4,6},{5,7},{6,4},{7,5},{8,10},{9,11},{10,... | collective-permute-start | bytes 1572872 | tf_op jit(solution)/shard_map/ppermute | solution.py:534
  53.5 15.0 %collective-permute-start.9 = (bf16[512,512]{1,0:T(8,128)(2,1)}, bf16[512,512]{1,0:T(8,128)(2,1)}, u32[]{:S(2)}, u32[]{:S(2)}) collective-permute-start(bf16[512,512]{1,0:T(8,128)(2,1)} %get-tuple-element.79.e0), channel_id=1, source_target_pairs={{0,1},{1,0},{2,3},{3,2},{4,5},{5,4},{6,7},{7,6},{8,9},{9,8},{10,11... | collective-permute-start | bytes 1572872 | tf_op jit(solution)/shard_map/ppermute | solution.py:534
  72.6 14.8 %collective-permute-start.12 = (bf16[2,512,128]{2,1,0:T(8,128)(2,1)S(1)}, bf16[2,512,128]{2,1,0:T(8,128)(2,1)S(1)}, u32[]{:S(2)}, u32[]{:S(2)}) collective-permute-start(bf16[2,512,128]{2,1,0:T(8,128)(2,1)S(1)} %get-tuple-element.89.refs_0_), channel_id=1, source_target_pairs={{0,16},{8,24},{16,0},{24,8},{1,17},{9,25},{17,1},{25,9},{2,18},{10... | collective-permute-start | bytes 786440 | tf_op jit(solution)/shard_map/ppermute | solution.py:534
  76.3 13.6 %collective-permute-start.13 = (bf16[2,512,128]{2,1,0:T(8,128)(2,1)S(1)}, bf16[2,512,128]{2,1,0:T(8,128)(2,1)S(1)}, u32[]{:S(2)}, u32[]{:S(2)}) collective-permute-start(bf16[2,512,128]{2,1,0:T(8,128)(2,1)S(1)} %get-tuple-element.89.refs_0_), channel_id=1, source_target_pairs={{0,8},{8,0},{16,24},{24,16},{1,9},{9,1},{17,25},{25,17},{2,10},{10... | collective-permute-start | bytes 786440 | tf_op jit(solution)/shard_map/ppermute | solution.py:534
  81.2 14.9 %collective-permute-start.14 = (bf16[384,768]{1,0:T(8,128)(2,1)S(1)}, bf16[384,768]{1,0:T(8,128)(2,1)S(1)}, u32[]{:S(2)}, u32[]{:S(2)}) collective-permute-start(bf16[384,768]{1,0:T(8,128)(2,1)S(1)} %convolution_convert_fusion), channel_id=1, source_target_pairs={{0,4},{4,0},{1,5},{5,1},{2,6},{6,2},{3,7},{7,3},{8,12},{12,8},{9,1... | collective-permute-start | bytes 1769480 | tf_op jit(solution)/shard_map/ppermute | solution.py:534
  108.0 14.3 %collective-permute-start.17 = (bf16[128,2048]{1,0:T(8,128)(2,1)}, bf16[128,2048]{1,0:T(8,128)(2,1)}, u32[]{:S(2)}, u32[]{:S(2)}) collective-permute-start(bf16[128,2048]{1,0:T(8,128)(2,1)} %add_convert_fusion), channel_id=1, source_target_pairs={{0,2},{1,3},{2,0},{3,1},{4,6},{5,7},{6,4},{7,5},{8,10},{9,11},{10,... | collective-permute-start | bytes 1572872 | tf_op jit(solution)/shard_map/ppermute | solution.py:534
  109.1 30.5 %collective-permute-start.27 = (bf16[512,512]{1,0:T(8,128)(2,1)}, bf16[512,512]{1,0:T(8,128)(2,1)}, u32[]{:S(2)}, u32[]{:S(2)}) collective-permute-start(bf16[512,512]{1,0:T(8,128)(2,1)} %attend_close.3.att_ref), channel_id=1, source_target_pairs={{0,4},{4,0},{1,5},{5,1},{2,6},{6,2},{3,7},{7,3},{8,12},{12,8},{9,1... | collective-permute-start | bytes 1572872 | tf_op jit(solution)/shard_map/ppermute | solution.py:534
  125.6 13.4 %collective-permute-start.21 = (bf16[128,1024]{1,0:T(8,128)(2,1)S(1)}, bf16[128,1024]{1,0:T(8,128)(2,1)S(1)}, u32[]{:S(2)}, u32[]{:S(2)}) collective-permute-start(bf16[128,1024]{1,0:T(8,128)(2,1)S(1)} %get-tuple-element.107), channel_id=1, source_target_pairs={{0,6},{1,7},{2,4},{3,5},{4,2},{5,3},{6,0},{7,1},{8,14},{9,15},{10,... | collective-permute-start | bytes 786440 | tf_op jit(solution)/shard_map/ppermute | solution.py:534
  127.4 11.6 %collective-permute-start.19 = (bf16[128,1024]{1,0:T(8,128)(2,1)S(1)}, bf16[128,1024]{1,0:T(8,128)(2,1)S(1)}, u32[]{:S(2)}, u32[]{:S(2)}) collective-permute-start(bf16[128,1024]{1,0:T(8,128)(2,1)S(1)} %get-tuple-element.107), channel_id=1, source_target_pairs={{0,4},{4,0},{1,5},{5,1},{2,6},{6,2},{3,7},{7,3},{8,12},{12,8},{9,1... | collective-permute-start | bytes 786440 | tf_op jit(solution)/shard_map/ppermute | solution.py:534
  129.8 11.7 %collective-permute-start.24 = (bf16[128,1024]{1,0:T(8,128)(2,1)S(1)}, bf16[128,1024]{1,0:T(8,128)(2,1)}, u32[]{:S(2)}, u32[]{:S(2)}) collective-permute-start(bf16[128,1024]{1,0:T(8,128)(2,1)S(1)} %get-tuple-element.113), channel_id=1, source_target_pairs={{0,2},{1,3},{2,0},{3,1},{4,6},{5,7},{6,4},{7,5},{8,10},{9,11},{10,... | collective-permute-start | bytes 786440 | tf_op jit(solution)/shard_map/ppermute | solution.py:534
  145.2 20.6 %collective-permute-start.28 = (bf16[256,1024]{1,0:T(8,128)(2,1)S(1)}, bf16[256,1024]{1,0:T(8,128)(2,1)S(1)}, u32[]{:S(2)}, u32[]{:S(2)}) collective-permute-start(bf16[256,1024]{1,0:T(8,128)(2,1)S(1)} %get-tuple-element.116), channel_id=1, source_target_pairs={{0,8},{8,0},{16,24},{24,16},{1,9},{9,1},{17,25},{25,17},{2,10},{10... | collective-permute-start | bytes 1572872 | tf_op jit(solution)/shard_map/ppermute | solution.py:534
  147.2 18.6 %collective-permute-start.30 = (bf16[96,768]{1,0:T(8,128)(2,1)S(1)}, bf16[96,768]{1,0:T(8,128)(2,1)S(1)}, u32[]{:S(2)}, u32[]{:S(2)}) collective-permute-start(bf16[96,768]{1,0:T(8,128)(2,1)S(1)} %fusion.24.refs_0_), channel_id=1, source_target_pairs={{0,8},{8,0},{16,24},{24,16},{1,9},{9,1},{17,25},{25,17},{2,10},{10... | collective-permute-start | bytes 442376 | tf_op jit(solution)/shard_map/ppermute | solution.py:534
  148.9 16.9 %collective-permute-start.29 = (bf16[96,768]{1,0:T(8,128)(2,1)S(1)}, bf16[96,768]{1,0:T(8,128)(2,1)S(1)}, u32[]{:S(2)}, u32[]{:S(2)}) collective-permute-start(bf16[96,768]{1,0:T(8,128)(2,1)S(1)} %fusion.24.refs_0_), channel_id=1, source_target_pairs={{0,16},{8,24},{16,0},{24,8},{1,17},{9,25},{17,1},{25,9},{2,18},{10... | collective-permute-start | bytes 442376 | tf_op jit(solution)/shard_map/ppermute | solution.py:534
  166.0 14.3 %collective-permute-start.32 = (bf16[128,1024]{1,0:T(8,128)(2,1)S(1)}, bf16[128,1024]{1,0:T(8,128)(2,1)S(1)}, u32[]{:S(2)}, u32[]{:S(2)}) collective-permute-start(bf16[128,1024]{1,0:T(8,128)(2,1)S(1)} %slice.51), channel_id=1, source_target_pairs={{0,16},{8,24},{16,0},{24,8},{1,17},{9,25},{17,1},{25,9},{2,18},{10... | collective-permute-start | bytes 786440 | tf_op jit(solution)/shard_map/ppermute | solution.py:534
  180.4 11.3 %collective-permute-start.38 = (bf16[128,1024]{1,0:T(8,128)(2,1)S(1)}, bf16[128,1024]{1,0:T(8,128)(2,1)S(1)}, u32[]{:S(2)}, u32[]{:S(2)}) collective-permute-start(bf16[128,1024]{1,0:T(8,128)(2,1)S(1)} %fusion.15.refs_0_), channel_id=1, source_target_pairs={{0,4},{4,0},{1,5},{5,1},{2,6},{6,2},{3,7},{7,3},{8,12},{12,8},{9,1... | collective-permute-start | bytes 786440 | tf_op jit(solution)/shard_map/ppermute | solution.py:534
  182.0 12.6 %collective-permute-start.37 = (bf16[128,1024]{1,0:T(8,128)(2,1)S(1)}, bf16[128,1024]{1,0:T(8,128)(2,1)S(1)}, u32[]{:S(2)}, u32[]{:S(2)}) collective-permute-start(bf16[128,1024]{1,0:T(8,128)(2,1)S(1)} %fusion.15.refs_0_), channel_id=1, source_target_pairs={{0,8},{8,0},{16,24},{24,16},{1,9},{9,1},{17,25},{25,17},{2,10},{10... | collective-permute-start | bytes 786440 | tf_op jit(solution)/shard_map/ppermute | solution.py:534
  182.0 14.4 %collective-permute-start.36 = (bf16[128,1024]{1,0:T(8,128)(2,1)S(1)}, bf16[128,1024]{1,0:T(8,128)(2,1)S(1)}, u32[]{:S(2)}, u32[]{:S(2)}) collective-permute-start(bf16[128,1024]{1,0:T(8,128)(2,1)S(1)} %fusion.15.refs_0_), channel_id=1, source_target_pairs={{0,16},{8,24},{16,0},{24,8},{1,17},{9,25},{17,1},{25,9},{2,18},{10... | collective-permute-start | bytes 786440 | tf_op jit(solution)/shard_map/ppermute | solution.py:534
  196.9 11.6 %collective-permute-start.41 = (bf16[128,1024]{1,0:T(8,128)(2,1)S(1)}, bf16[128,1024]{1,0:T(8,128)(2,1)S(1)}, u32[]{:S(2)}, u32[]{:S(2)}) collective-permute-start(bf16[128,1024]{1,0:T(8,128)(2,1)S(1)} %collective-permute-done.36.refs_1_), channel_id=1, source_target_pairs={{0,4},{4,0},{1,5},{5,1},{2,6},{6,2},{3,7},{7,3},{8,12},{12,8},{9,1... | collective-permute-start | bytes 786440 | tf_op jit(solution)/shard_map/ppermute | solution.py:534
  (43 other events, 320.4 us)

commit v12 on v11

--- a/solution.py
+++ b/solution.py
@@ -15,7 +15,7 @@
 LOG2E = 1.4426950408889634
 F32 = jnp.float32
 BF16 = jnp.bfloat16
-CHUNKS = 1
+CHUNKS = 2
 TABLE = 6
 ROWS = (0, 2, 1, 3)
 LIMIT = 40 * 2**20
@@ -729,7 +729,7 @@
             extra = [chunks[c][0] for c in range(1, CHUNKS)]
         if tick == levels:
             extra = chunks[CHUNKS][3]
-        if tick == 2 * levels - 1:
+        if tick == last:
             _, _, mine, crossing, theirs = chunks[CHUNKS]
             spots = [(0, side, code) for side in range(2) for code in codes]
             extra = extra + [assemble(place, mine + theirs + crossing, spots, rep_count, 1, [])]
@@ -747,7 +747,7 @@
                 chunks[c][0] = outs[len(waited) + c - 1]
         if tick == levels:
             chunks[CHUNKS][3] = outs[len(waited) :]
-        if tick == 2 * levels - 1:
+        if tick == last:
             actor_summed = outs[len(waited)]
         if tick == last:
             result = outs[-1]

time: 218 us -> 215 us (0.986)
  waiting for transfers between devices: 109 us -> 93.4 us
  starting transfers between devices: 38.7 us -> 48.6 us
  Pallas kernels: 43.1 us -> 45.6 us
    ppermute x44 -> x53, waiting for transfers between devices: 109 us -> 93.4 us  [swap(): return lax.ppermute(block, axis, [(i, i ^ bit) for i in range(size)])]
    ppermute x44 -> x53, starting transfers between devices: 38.7 us -> 48.6 us  [swap(): return lax.ppermute(block, axis, [(i, i ^ bit) for i in range(size)])]
    pallas_call x3, Pallas kernels: 7.68 us -> 10.3 us  [assemble(): pl.pallas_call(functools.partial(assemble_kernel, spots, chunks), in_spec...]
    unnamed x46 -> x49, local copies, waits for them, and re-layouts: 6.1 us -> 6.17 us
  transfers between devices with their start and end apart: 44 -> 53, of which waited for: 30 -> 28; matrix products, arithmetic and copies ran while one was open for 6% -> 7% of each run, Pallas kernels for 12% -> 13%
where the time goes in v12:
time: 215 us; the launch traced here: 214 us
  waiting for transfers between devices  93.4 us (43%)
  starting transfers between devices  48.6 us (23%)
  Pallas kernels  45.6 us (21%)
  local copies, waits for them, and re-layouts  11.9 us (6%)
  matrix products  5.6 us (3%)
  between operations  4.82 us (2%)
  other arithmetic  4.41 us (2%)
    ppermute x53, waiting for transfers between devices, swap(): return lax.ppermute(block, axis, [(i, i ^ bit) for i in range(size)])  93.4 us
    ppermute x53, starting transfers between devices, swap(): return lax.ppermute(block, axis, [(i, i ^ bit) for i in range(size)])  48.6 us
    pallas_call x4, Pallas kernels, attend_call(): pl.pallas_call(functools.partial(body, groups, units, TABLE + first), in_...  15 us
    pallas_call x3, Pallas kernels, assemble(): pl.pallas_call(functools.partial(assemble_kernel, spots, chunks), in_spec...  10.3 us
    unnamed x49, local copies, waits for them, and re-layouts  6.17 us
    pallas_call x1, Pallas kernels, hidden_rows(): pl.pallas_call(hidden_kernel, in_specs=[VMEM] * 3 + [ANY] * 2 + [HBM], ou...  4.46 us
  transfers between devices with their start and end apart: 53, of which 28 were waited for; matrix products, arithmetic and copies ran while one was open for 7% of the time, Pallas kernels for 13%

profile of v12, /device:TPU:0, one launch (start us, length us, event | category | flops | bytes accessed | tf_op | source)
XLA Modules:
  0.0 214.3 jit_solution(5765331762014229611)
XLA Ops:
  0.7 3.0 %collective-permute-start.3 = (bf16[384,1536]{1,0:T(8,128)(2,1)}, bf16[384,1536]{1,0:T(8,128)(2,1)}, u32[]{:S(2)}, u32[]{:S(2)}) collective-permute-start(bf16[384,1536]{1,0:T(8,128)(2,1)} %w0.1), channel_id=1, source_target_pairs={{0,2},{1,3},{2,0},{3,1},{4,6},{5,7},{6,4},{7,5},{8,10},{9,11},{10,... | collective-permute-start | bytes 3538952 | tf_op jit(solution)/shard_map/ppermute | solution.py:534
  3.7 3.5 %first_projection.1 = (bf16[2,512,128]{2,1,0:T(8,128)(2,1)}, f32[512,128]{1,0:T(8,128)}) custom-call(bf16[512,1536]{1,0:T(8,128)(2,1)} %bitcast.30, bf16[2,1536,128]{2,1,0:T(8,128)(2,1)} %w_hbm.2), custom_call_target="tpu_custom_call" | custom-call | flops 402653184 | bytes 1572864 | tf_op jit(solution)/shard_map/first_projection/pallas_call | solution.py:77
  7.2 2.7 %collective-permute-start = (bf16[2,512,128]{2,1,0:T(8,128)(2,1)}, bf16[2,512,128]{2,1,0:T(8,128)(2,1)S(1)}, u32[]{:S(2)}, u32[]{:S(2)}) collective-permute-start(bf16[2,512,128]{2,1,0:T(8,128)(2,1)} %get-tuple-element.83.refs_0_), channel_id=1, source_target_pairs={{0,16},{8,24},{16,0},{24,8},{1,17},{9,25},{17,1},{25,9},{2,18},{10... | collective-permute-start | bytes 786440 | tf_op jit(solution)/shard_map/ppermute | solution.py:534
  22.6 4.1 %collective-permute-done.1.refs_2_ = bf16[2,512,128]{2,1,0:T(8,128)(2,1)S(1)} collective-permute-done((bf16[2,512,128]{2,1,0:T(8,128)(2,1)S(1)}, bf16[2,512,128]{2,1,0:T(8,128)(2,1)S(1)}, u32[]{:S(2)}, u32[]{:S(2)}) %collective-permute-start.1) | collective-permute-done | bytes 262176 | tf_op jit(solution)/shard_map/ppermute | solution.py:534
  26.7 3.6 %attend_open.2 = (f32[512,768]{1,0:T(8,128)S(1)}, f32[512,384]{1,0:T(8,128)S(1)}) custom-call(s32[10]{0:T(128)S(1)} %stack.39.left_ref.place_ref, bf16[512,384]{1,0:T(8,128)(2,1)S(1)} %query_projection.1.q_ref, bf16[2,512,128]{2,1,0:T(8,128)(2,1)S(1)} %copy-done.16, bf16[2,512,128]{2,1,0:T(8,128)(2,1)S(1)} %collective-permute-done.refs_1_, ...), custom_call_target="tpu_custom_call" | custom-call | flops 7247757312 | bytes 786432 | tf_op jit(solution)/shard_map/attend_open/pallas_call | solution.py:219
  36.8 3.1 %near_rows.1.sum_ref = f32[512,1536]{1,0:T(8,128)S(1)} custom-call(bf16[512,1536]{1,0:T(8,128)(2,1)S(1)} %bitcast.32, bf16[512,384]{1,0:T(8,128)(2,1)S(1)} %attend_close.2.t0, bf16[512,384]{1,0:T(8,128)(2,1)S(1)} %collective-permute-done.5.t1, bf16[384,1536]{1,0:T(8,128)(2,1)} %w0.1, bf16[384,1536]{1,0:T(8,128)(2,1)} %collective-permute-done.6.w1), custom_call_target="tpu_custom_call" | custom-call | flops 1207959552 | bytes 2359296 | tf_op jit(solution)/shard_map/near_rows/pallas_call | solution.py:249
  40.0 5.4 %collective-permute-done.4.t2 = bf16[512,384]{1,0:T(8,128)(2,1)S(1)} collective-permute-done((bf16[512,384]{1,0:T(8,128)(2,1)S(1)}, bf16[512,384]{1,0:T(8,128)(2,1)S(1)}, u32[]{:S(2)}, u32[]{:S(2)}) %collective-permute-start.4) | collective-permute-done | bytes 393248 | tf_op jit(solution)/shard_map/ppermute | solution.py:534
  47.1 4.5 %hidden_rows.1 = (bf16[512,1536]{1,0:T(8,128)(2,1)S(1)}, bf16[512,512]{1,0:T(8,128)(2,1)}) custom-call(f32[512,1536]{1,0:T(8,128)S(1)} %near_rows.1.sum_ref, bf16[512,384]{1,0:T(8,128)(2,1)S(1)} %collective-permute-done.4.t2, bf16[512,384]{1,0:T(8,128)(2,1)S(1)} %collective-permute-done.7.t3, bf16[384,1536]{1,0:T(8,128)(2,1)} %collective-permute-done.3.w2, ...), custom_call_target="tpu_custom_call" | custom-call | flops 2415919104 | bytes 4718592 | tf_op jit(solution)/shard_map/hidden_rows/pallas_call | solution.py:287
  53.5 13.5 %collective-permute-done.10.e2 = bf16[512,512]{1,0:T(8,128)(2,1)} collective-permute-done((bf16[512,512]{1,0:T(8,128)(2,1)}, bf16[512,512]{1,0:T(8,128)(2,1)}, u32[]{:S(2)}, u32[]{:S(2)}) %collective-permute-start.10) | collective-permute-done | bytes 524320 | tf_op jit(solution)/shard_map/ppermute | solution.py:534
  69.2 2.7 %join_rows.1 = (bf16[2,512,128]{2,1,0:T(8,128)(2,1)S(1)}, f32[512,128]{1,0:T(8,128)S(1)}, bf16[512,2048]{1,0:T(8,128)(2,1)S(1)}) custom-call(s32[10]{0:T(128)S(1)} %stack.39.left_ref.place_ref, bf16[512,512]{1,0:T(8,128)(2,1)} %get-tuple-element.90.e0, bf16[512,512]{1,0:T(8,128)(2,1)} %collective-permute-done.9.e1, ...), custom_call_target="tpu_custom_call" | custom-call | flops 536870912 | bytes 4194304 | tf_op jit(solution)/shard_map/join_rows/pallas_call | solution.py:340
  82.8 4.5 %collective-permute-done.12.refs_1_ = bf16[2,512,128]{2,1,0:T(8,128)(2,1)S(1)} collective-permute-done((bf16[2,512,128]{2,1,0:T(8,128)(2,1)S(1)}, bf16[2,512,128]{2,1,0:T(8,128)(2,1)S(1)}, u32[]{:S(2)}, u32[]{:S(2)}) %collective-permute-start.12) | collective-permute-done | bytes 262176 | tf_op jit(solution)/shard_map/ppermute | solution.py:534
  87.3 2.7 %collective-permute-done.13.refs_2_ = bf16[2,512,128]{2,1,0:T(8,128)(2,1)S(1)} collective-permute-done((bf16[2,512,128]{2,1,0:T(8,128)(2,1)S(1)}, bf16[2,512,128]{2,1,0:T(8,128)(2,1)S(1)}, u32[]{:S(2)}, u32[]{:S(2)}) %collective-permute-start.13) | collective-permute-done | bytes 262176 | tf_op jit(solution)/shard_map/ppermute | solution.py:534
  90.0 4.8 %attend_open.3 = (f32[512,1024]{1,0:T(8,128)S(1)}, f32[512,512]{1,0:T(8,128)S(1)}) custom-call(s32[10]{0:T(128)S(1)} %stack.39.left_ref.place_ref, bf16[512,512]{1,0:T(8,128)(2,1)S(1)} %fusion.3.q_ref, bf16[2,512,128]{2,1,0:T(8,128)(2,1)S(1)} %get-tuple-element.100.refs_0_, bf16[2,512,128]{2,1,0:T(8,128)(2,1)S(1)} %collective-permute-done.12.refs_1_, ...), custom_call_target="tpu_custom_call" | custom-call | flops 9663676416 | bytes 1048576 | tf_op jit(solution)/shard_map/attend_open/pallas_call | solution.py:219
  97.0 4.1 %attend_close.3.att_ref = bf16[512,512]{1,0:T(8,128)(2,1)} custom-call(s32[10]{0:T(128)S(1)} %stack.39.left_ref.place_ref, bf16[512,512]{1,0:T(8,128)(2,1)S(1)} %fusion.3.q_ref, f32[512,1024]{1,0:T(8,128)S(1)} %get-tuple-element.108.wide_ref, f32[512,512]{1,0:T(8,128)S(1)} %get-tuple-element.109.top_ref, bf16[2,512,128]{2,1,0:T(8,128)(2,1)S(1)} %collective-permute-done.15.refs_0_), custom_call_target="tpu_custom_call" | custom-call | flops 134217728 | bytes 1048576 | tf_op jit(solution)/shard_map/attend_close/pallas_call | solution.py:219
  101.1 2.6 %part_rows.1 = (bf16[256,2048]{1,0:T(8,128)(2,1)S(1)}, f32[256,2048]{1,0:T(8,128)S(1)}, bf16[512,512]{1,0:T(8,128)(2,1)S(1)}) custom-call(s32[10]{0:T(128)S(1)} %stack.39.left_ref.place_ref, bf16[512,512]{1,0:T(8,128)(2,1)} %attend_close.3.att_ref, bf16[512,2048]{1,0:T(8,128)(2,1)S(1)} %copy-done.14), custom_call_target="tpu_custom_call" | custom-call | flops 1073741824 | bytes 8388608 | tf_op jit(solution)/shard_map/part_rows/pallas_call | solution.py:380
  109.3 9.9 %collective-permute-done.27 = bf16[512,512]{1,0:T(8,128)(2,1)} collective-permute-done((bf16[512,512]{1,0:T(8,128)(2,1)}, bf16[512,512]{1,0:T(8,128)(2,1)}, u32[]{:S(2)}, u32[]{:S(2)}) %collective-permute-start.27) | collective-permute-done | bytes 524320 | tf_op jit(solution)/shard_map/ppermute | solution.py:534
  131.6 8.6 %collective-permute-done.20 = bf16[96,768]{1,0:T(8,128)(2,1)S(1)} collective-permute-done((bf16[96,768]{1,0:T(8,128)(2,1)S(1)}, bf16[96,768]{1,0:T(8,128)(2,1)S(1)}, u32[]{:S(2)}, u32[]{:S(2)}) %collective-permute-start.20) | collective-permute-done | bytes 147488 | tf_op jit(solution)/shard_map/ppermute | solution.py:534
  152.9 4.8 %collective-permute-done.28 = bf16[256,512]{1,0:T(8,128)(2,1)S(1)} collective-permute-done((bf16[256,512]{1,0:T(8,128)(2,1)S(1)}, bf16[256,512]{1,0:T(8,128)(2,1)S(1)}, u32[]{:S(2)}, u32[]{:S(2)}) %collective-permute-start.28) | collective-permute-done | bytes 262176 | tf_op jit(solution)/shard_map/ppermute | solution.py:534
  162.2 3.9 %collective-permute-done.33 = bf16[256,512]{1,0:T(8,128)(2,1)S(1)} collective-permute-done((bf16[256,512]{1,0:T(8,128)(2,1)S(1)}, bf16[256,512]{1,0:T(8,128)(2,1)S(1)}, u32[]{:S(2)}, u32[]{:S(2)}) %collective-permute-start.33) | collective-permute-done | bytes 262176 | tf_op jit(solution)/shard_map/ppermute | solution.py:534
  174.8 6.8 %collective-permute-done.40 = bf16[128,512]{1,0:T(8,128)(2,1)S(1)} collective-permute-done((bf16[128,512]{1,0:T(8,128)(2,1)S(1)}, bf16[128,512]{1,0:T(8,128)(2,1)S(1)}, u32[]{:S(2)}, u32[]{:S(2)}) %collective-permute-start.40) | collective-permute-done | bytes 131104 | tf_op jit(solution)/shard_map/ppermute | solution.py:534
  189.8 4.3 %collective-permute-done.46.refs_9_ = bf16[128,512]{1,0:T(8,128)(2,1)S(1)} collective-permute-done((bf16[128,512]{1,0:T(8,128)(2,1)S(1)}, bf16[128,512]{1,0:T(8,128)(2,1)S(1)}, u32[]{:S(2)}, u32[]{:S(2)}) %collective-permute-start.46) | collective-permute-done | bytes 131104 | tf_op jit(solution)/shard_map/ppermute | solution.py:534
  198.1 3.6 %assemble.3 = f32[384,1536]{1,0:T(8,128)} custom-call(s32[10]{0:T(128)S(1)} %stack.39.left_ref.place_ref, bf16[96,768]{1,0:T(8,128)(2,1)S(1)} %fusion.15.refs_0_, bf16[96,768]{1,0:T(8,128)(2,1)S(1)} %collective-permute-done.29.refs_1_, bf16[96,768]{1,0:T(8,128)(2,1)S(1)} %collective-permute-done.30.refs_2_, ...), custom_call_target="tpu_custom_call" | custom-call | flops 589824 | bytes 3538944 | tf_op jit(solution)/shard_map/assemble/pallas_call | solution.py:512
  202.4 4.2 %assemble.4.refs_5_ = f32[512,2048]{1,0:T(8,128)} custom-call(s32[10]{0:T(128)S(1)} %stack.39.left_ref.place_ref, bf16[128,512]{1,0:T(8,128)(2,1)S(1)} %fusion.17.refs_0_, bf16[128,512]{1,0:T(8,128)(2,1)S(1)} %collective-permute-done.37.refs_1_, bf16[128,512]{1,0:T(8,128)(2,1)S(1)} %collective-permute-done.38.refs_2_, ...), custom_call_target="tpu_custom_call" | custom-call | flops 1048576 | bytes 6291456 | tf_op jit(solution)/shard_map/assemble/pallas_call | solution.py:512
  208.1 3.5 %collective-permute-done.52.refs_4_ = bf16[128,512]{1,0:T(8,128)(2,1)S(1)} collective-permute-done((bf16[128,512]{1,0:T(8,128)(2,1)S(1)}, bf16[128,512]{1,0:T(8,128)(2,1)S(1)}, u32[]{:S(2)}, u32[]{:S(2)}) %collective-permute-start.52) | collective-permute-done | bytes 131104 | tf_op jit(solution)/shard_map/ppermute | solution.py:534
  (188 shorter events, 95.3 us)
Async XLA Ops:
  0.7 33.0 %collective-permute-start.3 = (bf16[384,1536]{1,0:T(8,128)(2,1)}, bf16[384,1536]{1,0:T(8,128)(2,1)}, u32[]{:S(2)}, u32[]{:S(2)}) collective-permute-start(bf16[384,1536]{1,0:T(8,128)(2,1)} %w0.1), channel_id=1, source_target_pairs={{0,2},{1,3},{2,0},{3,1},{4,6},{5,7},{6,4},{7,5},{8,10},{9,11},{10,... | collective-permute-start | bytes 3538952 | tf_op jit(solution)/shard_map/ppermute | solution.py:534
  7.2 14.7 %collective-permute-start = (bf16[2,512,128]{2,1,0:T(8,128)(2,1)}, bf16[2,512,128]{2,1,0:T(8,128)(2,1)S(1)}, u32[]{:S(2)}, u32[]{:S(2)}) collective-permute-start(bf16[2,512,128]{2,1,0:T(8,128)(2,1)} %get-tuple-element.83.refs_0_), channel_id=1, source_target_pairs={{0,16},{8,24},{16,0},{24,8},{1,17},{9,25},{17,1},{25,9},{2,18},{10... | collective-permute-start | bytes 786440 | tf_op jit(solution)/shard_map/ppermute | solution.py:534
  13.4 13.2 %collective-permute-start.1 = (bf16[2,512,128]{2,1,0:T(8,128)(2,1)S(1)}, bf16[2,512,128]{2,1,0:T(8,128)(2,1)S(1)}, u32[]{:S(2)}, u32[]{:S(2)}) collective-permute-start(bf16[2,512,128]{2,1,0:T(8,128)(2,1)S(1)} %copy-done.16), channel_id=1, source_target_pairs={{0,8},{8,0},{16,24},{24,16},{1,9},{9,1},{17,25},{25,17},{2,10},{10... | collective-permute-start | bytes 786440 | tf_op jit(solution)/shard_map/ppermute | solution.py:534
  15.1 19.9 %collective-permute-start.6 = (bf16[384,1536]{1,0:T(8,128)(2,1)}, bf16[384,1536]{1,0:T(8,128)(2,1)}, u32[]{:S(2)}, u32[]{:S(2)}) collective-permute-start(bf16[384,1536]{1,0:T(8,128)(2,1)} %w0.1), channel_id=1, source_target_pairs={{0,1},{1,0},{2,3},{3,2},{4,5},{5,4},{6,7},{7,6},{8,9},{9,8},{10,11... | collective-permute-start | bytes 3538952 | tf_op jit(solution)/shard_map/ppermute | solution.py:534
  33.7 13.4 %collective-permute-start.8 = (bf16[384,1536]{1,0:T(8,128)(2,1)}, bf16[384,1536]{1,0:T(8,128)(2,1)S(1)}, u32[]{:S(2)}, u32[]{:S(2)}) collective-permute-start(bf16[384,1536]{1,0:T(8,128)(2,1)} %collective-permute-done.3.w2), channel_id=1, source_target_pairs={{0,1},{1,0},{2,3},{3,2},{4,5},{5,4},{6,7},{7,6},{8,9},{9,8},{10,11... | collective-permute-start | bytes 3538952 | tf_op jit(solution)/shard_map/ppermute | solution.py:534
  34.2 11.1 %collective-permute-start.4 = (bf16[512,384]{1,0:T(8,128)(2,1)S(1)}, bf16[512,384]{1,0:T(8,128)(2,1)S(1)}, u32[]{:S(2)}, u32[]{:S(2)}) collective-permute-start(bf16[512,384]{1,0:T(8,128)(2,1)S(1)} %attend_close.2.t0), channel_id=1, source_target_pairs={{0,2},{1,3},{2,0},{3,1},{4,6},{5,7},{6,4},{7,5},{8,10},{9,11},{10,... | collective-permute-start | bytes 1179656 | tf_op jit(solution)/shard_map/ppermute | solution.py:534
  52.7 14.3 %collective-permute-start.10 = (bf16[512,512]{1,0:T(8,128)(2,1)}, bf16[512,512]{1,0:T(8,128)(2,1)}, u32[]{:S(2)}, u32[]{:S(2)}) collective-permute-start(bf16[512,512]{1,0:T(8,128)(2,1)} %get-tuple-element.90.e0), channel_id=1, source_target_pairs={{0,2},{1,3},{2,0},{3,1},{4,6},{5,7},{6,4},{7,5},{8,10},{9,11},{10,... | collective-permute-start | bytes 1572872 | tf_op jit(solution)/shard_map/ppermute | solution.py:534
  53.4 15.0 %collective-permute-start.9 = (bf16[512,512]{1,0:T(8,128)(2,1)}, bf16[512,512]{1,0:T(8,128)(2,1)}, u32[]{:S(2)}, u32[]{:S(2)}) collective-permute-start(bf16[512,512]{1,0:T(8,128)(2,1)} %get-tuple-element.90.e0), channel_id=1, source_target_pairs={{0,1},{1,0},{2,3},{3,2},{4,5},{5,4},{6,7},{7,6},{8,9},{9,8},{10,11... | collective-permute-start | bytes 1572872 | tf_op jit(solution)/shard_map/ppermute | solution.py:534
  72.5 14.8 %collective-permute-start.12 = (bf16[2,512,128]{2,1,0:T(8,128)(2,1)S(1)}, bf16[2,512,128]{2,1,0:T(8,128)(2,1)S(1)}, u32[]{:S(2)}, u32[]{:S(2)}) collective-permute-start(bf16[2,512,128]{2,1,0:T(8,128)(2,1)S(1)} %get-tuple-element.100.refs_0_), channel_id=1, source_target_pairs={{0,16},{8,24},{16,0},{24,8},{1,17},{9,25},{17,1},{25,9},{2,18},{10... | collective-permute-start | bytes 786440 | tf_op jit(solution)/shard_map/ppermute | solution.py:534
  76.3 13.7 %collective-permute-start.13 = (bf16[2,512,128]{2,1,0:T(8,128)(2,1)S(1)}, bf16[2,512,128]{2,1,0:T(8,128)(2,1)S(1)}, u32[]{:S(2)}, u32[]{:S(2)}) collective-permute-start(bf16[2,512,128]{2,1,0:T(8,128)(2,1)S(1)} %get-tuple-element.100.refs_0_), channel_id=1, source_target_pairs={{0,8},{8,0},{16,24},{24,16},{1,9},{9,1},{17,25},{25,17},{2,10},{10... | collective-permute-start | bytes 786440 | tf_op jit(solution)/shard_map/ppermute | solution.py:534
  81.2 14.9 %collective-permute-start.14 = (bf16[384,768]{1,0:T(8,128)(2,1)S(1)}, bf16[384,768]{1,0:T(8,128)(2,1)S(1)}, u32[]{:S(2)}, u32[]{:S(2)}) collective-permute-start(bf16[384,768]{1,0:T(8,128)(2,1)S(1)} %convolution_convert_fusion), channel_id=1, source_target_pairs={{0,4},{4,0},{1,5},{5,1},{2,6},{6,2},{3,7},{7,3},{8,12},{12,8},{9,1... | collective-permute-start | bytes 1769480 | tf_op jit(solution)/shard_map/ppermute | solution.py:534
  104.5 14.7 %collective-permute-start.27 = (bf16[512,512]{1,0:T(8,128)(2,1)}, bf16[512,512]{1,0:T(8,128)(2,1)}, u32[]{:S(2)}, u32[]{:S(2)}) collective-permute-start(bf16[512,512]{1,0:T(8,128)(2,1)} %attend_close.3.att_ref), channel_id=1, source_target_pairs={{0,4},{4,0},{1,5},{5,1},{2,6},{6,2},{3,7},{7,3},{8,12},{12,8},{9,1... | collective-permute-start | bytes 1572872 | tf_op jit(solution)/shard_map/ppermute | solution.py:534
  108.1 14.3 %collective-permute-start.17 = (bf16[128,2048]{1,0:T(8,128)(2,1)}, bf16[128,2048]{1,0:T(8,128)(2,1)}, u32[]{:S(2)}, u32[]{:S(2)}) collective-permute-start(bf16[128,2048]{1,0:T(8,128)(2,1)} %add_convert_fusion), channel_id=1, source_target_pairs={{0,2},{1,3},{2,0},{3,1},{4,6},{5,7},{6,4},{7,5},{8,10},{9,11},{10,... | collective-permute-start | bytes 1572872 | tf_op jit(solution)/shard_map/ppermute | solution.py:534
  108.9 11.5 %collective-permute-start.18 = (bf16[192,768]{1,0:T(8,128)(2,1)S(1)}, bf16[192,768]{1,0:T(8,128)(2,1)}, u32[]{:S(2)}, u32[]{:S(2)}) collective-permute-start(bf16[192,768]{1,0:T(8,128)(2,1)S(1)} %get-tuple-element.113), channel_id=1, source_target_pairs={{0,8},{8,0},{16,24},{24,16},{1,9},{9,1},{17,25},{25,17},{2,10},{10... | collective-permute-start | bytes 884744 | tf_op jit(solution)/shard_map/ppermute | solution.py:534
  125.7 14.5 %collective-permute-start.21 = (bf16[128,1024]{1,0:T(8,128)(2,1)S(1)}, bf16[128,1024]{1,0:T(8,128)(2,1)S(1)}, u32[]{:S(2)}, u32[]{:S(2)}) collective-permute-start(bf16[128,1024]{1,0:T(8,128)(2,1)S(1)} %get-tuple-element.118), channel_id=1, source_target_pairs={{0,6},{1,7},{2,4},{3,5},{4,2},{5,3},{6,0},{7,1},{8,14},{9,15},{10,... | collective-permute-start | bytes 786440 | tf_op jit(solution)/shard_map/ppermute | solution.py:534
  127.4 12.7 %collective-permute-start.19 = (bf16[128,1024]{1,0:T(8,128)(2,1)S(1)}, bf16[128,1024]{1,0:T(8,128)(2,1)S(1)}, u32[]{:S(2)}, u32[]{:S(2)}) collective-permute-start(bf16[128,1024]{1,0:T(8,128)(2,1)S(1)} %get-tuple-element.118), channel_id=1, source_target_pairs={{0,4},{4,0},{1,5},{5,1},{2,6},{6,2},{3,7},{7,3},{8,12},{12,8},{9,1... | collective-permute-start | bytes 786440 | tf_op jit(solution)/shard_map/ppermute | solution.py:534
  128.0 14.3 %collective-permute-start.25 = (bf16[128,1024]{1,0:T(8,128)(2,1)S(1)}, bf16[128,1024]{1,0:T(8,128)(2,1)S(1)}, u32[]{:S(2)}, u32[]{:S(2)}) collective-permute-start(bf16[128,1024]{1,0:T(8,128)(2,1)S(1)} %get-tuple-element.124), channel_id=1, source_target_pairs={{0,1},{1,0},{2,3},{3,2},{4,5},{5,4},{6,7},{7,6},{8,9},{9,8},{10,11... | collective-permute-start | bytes 786440 | tf_op jit(solution)/shard_map/ppermute | solution.py:534
  128.0 14.2 %collective-permute-start.24 = (bf16[128,1024]{1,0:T(8,128)(2,1)S(1)}, bf16[128,1024]{1,0:T(8,128)(2,1)S(1)}, u32[]{:S(2)}, u32[]{:S(2)}) collective-permute-start(bf16[128,1024]{1,0:T(8,128)(2,1)S(1)} %get-tuple-element.124), channel_id=1, source_target_pairs={{0,2},{1,3},{2,0},{3,1},{4,6},{5,7},{6,4},{7,5},{8,10},{9,11},{10,... | collective-permute-start | bytes 786440 | tf_op jit(solution)/shard_map/ppermute | solution.py:534
  146.3 11.4 %collective-permute-start.28 = (bf16[256,512]{1,0:T(8,128)(2,1)S(1)}, bf16[256,512]{1,0:T(8,128)(2,1)S(1)}, u32[]{:S(2)}, u32[]{:S(2)}) collective-permute-start(bf16[256,512]{1,0:T(8,128)(2,1)S(1)} %get-tuple-element.127), channel_id=1, source_target_pairs={{0,8},{8,0},{16,24},{24,16},{1,9},{9,1},{17,25},{25,17},{2,10},{10... | collective-permute-start | bytes 786440 | tf_op jit(solution)/shard_map/ppermute | solution.py:534
  147.0 19.2 %collective-permute-start.33 = (bf16[256,512]{1,0:T(8,128)(2,1)S(1)}, bf16[256,512]{1,0:T(8,128)(2,1)S(1)}, u32[]{:S(2)}, u32[]{:S(2)}) collective-permute-start(bf16[256,512]{1,0:T(8,128)(2,1)S(1)} %get-tuple-element.131), channel_id=1, source_target_pairs={{0,8},{8,0},{16,24},{24,16},{1,9},{9,1},{17,25},{25,17},{2,10},{10... | collective-permute-start | bytes 786440 | tf_op jit(solution)/shard_map/ppermute | solution.py:534
  158.3 10.7 %collective-permute-start.34 = (bf16[96,768]{1,0:T(8,128)(2,1)S(1)}, bf16[96,768]{1,0:T(8,128)(2,1)S(1)}, u32[]{:S(2)}, u32[]{:S(2)}) collective-permute-start(bf16[96,768]{1,0:T(8,128)(2,1)S(1)} %collective-permute-done.29.refs_1_), channel_id=1, source_target_pairs={{0,8},{8,0},{16,24},{24,16},{1,9},{9,1},{17,25},{25,17},{2,10},{10... | collective-permute-start | bytes 442376 | tf_op jit(solution)/shard_map/ppermute | solution.py:534
  168.9 14.9 %collective-permute-start.41 = (bf16[96,768]{1,0:T(8,128)(2,1)S(1)}, bf16[96,768]{1,0:T(8,128)(2,1)S(1)}, u32[]{:S(2)}, u32[]{:S(2)}) collective-permute-start(bf16[96,768]{1,0:T(8,128)(2,1)S(1)} %collective-permute-done.34.refs_3_), channel_id=1, source_target_pairs={{0,4},{4,0},{1,5},{5,1},{2,6},{6,2},{3,7},{7,3},{8,12},{12,8},{9,1... | collective-permute-start | bytes 442376 | tf_op jit(solution)/shard_map/ppermute | solution.py:534
  169.6 11.9 %collective-permute-start.40 = (bf16[128,512]{1,0:T(8,128)(2,1)S(1)}, bf16[128,512]{1,0:T(8,128)(2,1)S(1)}, u32[]{:S(2)}, u32[]{:S(2)}) collective-permute-start(bf16[128,512]{1,0:T(8,128)(2,1)S(1)} %slice.93), channel_id=1, source_target_pairs={{0,16},{8,24},{16,0},{24,8},{1,17},{9,25},{17,1},{25,9},{2,18},{10... | collective-permute-start | bytes 393224 | tf_op jit(solution)/shard_map/ppermute | solution.py:534
  195.8 10.7 %collective-permute-start.50 = (bf16[128,512]{1,0:T(8,128)(2,1)S(1)}, bf16[128,512]{1,0:T(8,128)(2,1)S(1)}, u32[]{:S(2)}, u32[]{:S(2)}) collective-permute-start(bf16[128,512]{1,0:T(8,128)(2,1)S(1)} %collective-permute-done.46.refs_9_), channel_id=1, source_target_pairs={{0,4},{4,0},{1,5},{5,1},{2,6},{6,2},{3,7},{7,3},{8,12},{12,8},{9,1... | collective-permute-start | bytes 393224 | tf_op jit(solution)/shard_map/ppermute | solution.py:534
  (52 other events, 427.0 us)

commit v13 on v10

--- a/solution.py
+++ b/solution.py
@@ -18,7 +18,7 @@
 CHUNKS = 2
 TABLE = 6
 ROWS = (0, 2, 1, 3)
-LIMIT = 40 * 2**20
+LIMIT = 28 * 2**20
 HIGH = 56 * 2**20
 VMEM = pl.BlockSpec(memory_space=pltpu.VMEM)
 SMEM = pl.BlockSpec(memory_space=pltpu.SMEM)

time: 214 us -> 215 us (level)
  no operation moved by 1% of the time
where the time goes in v13:
time: 215 us; the launch traced here: 214 us
  waiting for transfers between devices  96.2 us (45%)
  Pallas kernels  45.6 us (21%)
  starting transfers between devices  45.4 us (21%)
  local copies, waits for them, and re-layouts  11.9 us (6%)
  matrix products  5.6 us (3%)
  between operations  4.84 us (2%)
  other arithmetic  4.4 us (2%)
    ppermute x53, waiting for transfers between devices, swap(): return lax.ppermute(block, axis, [(i, i ^ bit) for i in range(size)])  96.2 us
    ppermute x53, starting transfers between devices, swap(): return lax.ppermute(block, axis, [(i, i ^ bit) for i in range(size)])  45.4 us
    pallas_call x4, Pallas kernels, attend_call(): pl.pallas_call(functools.partial(body, groups, units, TABLE + first), in_...  15 us
    pallas_call x3, Pallas kernels, assemble(): pl.pallas_call(functools.partial(assemble_kernel, spots, chunks), in_spec...  10.3 us
    unnamed x49, local copies, waits for them, and re-layouts  6.17 us
    pallas_call x1, Pallas kernels, hidden_rows(): pl.pallas_call(hidden_kernel, in_specs=[VMEM] * 3 + [ANY] * 2 + [HBM], ou...  4.46 us
  transfers between devices with their start and end apart: 53, of which 30 were waited for; matrix products, arithmetic and copies ran while one was open for 7% of the time, Pallas kernels for 12%

profile of v13, /device:TPU:0, one launch (start us, length us, event | category | flops | bytes accessed | tf_op | source)
XLA Modules:
  0.0 213.9 jit_solution(15832260327334617550)
XLA Ops:
  0.7 3.0 %collective-permute-start.3 = (bf16[384,1536]{1,0:T(8,128)(2,1)}, bf16[384,1536]{1,0:T(8,128)(2,1)}, u32[]{:S(2)}, u32[]{:S(2)}) collective-permute-start(bf16[384,1536]{1,0:T(8,128)(2,1)} %w0.1), channel_id=1, source_target_pairs={{0,2},{1,3},{2,0},{3,1},{4,6},{5,7},{6,4},{7,5},{8,10},{9,11},{10,... | collective-permute-start | bytes 3538952 | tf_op jit(solution)/shard_map/ppermute | solution.py:534
  3.7 3.5 %first_projection.1 = (bf16[2,512,128]{2,1,0:T(8,128)(2,1)}, f32[512,128]{1,0:T(8,128)}) custom-call(bf16[512,1536]{1,0:T(8,128)(2,1)} %bitcast.30, bf16[2,1536,128]{2,1,0:T(8,128)(2,1)} %w_hbm.2), custom_call_target="tpu_custom_call" | custom-call | flops 402653184 | bytes 1572864 | tf_op jit(solution)/shard_map/first_projection/pallas_call | solution.py:77
  22.6 4.1 %collective-permute-done.1.refs_2_ = bf16[2,512,128]{2,1,0:T(8,128)(2,1)S(1)} collective-permute-done((bf16[2,512,128]{2,1,0:T(8,128)(2,1)S(1)}, bf16[2,512,128]{2,1,0:T(8,128)(2,1)S(1)}, u32[]{:S(2)}, u32[]{:S(2)}) %collective-permute-start.1) | collective-permute-done | bytes 262176 | tf_op jit(solution)/shard_map/ppermute | solution.py:534
  26.7 3.6 %attend_open.2 = (f32[512,768]{1,0:T(8,128)S(1)}, f32[512,384]{1,0:T(8,128)S(1)}) custom-call(s32[10]{0:T(128)S(1)} %stack.39.left_ref.place_ref, bf16[512,384]{1,0:T(8,128)(2,1)S(1)} %query_projection.1.q_ref, bf16[2,512,128]{2,1,0:T(8,128)(2,1)S(1)} %copy-done.16, bf16[2,512,128]{2,1,0:T(8,128)(2,1)S(1)} %collective-permute-done.refs_1_, ...), custom_call_target="tpu_custom_call" | custom-call | flops 7247757312 | bytes 786432 | tf_op jit(solution)/shard_map/attend_open/pallas_call | solution.py:219
  36.8 3.1 %near_rows.1.sum_ref = f32[512,1536]{1,0:T(8,128)S(1)} custom-call(bf16[512,1536]{1,0:T(8,128)(2,1)S(1)} %bitcast.32, bf16[512,384]{1,0:T(8,128)(2,1)S(1)} %attend_close.2.t0, bf16[512,384]{1,0:T(8,128)(2,1)S(1)} %collective-permute-done.5.t1, bf16[384,1536]{1,0:T(8,128)(2,1)} %w0.1, bf16[384,1536]{1,0:T(8,128)(2,1)} %collective-permute-done.6.w1), custom_call_target="tpu_custom_call" | custom-call | flops 1207959552 | bytes 2359296 | tf_op jit(solution)/shard_map/near_rows/pallas_call | solution.py:249
  40.0 5.4 %collective-permute-done.4.t2 = bf16[512,384]{1,0:T(8,128)(2,1)S(1)} collective-permute-done((bf16[512,384]{1,0:T(8,128)(2,1)S(1)}, bf16[512,384]{1,0:T(8,128)(2,1)S(1)}, u32[]{:S(2)}, u32[]{:S(2)}) %collective-permute-start.4) | collective-permute-done | bytes 393248 | tf_op jit(solution)/shard_map/ppermute | solution.py:534
  47.1 4.5 %hidden_rows.1 = (bf16[512,1536]{1,0:T(8,128)(2,1)S(1)}, bf16[512,512]{1,0:T(8,128)(2,1)}) custom-call(f32[512,1536]{1,0:T(8,128)S(1)} %near_rows.1.sum_ref, bf16[512,384]{1,0:T(8,128)(2,1)S(1)} %collective-permute-done.4.t2, bf16[512,384]{1,0:T(8,128)(2,1)S(1)} %collective-permute-done.7.t3, bf16[384,1536]{1,0:T(8,128)(2,1)} %collective-permute-done.3.w2, ...), custom_call_target="tpu_custom_call" | custom-call | flops 2415919104 | bytes 4718592 | tf_op jit(solution)/shard_map/hidden_rows/pallas_call | solution.py:287
  53.5 13.5 %collective-permute-done.10.e2 = bf16[512,512]{1,0:T(8,128)(2,1)} collective-permute-done((bf16[512,512]{1,0:T(8,128)(2,1)}, bf16[512,512]{1,0:T(8,128)(2,1)}, u32[]{:S(2)}, u32[]{:S(2)}) %collective-permute-start.10) | collective-permute-done | bytes 524320 | tf_op jit(solution)/shard_map/ppermute | solution.py:534
  69.2 2.7 %join_rows.1 = (bf16[2,512,128]{2,1,0:T(8,128)(2,1)S(1)}, f32[512,128]{1,0:T(8,128)S(1)}, bf16[512,2048]{1,0:T(8,128)(2,1)S(1)}) custom-call(s32[10]{0:T(128)S(1)} %stack.39.left_ref.place_ref, bf16[512,512]{1,0:T(8,128)(2,1)} %get-tuple-element.88.e0, bf16[512,512]{1,0:T(8,128)(2,1)} %collective-permute-done.9.e1, ...), custom_call_target="tpu_custom_call" | custom-call | flops 536870912 | bytes 4194304 | tf_op jit(solution)/shard_map/join_rows/pallas_call | solution.py:340
  82.8 4.5 %collective-permute-done.12.refs_1_ = bf16[2,512,128]{2,1,0:T(8,128)(2,1)S(1)} collective-permute-done((bf16[2,512,128]{2,1,0:T(8,128)(2,1)S(1)}, bf16[2,512,128]{2,1,0:T(8,128)(2,1)S(1)}, u32[]{:S(2)}, u32[]{:S(2)}) %collective-permute-start.12) | collective-permute-done | bytes 262176 | tf_op jit(solution)/shard_map/ppermute | solution.py:534
  87.3 2.7 %collective-permute-done.13.refs_2_ = bf16[2,512,128]{2,1,0:T(8,128)(2,1)S(1)} collective-permute-done((bf16[2,512,128]{2,1,0:T(8,128)(2,1)S(1)}, bf16[2,512,128]{2,1,0:T(8,128)(2,1)S(1)}, u32[]{:S(2)}, u32[]{:S(2)}) %collective-permute-start.13) | collective-permute-done | bytes 262176 | tf_op jit(solution)/shard_map/ppermute | solution.py:534
  90.0 4.8 %attend_open.3 = (f32[512,1024]{1,0:T(8,128)S(1)}, f32[512,512]{1,0:T(8,128)S(1)}) custom-call(s32[10]{0:T(128)S(1)} %stack.39.left_ref.place_ref, bf16[512,512]{1,0:T(8,128)(2,1)S(1)} %fusion.3.q_ref, bf16[2,512,128]{2,1,0:T(8,128)(2,1)S(1)} %get-tuple-element.98.refs_0_, bf16[2,512,128]{2,1,0:T(8,128)(2,1)S(1)} %collective-permute-done.12.refs_1_, ...), custom_call_target="tpu_custom_call" | custom-call | flops 9663676416 | bytes 1048576 | tf_op jit(solution)/shard_map/attend_open/pallas_call | solution.py:219
  97.0 4.1 %attend_close.3.att_ref = bf16[512,512]{1,0:T(8,128)(2,1)} custom-call(s32[10]{0:T(128)S(1)} %stack.39.left_ref.place_ref, bf16[512,512]{1,0:T(8,128)(2,1)S(1)} %fusion.3.q_ref, f32[512,1024]{1,0:T(8,128)S(1)} %get-tuple-element.106.wide_ref, f32[512,512]{1,0:T(8,128)S(1)} %get-tuple-element.107.top_ref, bf16[2,512,128]{2,1,0:T(8,128)(2,1)S(1)} %collective-permute-done.15.refs_0_), custom_call_target="tpu_custom_call" | custom-call | flops 134217728 | bytes 1048576 | tf_op jit(solution)/shard_map/attend_close/pallas_call | solution.py:219
  109.3 9.9 %collective-permute-done.27 = bf16[512,512]{1,0:T(8,128)(2,1)} collective-permute-done((bf16[512,512]{1,0:T(8,128)(2,1)}, bf16[512,512]{1,0:T(8,128)(2,1)}, u32[]{:S(2)}, u32[]{:S(2)}) %collective-permute-start.27) | collective-permute-done | bytes 524320 | tf_op jit(solution)/shard_map/ppermute | solution.py:534
  131.6 8.6 %collective-permute-done.20 = bf16[96,768]{1,0:T(8,128)(2,1)S(1)} collective-permute-done((bf16[96,768]{1,0:T(8,128)(2,1)S(1)}, bf16[96,768]{1,0:T(8,128)(2,1)S(1)}, u32[]{:S(2)}, u32[]{:S(2)}) %collective-permute-start.20) | collective-permute-done | bytes 147488 | tf_op jit(solution)/shard_map/ppermute | solution.py:534
  149.1 2.7 %collective-permute-done.29.refs_1_ = bf16[96,768]{1,0:T(8,128)(2,1)S(1)} collective-permute-done((bf16[96,768]{1,0:T(8,128)(2,1)S(1)}, bf16[96,768]{1,0:T(8,128)(2,1)S(1)}, u32[]{:S(2)}, u32[]{:S(2)}) %collective-permute-start.29) | collective-permute-done | bytes 147488 | tf_op jit(solution)/shard_map/ppermute | solution.py:534
  151.8 5.6 %collective-permute-done.28 = bf16[256,512]{1,0:T(8,128)(2,1)S(1)} collective-permute-done((bf16[256,512]{1,0:T(8,128)(2,1)S(1)}, bf16[256,512]{1,0:T(8,128)(2,1)S(1)}, u32[]{:S(2)}, u32[]{:S(2)}) %collective-permute-start.28) | collective-permute-done | bytes 262176 | tf_op jit(solution)/shard_map/ppermute | solution.py:534
  162.0 7.0 %collective-permute-done.32 = bf16[256,512]{1,0:T(8,128)(2,1)S(1)} collective-permute-done((bf16[256,512]{1,0:T(8,128)(2,1)S(1)}, bf16[256,512]{1,0:T(8,128)(2,1)S(1)}, u32[]{:S(2)}, u32[]{:S(2)}) %collective-permute-start.32) | collective-permute-done | bytes 262176 | tf_op jit(solution)/shard_map/ppermute | solution.py:534
  174.4 2.8 %collective-permute-start.37 = (bf16[128,512]{1,0:T(8,128)(2,1)S(1)}, bf16[128,512]{1,0:T(8,128)(2,1)S(1)}, u32[]{:S(2)}, u32[]{:S(2)}) collective-permute-start(bf16[128,512]{1,0:T(8,128)(2,1)S(1)} %fusion.17.refs_0_), channel_id=1, source_target_pairs={{0,16},{8,24},{16,0},{24,8},{1,17},{9,25},{17,1},{25,9},{2,18},{10... | collective-permute-start | bytes 393224 | tf_op jit(solution)/shard_map/ppermute | solution.py:534
  177.3 4.9 %collective-permute-done.39 = bf16[128,512]{1,0:T(8,128)(2,1)S(1)} collective-permute-done((bf16[128,512]{1,0:T(8,128)(2,1)S(1)}, bf16[128,512]{1,0:T(8,128)(2,1)S(1)}, u32[]{:S(2)}, u32[]{:S(2)}) %collective-permute-start.39) | collective-permute-done | bytes 131104 | tf_op jit(solution)/shard_map/ppermute | solution.py:534
  189.8 3.6 %assemble.3 = f32[384,1536]{1,0:T(8,128)} custom-call(s32[10]{0:T(128)S(1)} %stack.39.left_ref.place_ref, bf16[96,768]{1,0:T(8,128)(2,1)S(1)} %fusion.15.refs_0_, bf16[96,768]{1,0:T(8,128)(2,1)S(1)} %collective-permute-done.29.refs_1_, bf16[96,768]{1,0:T(8,128)(2,1)S(1)} %collective-permute-done.33.refs_2_, ...), custom_call_target="tpu_custom_call" | custom-call | flops 589824 | bytes 3538944 | tf_op jit(solution)/shard_map/assemble/pallas_call | solution.py:512
  198.5 3.6 %assemble.4.refs_7_ = f32[512,2048]{1,0:T(8,128)} custom-call(s32[10]{0:T(128)S(1)} %stack.39.left_ref.place_ref, bf16[128,512]{1,0:T(8,128)(2,1)S(1)} %fusion.17.refs_0_, bf16[128,512]{1,0:T(8,128)(2,1)S(1)} %collective-permute-done.37.refs_1_, bf16[128,512]{1,0:T(8,128)(2,1)S(1)} %collective-permute-done.36.refs_2_, ...), custom_call_target="tpu_custom_call" | custom-call | flops 1048576 | bytes 6291456 | tf_op jit(solution)/shard_map/assemble/pallas_call | solution.py:512
  204.2 2.7 %collective-permute-done.47.refs_1_ = bf16[128,512]{1,0:T(8,128)(2,1)S(1)} collective-permute-done((bf16[128,512]{1,0:T(8,128)(2,1)S(1)}, bf16[128,512]{1,0:T(8,128)(2,1)S(1)}, u32[]{:S(2)}, u32[]{:S(2)}) %collective-permute-start.47) | collective-permute-done | bytes 131104 | tf_op jit(solution)/shard_map/ppermute | solution.py:534
  210.6 3.1 %assemble.5 = f32[512,2048]{1,0:T(8,128)} custom-call(s32[10]{0:T(128)S(1)} %stack.39.left_ref.place_ref, bf16[128,512]{1,0:T(8,128)(2,1)S(1)} %collective-permute-done.46.refs_0_, bf16[128,512]{1,0:T(8,128)(2,1)S(1)} %collective-permute-done.47.refs_1_, bf16[128,512]{1,0:T(8,128)(2,1)S(1)} %collective-permute-done.48.refs_2_, ...), custom_call_target="tpu_custom_call", output_to_operand_aliasing={{}: (8, {})} | custom-call | flops 1048576 | bytes 6291456 | tf_op jit(solution)/shard_map/assemble/pallas_call | solution.py:512
  (188 shorter events, 95.0 us)
Async XLA Ops:
  0.7 33.0 %collective-permute-start.3 = (bf16[384,1536]{1,0:T(8,128)(2,1)}, bf16[384,1536]{1,0:T(8,128)(2,1)}, u32[]{:S(2)}, u32[]{:S(2)}) collective-permute-start(bf16[384,1536]{1,0:T(8,128)(2,1)} %w0.1), channel_id=1, source_target_pairs={{0,2},{1,3},{2,0},{3,1},{4,6},{5,7},{6,4},{7,5},{8,10},{9,11},{10,... | collective-permute-start | bytes 3538952 | tf_op jit(solution)/shard_map/ppermute | solution.py:534
  7.2 14.7 %collective-permute-start = (bf16[2,512,128]{2,1,0:T(8,128)(2,1)}, bf16[2,512,128]{2,1,0:T(8,128)(2,1)S(1)}, u32[]{:S(2)}, u32[]{:S(2)}) collective-permute-start(bf16[2,512,128]{2,1,0:T(8,128)(2,1)} %get-tuple-element.81.refs_0_), channel_id=1, source_target_pairs={{0,16},{8,24},{16,0},{24,8},{1,17},{9,25},{17,1},{25,9},{2,18},{10... | collective-permute-start | bytes 786440 | tf_op jit(solution)/shard_map/ppermute | solution.py:534
  13.4 13.2 %collective-permute-start.1 = (bf16[2,512,128]{2,1,0:T(8,128)(2,1)S(1)}, bf16[2,512,128]{2,1,0:T(8,128)(2,1)S(1)}, u32[]{:S(2)}, u32[]{:S(2)}) collective-permute-start(bf16[2,512,128]{2,1,0:T(8,128)(2,1)S(1)} %copy-done.16), channel_id=1, source_target_pairs={{0,8},{8,0},{16,24},{24,16},{1,9},{9,1},{17,25},{25,17},{2,10},{10... | collective-permute-start | bytes 786440 | tf_op jit(solution)/shard_map/ppermute | solution.py:534
  15.1 19.9 %collective-permute-start.6 = (bf16[384,1536]{1,0:T(8,128)(2,1)}, bf16[384,1536]{1,0:T(8,128)(2,1)}, u32[]{:S(2)}, u32[]{:S(2)}) collective-permute-start(bf16[384,1536]{1,0:T(8,128)(2,1)} %w0.1), channel_id=1, source_target_pairs={{0,1},{1,0},{2,3},{3,2},{4,5},{5,4},{6,7},{7,6},{8,9},{9,8},{10,11... | collective-permute-start | bytes 3538952 | tf_op jit(solution)/shard_map/ppermute | solution.py:534
  33.7 13.4 %collective-permute-start.8 = (bf16[384,1536]{1,0:T(8,128)(2,1)}, bf16[384,1536]{1,0:T(8,128)(2,1)S(1)}, u32[]{:S(2)}, u32[]{:S(2)}) collective-permute-start(bf16[384,1536]{1,0:T(8,128)(2,1)} %collective-permute-done.3.w2), channel_id=1, source_target_pairs={{0,1},{1,0},{2,3},{3,2},{4,5},{5,4},{6,7},{7,6},{8,9},{9,8},{10,11... | collective-permute-start | bytes 3538952 | tf_op jit(solution)/shard_map/ppermute | solution.py:534
  52.7 14.3 %collective-permute-start.10 = (bf16[512,512]{1,0:T(8,128)(2,1)}, bf16[512,512]{1,0:T(8,128)(2,1)}, u32[]{:S(2)}, u32[]{:S(2)}) collective-permute-start(bf16[512,512]{1,0:T(8,128)(2,1)} %get-tuple-element.88.e0), channel_id=1, source_target_pairs={{0,2},{1,3},{2,0},{3,1},{4,6},{5,7},{6,4},{7,5},{8,10},{9,11},{10,... | collective-permute-start | bytes 1572872 | tf_op jit(solution)/shard_map/ppermute | solution.py:534
  53.4 15.0 %collective-permute-start.9 = (bf16[512,512]{1,0:T(8,128)(2,1)}, bf16[512,512]{1,0:T(8,128)(2,1)}, u32[]{:S(2)}, u32[]{:S(2)}) collective-permute-start(bf16[512,512]{1,0:T(8,128)(2,1)} %get-tuple-element.88.e0), channel_id=1, source_target_pairs={{0,1},{1,0},{2,3},{3,2},{4,5},{5,4},{6,7},{7,6},{8,9},{9,8},{10,11... | collective-permute-start | bytes 1572872 | tf_op jit(solution)/shard_map/ppermute | solution.py:534
  72.5 14.8 %collective-permute-start.12 = (bf16[2,512,128]{2,1,0:T(8,128)(2,1)S(1)}, bf16[2,512,128]{2,1,0:T(8,128)(2,1)S(1)}, u32[]{:S(2)}, u32[]{:S(2)}) collective-permute-start(bf16[2,512,128]{2,1,0:T(8,128)(2,1)S(1)} %get-tuple-element.98.refs_0_), channel_id=1, source_target_pairs={{0,16},{8,24},{16,0},{24,8},{1,17},{9,25},{17,1},{25,9},{2,18},{10... | collective-permute-start | bytes 786440 | tf_op jit(solution)/shard_map/ppermute | solution.py:534
  76.3 13.7 %collective-permute-start.13 = (bf16[2,512,128]{2,1,0:T(8,128)(2,1)S(1)}, bf16[2,512,128]{2,1,0:T(8,128)(2,1)S(1)}, u32[]{:S(2)}, u32[]{:S(2)}) collective-permute-start(bf16[2,512,128]{2,1,0:T(8,128)(2,1)S(1)} %get-tuple-element.98.refs_0_), channel_id=1, source_target_pairs={{0,8},{8,0},{16,24},{24,16},{1,9},{9,1},{17,25},{25,17},{2,10},{10... | collective-permute-start | bytes 786440 | tf_op jit(solution)/shard_map/ppermute | solution.py:534
  81.2 14.9 %collective-permute-start.14 = (bf16[384,768]{1,0:T(8,128)(2,1)S(1)}, bf16[384,768]{1,0:T(8,128)(2,1)S(1)}, u32[]{:S(2)}, u32[]{:S(2)}) collective-permute-start(bf16[384,768]{1,0:T(8,128)(2,1)S(1)} %convolution_convert_fusion), channel_id=1, source_target_pairs={{0,4},{4,0},{1,5},{5,1},{2,6},{6,2},{3,7},{7,3},{8,12},{12,8},{9,1... | collective-permute-start | bytes 1769480 | tf_op jit(solution)/shard_map/ppermute | solution.py:534
  104.5 14.7 %collective-permute-start.27 = (bf16[512,512]{1,0:T(8,128)(2,1)}, bf16[512,512]{1,0:T(8,128)(2,1)}, u32[]{:S(2)}, u32[]{:S(2)}) collective-permute-start(bf16[512,512]{1,0:T(8,128)(2,1)} %attend_close.3.att_ref), channel_id=1, source_target_pairs={{0,4},{4,0},{1,5},{5,1},{2,6},{6,2},{3,7},{7,3},{8,12},{12,8},{9,1... | collective-permute-start | bytes 1572872 | tf_op jit(solution)/shard_map/ppermute | solution.py:534
  108.1 14.3 %collective-permute-start.17 = (bf16[128,2048]{1,0:T(8,128)(2,1)}, bf16[128,2048]{1,0:T(8,128)(2,1)}, u32[]{:S(2)}, u32[]{:S(2)}) collective-permute-start(bf16[128,2048]{1,0:T(8,128)(2,1)} %add_convert_fusion), channel_id=1, source_target_pairs={{0,2},{1,3},{2,0},{3,1},{4,6},{5,7},{6,4},{7,5},{8,10},{9,11},{10,... | collective-permute-start | bytes 1572872 | tf_op jit(solution)/shard_map/ppermute | solution.py:534
  108.9 11.5 %collective-permute-start.18 = (bf16[192,768]{1,0:T(8,128)(2,1)S(1)}, bf16[192,768]{1,0:T(8,128)(2,1)}, u32[]{:S(2)}, u32[]{:S(2)}) collective-permute-start(bf16[192,768]{1,0:T(8,128)(2,1)S(1)} %get-tuple-element.111), channel_id=1, source_target_pairs={{0,8},{8,0},{16,24},{24,16},{1,9},{9,1},{17,25},{25,17},{2,10},{10... | collective-permute-start | bytes 884744 | tf_op jit(solution)/shard_map/ppermute | solution.py:534
  125.7 14.5 %collective-permute-start.21 = (bf16[128,1024]{1,0:T(8,128)(2,1)S(1)}, bf16[128,1024]{1,0:T(8,128)(2,1)S(1)}, u32[]{:S(2)}, u32[]{:S(2)}) collective-permute-start(bf16[128,1024]{1,0:T(8,128)(2,1)S(1)} %get-tuple-element.116), channel_id=1, source_target_pairs={{0,6},{1,7},{2,4},{3,5},{4,2},{5,3},{6,0},{7,1},{8,14},{9,15},{10,... | collective-permute-start | bytes 786440 | tf_op jit(solution)/shard_map/ppermute | solution.py:534
  127.4 12.7 %collective-permute-start.19 = (bf16[128,1024]{1,0:T(8,128)(2,1)S(1)}, bf16[128,1024]{1,0:T(8,128)(2,1)S(1)}, u32[]{:S(2)}, u32[]{:S(2)}) collective-permute-start(bf16[128,1024]{1,0:T(8,128)(2,1)S(1)} %get-tuple-element.116), channel_id=1, source_target_pairs={{0,4},{4,0},{1,5},{5,1},{2,6},{6,2},{3,7},{7,3},{8,12},{12,8},{9,1... | collective-permute-start | bytes 786440 | tf_op jit(solution)/shard_map/ppermute | solution.py:534
  128.0 14.3 %collective-permute-start.25 = (bf16[128,1024]{1,0:T(8,128)(2,1)S(1)}, bf16[128,1024]{1,0:T(8,128)(2,1)S(1)}, u32[]{:S(2)}, u32[]{:S(2)}) collective-permute-start(bf16[128,1024]{1,0:T(8,128)(2,1)S(1)} %get-tuple-element.122), channel_id=1, source_target_pairs={{0,1},{1,0},{2,3},{3,2},{4,5},{5,4},{6,7},{7,6},{8,9},{9,8},{10,11... | collective-permute-start | bytes 786440 | tf_op jit(solution)/shard_map/ppermute | solution.py:534
  128.0 14.2 %collective-permute-start.24 = (bf16[128,1024]{1,0:T(8,128)(2,1)S(1)}, bf16[128,1024]{1,0:T(8,128)(2,1)S(1)}, u32[]{:S(2)}, u32[]{:S(2)}) collective-permute-start(bf16[128,1024]{1,0:T(8,128)(2,1)S(1)} %get-tuple-element.122), channel_id=1, source_target_pairs={{0,2},{1,3},{2,0},{3,1},{4,6},{5,7},{6,4},{7,5},{8,10},{9,11},{10,... | collective-permute-start | bytes 786440 | tf_op jit(solution)/shard_map/ppermute | solution.py:534
  145.3 12.1 %collective-permute-start.28 = (bf16[256,512]{1,0:T(8,128)(2,1)S(1)}, bf16[256,512]{1,0:T(8,128)(2,1)S(1)}, u32[]{:S(2)}, u32[]{:S(2)}) collective-permute-start(bf16[256,512]{1,0:T(8,128)(2,1)S(1)} %get-tuple-element.125), channel_id=1, source_target_pairs={{0,8},{8,0},{16,24},{24,16},{1,9},{9,1},{17,25},{25,17},{2,10},{10... | collective-permute-start | bytes 786440 | tf_op jit(solution)/shard_map/ppermute | solution.py:534
  146.8 15.2 %collective-permute-start.33 = (bf16[96,768]{1,0:T(8,128)(2,1)S(1)}, bf16[96,768]{1,0:T(8,128)(2,1)S(1)}, u32[]{:S(2)}, u32[]{:S(2)}) collective-permute-start(bf16[96,768]{1,0:T(8,128)(2,1)S(1)} %fusion.15.refs_0_), channel_id=1, source_target_pairs={{0,8},{8,0},{16,24},{24,16},{1,9},{9,1},{17,25},{25,17},{2,10},{10... | collective-permute-start | bytes 442376 | tf_op jit(solution)/shard_map/ppermute | solution.py:534
  148.0 21.0 %collective-permute-start.32 = (bf16[256,512]{1,0:T(8,128)(2,1)S(1)}, bf16[256,512]{1,0:T(8,128)(2,1)S(1)}, u32[]{:S(2)}, u32[]{:S(2)}) collective-permute-start(bf16[256,512]{1,0:T(8,128)(2,1)S(1)} %get-tuple-element.129), channel_id=1, source_target_pairs={{0,8},{8,0},{16,24},{24,16},{1,9},{9,1},{17,25},{25,17},{2,10},{10... | collective-permute-start | bytes 786440 | tf_op jit(solution)/shard_map/ppermute | solution.py:534
  157.4 11.6 %collective-permute-start.35 = (bf16[96,768]{1,0:T(8,128)(2,1)S(1)}, bf16[96,768]{1,0:T(8,128)(2,1)S(1)}, u32[]{:S(2)}, u32[]{:S(2)}) collective-permute-start(bf16[96,768]{1,0:T(8,128)(2,1)S(1)} %collective-permute-done.29.refs_1_), channel_id=1, source_target_pairs={{0,4},{4,0},{1,5},{5,1},{2,6},{6,2},{3,7},{7,3},{8,12},{12,8},{9,1... | collective-permute-start | bytes 442376 | tf_op jit(solution)/shard_map/ppermute | solution.py:534
  158.0 13.6 %collective-permute-start.34 = (bf16[96,768]{1,0:T(8,128)(2,1)S(1)}, bf16[96,768]{1,0:T(8,128)(2,1)S(1)}, u32[]{:S(2)}, u32[]{:S(2)}) collective-permute-start(bf16[96,768]{1,0:T(8,128)(2,1)S(1)} %collective-permute-done.29.refs_1_), channel_id=1, source_target_pairs={{0,8},{8,0},{16,24},{24,16},{1,9},{9,1},{17,25},{25,17},{2,10},{10... | collective-permute-start | bytes 442376 | tf_op jit(solution)/shard_map/ppermute | solution.py:534
  171.7 13.3 %collective-permute-start.40 = (bf16[96,768]{1,0:T(8,128)(2,1)S(1)}, bf16[96,768]{1,0:T(8,128)(2,1)S(1)}, u32[]{:S(2)}, u32[]{:S(2)}) collective-permute-start(bf16[96,768]{1,0:T(8,128)(2,1)S(1)} %collective-permute-done.33.refs_2_), channel_id=1, source_target_pairs={{0,4},{4,0},{1,5},{5,1},{2,6},{6,2},{3,7},{7,3},{8,12},{12,8},{9,1... | collective-permute-start | bytes 442376 | tf_op jit(solution)/shard_map/ppermute | solution.py:534
  172.3 12.7 %collective-permute-start.41 = (bf16[96,768]{1,0:T(8,128)(2,1)S(1)}, bf16[96,768]{1,0:T(8,128)(2,1)S(1)}, u32[]{:S(2)}, u32[]{:S(2)}) collective-permute-start(bf16[96,768]{1,0:T(8,128)(2,1)S(1)} %collective-permute-done.34.refs_3_), channel_id=1, source_target_pairs={{0,4},{4,0},{1,5},{5,1},{2,6},{6,2},{3,7},{7,3},{8,12},{12,8},{9,1... | collective-permute-start | bytes 442376 | tf_op jit(solution)/shard_map/ppermute | solution.py:534
  (52 other events, 435.7 us)
